TPU v7x, 256 devices: a whole 4x4x8 slice. The times are simulated.
256 devices in a mesh: ctx: 16 (over z, x_lo), tp: 16 (over x_hi, y, core).
Axes of the slice: x: 4 (x_hi: 2, x_lo: 2; x = x_hi * 2 + x_lo), y: 4, z: 8, core: 2. Of those that a mesh axis runs over, the one named last changes fastest.
Arguments:
- queries: bfloat16 [4096, 16384], P('ctx', 'tp'), may hold values from -96 to 96
- keys_values: bfloat16 [2, 4096, 1024], P(None, 'ctx'), may hold values from -4 to 4
- out_grad: bfloat16 [4096, 16384], P(('ctx', 'tp')), may hold values from -6 to 6
- place: int32 [4096], P('ctx'), may hold values from 0 to 4095, as said below
- segments: int32 [4096], replicated, may hold values from 0 to 3, never falling along the last dimension, each value on 1 to 2304 neighbouring positions
- allow: int32 [32, 32], replicated, may hold values from 0 to 1, as said below
Outputs:
- grad_q: bfloat16 [4096, 16384], P('ctx', 'tp')
- key_value_gradient: bfloat16 [2, 4096, 1024], P(None, ('ctx', 'tp'))
Inputs may be any that keep to these rules, and one draw needn't show every extreme that they name: place is a permutation of the packed positions; position p lies on context shard p // 256; the rows of one generator shard send at most 32 rows to one context shard, some pair sends exactly 32, and every context shard receives 256 rows. allow[i, i] is 1 and allow[i, j] is 0 for j > i.
All inputs are finite; a program needn't handle non-finite values.
Results may differ from a plain program's by a relative error of at most 0.019.
Values may be sent and summed in bfloat16 or wider, within the bound.
No kernel may reach another device: no remote copies, remote signals or barrier semaphores. Data moves between devices by JAX's collectives and lax.ppermute only.
A program may use at most 128 MiB of HBM per device.

v0:
```python
import math

import jax
import jax.numpy as jnp
from jax import lax
from jax.sharding import PartitionSpec as P

QUERY_HEAD_COUNT = 128
KEY_VALUE_HEADS = 8
HEAD_SIZE = 128
BLK = 128


NEG_FILL = -1e30


def visible(query_pos, query_seg, query_allow, key_pos, key_seg):
    same_doc = query_seg[:, None] == key_seg[None, :]
    causal = key_pos[None, :] <= query_pos[:, None]
    block_ok = jnp.take(query_allow, key_pos // BLK, axis=1) > 0
    return same_doc & causal & block_ok


def blocked(count, widest, step_fn, running):

    def turn_once(turn_index, inner_state):
        return step_fn(inner_state, turn_index * widest, widest)

    return lax.fori_loop(0, count // widest, turn_once, running)


def split_heads(key_block, kv_local):
    block_rows = key_block.shape[0]
    half_cols = kv_local * HEAD_SIZE
    key_heads = key_block[:, :half_cols].reshape(block_rows, kv_local, HEAD_SIZE).transpose(1, 0, 2)
    value_heads = (
        key_block[:, half_cols:].reshape(block_rows, kv_local, HEAD_SIZE).transpose(1, 0, 2)
    )
    return (key_heads, value_heads)


def group_heads(row_matrix, kv_local):
    count_of_rows = row_matrix.shape[0]
    queries_per_key_head = row_matrix.shape[1] // (kv_local * HEAD_SIZE)
    return row_matrix.reshape(count_of_rows, kv_local, queries_per_key_head, HEAD_SIZE).transpose(
        1, 2, 0, 3
    )


def flat_heads(head_grads):
    return head_grads.transpose(1, 0, 2).reshape(
        head_grads.shape[1], head_grads.shape[0] * HEAD_SIZE
    )


def masked_scores(query_heads, key_heads, visible_mask, score_scale):
    scores = (
        jnp.einsum("ghqd,gkd->ghqk", query_heads, key_heads, preferred_element_type=jnp.float32)
        * score_scale
    )
    return jnp.where(visible_mask[None, None], scores, NEG_FILL)


def forward_tile(running, query_heads, key_heads, value_heads, visible_mask, score_scale):
    run_top, run_total, run_acc = running
    scores = masked_scores(query_heads, key_heads, visible_mask, score_scale)
    new_top = jnp.maximum(run_top, jnp.max(scores, axis=-1))
    weights = jnp.where(visible_mask[None, None], jnp.exp(scores - new_top[..., None]), 0.0)
    factor = jnp.exp(run_top - new_top)
    run_total = run_total * factor + jnp.sum(weights, axis=-1)
    run_acc = run_acc * factor[..., None] + jnp.einsum(
        "ghqk,gkd->ghqd", weights, value_heads.astype(jnp.float32), precision=lax.Precision.HIGHEST
    )
    return (new_top, run_total, run_acc)


def backward_tile(
    query_heads, grad_heads, log_norm, out_dot, key_heads, value_heads, visible_mask, score_scale
):
    scores = masked_scores(query_heads, key_heads, visible_mask, score_scale)
    weights = jnp.where(visible_mask[None, None], jnp.exp(scores - log_norm[..., None]), 0.0)
    weights_low = weights.astype(jnp.bfloat16)
    value_grad = jnp.einsum(
        "ghqk,ghqd->gkd", weights_low, grad_heads, preferred_element_type=jnp.float32
    )
    prob_grad = jnp.einsum(
        "ghqd,gkd->ghqk", grad_heads, value_heads, preferred_element_type=jnp.float32
    )
    score_grad = (weights * (prob_grad - out_dot[..., None])).astype(jnp.bfloat16)
    query_grad = jnp.einsum(
        "ghqk,gkd->ghqd", score_grad, key_heads, preferred_element_type=jnp.float32
    )
    key_grad = jnp.einsum(
        "ghqk,ghqd->gkd", score_grad, query_heads, preferred_element_type=jnp.float32
    )
    return (query_grad, key_grad, value_grad)


def on_device(queries, keys_values, out_grad, place, segments, allow):
    shard_count = lax.axis_size("ctx")
    count_of_rows = queries.shape[0]
    local_heads = queries.shape[1] // HEAD_SIZE
    group_head_count = QUERY_HEAD_COUNT // KEY_VALUE_HEADS
    kv_local = max(local_heads // group_head_count, 1)
    queries_per_key_head = local_heads // kv_local
    tp_index = lax.axis_index("tp")
    ctx_index = lax.axis_index("ctx")
    kv_first = tp_index * local_heads // group_head_count
    score_scale = 1.0 / math.sqrt(HEAD_SIZE)
    capacity = 2 * count_of_rows // shard_count
    kv_mine = lax.dynamic_slice_in_dim(keys_values, kv_first * HEAD_SIZE, kv_local * HEAD_SIZE, 2)
    kv_rows = jnp.concatenate([kv_mine[0], kv_mine[1]], axis=1)
    owner_shard = place // count_of_rows
    within = place - owner_shard * count_of_rows
    owner_hits = (owner_shard[:, None] == jnp.arange(shard_count, dtype=jnp.int32)[None, :]).astype(
        jnp.int32
    )
    slot_index = jnp.sum((jnp.cumsum(owner_hits, axis=0) - 1) * owner_hits, axis=1)
    q_send = (
        jnp.zeros((shard_count, capacity, queries.shape[1]), jnp.bfloat16)
        .at[owner_shard, slot_index]
        .set(queries)
    )
    kv_send = (
        jnp.zeros((shard_count, capacity, kv_rows.shape[1]), jnp.bfloat16)
        .at[owner_shard, slot_index]
        .set(kv_rows)
    )
    pos_send = (
        jnp.full((shard_count, capacity), count_of_rows, jnp.int32)
        .at[owner_shard, slot_index]
        .set(within)
    )
    q_recv, kv_recv, pos_recv = (
        lax.all_to_all(q_send, "ctx", split_axis=0, concat_axis=0, tiled=True),
        lax.all_to_all(kv_send, "ctx", split_axis=0, concat_axis=0, tiled=True),
        lax.all_to_all(pos_send, "ctx", split_axis=0, concat_axis=0, tiled=True),
    )
    landing = pos_recv.reshape(-1)
    q_packed = (
        jnp.zeros_like(queries).at[landing].set(q_recv.reshape(-1, queries.shape[1]), mode="drop")
    )
    kv_packed = (
        jnp.zeros_like(kv_rows).at[landing].set(kv_recv.reshape(-1, kv_rows.shape[1]), mode="drop")
    )
    g_local = lax.all_to_all(out_grad, "tp", split_axis=1, concat_axis=0, tiled=True)
    query_heads = group_heads(q_packed, kv_local)
    grad_heads = group_heads(g_local, kv_local)
    query_pos = ctx_index * count_of_rows + jnp.arange(count_of_rows, dtype=jnp.int32)
    query_seg = lax.dynamic_slice_in_dim(segments, ctx_index * count_of_rows, count_of_rows)
    query_allow = jnp.take(allow, query_pos // BLK, axis=0)

    def key_window(pieces, piece_start, block_offset, block_width):
        key_block = lax.dynamic_slice_in_dim(pieces, block_offset, block_width, 0)
        key_first = piece_start + block_offset
        key_pos = key_first + jnp.arange(block_width, dtype=jnp.int32)
        key_seg = lax.dynamic_slice_in_dim(segments, key_first, block_width)
        visible_mask = visible(query_pos, query_seg, query_allow, key_pos, key_seg)
        key_heads, value_heads = split_heads(key_block, kv_local)
        return (key_first, visible_mask, key_heads, value_heads)

    stat_shape = (kv_local, queries_per_key_head, count_of_rows)
    start_state = (
        jnp.full(stat_shape, NEG_FILL, jnp.float32),
        jnp.zeros(stat_shape, jnp.float32),
        jnp.zeros(stat_shape + (HEAD_SIZE,), jnp.float32),
    )
    all_keys = lax.all_gather(kv_packed, "ctx", axis=0, tiled=True)

    def step_fn(inner_state, block_offset, block_width):
        key_first, visible_mask, key_heads, value_heads = key_window(
            all_keys, 0, block_offset, block_width
        )
        return lax.cond(
            jnp.any(visible_mask),
            lambda carry_state: forward_tile(
                carry_state, query_heads, key_heads, value_heads, visible_mask, score_scale
            ),
            lambda carry_state: carry_state,
            inner_state,
        )

    run_top, run_total, run_acc = blocked(all_keys.shape[0], 512, step_fn, start_state)
    log_norm = run_top + jnp.log(run_total)
    attended = (run_acc / run_total[..., None]).astype(jnp.bfloat16)
    out_dot = jnp.sum(grad_heads.astype(jnp.float32) * attended.astype(jnp.float32), axis=-1)
    grad_start = (jnp.zeros(stat_shape + (HEAD_SIZE,), jnp.float32),)
    grad_start = grad_start + (
        jnp.zeros((2, count_of_rows * shard_count, kv_local * HEAD_SIZE), jnp.float32),
    )

    def step_fn(inner_state, block_offset, block_width):
        key_first, visible_mask, key_heads, value_heads = key_window(
            all_keys, 0, block_offset, block_width
        )

        def tile_work(carry_state):
            query_grad, key_grad, value_grad = backward_tile(
                query_heads,
                grad_heads,
                log_norm,
                out_dot,
                key_heads,
                value_heads,
                visible_mask,
                score_scale,
            )
            key_terms = jnp.stack([flat_heads(key_grad * score_scale), flat_heads(value_grad)])
            previous = lax.dynamic_slice_in_dim(carry_state[1], key_first, block_width, 1)
            return (
                carry_state[0] + query_grad,
                lax.dynamic_update_slice_in_dim(carry_state[1], previous + key_terms, key_first, 1),
            )

        return lax.cond(
            jnp.any(visible_mask), tile_work, lambda carry_state: carry_state, inner_state
        )

    grad_state = blocked(all_keys.shape[0], 512, step_fn, grad_start)
    grad_q = (
        (grad_state[0] * score_scale)
        .astype(jnp.bfloat16)
        .transpose(2, 0, 1, 3)
        .reshape(count_of_rows, local_heads * HEAD_SIZE)
    )
    owned = lax.psum_scatter(
        grad_state[1].astype(jnp.bfloat16), "ctx", scatter_dimension=1, tiled=True
    ).astype(jnp.float32)
    padded_length = jnp.zeros((2, count_of_rows, KEY_VALUE_HEADS * HEAD_SIZE), jnp.float32)
    padded_length = lax.dynamic_update_slice_in_dim(padded_length, owned, kv_first * HEAD_SIZE, 2)
    key_value_gradient = lax.psum_scatter(
        padded_length.astype(jnp.bfloat16), "tp", scatter_dimension=1, tiled=True
    )
    return (grad_q, key_value_gradient)


def solution(mesh):
    in_specs = (P("ctx", "tp"), P(None, "ctx", None), P(("ctx", "tp"), None), P("ctx"), P(), P())
    out_specs = (P("ctx", "tp"), P(None, ("ctx", "tp"), None))
    return jax.shard_map(
        on_device, mesh=mesh, in_specs=in_specs, out_specs=out_specs, check_vma=False
    )
```

profile of v0, /device:TPU:1, one launch (start us, length us, event | category | flops | bytes accessed | tf_op | source)
XLA Modules:
  0.0 577.1 jit_solution(13717886787053344139)
XLA Ops:
  9.5 35.4 %scatter_fusion = s32[16,32]{1,0:T(8,128)} fusion(s32[16,32]{1,0:T(8,128)} %broadcast_in_dim.127, s32[256]{0:T(256)S(1)} %bitcast.159, s32[256]{0:T(256)S(1)} %get-tuple-element.873), kind=kCustom, calls=%fused_computation.3 | custom fusion | bytes 5120 | tf_op jit(solution)/shard_map/scatter | solution.py:132
  44.9 10.0 %all-to-all-start = ((s32[16,1,32]{2,1,0:T(1,128)}), s32[16,1,32]{2,1,0:T(1,128)S(1)}, u32[]{:S(2)}, u32[]{:S(2)}) async-start(s32[16,1,32]{2,1,0:T(1,128)} %bitcast.29), calls=%async_computation | async-start | bytes 16384 | tf_op jit(solution)/shard_map/all_to_all | solution.py:137
  56.7 29.4 %scatter_fusion.1 = bf16[16,32,256]{2,1,0:T(8,128)(2,1)} fusion(bf16[16,32,256]{2,1,0:T(8,128)(2,1)} %broadcast_in_dim.129, s32[256]{0:T(256)S(1)} %bitcast.160, bf16[256,256]{1,0:T(8,128)(2,1)S(1)} %pad_maximum_fusion), kind=kCustom, calls=%fused_computation.4 | custom fusion | bytes 395264 | tf_op jit(solution)/shard_map/scatter | solution.py:127
  86.1 7.6 %all-to-all-start.1 = ((bf16[16,32,256]{2,1,0:T(8,128)(2,1)}), bf16[16,32,256]{2,1,0:T(8,128)(2,1)S(1)}, u32[]{:S(2)}, u32[]{:S(2)}) async-start(bf16[16,32,256]{2,1,0:T(8,128)(2,1)} %scatter_fusion.1), calls=%async_computation.1 | async-start | bytes 524288 | tf_op jit(solution)/shard_map/all_to_all | solution.py:136
  95.0 8.5 %all-to-all-done.1 = bf16[16,32,256]{2,1,0:T(8,128)(2,1)S(1)} async-done(((bf16[16,32,256]{2,1,0:T(8,128)(2,1)}), bf16[16,32,256]{2,1,0:T(8,128)(2,1)S(1)}, u32[]{:S(2)}, u32[]{:S(2)}) %all-to-all-start.1) | async-done | bytes 262176 | tf_op jit(solution)/shard_map/all_to_all | solution.py:136
  103.5 2.9 scatter_custom_fusion.2
  107.3 9.9 %all-to-all-start.3 = ((bf16[16,16,1024]{2,0,1:T(8,128)(2,1)}), bf16[16,16,1024]{2,0,1:T(8,128)(2,1)S(1)}, u32[]{:S(2)}, u32[]{:S(2)}) async-start(bf16[16,16,1024]{2,0,1:T(8,128)(2,1)} %bitcast.158), calls=%async_computation.3 | async-start | bytes 1048576 | tf_op jit(solution)/shard_map/all_to_all | solution.py:146
  117.2 1.1 broadcast_in_dim.131
  118.4 36.3 %scatter_fusion.2 = bf16[16,32,1024]{2,1,0:T(8,128)(2,1)} fusion(bf16[16,32,1024]{2,1,0:T(8,128)(2,1)} %broadcast_in_dim.131, s32[256]{0:T(256)S(1)} %bitcast.161, bf16[256,1024]{1,0:T(8,128)(2,1)S(1)} %copy-done.4), kind=kCustom, calls=%fused_computation.6 | custom fusion | bytes 1574912 | tf_op jit(solution)/shard_map/scatter | solution.py:122
  154.7 3.7 all-to-all-start.2
  161.1 28.7 %all-to-all-done.2 = bf16[16,32,1024]{2,1,0:T(8,128)(2,1)S(1)} async-done(((bf16[16,32,1024]{2,1,0:T(8,128)(2,1)}), bf16[16,32,1024]{2,1,0:T(8,128)(2,1)S(1)}, u32[]{:S(2)}, u32[]{:S(2)}) %all-to-all-start.2) | async-done | bytes 1048608 | tf_op jit(solution)/shard_map/all_to_all | solution.py:135
  189.7 3.0 scatter_custom_fusion.4
  193.3 43.2 %while.38 = (s32[]{:T(128)}, f32[1,8,256]{2,1,0:T(8,128)S(1)}, f32[1,8,256]{2,1,0:T(8,128)S(1)}, f32[1,8,256,128]{3,2,1,0:T(8,128)S(1)}, s32[256]{0:T(256)S(1)},...) while((s32[]{:T(128)}, f32[1,8,256]{2,1,0:T(8,128)S(1)}, ...), condition=%wide.region_14.16_spmd.clone, body=%wide.region_8.15_spmd.clone.sunk | while | flops 1893101312 | bytes 34497892 | solution.py:29
  194.2 1.6 gather_fusion
  197.3 11.2 %conditional.6 = ((f32[1,8,256]{2,1,0:T(8,128)S(1)}, f32[1,8,256]{2,1,0:T(8,128)S(1)}, f32[1,8,256,128]{3,2,1,0:T(8,128)S(1)})) conditional(s32[]{:T(128)} %convert_element_type.84, (f32[1,8,256]{2,1,0:T(8,128)S(1)}, f32[1,8,256]{2,1,0:T(8,128)S(1)}, f32[1,8,256,128]{3,2,1,0:T(8,128)S(1)}) %tuple.125, (pred[256,512]{0,1:T(8,128)(4,1)S(1)}, ...), branch_computations={%region_10.11_spmd, %region_11.14_spmd} | conditional | flops 1892161536 | bytes 32769100 | solution.py:174
  197.3 3.6 fusion.4
  201.0 6.5 %fusion.13 = f32[1,8,256,128]{3,2,1,0:T(8,128)S(1)} fusion(f32[512,8,256]{2,0,1:T(8,128)} %get-tuple-element.876, f32[8,256]{1,0:T(8,128)S(1)} %bitcast.164, pred[256,512]{0,1:T(8,128)(4,1)S(1)} %get-tuple-element.623, f32[1,8,256,128]{3,2,1,0:T(8,128)S(1)} %get-tuple-element.628, f32[8,256]{1,0:T(8,128)S(1)} %get-tuple-element.867, ...), kind=kOutput, calls=%fused_computation.21 | convolution fusion | flops 1615331328 | bytes 6570500 | tf_op jit(solution)/shard_map/while/body/eval_jaxpr/cond/branch_1_fun/ghqk,gkd->ghqd/dot_general | solution.py:71
  207.5 1.0 fusion.6
  209.4 1.6 gather_fusion
  213.4 1.6 gather_fusion
  217.4 1.6 gather_fusion
  221.4 1.6 gather_fusion
  225.4 1.6 gather_fusion
  229.4 1.6 gather_fusion
  233.4 1.6 gather_fusion
  237.6 2.2 broadcast_in_dim.123
  239.9 1.1 broadcast.335
  240.9 47.3 %while.39 = (s32[]{:T(128)}, f32[1,8,256,128]{3,2,1,0:T(8,128)}, f32[2,4096,128]{2,1,0:T(8,128)}, s32[256]{0:T(256)S(1)}, s32[4096]{0:T(1024)}, /*index=5*/s32[2...) while((s32[]{:T(128)}, f32[1,8,256,128]{3,2,1,0:T(8,128)}, ...), condition=%wide.region_20.22_spmd.clone, body=%wide.region_16.21_spmd.clone.sunk | while | flops 1356289792 | bytes 44353444 | solution.py:29
  241.7 1.6 gather_fusion.1
  244.9 15.5 %conditional.7 = ((f32[1,8,256,128]{3,2,1,0:T(8,128)}, f32[2,4096,128]{2,1,0:T(8,128)})) conditional(s32[]{:T(128)} %convert_element_type.85, (f32[1,8,256,128]{3,2,1,0:T(8,128)}, f32[2,4096,128]{2,1,0:T(8,128)}) %tuple.130, (pred[256,512]{0,1:T(8,128)(4,1)S(1)}, bf16[4096,256]{1,0:T(8,128)(2,1)}, s32[]{:T(128)}, ...), branch_computations={%region_18.19_spmd, %region_19.20_spmd} | conditional | flops 1355350016 | bytes 42624620 | solution.py:215
  244.9 3.6 fusion.39
  248.5 4.0 fusion.21
  253.2 2.2 fusion.30
  255.4 1.9 fusion.35
  257.3 3.0 fusion.29
  261.1 1.6 gather_fusion.1
  265.1 1.6 gather_fusion.1
  269.1 1.6 gather_fusion.1
  273.0 1.6 gather_fusion.1
  277.0 1.6 gather_fusion.1
  281.0 1.6 gather_fusion.1
  285.0 1.6 gather_fusion.1
  288.2 3.8 convert_element_type.62
  292.1 190.5 %reduce-scatter.3.cloned.1.call-done = bf16[2,256,128]{2,1,0:T(8,128)(2,1)} async-done(((bf16[2,4096,128]{2,1,0:T(8,128)(2,1)}), bf16[2,256,128]{2,1,0:T(8,128)(2,1)}) %reduce-scatter.3.cloned.1.call-update) | async-done | bytes 131088 | tf_op jit(solution)/shard_map/reduce_scatter | solution.py:226
  482.6 0.9 convert_dynamic-update-slice_fusion
  483.6 1.0 copy-done.3
  484.6 1.3 fusion.55
  487.2 83.3 %reduce-scatter.5.cloned.1.call-done = bf16[2,16,1024]{2,1,0:T(8,128)(2,1)} async-done(((bf16[2,256,1024]{2,1,0:T(8,128)(2,1)}), bf16[2,16,1024]{2,1,0:T(8,128)(2,1)}) %reduce-scatter.5.cloned.1.call-update) | async-done | bytes 65552 | tf_op jit(solution)/shard_map/reduce_scatter | solution.py:231
  (173 shorter events, 40.5 us)
Async XLA Ops:
  7.2 151.2 %copy-start = (s32[32,32]{1,0:T(8,128)S(1)}, s32[32,32]{1,0:T(8,128)}, u32[]{:S(2)}) copy-start(s32[32,32]{1,0:T(8,128)} %param.21) | copy-start | bytes 12292
  7.2 99.3 %copy-start.5 = (bf16[16,16384]{1,0:T(8,128)(2,1)S(1)}, bf16[16,16384]{1,0:T(8,128)(2,1)}, u32[]{:S(2)}) copy-start(bf16[16,16384]{1,0:T(8,128)(2,1)} %param.18) | copy-start | bytes 1572868
  9.5 108.9 %copy-start.4 = (bf16[256,1024]{1,0:T(8,128)(2,1)S(1)}, bf16[256,1024]{1,0:T(8,128)(2,1)}, u32[]{:S(2)}) copy-start(bf16[256,1024]{1,0:T(8,128)(2,1)} %param.16) | copy-start | bytes 1572868
  44.9 41.2 %all-to-all-start = ((s32[16,1,32]{2,1,0:T(1,128)}), s32[16,1,32]{2,1,0:T(1,128)S(1)}, u32[]{:S(2)}, u32[]{:S(2)}) async-start(s32[16,1,32]{2,1,0:T(1,128)} %bitcast.29), calls=%async_computation | async-start | bytes 16384 | tf_op jit(solution)/shard_map/all_to_all | solution.py:137
  86.1 17.4 %all-to-all-start.1 = ((bf16[16,32,256]{2,1,0:T(8,128)(2,1)}), bf16[16,32,256]{2,1,0:T(8,128)(2,1)S(1)}, u32[]{:S(2)}, u32[]{:S(2)}) async-start(bf16[16,32,256]{2,1,0:T(8,128)(2,1)} %scatter_fusion.1), calls=%async_computation.1 | async-start | bytes 524288 | tf_op jit(solution)/shard_map/all_to_all | solution.py:136
  93.7 99.5 %all-gather.2.cloned.1.call-start = ((), (), s32[]{:S(2)}) async-start(), calls=%async_computation.6 | async-start | bytes 2228224 | tf_op jit(solution)/shard_map/all_gather | solution.py:168
  107.3 47.4 %all-to-all-start.3 = ((bf16[16,16,1024]{2,0,1:T(8,128)(2,1)}), bf16[16,16,1024]{2,0,1:T(8,128)(2,1)S(1)}, u32[]{:S(2)}, u32[]{:S(2)}) async-start(bf16[16,16,1024]{2,0,1:T(8,128)(2,1)} %bitcast.158), calls=%async_computation.3 | async-start | bytes 1048576 | tf_op jit(solution)/shard_map/all_to_all | solution.py:146
  154.7 35.1 %all-to-all-start.2 = ((bf16[16,32,1024]{2,1,0:T(8,128)(2,1)}), bf16[16,32,1024]{2,1,0:T(8,128)(2,1)S(1)}, u32[]{:S(2)}, u32[]{:S(2)}) async-start(bf16[16,32,1024]{2,1,0:T(8,128)(2,1)} %scatter_fusion.2), calls=%async_computation.2 | async-start | bytes 2097152 | tf_op jit(solution)/shard_map/all_to_all | solution.py:135
  158.3 324.2 %reduce-scatter.3.cloned.1.call-start = ((), (), s32[]{:S(2)}) async-start(), calls=%async_computation.7 | async-start | bytes 2228224 | tf_op jit(solution)/shard_map/reduce_scatter | solution.py:226
  201.0 6.5 %copy-start.1 = (f32[512,8,256]{2,0,1:T(8,128)S(1)}, f32[512,8,256]{2,0,1:T(8,128)}, u32[]{:S(2)}) copy-start(f32[512,8,256]{2,0,1:T(8,128)} %get-tuple-element.876) | copy-start | bytes 12582916 | tf_op jit(solution)/shard_map/while/body/eval_jaxpr/cond
  248.5 4.7 copy-start.2
  292.0 278.5 %reduce-scatter.5.cloned.1.call-start = ((), (), s32[]{:S(2)}) async-start(), calls=%async_computation.8 | async-start | bytes 1114112 | tf_op jit(solution)/shard_map/reduce_scatter | solution.py:231
  483.6 1.0 copy-start.3
Sparse Core Ops, SparseCore 0:
  106.6 72.1 all-gather.1
  292.1 190.3 reduce-scatter.2
  487.2 83.3 reduce-scatter.4
where the time goes:
time: 582 us; the launch traced here: 577 us
  waiting for transfers between devices  311 us (53%)
  local copies, waits for them, and re-layouts  158 us (27%)
  starting transfers between devices  31.4 us (5%)
  other arithmetic  27.7 us (5%)
  matrix products  23.6 us (4%)
  between operations  14 us (2%)
  loops' own time  11.1 us (2%)
    reduce_scatter x1, waiting for transfers between devices, on_device(): lax.psum_scatter(grad_state[1].astype(jnp.bfloat16), 'ctx', scatter_dimen...  190 us
    reduce_scatter x1, waiting for transfers between devices, on_device(): lax.psum_scatter(padded_length.astype(jnp.bfloat16), 'tp', scatter_dimens...  83.3 us
    scatter x1, local copies, waits for them, and re-layouts, on_device(): q_send = jnp.zeros((shard_count, capacity, queries.shape[1]), jnp.bfloat1...  36.3 us
    scatter x1, local copies, waits for them, and re-layouts, on_device(): pos_send = jnp.full((shard_count, capacity), count_of_rows, jnp.int32).at...  35.4 us
    scatter x1, local copies, waits for them, and re-layouts, on_device(): kv_send = jnp.zeros((shard_count, capacity, kv_rows.shape[1]), jnp.bfloat...  29.4 us
    all_to_all x1, waiting for transfers between devices, on_device(): lax.all_to_all(q_send, 'ctx', split_axis=0, concat_axis=0, tiled=True)  28.7 us
    gather x16, local copies, waits for them, and re-layouts, visible(): block_ok = jnp.take(query_allow, key_pos // BLK, axis=1) > 0  25.2 us
    reduce_or x16, other arithmetic, step_fn(): jnp.any(visible_mask)  14.9 us
  transfers between devices with their start and end apart: 7, of which 4 were waited for; matrix products, arithmetic and copies ran while one was open for 14% of the time, Pallas kernels for 0%

commit v1 on v0

v1 whole, which is shorter than its diff:
```python
import functools
import math

import jax
import jax.numpy as jnp
from jax import lax
from jax.experimental import pallas as pl
from jax.experimental.pallas import tpu as pltpu
from jax.sharding import PartitionSpec as P

QUERY_HEAD_COUNT = 128
KEY_VALUE_HEADS = 8
HEAD_SIZE = 128
BLK = 128
TOK = 256
SHARDS = 16
SLOTS = 32
DOC_MOST = 2304
BACK = -(-DOC_MOST // TOK)
WINDOW = BACK + 1
BLOCKS_BACK = -(-DOC_MOST // BLK)
MOST_BLOCKS = 2 * ((BLOCKS_BACK + 2) // 2)
LOCAL_HEADS = 8
GROUP = 4
LANES = GROUP * BLK
CHUNK = 2 * BLK
MOST_CHUNKS = MOST_BLOCKS // 2
NEG_FILL = -1e30
SCALE = 1.0 / math.sqrt(HEAD_SIZE)
EXP2_SCALE = SCALE * math.log2(math.e)
F32 = jnp.float32
BF16 = jnp.bfloat16


def iota(shape, dim):
    return lax.broadcasted_iota(jnp.int32, shape, dim)


def dot(a, b):
    return jnp.dot(a, b, preferred_element_type=F32)


def ranks_within(member):
    earlier = (iota((TOK, TOK), 0) < iota((TOK, TOK), 1)).astype(F32).astype(BF16)
    counts = dot(member.astype(F32).astype(BF16), earlier)
    return jnp.where(member, counts, -1.0)


def pack_kernel(place_ref, rows_ref, out_ref):
    owner = place_ref[...] >> 8
    rank = ranks_within(owner == iota((SHARDS, TOK), 0))
    slot = iota((SLOTS, TOK), 0).astype(F32)
    picks = jnp.concatenate(
        [(rank[s : s + 1, :] == slot).astype(F32) for s in range(SHARDS)], axis=0
    ).astype(BF16)
    for first in range(0, rows_ref.shape[1], 256):
        cols = pl.ds(first, 256)
        out_ref[:, cols] = dot(picks, rows_ref[:, cols]).astype(BF16)


def permute_kernel(info_ref, place_ref, kv_ref, out_ref, unpack_ref):
    shard = info_ref[0]
    base = jnp.maximum(shard - BACK, 0)
    place = place_ref[...]
    rank = ranks_within((place >> 8) == shard)
    within = ((place & (TOK - 1)) + 1).astype(F32)
    slot = iota((SLOTS, TOK), 0).astype(F32)
    lane = (iota((SLOTS, TOK), 1) + 1).astype(F32)
    for s in range(SHARDS):
        hit = rank[s : s + 1, :] == slot
        landing = jnp.sum(jnp.where(hit, within[s : s + 1, :], 0.0), axis=1, keepdims=True)
        unpack_ref[s * SLOTS : (s + 1) * SLOTS, :] = (landing == lane).astype(F32).astype(BF16)

    def one_shard(i, carry):
        rows = iota((TOK, TOK), 0) + (base + i) * TOK
        total = jnp.zeros((TOK, 2 * HEAD_SIZE), F32)
        for s in range(SHARDS):
            picks = (place_ref[s : s + 1, :] == rows).astype(F32).astype(BF16)
            total = total + dot(picks, kv_ref[s * TOK : (s + 1) * TOK, :])
        out_ref[pl.ds(pl.multiple_of(i * TOK, TOK), TOK), :] = total.astype(BF16)
        return carry

    lax.fori_loop(0, shard - base + 1, one_shard, 0)


def attention_kernel(
    info_ref,
    seg_ref,
    allow_ref,
    segv_ref,
    unpack_ref,
    recv_ref,
    grad_ref,
    kv_ref,
    dq_ref,
    keep_ref,
    send_ref,
    q_s,
    qr_s,
    gr_s,
    qt_s,
    gt_s,
    k_s,
    v_s,
    kt_s,
    bias_s,
    e_s,
    dp_s,
    top_s,
    dqt_s,
    dk_s,
    dv_s,
    acc_s,
    list_s,
):
    shard = info_ref[0]
    core = info_ref[1]
    base = jnp.maximum(shard - BACK, 0)
    acc_s[...] = jnp.zeros_like(acc_s)
    for first in range(0, LOCAL_HEADS * HEAD_SIZE, 256):
        cols = pl.ds(first, 256)
        q_s[:, cols] = lax.dot_general(
            unpack_ref[...],
            recv_ref[:, cols],
            (((0,), (0,)), ((), ())),
            preferred_element_type=F32,
        ).astype(BF16)

    def query_block(half, carry):
        qb = shard * 2 + half
        row0 = pl.multiple_of(half * BLK, BLK)
        q_seg = segv_ref[pl.ds(qb, 1), :]
        q_first = seg_ref[qb * BLK]

        def scan(kb, count):
            seen = jnp.logical_and(
                seg_ref[kb * BLK + BLK - 1] >= q_first, allow_ref[qb, kb] != 0
            )

            @pl.when(seen)
            def _():
                list_s[count] = kb
                src = pl.ds(pl.multiple_of((kb - 2 * base) * BLK, BLK), BLK)
                dst = pl.ds(pl.multiple_of(count * BLK, BLK), BLK)
                k_blk = kv_ref[src, :HEAD_SIZE]
                k_s[dst, :] = k_blk
                v_s[dst, :] = kv_ref[src, HEAD_SIZE:]
                lanes = pl.ds(pl.multiple_of((count % 2) * BLK, BLK), BLK)
                kt_s[count // 2, :, lanes] = k_blk.astype(F32).T.astype(BF16)
                k_seg = jnp.broadcast_to(segv_ref[pl.ds(kb, 1), :].astype(F32), (BLK, BLK)).T
                k_pos = kb * BLK + iota((BLK, BLK), 0)
                q_pos = qb * BLK + iota((BLK, BLK), 1)
                ok = (k_seg == q_seg.astype(F32)) & (k_pos <= q_pos)
                bias_s[dst, :] = jnp.where(ok, 0.0, NEG_FILL)

            return count + seen.astype(jnp.int32)

        count = lax.fori_loop(jnp.maximum(qb - BLOCKS_BACK, 0), qb + 1, scan, 0)

        @pl.when(count % 2 == 1)
        def _():
            dst = pl.ds(pl.multiple_of(count * BLK, BLK), BLK)
            k_s[dst, :] = jnp.zeros((BLK, HEAD_SIZE), BF16)
            v_s[dst, :] = jnp.zeros((BLK, HEAD_SIZE), BF16)
            kt_s[count // 2, :, BLK:] = jnp.zeros((HEAD_SIZE, BLK), BF16)
            bias_s[dst, :] = jnp.full((BLK, BLK), NEG_FILL, F32)

        chunks = (count + 1) // 2

        def clear(ch, c):
            rows = pl.ds(pl.multiple_of(ch * CHUNK, CHUNK), CHUNK)
            dk_s[rows, :] = jnp.zeros((CHUNK, HEAD_SIZE), F32)
            dv_s[rows, :] = jnp.zeros((CHUNK, HEAD_SIZE), F32)
            return c

        lax.fori_loop(0, chunks, clear, 0)
        rows = pl.ds(row0, BLK)
        for hg in range(LOCAL_HEADS // GROUP):
            for i in range(GROUP):
                cols = pl.ds((hg * GROUP + i) * HEAD_SIZE, HEAD_SIZE)
                mine = pl.ds(i * BLK, BLK)
                q_blk = q_s[rows, cols]
                g_blk = grad_ref[rows, cols]
                qr_s[mine, :] = q_blk
                gr_s[mine, :] = g_blk
                qt_s[:, mine] = q_blk.astype(F32).T.astype(BF16)
                gt_s[:, mine] = g_blk.astype(F32).T.astype(BF16)

            def first_pass(ch, state):
                top, total, weighed = state
                rows_c = pl.ds(pl.multiple_of(ch * CHUNK, CHUNK), CHUNK)
                scores = dot(k_s[rows_c, :], qt_s[...])
                scores = scores + jnp.concatenate([bias_s[rows_c, :]] * GROUP, axis=1)
                new_top = jnp.maximum(top, jnp.max(scores, axis=0, keepdims=True))
                factor = jnp.exp2((top - new_top) * EXP2_SCALE)
                e = jnp.exp2((scores - new_top) * EXP2_SCALE)
                dp = dot(v_s[rows_c, :], gt_s[...])
                e_s[ch] = e
                dp_s[ch] = dp
                top_s[ch] = new_top
                total = total * factor + jnp.sum(e.reshape(-1, 8, LANES), axis=0)
                weighed = weighed * factor + jnp.sum((e * dp).reshape(-1, 8, LANES), axis=0)
                return (new_top, total, weighed)

            start = (
                jnp.full((1, LANES), NEG_FILL, F32),
                jnp.zeros((8, LANES), F32),
                jnp.zeros((8, LANES), F32),
            )
            top, total, weighed = lax.fori_loop(0, chunks, first_pass, start)
            inverse = 1.0 / jnp.sum(total, axis=0, keepdims=True)
            out_dot = jnp.sum(weighed, axis=0, keepdims=True) * inverse
            dqt_s[...] = jnp.zeros_like(dqt_s)

            def second_pass(ch, c):
                rows_c = pl.ds(pl.multiple_of(ch * CHUNK, CHUNK), CHUNK)
                factor = jnp.exp2((top_s[ch] - top) * EXP2_SCALE) * inverse
                weights = e_s[ch] * factor
                score_grad = (weights * (dp_s[ch] - out_dot)).astype(BF16)
                dv_s[rows_c, :] += dot(weights.astype(BF16), gr_s[...])
                dk_s[rows_c, :] += dot(score_grad, qr_s[...])
                dqt_s[...] += dot(kt_s[ch], score_grad)
                return c

            lax.fori_loop(0, chunks, second_pass, 0)
            for i in range(GROUP):
                cols = pl.ds((hg * GROUP + i) * HEAD_SIZE, HEAD_SIZE)
                dq_ref[rows, cols] = (dqt_s[:, i * BLK : (i + 1) * BLK] * SCALE).T.astype(BF16)

        def spread(n, c):
            src = pl.ds(pl.multiple_of(n * BLK, BLK), BLK)
            dst = pl.ds(pl.multiple_of((list_s[n] - 2 * base) * BLK, BLK), BLK)
            acc_s[0, dst, :] += dk_s[src, :]
            acc_s[1, dst, :] += dv_s[src, :]
            return c

        lax.fori_loop(0, count, spread, 0)
        return carry

    lax.fori_loop(0, 2, query_block, 0)

    @pl.when(core == 0)
    def _():
        keep_ref[...] = acc_s[0] * SCALE
        send_ref[...] = acc_s[1].astype(BF16)

    @pl.when(core == 1)
    def _():
        keep_ref[...] = acc_s[1]
        send_ref[...] = (acc_s[0] * SCALE).astype(BF16)


def merge_kernel(info_ref, keep_ref, recv_ref, out_ref):
    base = jnp.maximum(info_ref[0] - BACK, 0)
    out_ref[...] = jnp.zeros_like(out_ref)
    rows = pl.ds(pl.multiple_of(base * TOK, TOK), WINDOW * TOK)
    out_ref[rows, :] = (keep_ref[...] + recv_ref[...].astype(F32)).astype(BF16)


VMEM = pl.BlockSpec(memory_space=pltpu.VMEM)
SMEM = pl.BlockSpec(memory_space=pltpu.SMEM)


def call_attention(info, segments, allow, unpack, q_recv, g_local, kv_window):
    width = g_local.shape[1]
    return pl.pallas_call(
        attention_kernel,
        in_specs=[SMEM, SMEM, SMEM] + [VMEM] * 5,
        out_specs=[VMEM, VMEM, VMEM],
        out_shape=[
            jax.ShapeDtypeStruct((TOK, width), BF16),
            jax.ShapeDtypeStruct((WINDOW * TOK, HEAD_SIZE), F32),
            jax.ShapeDtypeStruct((WINDOW * TOK, HEAD_SIZE), BF16),
        ],
        scratch_shapes=[
            pltpu.VMEM((TOK, width), BF16),
            pltpu.VMEM((LANES, HEAD_SIZE), BF16),
            pltpu.VMEM((LANES, HEAD_SIZE), BF16),
            pltpu.VMEM((HEAD_SIZE, LANES), BF16),
            pltpu.VMEM((HEAD_SIZE, LANES), BF16),
            pltpu.VMEM((MOST_BLOCKS * BLK, HEAD_SIZE), BF16),
            pltpu.VMEM((MOST_BLOCKS * BLK, HEAD_SIZE), BF16),
            pltpu.VMEM((MOST_CHUNKS, HEAD_SIZE, CHUNK), BF16),
            pltpu.VMEM((MOST_BLOCKS * BLK, BLK), F32),
            pltpu.VMEM((MOST_CHUNKS, CHUNK, LANES), F32),
            pltpu.VMEM((MOST_CHUNKS, CHUNK, LANES), F32),
            pltpu.VMEM((MOST_CHUNKS, 1, LANES), F32),
            pltpu.VMEM((HEAD_SIZE, LANES), F32),
            pltpu.VMEM((MOST_BLOCKS * BLK, HEAD_SIZE), F32),
            pltpu.VMEM((MOST_BLOCKS * BLK, HEAD_SIZE), F32),
            pltpu.VMEM((2, WINDOW * TOK, HEAD_SIZE), F32),
            pltpu.SMEM((MOST_BLOCKS,), jnp.int32),
        ],
        compiler_params=pltpu.CompilerParams(vmem_limit_bytes=48 * 2**20),
        name="attention",
    )(info, segments, allow, segments.reshape(-1, BLK), unpack, q_recv, g_local, kv_window)


def on_device(queries, keys_values, out_grad, place, segments, allow):
    tp_index = lax.axis_index("tp")
    ctx_index = lax.axis_index("ctx")
    tp_size = lax.axis_size("tp")
    width = LOCAL_HEADS * HEAD_SIZE
    info = jnp.stack([ctx_index, tp_index % 2]).astype(jnp.int32)
    kv_first = (tp_index // 2) * HEAD_SIZE
    kv_mine = lax.dynamic_slice_in_dim(keys_values, kv_first, HEAD_SIZE, 2)
    kv_rows = jnp.concatenate([kv_mine[0], kv_mine[1]], axis=1)
    place_all = lax.all_gather(place, "ctx", axis=0, tiled=True).reshape(SHARDS, TOK)
    kv_all = lax.all_gather(kv_rows, "ctx", axis=0, tiled=True)
    g_local = lax.all_to_all(out_grad, "tp", split_axis=1, concat_axis=0, tiled=True)
    q_send = pl.pallas_call(
        pack_kernel,
        in_specs=[VMEM, VMEM],
        out_specs=VMEM,
        out_shape=jax.ShapeDtypeStruct((SHARDS * SLOTS, width), BF16),
        name="pack",
    )(place.reshape(1, TOK), queries)
    q_recv = lax.all_to_all(q_send, "ctx", split_axis=0, concat_axis=0, tiled=True)
    kv_window, unpack = pl.pallas_call(
        permute_kernel,
        in_specs=[SMEM, VMEM, VMEM],
        out_specs=[VMEM, VMEM],
        out_shape=[
            jax.ShapeDtypeStruct((WINDOW * TOK, 2 * HEAD_SIZE), BF16),
            jax.ShapeDtypeStruct((SHARDS * SLOTS, TOK), BF16),
        ],
        compiler_params=pltpu.CompilerParams(vmem_limit_bytes=32 * 2**20),
        name="permute",
    )(info, place_all, kv_all)
    grad_q, keep, send = call_attention(
        info, segments, allow, unpack, q_recv, g_local, kv_window
    )
    recv = lax.ppermute(send, "tp", [(k, k ^ 1) for k in range(tp_size)])
    part = pl.pallas_call(
        merge_kernel,
        in_specs=[SMEM, VMEM, VMEM],
        out_specs=VMEM,
        out_shape=jax.ShapeDtypeStruct((SHARDS * TOK, HEAD_SIZE), BF16),
        name="merge",
    )(info, keep, recv)
    parts = lax.all_to_all(
        part.reshape(SHARDS, TOK, HEAD_SIZE), "ctx", split_axis=0, concat_axis=0, tiled=True
    )
    owned = jnp.sum(parts.astype(F32), axis=0).astype(BF16)
    heads = lax.all_to_all(
        owned.reshape(tp_size, TOK // tp_size, HEAD_SIZE),
        "tp",
        split_axis=0,
        concat_axis=0,
        tiled=True,
    )
    key_value_gradient = (
        heads.reshape(KEY_VALUE_HEADS, 2, TOK // tp_size, HEAD_SIZE)
        .transpose(1, 2, 0, 3)
        .reshape(2, TOK // tp_size, KEY_VALUE_HEADS * HEAD_SIZE)
    )
    return (grad_q, key_value_gradient)


def solution(mesh):
    in_specs = (P("ctx", "tp"), P(None, "ctx", None), P(("ctx", "tp"), None), P("ctx"), P(), P())
    out_specs = (P("ctx", "tp"), P(None, ("ctx", "tp"), None))
    return jax.shard_map(
        on_device, mesh=mesh, in_specs=in_specs, out_specs=out_specs, check_vma=False
    )
```

time: 582 us -> 202 us (0.35); the launches traced: 577 us -> 204 us
  waiting for transfers between devices: 311 us -> 10.4 us
  local copies, waits for them, and re-layouts: 158 us -> 6.94 us
  blocking collectives: 0 us -> 129 us
  other arithmetic: 27.7 us -> 0.89 us
  matrix products: 23.6 us -> 0 us
  Pallas kernels: 0 us -> 13.7 us
  loops' own time: 11.1 us -> 0 us
    reduce_scatter x2 -> x0, waiting for transfers between devices: 274 us -> none  [the longest x1 190 us: on_device(): lax.psum_scatter(grad_state[1].astype(jnp.bfloat16), 'ctx', scatter_dimen...]
    scatter x6 -> x0, local copies, waits for them, and re-layouts: 107 us -> none  [the longest x1 36.3 us: on_device(): q_send = jnp.zeros((shard_count, capacity, queries.shape[1]), jnp.bfloat1...]
    all_to_all x0 -> x2, blocking collectives: none -> 77.1 us  [the longest x1 58.3 us: on_device(): lax.all_to_all(part.reshape(SHARDS, TOK, HEAD_SIZE), 'ctx', split_axis=0,...]
    all_gather x0 -> x1, blocking collectives: none -> 51.8 us  [on_device(): lax.all_gather(place, 'ctx', axis=0, tiled=True).reshape(SHARDS, TOK)]
    all_to_all x1, waiting for transfers between devices: 28.7 us -> 0.01 us  [on_device(): lax.all_to_all(q_send, 'ctx', split_axis=0, concat_axis=0, tiled=True)]
    gather x17 -> x0, local copies, waits for them, and re-layouts: 25.9 us -> none  [the longest x16 25.2 us: visible(): block_ok = jnp.take(query_allow, key_pos // BLK, axis=1) > 0]
    dot_general x7 -> x0, matrix products: 23.6 us -> none  [the longest x2 7.19 us: masked_scores(): jnp.einsum('ghqd,gkd->ghqk', query_heads, key_heads, preferred_element_ty...]
    all_to_all x2 -> x0, starting transfers between devices: 17.6 us -> none  [the longest x1 10 us: on_device(): lax.all_to_all(pos_send, 'ctx', split_axis=0, concat_axis=0, tiled=True)]
  transfers between devices with their start and end apart: 7 -> 4, of which waited for: 4 -> 2; matrix products, arithmetic and copies ran while one was open for 14% -> 1% of each run, Pallas kernels for 0% -> 2%
where the time goes in v1:
time: 202 us; the launch traced here: 204 us
  blocking collectives  129 us (64%)
  starting transfers between devices  28.8 us (14%)
  between operations  14.1 us (7%)
  Pallas kernels  13.7 us (7%)
  waiting for transfers between devices  10.4 us (5%)
  local copies, waits for them, and re-layouts  6.94 us (3%)
    all_to_all x1, blocking collectives, on_device(): lax.all_to_all(part.reshape(SHARDS, TOK, HEAD_SIZE), 'ctx', split_axis=0,...  58.3 us
    all_gather x1, blocking collectives, on_device(): lax.all_gather(place, 'ctx', axis=0, tiled=True).reshape(SHARDS, TOK)  51.8 us
    all_to_all x1, blocking collectives, on_device(): lax.all_to_all(owned.reshape(tp_size, TOK // tp_size, HEAD_SIZE), 'tp', s...  18.8 us
    all_to_all x1, starting transfers between devices, on_device(): lax.all_to_all(q_send, 'ctx', split_axis=0, concat_axis=0, tiled=True)  12.7 us
    all_to_all x1, waiting for transfers between devices, on_device(): lax.all_to_all(out_grad, 'tp', split_axis=1, concat_axis=0, tiled=True)  8.68 us
    all_to_all x1, starting transfers between devices, on_device(): lax.all_to_all(out_grad, 'tp', split_axis=1, concat_axis=0, tiled=True)  8.45 us
    ppermute x1, starting transfers between devices, on_device(): recv = lax.ppermute(send, 'tp', [(k, k ^ 1) for k in range(tp_size)])  7.6 us
    pallas_call x1, Pallas kernels, call_attention(): pl.pallas_call(attention_kernel, in_specs=[SMEM, SMEM, SMEM] + [VMEM] * 5...  6.82 us
  transfers between devices with their start and end apart: 4, of which 2 were waited for; matrix products, arithmetic and copies ran while one was open for 1% of the time, Pallas kernels for 2%

profile of v1, /device:TPU:1, one launch (start us, length us, event | category | flops | bytes accessed | tf_op | source)
XLA Modules:
  0.0 203.7 jit_solution(14683870708495101033)
XLA Ops:
  7.2 0.0 all-gather.3.cloned.1.call-start
  7.2 0.9 dynamic-slice_bitcast_fusion.1
  8.1 0.7 pad_maximum_fusion
  8.8 0.0 all-gather.3.cloned.1.call-update
  8.8 1.9 copy.20
  10.7 8.4 %all-to-all-start.1 = ((bf16[16,16,1024]{2,0,1:T(8,128)(2,1)}), bf16[16,16,1024]{2,0,1:T(8,128)(2,1)S(1)}, u32[]{:S(2)}, u32[]{:S(2)}) async-start(bf16[16,16,1024]{2,0,1:T(8,128)(2,1)} %bitcast.27), calls=%async_computation.1 | async-start | bytes 1048576 | tf_op jit(solution)/shard_map/all_to_all | solution.py:310
  19.1 2.6 %pack.1 = bf16[512,1024]{1,0:T(8,128)(2,1)} custom-call(s32[1,256]{1,0:T(1,128)} %bitcast.40, bf16[256,1024]{1,0:T(8,128)(2,1)} %rows_ref.1), custom_call_target="tpu_custom_call" | custom-call | tf_op jit(solution)/shard_map/pack/pallas_call | solution.py:311
  21.8 0.0 copy-start.6
  21.8 8.7 %all-to-all-done.1 = bf16[16,16,1024]{2,0,1:T(8,128)(2,1)S(1)} async-done(((bf16[16,16,1024]{2,0,1:T(8,128)(2,1)}), bf16[16,16,1024]{2,0,1:T(8,128)(2,1)S(1)}, u32[]{:S(2)}, u32[]{:S(2)}) %all-to-all-start.1) | async-done | bytes 524320 | tf_op jit(solution)/shard_map/all_to_all | solution.py:310
  30.4 12.7 %all-to-all-start = ((bf16[16,32,1024]{2,1,0:T(8,128)(2,1)}), bf16[16,32,1024]{2,1,0:T(8,128)(2,1)S(1)}, u32[]{:S(2)}, u32[]{:S(2)}) async-start(bf16[16,32,1024]{2,1,0:T(8,128)(2,1)} %bitcast.35), calls=%async_computation | async-start | bytes 2097152 | tf_op jit(solution)/shard_map/all_to_all | solution.py:318
  43.1 0.0 copy-start.2
  43.1 0.0 copy-start.3
  43.2 0.0 copy-done.6
  43.2 51.8 %all-gather = s32[16,1,256]{2,1,0:T(1,128)S(1)} all-gather(s32[1,1,256]{2,1,0:T(1,128)S(1)} %bitcast.41), channel_id=1, replica_groups=mesh['ctx'=16,'tp'=16] {'ctx'}, dimensions={0}, use_global_device_ids=true | all-gather | bytes 17408 | tf_op jit(solution)/shard_map/all_gather | solution.py:308
  94.9 0.1 pad_add_fusion.info_ref
  95.0 0.0 copy-start.4
  95.0 0.0 all-gather.3.cloned.1.call-done.kv_ref
  95.0 0.0 copy-start
  95.0 1.6 copy-done
  96.6 1.5 permute.1
  98.2 0.0 all-to-all-done
  98.2 0.0 copy-done.2
  98.2 0.0 copy-done.3
  98.2 6.8 %attention.1 = (bf16[256,1024]{1,0:T(8,128)(2,1)}, f32[2560,128]{1,0:T(8,128)S(1)}, bf16[2560,128]{1,0:T(8,128)(2,1)S(1)}) custom-call(s32[2]{0:T(128)S(1)} %pad_add_fusion.info_ref, s32[4096]{0:T(1024)S(1)} %copy-done.2, s32[32,32]{1,0:T(8,128)S(1)} %copy-done.3, s32[32,128]{1,0:T(8,128)S(1)} %bitcast.32, bf16[512,256]{1,0:T(8,128)(2,1)S(1)} %get-tuple-element.7.unpack_ref, ...), custom_call_target="tpu_custom_call" | custom-call | tf_op jit(solution)/shard_map/attention/pallas_call | solution.py:266
  105.0 0.0 copy-done.4
  105.0 0.0 copy-start.1
  105.0 1.1 copy-done.1
  106.1 7.6 %collective-permute-start = (bf16[2560,128]{1,0:T(8,128)(2,1)S(1)}, bf16[2560,128]{1,0:T(8,128)(2,1)S(1)}, u32[]{:S(2)}, u32[]{:S(2)}) collective-permute-start(bf16[2560,128]{1,0:T(8,128)(2,1)S(1)} %get-tuple-element.11), channel_id=1, source_target_pairs={{0,1},{1,0},{2,3},{3,2},{4,5},{5,4},{6,7},{7,6},{8,9},{9,8},{10,11... | collective-permute-start | bytes 1966088 | tf_op jit(solution)/shard_map/ppermute | solution.py:333
  113.7 1.7 collective-permute-done.recv_ref
  115.4 0.0 copy-start.5
  115.4 0.8 copy-done.5
  116.3 2.7 %merge.1 = bf16[4096,128]{1,0:T(8,128)(2,1)} custom-call(s32[2]{0:T(128)} %copy-done.4, f32[2560,128]{1,0:T(8,128)} %copy-done.1, bf16[2560,128]{1,0:T(8,128)(2,1)} %copy-done.5), custom_call_target="tpu_custom_call" | custom-call | tf_op jit(solution)/shard_map/merge/pallas_call | solution.py:334
  118.9 58.3 %all_to_all.40 = bf16[16,256,128]{2,1,0:T(8,128)(2,1)S(1)} all-to-all(bf16[16,256,128]{2,1,0:T(8,128)(2,1)} %bitcast.34), channel_id=1, replica_groups=mesh['ctx'=16,'tp'=16] {'ctx'}, dimensions={0} | all-to-all | bytes 2097152 | tf_op jit(solution)/shard_map/all_to_all | solution.py:341
  177.2 0.1 reduce_sum.12
  177.4 18.8 %all_to_all.41 = bf16[16,16,128]{2,1,0:T(8,128)(2,1)S(1)} all-to-all(bf16[16,16,128]{2,1,0:T(8,128)(2,1)S(1)} %bitcast.37), channel_id=1, replica_groups=mesh['ctx'=16,'tp'=16] {'tp'}, dimensions={0} | all-to-all | bytes 131072 | tf_op jit(solution)/shard_map/all_to_all | solution.py:345
  196.2 0.6 copy.21
  (1 shorter events, 0.0 us)
Async XLA Ops:
  7.2 87.8 %all-gather.3.cloned.1.call-start = ((), (), s32[]{:S(2)}) async-start(), calls=%async_computation.4 | async-start | bytes 2228224 | tf_op jit(solution)/shard_map/all_gather | solution.py:309
  10.7 19.7 %all-to-all-start.1 = ((bf16[16,16,1024]{2,0,1:T(8,128)(2,1)}), bf16[16,16,1024]{2,0,1:T(8,128)(2,1)S(1)}, u32[]{:S(2)}, u32[]{:S(2)}) async-start(bf16[16,16,1024]{2,0,1:T(8,128)(2,1)} %bitcast.27), calls=%async_computation.1 | async-start | bytes 1048576 | tf_op jit(solution)/shard_map/all_to_all | solution.py:310
  21.8 21.4 %copy-start.6 = (s32[256]{0:T(256)S(1)}, s32[256]{0:T(256)}, u32[]{:S(2)}) copy-start(s32[256]{0:T(256)} %param.9) | copy-start | bytes 3076
  30.4 67.7 %all-to-all-start = ((bf16[16,32,1024]{2,1,0:T(8,128)(2,1)}), bf16[16,32,1024]{2,1,0:T(8,128)(2,1)S(1)}, u32[]{:S(2)}, u32[]{:S(2)}) async-start(bf16[16,32,1024]{2,1,0:T(8,128)(2,1)} %bitcast.35), calls=%async_computation | async-start | bytes 2097152 | tf_op jit(solution)/shard_map/all_to_all | solution.py:318
  43.1 55.0 %copy-start.2 = (s32[4096]{0:T(1024)S(1)}, s32[4096]{0:T(1024)}, u32[]{:S(2)}) copy-start(s32[4096]{0:T(1024)} %seg_ref.1) | copy-start | bytes 49156
  43.1 55.0 %copy-start.3 = (s32[32,32]{1,0:T(8,128)S(1)}, s32[32,32]{1,0:T(8,128)}, u32[]{:S(2)}) copy-start(s32[32,32]{1,0:T(8,128)} %allow_ref.1) | copy-start | bytes 12292
  95.0 10.0 %copy-start.4 = (s32[2]{0:T(128)}, s32[2]{0:T(128)S(1)}, u32[]{:S(2)}) copy-start(s32[2]{0:T(128)S(1)} %pad_add_fusion.info_ref) | copy-start | bytes 28
  95.0 1.6 copy-start
  105.0 1.1 copy-start.1
  106.1 9.3 %collective-permute-start = (bf16[2560,128]{1,0:T(8,128)(2,1)S(1)}, bf16[2560,128]{1,0:T(8,128)(2,1)S(1)}, u32[]{:S(2)}, u32[]{:S(2)}) collective-permute-start(bf16[2560,128]{1,0:T(8,128)(2,1)S(1)} %get-tuple-element.11), channel_id=1, source_target_pairs={{0,1},{1,0},{2,3},{3,2},{4,5},{5,4},{6,7},{7,6},{8,9},{9,8},{10,11... | collective-permute-start | bytes 1966088 | tf_op jit(solution)/shard_map/ppermute | solution.py:333
  115.4 0.8 copy-start.5
Sparse Core Ops, SparseCore 0:
  9.8 84.4 all-gather.2

commit v2 on v1

--- a/solution.py
+++ b/solution.py
@@ -15,6 +15,9 @@
 TOK = 256
 SHARDS = 16
 SLOTS = 32
+META = 16
+Z_CHIPS = SHARDS // 2
+RING = Z_CHIPS // 2
 DOC_MOST = 2304
 BACK = -(-DOC_MOST // TOK)
 WINDOW = BACK + 1
@@ -58,25 +61,49 @@
         out_ref[:, cols] = dot(picks, rows_ref[:, cols]).astype(BF16)
 
 
-def permute_kernel(info_ref, place_ref, kv_ref, out_ref, unpack_ref):
+def stage_kernel(info_ref, place_ref, kv_ref, out_ref):
+    place = place_ref[...]
+    out_ref[:TOK, :HEAD_SIZE] = kv_ref[0]
+    out_ref[:TOK, HEAD_SIZE:] = kv_ref[1]
+    row = iota((META, TOK), 0)
+    owner = jnp.broadcast_to((place >> 8).astype(F32), (META, TOK))
+    within = jnp.broadcast_to((place & (TOK - 1)).astype(F32), (META, TOK))
+    meta = jnp.where(row == 0, owner, jnp.where(row == 1, within, 0.0))
+    out_ref[TOK:, :] = meta.astype(BF16)
+
+
+def permute_kernel(info_ref, own_ref, *refs):
+    mine, theirs = refs[:RING], refs[RING : 2 * RING]
+    out_ref, unpack_ref = refs[2 * RING :]
     shard = info_ref[0]
+    core = info_ref[1]
     base = jnp.maximum(shard - BACK, 0)
-    place = place_ref[...]
-    rank = ranks_within((place >> 8) == shard)
-    within = ((place & (TOK - 1)) + 1).astype(F32)
+    z, x = shard // 2, shard % 2
+    sources = [(own_ref.at[j], shard ^ j) for j in range(2)]
+    for refs_k, side in ((mine, core), (theirs, 1 - core)):
+        for k in range(1, RING):
+            far = (z + k * (2 * side - 1) + Z_CHIPS) % Z_CHIPS
+            sources += [(refs_k[k - 1].at[j], 2 * far + (x ^ j)) for j in range(2)]
+        far = (z + RING) % Z_CHIPS
+        sources += [(refs_k[RING - 1], 2 * far + (x ^ side))]
+    owners = jnp.concatenate([ref[TOK : TOK + 1, :].astype(F32) for ref, _ in sources], axis=0)
+    within = jnp.concatenate([ref[TOK + 1 : TOK + 2, :].astype(F32) for ref, _ in sources], axis=0)
+    rank = ranks_within(owners == shard.astype(F32))
     slot = iota((SLOTS, TOK), 0).astype(F32)
-    lane = (iota((SLOTS, TOK), 1) + 1).astype(F32)
-    for s in range(SHARDS):
-        hit = rank[s : s + 1, :] == slot
-        landing = jnp.sum(jnp.where(hit, within[s : s + 1, :], 0.0), axis=1, keepdims=True)
-        unpack_ref[s * SLOTS : (s + 1) * SLOTS, :] = (landing == lane).astype(F32).astype(BF16)
+    lane = iota((SLOTS, TOK), 1).astype(F32)
+    for i, (_, source) in enumerate(sources):
+        hit = rank[i : i + 1, :] == slot
+        landing = jnp.sum(jnp.where(hit, within[i : i + 1, :] + 1.0, 0.0), axis=1, keepdims=True)
+        rows = pl.ds(pl.multiple_of(source * SLOTS, SLOTS), SLOTS)
+        unpack_ref[rows, :] = (landing == lane + 1.0).astype(F32).astype(BF16)
 
     def one_shard(i, carry):
-        rows = iota((TOK, TOK), 0) + (base + i) * TOK
+        rows = iota((TOK, TOK), 0).astype(F32)
+        goal = jnp.where(owners == (base + i).astype(F32), within, -1.0)
         total = jnp.zeros((TOK, 2 * HEAD_SIZE), F32)
-        for s in range(SHARDS):
-            picks = (place_ref[s : s + 1, :] == rows).astype(F32).astype(BF16)
-            total = total + dot(picks, kv_ref[s * TOK : (s + 1) * TOK, :])
+        for n, (ref, _) in enumerate(sources):
+            picks = (goal[n : n + 1, :] == rows).astype(F32).astype(BF16)
+            total = total + dot(picks, ref[:TOK, :])
         out_ref[pl.ds(pl.multiple_of(i * TOK, TOK), TOK), :] = total.astype(BF16)
         return carry
 
@@ -301,12 +328,37 @@
     ctx_index = lax.axis_index("ctx")
     tp_size = lax.axis_size("tp")
     width = LOCAL_HEADS * HEAD_SIZE
-    info = jnp.stack([ctx_index, tp_index % 2]).astype(jnp.int32)
-    kv_first = (tp_index // 2) * HEAD_SIZE
-    kv_mine = lax.dynamic_slice_in_dim(keys_values, kv_first, HEAD_SIZE, 2)
-    kv_rows = jnp.concatenate([kv_mine[0], kv_mine[1]], axis=1)
-    place_all = lax.all_gather(place, "ctx", axis=0, tiled=True).reshape(SHARDS, TOK)
-    kv_all = lax.all_gather(kv_rows, "ctx", axis=0, tiled=True)
+    info = jnp.stack([ctx_index, tp_index % 2, tp_index // 2]).astype(jnp.int32)
+    staged = pl.pallas_call(
+        stage_kernel,
+        grid_spec=pltpu.PrefetchScalarGridSpec(
+            num_scalar_prefetch=1,
+            grid=(1,),
+            in_specs=[
+                pl.BlockSpec((1, TOK), lambda i, info: (0, 0)),
+                pl.BlockSpec((2, TOK, HEAD_SIZE), lambda i, info: (0, 0, info[2])),
+            ],
+            out_specs=pl.BlockSpec((TOK + META, 2 * HEAD_SIZE), lambda i, info: (0, 0)),
+        ),
+        out_shape=jax.ShapeDtypeStruct((TOK + META, 2 * HEAD_SIZE), BF16),
+        name="stage",
+    )(info, place.reshape(1, TOK), keys_values)
+    beside = lax.ppermute(staged, "ctx", [(k, k ^ 1) for k in range(SHARDS)])
+    own = jnp.stack([staged, beside])
+    turn = []
+    for k in range(SHARDS * tp_size):
+        ctx, tp = k // tp_size, k % tp_size
+        near = (ctx + (2 if tp % 2 == 0 else SHARDS - 2)) % SHARDS
+        turn.append((k, near * tp_size + tp))
+    swap = [(k, k ^ 1) for k in range(tp_size)]
+    mine, theirs = [], []
+    moving = own
+    for step in range(1, RING + 1):
+        if step == RING:
+            moving = lax.dynamic_index_in_dim(moving, tp_index % 2, 0, keepdims=False)
+        moving = lax.ppermute(moving, ("ctx", "tp"), turn)
+        mine.append(moving)
+        theirs.append(lax.ppermute(moving, "tp", swap))
     g_local = lax.all_to_all(out_grad, "tp", split_axis=1, concat_axis=0, tiled=True)
     q_send = pl.pallas_call(
         pack_kernel,
@@ -318,7 +370,7 @@
     q_recv = lax.all_to_all(q_send, "ctx", split_axis=0, concat_axis=0, tiled=True)
     kv_window, unpack = pl.pallas_call(
         permute_kernel,
-        in_specs=[SMEM, VMEM, VMEM],
+        in_specs=[SMEM] + [VMEM] * (2 * RING + 1),
         out_specs=[VMEM, VMEM],
         out_shape=[
             jax.ShapeDtypeStruct((WINDOW * TOK, 2 * HEAD_SIZE), BF16),
@@ -326,11 +378,11 @@
         ],
         compiler_params=pltpu.CompilerParams(vmem_limit_bytes=32 * 2**20),
         name="permute",
-    )(info, place_all, kv_all)
+    )(info, own, *mine, *theirs)
     grad_q, keep, send = call_attention(
         info, segments, allow, unpack, q_recv, g_local, kv_window
     )
-    recv = lax.ppermute(send, "tp", [(k, k ^ 1) for k in range(tp_size)])
+    recv = lax.ppermute(send, "tp", swap)
     part = pl.pallas_call(
         merge_kernel,
         in_specs=[SMEM, VMEM, VMEM],

time: 202 us -> 173 us (0.86)
  blocking collectives: 129 us -> 71.2 us
  waiting for transfers between devices: 10.4 us -> 37.1 us
  between operations: 14.1 us -> 0.74 us
  starting transfers between devices: 28.8 us -> 38.4 us
  Pallas kernels: 13.7 us -> 16.1 us
    all_gather x1 -> x0, blocking collectives: 51.8 us -> none  [on_device(): lax.all_gather(place, 'ctx', axis=0, tiled=True).reshape(SHARDS, TOK)]
    ppermute x1 -> x10, waiting for transfers between devices: 1.72 us -> 28.5 us  [the longest x4 22.7 us: on_device(): moving = lax.ppermute(moving, ('ctx', 'tp'), turn)]
    ppermute x1 -> x10, starting transfers between devices: 7.6 us -> 21.6 us  [the longest x4 11.1 us: on_device(): theirs.append(lax.ppermute(moving, 'tp', swap))]
    all_to_all x1, blocking collectives: 18.8 us -> 13.8 us  [on_device(): lax.all_to_all(owned.reshape(tp_size, TOK // tp_size, HEAD_SIZE), 'tp', s...]
    all_to_all x1, starting transfers between devices: 12.7 us -> 8.33 us  [on_device(): lax.all_to_all(q_send, 'ctx', split_axis=0, concat_axis=0, tiled=True)]
    unnamed x15 -> x22, local copies, waits for them, and re-layouts: 3.53 us -> 6.18 us
    pallas_call x1 -> x2, Pallas kernels: 1.54 us -> 3.97 us  [the longest x1 2.4 us: on_device(): pl.pallas_call(stage_kernel, grid_spec=pltpu.PrefetchScalarGridSpec(num_s...]
  transfers between devices with their start and end apart: 4 -> 12, of which waited for: 2 -> 7; matrix products, arithmetic and copies ran while one was open for 1% -> 1% of each run, Pallas kernels for 2% -> 4%
where the time goes in v2:
time: 173 us; the launch traced here: 174 us
  blocking collectives  71.2 us (41%)
  starting transfers between devices  38.4 us (22%)
  waiting for transfers between devices  37.1 us (21%)
  Pallas kernels  16.1 us (9%)
  local copies, waits for them, and re-layouts  8.71 us (5%)
  other arithmetic  1.74 us (1%)
    all_to_all x1, blocking collectives, on_device(): lax.all_to_all(part.reshape(SHARDS, TOK, HEAD_SIZE), 'ctx', split_axis=0,...  57.4 us
    ppermute x4, waiting for transfers between devices, on_device(): moving = lax.ppermute(moving, ('ctx', 'tp'), turn)  22.7 us
    all_to_all x1, blocking collectives, on_device(): lax.all_to_all(owned.reshape(tp_size, TOK // tp_size, HEAD_SIZE), 'tp', s...  13.8 us
    ppermute x4, starting transfers between devices, on_device(): theirs.append(lax.ppermute(moving, 'tp', swap))  11.1 us
    ppermute x4, starting transfers between devices, on_device(): moving = lax.ppermute(moving, ('ctx', 'tp'), turn)  8.8 us
    all_to_all x1, waiting for transfers between devices, on_device(): lax.all_to_all(out_grad, 'tp', split_axis=1, concat_axis=0, tiled=True)  8.66 us
    all_to_all x1, starting transfers between devices, on_device(): lax.all_to_all(out_grad, 'tp', split_axis=1, concat_axis=0, tiled=True)  8.45 us
    all_to_all x1, starting transfers between devices, on_device(): lax.all_to_all(q_send, 'ctx', split_axis=0, concat_axis=0, tiled=True)  8.33 us
  transfers between devices with their start and end apart: 12, of which 7 were waited for; matrix products, arithmetic and copies ran while one was open for 1% of the time, Pallas kernels for 4%

profile of v2, /device:TPU:1, one launch (start us, length us, event | category | flops | bytes accessed | tf_op | source)
XLA Modules:
  0.0 174.0 jit_solution(10620850915002826210)
XLA Ops:
  0.6 1.9 %copy.16 = bf16[2,16,8,1024]{3,2,0,1:T(8,128)(2,1)} copy(bf16[2,16,8,1024]{3,2,1,0:T(8,128)(2,1)} %bitcast.33) | data formatting | bytes 1048576 | tf_op jit(solution)/shard_map/all_to_all | solution.py:362
  2.5 8.4 %all-to-all-start.1 = ((bf16[16,16,1024]{2,0,1:T(8,128)(2,1)}), bf16[16,16,1024]{2,0,1:T(8,128)(2,1)S(1)}, u32[]{:S(2)}, u32[]{:S(2)}) async-start(bf16[16,16,1024]{2,0,1:T(8,128)(2,1)} %bitcast.25), calls=%async_computation.1 | async-start | bytes 1048576 | tf_op jit(solution)/shard_map/all_to_all | solution.py:362
  11.0 2.6 %pack.1 = bf16[512,1024]{1,0:T(8,128)(2,1)} custom-call(s32[1,256]{1,0:T(1,128)} %bitcast.38, bf16[256,1024]{1,0:T(8,128)(2,1)} %rows_ref.1), custom_call_target="tpu_custom_call" | custom-call | tf_op jit(solution)/shard_map/pack/pallas_call | solution.py:363
  13.6 8.7 %all-to-all-done.1 = bf16[16,16,1024]{2,0,1:T(8,128)(2,1)S(1)} async-done(((bf16[16,16,1024]{2,0,1:T(8,128)(2,1)}), bf16[16,16,1024]{2,0,1:T(8,128)(2,1)S(1)}, u32[]{:S(2)}, u32[]{:S(2)}) %all-to-all-start.1) | async-done | bytes 524320 | tf_op jit(solution)/shard_map/all_to_all | solution.py:362
  22.3 8.3 %all-to-all-start = ((bf16[16,32,1024]{2,1,0:T(8,128)(2,1)}), bf16[16,32,1024]{2,1,0:T(8,128)(2,1)S(1)}, u32[]{:S(2)}, u32[]{:S(2)}) async-start(bf16[16,32,1024]{2,1,0:T(8,128)(2,1)} %bitcast.31), calls=%async_computation | async-start | bytes 2097152 | tf_op jit(solution)/shard_map/all_to_all | solution.py:370
  30.6 0.7 pad_add_fusion.info_ref
  31.3 2.4 %stage.1 = bf16[272,256]{1,0:T(8,128)(2,1)} custom-call(s32[3]{0:T(128)} %pad_add_fusion.info_ref, s32[1,256]{1,0:T(1,128)} %bitcast.39, bf16[2,256,1024]{2,1,0:T(8,128)(2,1)} %kv_ref.1), custom_call_target="tpu_custom_call" | custom-call | tf_op jit(solution)/shard_map/stage/pallas_call | solution.py:332
  33.7 1.3 collective-permute-start
  35.0 3.1 %collective-permute-done = bf16[272,256]{1,0:T(8,128)(2,1)S(1)} collective-permute-done((bf16[272,256]{1,0:T(8,128)(2,1)}, bf16[272,256]{1,0:T(8,128)(2,1)S(1)}, u32[]{:S(2)}, u32[]{:S(2)}) %collective-permute-start) | collective-permute-done | bytes 139296 | tf_op jit(solution)/shard_map/ppermute | solution.py:346
  38.1 0.9 pad_maximum_fusion.own_ref
  39.0 0.0 copy-start.7
  39.0 0.0 copy-start.8
  39.0 2.6 %collective-permute-start.1 = (bf16[2,272,256]{2,1,0:T(8,128)(2,1)S(1)}, bf16[2,272,256]{2,1,0:T(8,128)(2,1)S(1)}, u32[]{:S(2)}, u32[]{:S(2)}) collective-permute-start(bf16[2,272,256]{2,1,0:T(8,128)(2,1)S(1)} %pad_maximum_fusion.own_ref), channel_id=1, source_target_pairs={{0,32},{1,225},{2,34},{3,227},{4,36},{5,229},{6,38},{7,231},{8,40}... | collective-permute-start | bytes 835592 | tf_op jit(solution)/shard_map/ppermute | solution.py:359
  41.7 17.2 %collective-permute-done.1.refs_0_ = bf16[2,272,256]{2,1,0:T(8,128)(2,1)S(1)} collective-permute-done((bf16[2,272,256]{2,1,0:T(8,128)(2,1)S(1)}, bf16[2,272,256]{2,1,0:T(8,128)(2,1)S(1)}, u32[]{:S(2)}, u32[]{:S(2)}) %collective-permute-start.1) | collective-permute-done | bytes 278560 | tf_op jit(solution)/shard_map/ppermute | solution.py:359
  58.9 0.9 collective-permute-start.2
  59.8 4.5 %collective-permute-done.2.refs_1_ = bf16[2,272,256]{2,1,0:T(8,128)(2,1)S(1)} collective-permute-done((bf16[2,272,256]{2,1,0:T(8,128)(2,1)S(1)}, bf16[2,272,256]{2,1,0:T(8,128)(2,1)S(1)}, u32[]{:S(2)}, u32[]{:S(2)}) %collective-permute-start.2) | collective-permute-done | bytes 278560 | tf_op jit(solution)/shard_map/ppermute | solution.py:359
  64.3 2.1 %collective-permute-start.3 = (bf16[2,272,256]{2,1,0:T(8,128)(2,1)S(1)}, bf16[2,272,256]{2,1,0:T(8,128)(2,1)S(1)}, u32[]{:S(2)}, u32[]{:S(2)}) collective-permute-start(bf16[2,272,256]{2,1,0:T(8,128)(2,1)S(1)} %collective-permute-done.2.refs_1_), channel_id=1, source_target_pairs={{0,32},{1,225},{2,34},{3,227},{4,36},{5,229},{6,38},{7,231},{8,40}... | collective-permute-start | bytes 835592 | tf_op jit(solution)/shard_map/ppermute | solution.py:359
  66.4 1.8 %collective-permute-start.5 = (bf16[2,272,256]{2,1,0:T(8,128)(2,1)S(1)}, bf16[2,272,256]{2,1,0:T(8,128)(2,1)S(1)}, u32[]{:S(2)}, u32[]{:S(2)}) collective-permute-start(bf16[2,272,256]{2,1,0:T(8,128)(2,1)S(1)} %collective-permute-done.1.refs_0_), channel_id=1, source_target_pairs={{0,1},{1,0},{2,3},{3,2},{4,5},{5,4},{6,7},{7,6},{8,9},{9,8},{10,11... | collective-permute-start | bytes 835592 | tf_op jit(solution)/shard_map/ppermute | solution.py:361
  68.2 0.0 collective-permute-start.6
  68.2 0.7 copy-done.3
  68.9 0.9 collective-permute-done.3.refs_2_
  69.9 3.2 %collective-permute-start.4 = (bf16[272,256]{1,0:T(8,128)(2,1)S(1)}, bf16[272,256]{1,0:T(8,128)(2,1)S(1)}, u32[]{:S(2)}, u32[]{:S(2)}) collective-permute-start(bf16[272,256]{1,0:T(8,128)(2,1)S(1)} %dynamic-slice_bitcast_fusion), channel_id=1, source_target_pairs={{0,32},{1,225},{2,34},{3,227},{4,36},{5,229},{6,38},{7,231},{8,40}... | collective-permute-start | bytes 417800 | tf_op jit(solution)/shard_map/ppermute | solution.py:359
  73.1 3.1 %collective-permute-start.7 = (bf16[2,272,256]{2,1,0:T(8,128)(2,1)S(1)}, bf16[2,272,256]{2,1,0:T(8,128)(2,1)S(1)}, u32[]{:S(2)}, u32[]{:S(2)}) collective-permute-start(bf16[2,272,256]{2,1,0:T(8,128)(2,1)S(1)} %collective-permute-done.3.refs_2_), channel_id=1, source_target_pairs={{0,1},{1,0},{2,3},{3,2},{4,5},{5,4},{6,7},{7,6},{8,9},{9,8},{10,11... | collective-permute-start | bytes 835592 | tf_op jit(solution)/shard_map/ppermute | solution.py:361
  76.2 0.0 collective-permute-done.4.refs_3_
  76.2 6.2 %collective-permute-start.8 = (bf16[272,256]{1,0:T(8,128)(2,1)S(1)}, bf16[272,256]{1,0:T(8,128)(2,1)S(1)}, u32[]{:S(2)}, u32[]{:S(2)}) collective-permute-start(bf16[272,256]{1,0:T(8,128)(2,1)S(1)} %collective-permute-done.4.refs_3_), channel_id=1, source_target_pairs={{0,1},{1,0},{2,3},{3,2},{4,5},{5,4},{6,7},{7,6},{8,9},{9,8},{10,11... | collective-permute-start | bytes 417800 | tf_op jit(solution)/shard_map/ppermute | solution.py:361
  82.3 0.0 collective-permute-done.5.refs_4_
  82.3 0.0 collective-permute-done.6.refs_5_
  82.3 1.0 collective-permute-done.8.refs_7_
  83.3 0.0 copy-done.1
  83.3 0.0 collective-permute-done.7.refs_6_
  83.4 1.0 copy-done.2
  84.3 1.0 copy-done.4
  85.3 1.6 permute.1
  86.8 0.0 copy-start.5
  86.8 0.7 copy-done.5
  87.5 0.0 all-to-all-done
  87.5 0.0 copy-done.8
  87.6 0.9 copy-done.6
  88.5 6.8 %attention.1 = (bf16[256,1024]{1,0:T(8,128)(2,1)}, f32[2560,128]{1,0:T(8,128)S(1)}, bf16[2560,128]{1,0:T(8,128)(2,1)S(1)}) custom-call(s32[3]{0:T(128)S(1)} %copy-done.9, s32[4096]{0:T(1024)S(1)} %copy-done.7, s32[32,32]{1,0:T(8,128)S(1)} %copy-done.8, s32[32,128]{1,0:T(8,128)S(1)} %bitcast.29, bf16[512,256]{1,0:T(8,128)(2,1)S(1)} %copy-done.6, ...), custom_call_target="tpu_custom_call" | custom-call | tf_op jit(solution)/shard_map/attention/pallas_call | solution.py:293
  95.3 1.1 copy-done
  96.4 0.4 collective-permute-start.9
  96.7 1.7 collective-permute-done.9.recv_ref
  98.5 0.8 copy-done.10
  99.3 2.7 %merge.1 = bf16[4096,128]{1,0:T(8,128)(2,1)} custom-call(s32[3]{0:T(128)} %pad_add_fusion.info_ref, f32[2560,128]{1,0:T(8,128)} %copy-done, bf16[2560,128]{1,0:T(8,128)(2,1)} %copy-done.10), custom_call_target="tpu_custom_call" | custom-call | tf_op jit(solution)/shard_map/merge/pallas_call | solution.py:386
  102.0 57.4 %all_to_all.40 = bf16[16,256,128]{2,1,0:T(8,128)(2,1)S(1)} all-to-all(bf16[16,256,128]{2,1,0:T(8,128)(2,1)} %bitcast.30), channel_id=1, replica_groups=mesh['ctx'=16,'tp'=16] {'ctx'}, dimensions={0} | all-to-all | bytes 2097152 | tf_op jit(solution)/shard_map/all_to_all | solution.py:393
  159.4 0.1 reduce_sum.12
  159.6 13.8 %all_to_all.41 = bf16[16,16,128]{2,1,0:T(8,128)(2,1)S(1)} all-to-all(bf16[16,16,128]{2,1,0:T(8,128)(2,1)S(1)} %bitcast.34), channel_id=1, replica_groups=mesh['ctx'=16,'tp'=16] {'tp'}, dimensions={0} | all-to-all | bytes 131072 | tf_op jit(solution)/shard_map/all_to_all | solution.py:397
  173.3 0.6 copy.17
  (11 shorter events, 0.0 us)
Async XLA Ops:
  2.5 19.7 %all-to-all-start.1 = ((bf16[16,16,1024]{2,0,1:T(8,128)(2,1)}), bf16[16,16,1024]{2,0,1:T(8,128)(2,1)S(1)}, u32[]{:S(2)}, u32[]{:S(2)}) async-start(bf16[16,16,1024]{2,0,1:T(8,128)(2,1)} %bitcast.25), calls=%async_computation.1 | async-start | bytes 1048576 | tf_op jit(solution)/shard_map/all_to_all | solution.py:362
  22.3 65.3 %all-to-all-start = ((bf16[16,32,1024]{2,1,0:T(8,128)(2,1)}), bf16[16,32,1024]{2,1,0:T(8,128)(2,1)S(1)}, u32[]{:S(2)}, u32[]{:S(2)}) async-start(bf16[16,32,1024]{2,1,0:T(8,128)(2,1)} %bitcast.31), calls=%async_computation | async-start | bytes 2097152 | tf_op jit(solution)/shard_map/all_to_all | solution.py:370
  31.3 52.1 %copy-start.9 = (s32[3]{0:T(128)S(1)}, s32[3]{0:T(128)}, u32[]{:S(2)}) copy-start(s32[3]{0:T(128)} %pad_add_fusion.info_ref) | copy-start | bytes 40
  33.7 4.4 %collective-permute-start = (bf16[272,256]{1,0:T(8,128)(2,1)}, bf16[272,256]{1,0:T(8,128)(2,1)S(1)}, u32[]{:S(2)}, u32[]{:S(2)}) collective-permute-start(bf16[272,256]{1,0:T(8,128)(2,1)} %stage.1), channel_id=1, source_target_pairs={{0,16},{16,0},{32,48},{48,32},{64,80},{80,64},{96,112},{112,96},{1... | collective-permute-start | bytes 417800 | tf_op jit(solution)/shard_map/ppermute | solution.py:346
  39.0 48.5 %copy-start.7 = (s32[4096]{0:T(1024)S(1)}, s32[4096]{0:T(1024)}, u32[]{:S(2)}) copy-start(s32[4096]{0:T(1024)} %seg_ref.1) | copy-start | bytes 49156
  39.0 48.5 %copy-start.8 = (s32[32,32]{1,0:T(8,128)S(1)}, s32[32,32]{1,0:T(8,128)}, u32[]{:S(2)}) copy-start(s32[32,32]{1,0:T(8,128)} %allow_ref.1) | copy-start | bytes 12292
  39.0 19.9 %collective-permute-start.1 = (bf16[2,272,256]{2,1,0:T(8,128)(2,1)S(1)}, bf16[2,272,256]{2,1,0:T(8,128)(2,1)S(1)}, u32[]{:S(2)}, u32[]{:S(2)}) collective-permute-start(bf16[2,272,256]{2,1,0:T(8,128)(2,1)S(1)} %pad_maximum_fusion.own_ref), channel_id=1, source_target_pairs={{0,32},{1,225},{2,34},{3,227},{4,36},{5,229},{6,38},{7,231},{8,40}... | collective-permute-start | bytes 835592 | tf_op jit(solution)/shard_map/ppermute | solution.py:359
  58.9 24.4 %copy-start.1 = (bf16[2,272,256]{2,1,0:T(8,128)(2,1)}, bf16[2,272,256]{2,1,0:T(8,128)(2,1)S(1)}, u32[]{:S(2)}) copy-start(bf16[2,272,256]{2,1,0:T(8,128)(2,1)S(1)} %collective-permute-done.1.refs_0_) | copy-start | bytes 835588
  58.9 5.4 %collective-permute-start.2 = (bf16[2,272,256]{2,1,0:T(8,128)(2,1)S(1)}, bf16[2,272,256]{2,1,0:T(8,128)(2,1)S(1)}, u32[]{:S(2)}, u32[]{:S(2)}) collective-permute-start(bf16[2,272,256]{2,1,0:T(8,128)(2,1)S(1)} %collective-permute-done.1.refs_0_), channel_id=1, source_target_pairs={{0,32},{1,225},{2,34},{3,227},{4,36},{5,229},{6,38},{7,231},{8,40}... | collective-permute-start | bytes 835592 | tf_op jit(solution)/shard_map/ppermute | solution.py:359
  64.3 5.6 %collective-permute-start.3 = (bf16[2,272,256]{2,1,0:T(8,128)(2,1)S(1)}, bf16[2,272,256]{2,1,0:T(8,128)(2,1)S(1)}, u32[]{:S(2)}, u32[]{:S(2)}) collective-permute-start(bf16[2,272,256]{2,1,0:T(8,128)(2,1)S(1)} %collective-permute-done.2.refs_1_), channel_id=1, source_target_pairs={{0,32},{1,225},{2,34},{3,227},{4,36},{5,229},{6,38},{7,231},{8,40}... | collective-permute-start | bytes 835592 | tf_op jit(solution)/shard_map/ppermute | solution.py:359
  66.4 16.0 %collective-permute-start.5 = (bf16[2,272,256]{2,1,0:T(8,128)(2,1)S(1)}, bf16[2,272,256]{2,1,0:T(8,128)(2,1)S(1)}, u32[]{:S(2)}, u32[]{:S(2)}) collective-permute-start(bf16[2,272,256]{2,1,0:T(8,128)(2,1)S(1)} %collective-permute-done.1.refs_0_), channel_id=1, source_target_pairs={{0,1},{1,0},{2,3},{3,2},{4,5},{5,4},{6,7},{7,6},{8,9},{9,8},{10,11... | collective-permute-start | bytes 835592 | tf_op jit(solution)/shard_map/ppermute | solution.py:361
  68.2 14.1 %collective-permute-start.6 = (bf16[2,272,256]{2,1,0:T(8,128)(2,1)S(1)}, bf16[2,272,256]{2,1,0:T(8,128)(2,1)S(1)}, u32[]{:S(2)}, u32[]{:S(2)}) collective-permute-start(bf16[2,272,256]{2,1,0:T(8,128)(2,1)S(1)} %collective-permute-done.2.refs_1_), channel_id=1, source_target_pairs={{0,1},{1,0},{2,3},{3,2},{4,5},{5,4},{6,7},{7,6},{8,9},{9,8},{10,11... | collective-permute-start | bytes 835592 | tf_op jit(solution)/shard_map/ppermute | solution.py:361
  68.2 0.7 copy-start.3
  69.9 6.3 %collective-permute-start.4 = (bf16[272,256]{1,0:T(8,128)(2,1)S(1)}, bf16[272,256]{1,0:T(8,128)(2,1)S(1)}, u32[]{:S(2)}, u32[]{:S(2)}) collective-permute-start(bf16[272,256]{1,0:T(8,128)(2,1)S(1)} %dynamic-slice_bitcast_fusion), channel_id=1, source_target_pairs={{0,32},{1,225},{2,34},{3,227},{4,36},{5,229},{6,38},{7,231},{8,40}... | collective-permute-start | bytes 417800 | tf_op jit(solution)/shard_map/ppermute | solution.py:359
  73.1 10.3 %collective-permute-start.7 = (bf16[2,272,256]{2,1,0:T(8,128)(2,1)S(1)}, bf16[2,272,256]{2,1,0:T(8,128)(2,1)S(1)}, u32[]{:S(2)}, u32[]{:S(2)}) collective-permute-start(bf16[2,272,256]{2,1,0:T(8,128)(2,1)S(1)} %collective-permute-done.3.refs_2_), channel_id=1, source_target_pairs={{0,1},{1,0},{2,3},{3,2},{4,5},{5,4},{6,7},{7,6},{8,9},{9,8},{10,11... | collective-permute-start | bytes 835592 | tf_op jit(solution)/shard_map/ppermute | solution.py:361
  76.2 7.2 %collective-permute-start.8 = (bf16[272,256]{1,0:T(8,128)(2,1)S(1)}, bf16[272,256]{1,0:T(8,128)(2,1)S(1)}, u32[]{:S(2)}, u32[]{:S(2)}) collective-permute-start(bf16[272,256]{1,0:T(8,128)(2,1)S(1)} %collective-permute-done.4.refs_3_), channel_id=1, source_target_pairs={{0,1},{1,0},{2,3},{3,2},{4,5},{5,4},{6,7},{7,6},{8,9},{9,8},{10,11... | collective-permute-start | bytes 417800 | tf_op jit(solution)/shard_map/ppermute | solution.py:361
  83.3 1.0 copy-start.2
  84.3 1.0 copy-start.4
  86.8 0.7 copy-start.5
  87.6 1.0 copy-start.6
  95.3 1.1 copy-start
  96.4 2.1 %collective-permute-start.9 = (bf16[2560,128]{1,0:T(8,128)(2,1)S(1)}, bf16[2560,128]{1,0:T(8,128)(2,1)S(1)}, u32[]{:S(2)}, u32[]{:S(2)}) collective-permute-start(bf16[2560,128]{1,0:T(8,128)(2,1)S(1)} %get-tuple-element.11), channel_id=1, source_target_pairs={{0,1},{1,0},{2,3},{3,2},{4,5},{5,4},{6,7},{7,6},{8,9},{9,8},{10,11... | collective-permute-start | bytes 1966088 | tf_op jit(solution)/shard_map/ppermute | solution.py:385
  98.5 0.8 copy-start.10

commit v3 on v2

--- a/solution.py
+++ b/solution.py
@@ -357,6 +357,8 @@
         if step == RING:
             moving = lax.dynamic_index_in_dim(moving, tp_index % 2, 0, keepdims=False)
         moving = lax.ppermute(moving, ("ctx", "tp"), turn)
+        if step == 2:
+            moving, queries = lax.optimization_barrier((moving, queries))
         mine.append(moving)
         theirs.append(lax.ppermute(moving, "tp", swap))
     g_local = lax.all_to_all(out_grad, "tp", split_axis=1, concat_axis=0, tiled=True)

time: 173 us -> 170 us (0.983); the launches traced: 174 us -> 169 us
  starting transfers between devices: 38.4 us -> 31.9 us
  waiting for transfers between devices: 37.1 us -> 39.4 us
  local copies, waits for them, and re-layouts: 8.71 us -> 6.98 us
    ppermute x4, waiting for transfers between devices: 22.7 us -> 31.2 us  [on_device(): moving = lax.ppermute(moving, ('ctx', 'tp'), turn)]
    all_to_all x1, waiting for transfers between devices: 8.66 us -> 2.75 us  [on_device(): lax.all_to_all(out_grad, 'tp', split_axis=1, concat_axis=0, tiled=True)]
    ppermute x4, starting transfers between devices: 11.1 us -> 5.59 us  [on_device(): theirs.append(lax.ppermute(moving, 'tp', swap))]
    all_to_all x1, starting transfers between devices: 8.33 us -> 5.2 us  [on_device(): lax.all_to_all(q_send, 'ctx', split_axis=0, concat_axis=0, tiled=True)]
    ppermute x4, starting transfers between devices: 8.8 us -> 11.7 us  [on_device(): moving = lax.ppermute(moving, ('ctx', 'tp'), turn)]
    unnamed x22 -> x24, local copies, waits for them, and re-layouts: 6.18 us -> 5.49 us
  transfers between devices with their start and end apart: 12 -> 12, of which waited for: 7 -> 7; matrix products, arithmetic and copies ran while one was open for 1% -> 1% of each run, Pallas kernels for 4% -> 3%
where the time goes in v3:
time: 170 us; the launch traced here: 169 us
  blocking collectives  72.1 us (42%)
  waiting for transfers between devices  39.4 us (23%)
  starting transfers between devices  31.9 us (19%)
  Pallas kernels  16.2 us (10%)
  local copies, waits for them, and re-layouts  6.98 us (4%)
  other arithmetic  1.75 us (1%)
    all_to_all x1, blocking collectives, on_device(): lax.all_to_all(part.reshape(SHARDS, TOK, HEAD_SIZE), 'ctx', split_axis=0,...  57.2 us
    ppermute x4, waiting for transfers between devices, on_device(): moving = lax.ppermute(moving, ('ctx', 'tp'), turn)  31.2 us
    all_to_all x1, blocking collectives, on_device(): lax.all_to_all(owned.reshape(tp_size, TOK // tp_size, HEAD_SIZE), 'tp', s...  14.9 us
    ppermute x4, starting transfers between devices, on_device(): moving = lax.ppermute(moving, ('ctx', 'tp'), turn)  11.7 us
    all_to_all x1, starting transfers between devices, on_device(): lax.all_to_all(out_grad, 'tp', split_axis=1, concat_axis=0, tiled=True)  7.06 us
    pallas_call x1, Pallas kernels, call_attention(): pl.pallas_call(attention_kernel, in_specs=[SMEM, SMEM, SMEM] + [VMEM] * 5...  6.91 us
    ppermute x4, starting transfers between devices, on_device(): theirs.append(lax.ppermute(moving, 'tp', swap))  5.59 us
    unnamed x24, local copies, waits for them, and re-layouts  5.49 us
  transfers between devices with their start and end apart: 12, of which 7 were waited for; matrix products, arithmetic and copies ran while one was open for 1% of the time, Pallas kernels for 3%

profile of v3, /device:TPU:1, one launch (start us, length us, event | category | flops | bytes accessed | tf_op | source)
XLA Modules:
  0.0 169.1 jit_solution(7485994294394384931)
XLA Ops:
  0.6 0.0 copy-start.11
  0.7 0.7 pad_add_fusion.info_ref
  1.3 2.3 %stage.1 = bf16[272,256]{1,0:T(8,128)(2,1)} custom-call(s32[3]{0:T(128)} %pad_add_fusion.info_ref, s32[1,256]{1,0:T(1,128)} %bitcast.38, bf16[2,256,1024]{2,1,0:T(8,128)(2,1)} %kv_ref.1), custom_call_target="tpu_custom_call" | custom-call | tf_op jit(solution)/shard_map/stage/pallas_call | solution.py:332
  3.6 2.0 %collective-permute-start = (bf16[272,256]{1,0:T(8,128)(2,1)}, bf16[272,256]{1,0:T(8,128)(2,1)S(1)}, u32[]{:S(2)}, u32[]{:S(2)}) collective-permute-start(bf16[272,256]{1,0:T(8,128)(2,1)} %stage.1), channel_id=1, source_target_pairs={{0,16},{16,0},{32,48},{48,32},{64,80},{80,64},{96,112},{112,96},{1... | collective-permute-start | bytes 417800 | tf_op jit(solution)/shard_map/ppermute | solution.py:346
  5.6 2.7 %collective-permute-done = bf16[272,256]{1,0:T(8,128)(2,1)S(1)} collective-permute-done((bf16[272,256]{1,0:T(8,128)(2,1)}, bf16[272,256]{1,0:T(8,128)(2,1)S(1)}, u32[]{:S(2)}, u32[]{:S(2)}) %collective-permute-start) | collective-permute-done | bytes 139296 | tf_op jit(solution)/shard_map/ppermute | solution.py:346
  8.3 0.9 pad_maximum_fusion.own_ref
  9.2 6.5 %collective-permute-start.1 = (bf16[2,272,256]{2,1,0:T(8,128)(2,1)S(1)}, bf16[2,272,256]{2,1,0:T(8,128)(2,1)S(1)}, u32[]{:S(2)}, u32[]{:S(2)}) collective-permute-start(bf16[2,272,256]{2,1,0:T(8,128)(2,1)S(1)} %pad_maximum_fusion.own_ref), channel_id=1, source_target_pairs={{0,32},{1,225},{2,34},{3,227},{4,36},{5,229},{6,38},{7,231},{8,40}... | collective-permute-start | bytes 835592 | tf_op jit(solution)/shard_map/ppermute | solution.py:359
  15.8 0.0 copy-done.11
  15.8 0.8 copy.16
  16.6 7.1 %all-to-all-start.1 = ((bf16[16,16,1024]{2,0,1:T(8,128)(2,1)}), bf16[16,16,1024]{2,0,1:T(8,128)(2,1)S(1)}, u32[]{:S(2)}, u32[]{:S(2)}) async-start(bf16[16,16,1024]{2,0,1:T(8,128)(2,1)} %bitcast.25), calls=%async_computation.1 | async-start | bytes 1048576 | tf_op jit(solution)/shard_map/all_to_all | solution.py:364
  23.7 0.0 collective-permute-done.1.refs_0_
  23.7 0.0 copy-start.1
  23.7 1.5 collective-permute-start.2
  25.2 4.2 %collective-permute-done.2.refs_1_ = bf16[2,272,256]{2,1,0:T(8,128)(2,1)S(1)} collective-permute-done((bf16[2,272,256]{2,1,0:T(8,128)(2,1)S(1)}, bf16[2,272,256]{2,1,0:T(8,128)(2,1)S(1)}, u32[]{:S(2)}, u32[]{:S(2)}) %collective-permute-start.2) | collective-permute-done | bytes 278560 | tf_op jit(solution)/shard_map/ppermute | solution.py:359
  29.5 2.8 %pack.1 = bf16[512,1024]{1,0:T(8,128)(2,1)} custom-call(s32[1,256]{1,0:T(1,128)} %bitcast.39, bf16[256,1024]{1,0:T(8,128)(2,1)} %rows_ref), custom_call_target="tpu_custom_call" | custom-call | tf_op jit(solution)/shard_map/pack/pallas_call | solution.py:365
  32.2 2.8 %all-to-all-done.1 = bf16[16,16,1024]{2,0,1:T(8,128)(2,1)S(1)} async-done(((bf16[16,16,1024]{2,0,1:T(8,128)(2,1)}), bf16[16,16,1024]{2,0,1:T(8,128)(2,1)S(1)}, u32[]{:S(2)}, u32[]{:S(2)}) %all-to-all-start.1) | async-done | bytes 524320 | tf_op jit(solution)/shard_map/all_to_all | solution.py:364
  35.0 5.2 %all-to-all-start = ((bf16[16,32,1024]{2,1,0:T(8,128)(2,1)}), bf16[16,32,1024]{2,1,0:T(8,128)(2,1)S(1)}, u32[]{:S(2)}, u32[]{:S(2)}) async-start(bf16[16,32,1024]{2,1,0:T(8,128)(2,1)} %bitcast.31), calls=%async_computation | async-start | bytes 2097152 | tf_op jit(solution)/shard_map/all_to_all | solution.py:372
  40.2 0.0 copy-start.7
  40.2 0.0 copy-start.8
  40.2 2.7 %collective-permute-start.3 = (bf16[2,272,256]{2,1,0:T(8,128)(2,1)S(1)}, bf16[2,272,256]{2,1,0:T(8,128)(2,1)S(1)}, u32[]{:S(2)}, u32[]{:S(2)}) collective-permute-start(bf16[2,272,256]{2,1,0:T(8,128)(2,1)S(1)} %collective-permute-done.2.refs_1_), channel_id=1, source_target_pairs={{0,32},{1,225},{2,34},{3,227},{4,36},{5,229},{6,38},{7,231},{8,40}... | collective-permute-start | bytes 835592 | tf_op jit(solution)/shard_map/ppermute | solution.py:359
  42.9 0.8 collective-permute-start.5
  43.6 0.1 collective-permute-start.6
  43.7 24.7 %collective-permute-done.3.refs_2_ = bf16[2,272,256]{2,1,0:T(8,128)(2,1)S(1)} collective-permute-done((bf16[2,272,256]{2,1,0:T(8,128)(2,1)S(1)}, bf16[2,272,256]{2,1,0:T(8,128)(2,1)S(1)}, u32[]{:S(2)}, u32[]{:S(2)}) %collective-permute-start.3) | collective-permute-done | bytes 278560 | tf_op jit(solution)/shard_map/ppermute | solution.py:359
  68.5 1.0 collective-permute-start.4
  69.5 0.8 collective-permute-start.7
  70.2 2.2 %collective-permute-done.4.refs_3_ = bf16[272,256]{1,0:T(8,128)(2,1)S(1)} collective-permute-done((bf16[272,256]{1,0:T(8,128)(2,1)S(1)}, bf16[272,256]{1,0:T(8,128)(2,1)S(1)}, u32[]{:S(2)}, u32[]{:S(2)}) %collective-permute-start.4) | collective-permute-done | bytes 139296 | tf_op jit(solution)/shard_map/ppermute | solution.py:359
  72.5 3.9 %collective-permute-start.8 = (bf16[272,256]{1,0:T(8,128)(2,1)S(1)}, bf16[272,256]{1,0:T(8,128)(2,1)S(1)}, u32[]{:S(2)}, u32[]{:S(2)}) collective-permute-start(bf16[272,256]{1,0:T(8,128)(2,1)S(1)} %collective-permute-done.4.refs_3_), channel_id=1, source_target_pairs={{0,1},{1,0},{2,3},{3,2},{4,5},{5,4},{6,7},{7,6},{8,9},{9,8},{10,11... | collective-permute-start | bytes 417800 | tf_op jit(solution)/shard_map/ppermute | solution.py:363
  76.4 0.0 collective-permute-done.5.refs_4_
  76.4 0.0 collective-permute-done.6.refs_5_
  76.4 1.0 collective-permute-done.8.refs_7_
  77.4 0.0 collective-permute-done.7.refs_6_
  77.4 1.0 copy-done.2
  78.4 1.0 copy-done.4
  79.3 1.6 permute.1
  80.9 0.0 copy-start.5
  80.9 0.7 copy-done.5
  81.6 0.0 all-to-all-done
  81.6 0.9 copy-done.6
  82.6 6.9 %attention.1 = (bf16[256,1024]{1,0:T(8,128)(2,1)}, f32[2560,128]{1,0:T(8,128)S(1)}, bf16[2560,128]{1,0:T(8,128)(2,1)S(1)}) custom-call(s32[3]{0:T(128)S(1)} %copy-done.9, s32[4096]{0:T(1024)S(1)} %copy-done.7, s32[32,32]{1,0:T(8,128)S(1)} %copy-done.8, s32[32,128]{1,0:T(8,128)S(1)} %bitcast.29, bf16[512,256]{1,0:T(8,128)(2,1)S(1)} %copy-done.6, ...), custom_call_target="tpu_custom_call" | custom-call | tf_op jit(solution)/shard_map/attention/pallas_call | solution.py:293
  89.5 1.1 copy-done
  90.5 0.4 collective-permute-start.9
  90.9 1.7 %collective-permute-done.9.recv_ref = bf16[2560,128]{1,0:T(8,128)(2,1)S(1)} collective-permute-done((bf16[2560,128]{1,0:T(8,128)(2,1)S(1)}, bf16[2560,128]{1,0:T(8,128)(2,1)S(1)}, u32[]{:S(2)}, u32[]{:S(2)}) %collective-permute-start.9) | collective-permute-done | bytes 655392 | tf_op jit(solution)/shard_map/ppermute | solution.py:387
  92.6 0.8 copy-done.10
  93.5 2.7 %merge.1 = bf16[4096,128]{1,0:T(8,128)(2,1)} custom-call(s32[3]{0:T(128)} %pad_add_fusion.info_ref, f32[2560,128]{1,0:T(8,128)} %copy-done, bf16[2560,128]{1,0:T(8,128)(2,1)} %copy-done.10), custom_call_target="tpu_custom_call" | custom-call | tf_op jit(solution)/shard_map/merge/pallas_call | solution.py:388
  96.2 57.2 %all_to_all.40 = bf16[16,256,128]{2,1,0:T(8,128)(2,1)S(1)} all-to-all(bf16[16,256,128]{2,1,0:T(8,128)(2,1)} %bitcast.30), channel_id=1, replica_groups=mesh['ctx'=16,'tp'=16] {'ctx'}, dimensions={0} | all-to-all | bytes 2097152 | tf_op jit(solution)/shard_map/all_to_all | solution.py:395
  153.4 0.1 reduce_sum.12
  153.6 14.9 %all_to_all.41 = bf16[16,16,128]{2,1,0:T(8,128)(2,1)S(1)} all-to-all(bf16[16,16,128]{2,1,0:T(8,128)(2,1)S(1)} %bitcast.34), channel_id=1, replica_groups=mesh['ctx'=16,'tp'=16] {'tp'}, dimensions={0} | all-to-all | bytes 131072 | tf_op jit(solution)/shard_map/all_to_all | solution.py:399
  168.4 0.6 copy.17
  (13 shorter events, 0.0 us)
Async XLA Ops:
  0.6 15.1 %copy-start.11 = (bf16[16,16384]{1,0:T(8,128)(2,1)S(1)}, bf16[16,16384]{1,0:T(8,128)(2,1)}, u32[]{:S(2)}) copy-start(bf16[16,16384]{1,0:T(8,128)(2,1)} %param.8) | copy-start | bytes 1572868
  3.6 4.7 %collective-permute-start = (bf16[272,256]{1,0:T(8,128)(2,1)}, bf16[272,256]{1,0:T(8,128)(2,1)S(1)}, u32[]{:S(2)}, u32[]{:S(2)}) collective-permute-start(bf16[272,256]{1,0:T(8,128)(2,1)} %stage.1), channel_id=1, source_target_pairs={{0,16},{16,0},{32,48},{48,32},{64,80},{80,64},{96,112},{112,96},{1... | collective-permute-start | bytes 417800 | tf_op jit(solution)/shard_map/ppermute | solution.py:346
  9.2 14.4 %collective-permute-start.1 = (bf16[2,272,256]{2,1,0:T(8,128)(2,1)S(1)}, bf16[2,272,256]{2,1,0:T(8,128)(2,1)S(1)}, u32[]{:S(2)}, u32[]{:S(2)}) collective-permute-start(bf16[2,272,256]{2,1,0:T(8,128)(2,1)S(1)} %pad_maximum_fusion.own_ref), channel_id=1, source_target_pairs={{0,32},{1,225},{2,34},{3,227},{4,36},{5,229},{6,38},{7,231},{8,40}... | collective-permute-start | bytes 835592 | tf_op jit(solution)/shard_map/ppermute | solution.py:359
  16.6 18.4 %all-to-all-start.1 = ((bf16[16,16,1024]{2,0,1:T(8,128)(2,1)}), bf16[16,16,1024]{2,0,1:T(8,128)(2,1)S(1)}, u32[]{:S(2)}, u32[]{:S(2)}) async-start(bf16[16,16,1024]{2,0,1:T(8,128)(2,1)} %bitcast.25), calls=%async_computation.1 | async-start | bytes 1048576 | tf_op jit(solution)/shard_map/all_to_all | solution.py:364
  23.7 19.2 %copy-start.1 = (bf16[2,272,256]{2,1,0:T(8,128)(2,1)}, bf16[2,272,256]{2,1,0:T(8,128)(2,1)S(1)}, u32[]{:S(2)}) copy-start(bf16[2,272,256]{2,1,0:T(8,128)(2,1)S(1)} %collective-permute-done.1.refs_0_) | copy-start | bytes 835588
  23.7 5.8 %collective-permute-start.2 = (bf16[2,272,256]{2,1,0:T(8,128)(2,1)S(1)}, bf16[2,272,256]{2,1,0:T(8,128)(2,1)S(1)}, u32[]{:S(2)}, u32[]{:S(2)}) collective-permute-start(bf16[2,272,256]{2,1,0:T(8,128)(2,1)S(1)} %collective-permute-done.1.refs_0_), channel_id=1, source_target_pairs={{0,32},{1,225},{2,34},{3,227},{4,36},{5,229},{6,38},{7,231},{8,40}... | collective-permute-start | bytes 835592 | tf_op jit(solution)/shard_map/ppermute | solution.py:359
  29.5 14.2 %copy-start.3 = (bf16[2,272,256]{2,1,0:T(8,128)(2,1)}, bf16[2,272,256]{2,1,0:T(8,128)(2,1)S(1)}, u32[]{:S(2)}) copy-start(bf16[2,272,256]{2,1,0:T(8,128)(2,1)S(1)} %collective-permute-done.2.refs_1_) | copy-start | bytes 835588
  32.2 45.2 %copy-start.9 = (s32[3]{0:T(128)S(1)}, s32[3]{0:T(128)}, u32[]{:S(2)}) copy-start(s32[3]{0:T(128)} %pad_add_fusion.info_ref) | copy-start | bytes 40
  35.0 46.6 %all-to-all-start = ((bf16[16,32,1024]{2,1,0:T(8,128)(2,1)}), bf16[16,32,1024]{2,1,0:T(8,128)(2,1)S(1)}, u32[]{:S(2)}, u32[]{:S(2)}) async-start(bf16[16,32,1024]{2,1,0:T(8,128)(2,1)} %bitcast.31), calls=%async_computation | async-start | bytes 2097152 | tf_op jit(solution)/shard_map/all_to_all | solution.py:372
  40.2 41.4 %copy-start.7 = (s32[4096]{0:T(1024)S(1)}, s32[4096]{0:T(1024)}, u32[]{:S(2)}) copy-start(s32[4096]{0:T(1024)} %seg_ref.1) | copy-start | bytes 49156
  40.2 41.4 %copy-start.8 = (s32[32,32]{1,0:T(8,128)S(1)}, s32[32,32]{1,0:T(8,128)}, u32[]{:S(2)}) copy-start(s32[32,32]{1,0:T(8,128)} %allow_ref.1) | copy-start | bytes 12292
  40.2 28.3 %collective-permute-start.3 = (bf16[2,272,256]{2,1,0:T(8,128)(2,1)S(1)}, bf16[2,272,256]{2,1,0:T(8,128)(2,1)S(1)}, u32[]{:S(2)}, u32[]{:S(2)}) collective-permute-start(bf16[2,272,256]{2,1,0:T(8,128)(2,1)S(1)} %collective-permute-done.2.refs_1_), channel_id=1, source_target_pairs={{0,32},{1,225},{2,34},{3,227},{4,36},{5,229},{6,38},{7,231},{8,40}... | collective-permute-start | bytes 835592 | tf_op jit(solution)/shard_map/ppermute | solution.py:359
  42.9 33.6 %collective-permute-start.5 = (bf16[2,272,256]{2,1,0:T(8,128)(2,1)S(1)}, bf16[2,272,256]{2,1,0:T(8,128)(2,1)S(1)}, u32[]{:S(2)}, u32[]{:S(2)}) collective-permute-start(bf16[2,272,256]{2,1,0:T(8,128)(2,1)S(1)} %collective-permute-done.1.refs_0_), channel_id=1, source_target_pairs={{0,1},{1,0},{2,3},{3,2},{4,5},{5,4},{6,7},{7,6},{8,9},{9,8},{10,11... | collective-permute-start | bytes 835592 | tf_op jit(solution)/shard_map/ppermute | solution.py:363
  43.6 32.8 %collective-permute-start.6 = (bf16[2,272,256]{2,1,0:T(8,128)(2,1)S(1)}, bf16[2,272,256]{2,1,0:T(8,128)(2,1)S(1)}, u32[]{:S(2)}, u32[]{:S(2)}) collective-permute-start(bf16[2,272,256]{2,1,0:T(8,128)(2,1)S(1)} %collective-permute-done.2.refs_1_), channel_id=1, source_target_pairs={{0,1},{1,0},{2,3},{3,2},{4,5},{5,4},{6,7},{7,6},{8,9},{9,8},{10,11... | collective-permute-start | bytes 835592 | tf_op jit(solution)/shard_map/ppermute | solution.py:363
  68.5 4.0 %collective-permute-start.4 = (bf16[272,256]{1,0:T(8,128)(2,1)S(1)}, bf16[272,256]{1,0:T(8,128)(2,1)S(1)}, u32[]{:S(2)}, u32[]{:S(2)}) collective-permute-start(bf16[272,256]{1,0:T(8,128)(2,1)S(1)} %dynamic-slice_bitcast_fusion), channel_id=1, source_target_pairs={{0,32},{1,225},{2,34},{3,227},{4,36},{5,229},{6,38},{7,231},{8,40}... | collective-permute-start | bytes 417800 | tf_op jit(solution)/shard_map/ppermute | solution.py:359
  69.5 8.0 %collective-permute-start.7 = (bf16[2,272,256]{2,1,0:T(8,128)(2,1)S(1)}, bf16[2,272,256]{2,1,0:T(8,128)(2,1)S(1)}, u32[]{:S(2)}, u32[]{:S(2)}) collective-permute-start(bf16[2,272,256]{2,1,0:T(8,128)(2,1)S(1)} %collective-permute-done.3.refs_2_), channel_id=1, source_target_pairs={{0,1},{1,0},{2,3},{3,2},{4,5},{5,4},{6,7},{7,6},{8,9},{9,8},{10,11... | collective-permute-start | bytes 835592 | tf_op jit(solution)/shard_map/ppermute | solution.py:363
  72.5 4.9 %collective-permute-start.8 = (bf16[272,256]{1,0:T(8,128)(2,1)S(1)}, bf16[272,256]{1,0:T(8,128)(2,1)S(1)}, u32[]{:S(2)}, u32[]{:S(2)}) collective-permute-start(bf16[272,256]{1,0:T(8,128)(2,1)S(1)} %collective-permute-done.4.refs_3_), channel_id=1, source_target_pairs={{0,1},{1,0},{2,3},{3,2},{4,5},{5,4},{6,7},{7,6},{8,9},{9,8},{10,11... | collective-permute-start | bytes 417800 | tf_op jit(solution)/shard_map/ppermute | solution.py:363
  77.4 1.0 copy-start.2
  78.4 1.0 copy-start.4
  80.9 0.7 copy-start.5
  81.6 1.0 copy-start.6
  89.5 1.1 copy-start
  90.5 2.1 %collective-permute-start.9 = (bf16[2560,128]{1,0:T(8,128)(2,1)S(1)}, bf16[2560,128]{1,0:T(8,128)(2,1)S(1)}, u32[]{:S(2)}, u32[]{:S(2)}) collective-permute-start(bf16[2560,128]{1,0:T(8,128)(2,1)S(1)} %get-tuple-element.15), channel_id=1, source_target_pairs={{0,1},{1,0},{2,3},{3,2},{4,5},{5,4},{6,7},{7,6},{8,9},{9,8},{10,11... | collective-permute-start | bytes 1966088 | tf_op jit(solution)/shard_map/ppermute | solution.py:387
  92.6 0.8 copy-start.10

commit v4 on v2

--- a/solution.py
+++ b/solution.py
@@ -61,15 +61,26 @@
         out_ref[:, cols] = dot(picks, rows_ref[:, cols]).astype(BF16)
 
 
-def stage_kernel(info_ref, place_ref, kv_ref, out_ref):
+def stage_kernel(place_ref, kv_ref, out_ref, arrived):
+    cols = pl.ds(pl.multiple_of((lax.axis_index("tp") // 2) * HEAD_SIZE, HEAD_SIZE), HEAD_SIZE)
+    copies = [
+        pltpu.make_async_copy(
+            kv_ref.at[i, :, cols],
+            out_ref.at[pl.ds(0, TOK), pl.ds(i * HEAD_SIZE, HEAD_SIZE)],
+            arrived.at[i],
+        )
+        for i in range(2)
+    ]
+    for copy in copies:
+        copy.start()
     place = place_ref[...]
-    out_ref[:TOK, :HEAD_SIZE] = kv_ref[0]
-    out_ref[:TOK, HEAD_SIZE:] = kv_ref[1]
     row = iota((META, TOK), 0)
     owner = jnp.broadcast_to((place >> 8).astype(F32), (META, TOK))
     within = jnp.broadcast_to((place & (TOK - 1)).astype(F32), (META, TOK))
     meta = jnp.where(row == 0, owner, jnp.where(row == 1, within, 0.0))
     out_ref[TOK:, :] = meta.astype(BF16)
+    for copy in copies:
+        copy.wait()
 
 
 def permute_kernel(info_ref, own_ref, *refs):
@@ -328,37 +339,34 @@
     ctx_index = lax.axis_index("ctx")
     tp_size = lax.axis_size("tp")
     width = LOCAL_HEADS * HEAD_SIZE
-    info = jnp.stack([ctx_index, tp_index % 2, tp_index // 2]).astype(jnp.int32)
+    info = jnp.stack([ctx_index, tp_index % 2]).astype(jnp.int32)
     staged = pl.pallas_call(
         stage_kernel,
-        grid_spec=pltpu.PrefetchScalarGridSpec(
-            num_scalar_prefetch=1,
-            grid=(1,),
-            in_specs=[
-                pl.BlockSpec((1, TOK), lambda i, info: (0, 0)),
-                pl.BlockSpec((2, TOK, HEAD_SIZE), lambda i, info: (0, 0, info[2])),
-            ],
-            out_specs=pl.BlockSpec((TOK + META, 2 * HEAD_SIZE), lambda i, info: (0, 0)),
-        ),
+        in_specs=[VMEM, pl.BlockSpec(memory_space=pl.ANY)],
+        out_specs=VMEM,
         out_shape=jax.ShapeDtypeStruct((TOK + META, 2 * HEAD_SIZE), BF16),
+        scratch_shapes=[pltpu.SemaphoreType.DMA((2,))],
         name="stage",
-    )(info, place.reshape(1, TOK), keys_values)
+    )(place.reshape(1, TOK), keys_values)
     beside = lax.ppermute(staged, "ctx", [(k, k ^ 1) for k in range(SHARDS)])
     own = jnp.stack([staged, beside])
-    turn = []
-    for k in range(SHARDS * tp_size):
-        ctx, tp = k // tp_size, k % tp_size
-        near = (ctx + (2 if tp % 2 == 0 else SHARDS - 2)) % SHARDS
-        turn.append((k, near * tp_size + tp))
+
+    def around(hops):
+        pairs = []
+        for k in range(SHARDS * tp_size):
+            ctx, tp = k // tp_size, k % tp_size
+            far = (ctx + (2 * hops if tp % 2 == 0 else -2 * hops)) % SHARDS
+            pairs.append((k, far * tp_size + tp))
+        return pairs
+
     swap = [(k, k ^ 1) for k in range(tp_size)]
-    mine, theirs = [], []
-    moving = own
-    for step in range(1, RING + 1):
-        if step == RING:
-            moving = lax.dynamic_index_in_dim(moving, tp_index % 2, 0, keepdims=False)
-        moving = lax.ppermute(moving, ("ctx", "tp"), turn)
-        mine.append(moving)
-        theirs.append(lax.ppermute(moving, "tp", swap))
+    first = lax.ppermute(own, ("ctx", "tp"), around(1))
+    second = lax.ppermute(first, ("ctx", "tp"), around(1))
+    third = lax.ppermute(second, ("ctx", "tp"), around(1))
+    half = lax.dynamic_index_in_dim(second, tp_index % 2, 0, keepdims=False)
+    fourth = lax.ppermute(half, ("ctx", "tp"), around(2))
+    mine = [first, second, third, fourth]
+    theirs = [lax.ppermute(piece, "tp", swap) for piece in mine]
     g_local = lax.all_to_all(out_grad, "tp", split_axis=1, concat_axis=0, tiled=True)
     q_send = pl.pallas_call(
         pack_kernel,
@@ -367,6 +375,7 @@
         out_shape=jax.ShapeDtypeStruct((SHARDS * SLOTS, width), BF16),
         name="pack",
     )(place.reshape(1, TOK), queries)
+    q_send, theirs[1] = lax.optimization_barrier((q_send, theirs[1]))
     q_recv = lax.all_to_all(q_send, "ctx", split_axis=0, concat_axis=0, tiled=True)
     kv_window, unpack = pl.pallas_call(
         permute_kernel,

time: 173 us -> 178 us (1.029); the launches traced: 174 us -> 176 us
  starting transfers between devices: 38.4 us -> 33.6 us
  local copies, waits for them, and re-layouts: 8.71 us -> 12.4 us
  waiting for transfers between devices: 37.1 us -> 40.7 us
    unnamed x22 -> x36, local copies, waits for them, and re-layouts: 6.18 us -> 10.9 us
    ppermute x8, waiting for transfers between devices: 23.7 us -> 27.5 us  [the longest x1 22.4 us: on_device(): third = lax.ppermute(second, ('ctx', 'tp'), around(1))]
    all_to_all x1, starting transfers between devices: 8.33 us -> 5.9 us  [on_device(): lax.all_to_all(q_send, 'ctx', split_axis=0, concat_axis=0, tiled=True)]
  transfers between devices with their start and end apart: 12 -> 12, of which waited for: 7 -> 6; matrix products, arithmetic and copies ran while one was open for 1% -> 1% of each run, Pallas kernels for 4% -> 3%
where the time goes in v4:
time: 178 us; the launch traced here: 176 us
  blocking collectives  71.3 us (40%)
  waiting for transfers between devices  40.7 us (23%)
  starting transfers between devices  33.6 us (19%)
  Pallas kernels  16.6 us (9%)
  local copies, waits for them, and re-layouts  12.4 us (7%)
    all_to_all x1, blocking collectives, on_device(): lax.all_to_all(part.reshape(SHARDS, TOK, HEAD_SIZE), 'ctx', split_axis=0,...  57.7 us
    ppermute x1, waiting for transfers between devices, on_device(): third = lax.ppermute(second, ('ctx', 'tp'), around(1))  22.4 us
    all_to_all x1, blocking collectives, on_device(): lax.all_to_all(owned.reshape(tp_size, TOK // tp_size, HEAD_SIZE), 'tp', s...  13.7 us
    unnamed x36, local copies, waits for them, and re-layouts  10.9 us
    all_to_all x1, waiting for transfers between devices, on_device(): lax.all_to_all(out_grad, 'tp', split_axis=1, concat_axis=0, tiled=True)  8.47 us
    all_to_all x1, starting transfers between devices, on_device(): lax.all_to_all(out_grad, 'tp', split_axis=1, concat_axis=0, tiled=True)  7.06 us
    pallas_call x1, Pallas kernels, call_attention(): pl.pallas_call(attention_kernel, in_specs=[SMEM, SMEM, SMEM] + [VMEM] * 5...  6.9 us
    ppermute x1, starting transfers between devices, on_device(): first = lax.ppermute(own, ('ctx', 'tp'), around(1))  6.54 us
  transfers between devices with their start and end apart: 12, of which 6 were waited for; matrix products, arithmetic and copies ran while one was open for 1% of the time, Pallas kernels for 3%

profile of v4, /device:TPU:1, one launch (start us, length us, event | category | flops | bytes accessed | tf_op | source)
XLA Modules:
  0.0 176.4 jit_solution(10352496255485801412)
XLA Ops:
  0.6 2.3 %stage.1 = bf16[272,256]{1,0:T(8,128)(2,1)} custom-call(s32[1,256]{1,0:T(1,128)} %bitcast.37, bf16[2,256,1024]{2,1,0:T(8,128)(2,1)} %kv_ref.1), custom_call_target="tpu_custom_call" | custom-call | tf_op jit(solution)/shard_map/stage/pallas_call | solution.py:343
  2.9 2.1 %collective-permute-start = (bf16[272,256]{1,0:T(8,128)(2,1)}, bf16[272,256]{1,0:T(8,128)(2,1)S(1)}, u32[]{:S(2)}, u32[]{:S(2)}) collective-permute-start(bf16[272,256]{1,0:T(8,128)(2,1)} %stage.1), channel_id=1, source_target_pairs={{0,16},{16,0},{32,48},{48,32},{64,80},{80,64},{96,112},{112,96},{1... | collective-permute-start | bytes 417800 | tf_op jit(solution)/shard_map/ppermute | solution.py:351
  5.1 2.7 %collective-permute-done = bf16[272,256]{1,0:T(8,128)(2,1)S(1)} collective-permute-done((bf16[272,256]{1,0:T(8,128)(2,1)}, bf16[272,256]{1,0:T(8,128)(2,1)S(1)}, u32[]{:S(2)}, u32[]{:S(2)}) %collective-permute-start) | collective-permute-done | bytes 139296 | tf_op jit(solution)/shard_map/ppermute | solution.py:351
  7.7 0.9 pad_maximum_fusion.own_ref
  8.7 6.5 %collective-permute-start.1 = (bf16[2,272,256]{2,1,0:T(8,128)(2,1)S(1)}, bf16[2,272,256]{2,1,0:T(8,128)(2,1)S(1)}, u32[]{:S(2)}, u32[]{:S(2)}) collective-permute-start(bf16[2,272,256]{2,1,0:T(8,128)(2,1)S(1)} %pad_maximum_fusion.own_ref), channel_id=1, source_target_pairs={{0,32},{1,225},{2,34},{3,227},{4,36},{5,229},{6,38},{7,231},{8,40}... | collective-permute-start | bytes 835592 | tf_op jit(solution)/shard_map/ppermute | solution.py:363
  15.2 3.5 %collective-permute-done.1.refs_0_ = bf16[2,272,256]{2,1,0:T(8,128)(2,1)S(1)} collective-permute-done((bf16[2,272,256]{2,1,0:T(8,128)(2,1)S(1)}, bf16[2,272,256]{2,1,0:T(8,128)(2,1)S(1)}, u32[]{:S(2)}, u32[]{:S(2)}) %collective-permute-start.1) | collective-permute-done | bytes 278560 | tf_op jit(solution)/shard_map/ppermute | solution.py:363
  18.7 3.1 %collective-permute-start.2 = (bf16[2,272,256]{2,1,0:T(8,128)(2,1)S(1)}, bf16[2,272,256]{2,1,0:T(8,128)(2,1)S(1)}, u32[]{:S(2)}, u32[]{:S(2)}) collective-permute-start(bf16[2,272,256]{2,1,0:T(8,128)(2,1)S(1)} %collective-permute-done.1.refs_0_), channel_id=1, source_target_pairs={{0,32},{1,225},{2,34},{3,227},{4,36},{5,229},{6,38},{7,231},{8,40}... | collective-permute-start | bytes 835592 | tf_op jit(solution)/shard_map/ppermute | solution.py:364
  21.8 0.8 copy.16
  22.6 7.1 %all-to-all-start.1 = ((bf16[16,16,1024]{2,0,1:T(8,128)(2,1)}), bf16[16,16,1024]{2,0,1:T(8,128)(2,1)S(1)}, u32[]{:S(2)}, u32[]{:S(2)}) async-start(bf16[16,16,1024]{2,0,1:T(8,128)(2,1)} %bitcast.24), calls=%async_computation.1 | async-start | bytes 1048576 | tf_op jit(solution)/shard_map/all_to_all | solution.py:370
  29.7 0.2 collective-permute-start.6
  29.9 2.6 %pack.1 = bf16[512,1024]{1,0:T(8,128)(2,1)} custom-call(s32[1,256]{1,0:T(1,128)} %bitcast.38, bf16[256,1024]{1,0:T(8,128)(2,1)} %rows_ref.1), custom_call_target="tpu_custom_call" | custom-call | tf_op jit(solution)/shard_map/pack/pallas_call | solution.py:371
  32.5 0.0 collective-permute-done.6.refs_5_
  32.5 8.5 %all-to-all-done.1 = bf16[16,16,1024]{2,0,1:T(8,128)(2,1)S(1)} async-done(((bf16[16,16,1024]{2,0,1:T(8,128)(2,1)}), bf16[16,16,1024]{2,0,1:T(8,128)(2,1)S(1)}, u32[]{:S(2)}, u32[]{:S(2)}) %all-to-all-start.1) | async-done | bytes 524320 | tf_op jit(solution)/shard_map/all_to_all | solution.py:370
  41.0 5.9 %all-to-all-start = ((bf16[16,32,1024]{2,1,0:T(8,128)(2,1)}), bf16[16,32,1024]{2,1,0:T(8,128)(2,1)S(1)}, u32[]{:S(2)}, u32[]{:S(2)}) async-start(bf16[16,32,1024]{2,1,0:T(8,128)(2,1)} %bitcast.30), calls=%async_computation | async-start | bytes 2097152 | tf_op jit(solution)/shard_map/all_to_all | solution.py:379
  46.9 0.0 copy-start.13
  46.9 0.0 copy-start.14
  46.9 2.7 %collective-permute-start.3 = (bf16[2,272,256]{2,1,0:T(8,128)(2,1)S(1)}, bf16[2,272,256]{2,1,0:T(8,128)(2,1)S(1)}, u32[]{:S(2)}, u32[]{:S(2)}) collective-permute-start(bf16[2,272,256]{2,1,0:T(8,128)(2,1)S(1)} %collective-permute-done.2.refs_1_), channel_id=1, source_target_pairs={{0,32},{1,225},{2,34},{3,227},{4,36},{5,229},{6,38},{7,231},{8,40}... | collective-permute-start | bytes 835592 | tf_op jit(solution)/shard_map/ppermute | solution.py:365
  49.6 0.8 collective-permute-start.5
  50.4 2.5 %collective-permute-start.4 = (bf16[272,256]{1,0:T(8,128)(2,1)S(1)}, bf16[272,256]{1,0:T(8,128)(2,1)S(1)}, u32[]{:S(2)}, u32[]{:S(2)}) collective-permute-start(bf16[272,256]{1,0:T(8,128)(2,1)S(1)} %dynamic-slice_bitcast_fusion), channel_id=1, source_target_pairs={{0,64},{1,193},{2,66},{3,195},{4,68},{5,197},{6,70},{7,199},{8,72}... | collective-permute-start | bytes 417800 | tf_op jit(solution)/shard_map/ppermute | solution.py:367
  52.9 22.4 %collective-permute-done.3.refs_2_ = bf16[2,272,256]{2,1,0:T(8,128)(2,1)S(1)} collective-permute-done((bf16[2,272,256]{2,1,0:T(8,128)(2,1)S(1)}, bf16[2,272,256]{2,1,0:T(8,128)(2,1)S(1)}, u32[]{:S(2)}, u32[]{:S(2)}) %collective-permute-start.3) | collective-permute-done | bytes 278560 | tf_op jit(solution)/shard_map/ppermute | solution.py:365
  75.2 1.6 collective-permute-start.7
  76.8 0.7 copy-done.5
  77.5 1.7 collective-permute-done.4.refs_3_
  79.2 1.1 collective-permute-start.8
  80.3 0.6 copy-done.11
  80.9 0.1 pad_add_fusion.info_ref
  81.0 0.7 copy-done.7
  81.7 0.0 collective-permute-done.7.refs_6_
  81.7 0.9 copy-done.2
  82.7 1.0 copy-done.4
  83.6 1.0 copy-done.6
  84.6 1.0 copy-done.8
  85.5 0.9 copy-done.12
  86.5 2.0 %permute.1 = (bf16[2560,256]{1,0:T(8,128)(2,1)S(1)}, bf16[512,256]{1,0:T(8,128)(2,1)S(1)}) custom-call(s32[2]{0:T(128)S(1)} %pad_add_fusion.info_ref, bf16[2,272,256]{2,1,0:T(8,128)(2,1)S(1)} %pad_maximum_fusion.own_ref, bf16[2,272,256]{2,1,0:T(8,128)(2,1)S(1)} %copy-done.2, bf16[2,272,256]{2,1,0:T(8,128)(2,1)S(1)} %collective-permute-done.2.refs_1_, ...), custom_call_target="tpu_custom_call" | custom-call | tf_op jit(solution)/shard_map/permute/pallas_call | solution.py:380
  88.5 0.0 copy-start.9
  88.5 0.7 copy-done.9
  89.2 0.9 copy-done.10
  90.2 6.9 %attention.1 = (bf16[256,1024]{1,0:T(8,128)(2,1)}, f32[2560,128]{1,0:T(8,128)S(1)}, bf16[2560,128]{1,0:T(8,128)(2,1)S(1)}) custom-call(s32[2]{0:T(128)S(1)} %pad_add_fusion.info_ref, s32[4096]{0:T(1024)S(1)} %copy-done.13, s32[32,32]{1,0:T(8,128)S(1)} %copy-done.14, s32[32,128]{1,0:T(8,128)S(1)} %bitcast.28, bf16[512,256]{1,0:T(8,128)(2,1)S(1)} %copy-done.10, ...), custom_call_target="tpu_custom_call" | custom-call | tf_op jit(solution)/shard_map/attention/pallas_call | solution.py:304
  97.1 1.1 copy-done
  98.1 0.5 copy-done.15
  98.7 0.0 collective-permute-start.9
  98.7 2.1 %collective-permute-done.9.recv_ref = bf16[2560,128]{1,0:T(8,128)(2,1)S(1)} collective-permute-done((bf16[2560,128]{1,0:T(8,128)(2,1)S(1)}, bf16[2560,128]{1,0:T(8,128)(2,1)S(1)}, u32[]{:S(2)}, u32[]{:S(2)}) %collective-permute-start.9) | collective-permute-done | bytes 655392 | tf_op jit(solution)/shard_map/ppermute | solution.py:394
  100.8 0.8 copy-done.16
  101.6 2.7 %merge.1 = bf16[4096,128]{1,0:T(8,128)(2,1)} custom-call(s32[2]{0:T(128)} %copy-done.15, f32[2560,128]{1,0:T(8,128)} %copy-done, bf16[2560,128]{1,0:T(8,128)(2,1)} %copy-done.16), custom_call_target="tpu_custom_call" | custom-call | tf_op jit(solution)/shard_map/merge/pallas_call | solution.py:395
  104.3 57.7 %all_to_all.40 = bf16[16,256,128]{2,1,0:T(8,128)(2,1)S(1)} all-to-all(bf16[16,256,128]{2,1,0:T(8,128)(2,1)} %bitcast.29), channel_id=1, replica_groups=mesh['ctx'=16,'tp'=16] {'ctx'}, dimensions={0} | all-to-all | bytes 2097152 | tf_op jit(solution)/shard_map/all_to_all | solution.py:402
  162.0 0.1 reduce_sum.12
  162.1 13.7 %all_to_all.41 = bf16[16,16,128]{2,1,0:T(8,128)(2,1)S(1)} all-to-all(bf16[16,16,128]{2,1,0:T(8,128)(2,1)S(1)} %bitcast.33), channel_id=1, replica_groups=mesh['ctx'=16,'tp'=16] {'tp'}, dimensions={0} | all-to-all | bytes 131072 | tf_op jit(solution)/shard_map/all_to_all | solution.py:406
  175.8 0.6 copy.17
  (25 shorter events, 0.1 us)
Async XLA Ops:
  0.6 21.2 %copy-start.17 = (bf16[16,16384]{1,0:T(8,128)(2,1)S(1)}, bf16[16,16384]{1,0:T(8,128)(2,1)}, u32[]{:S(2)}) copy-start(bf16[16,16384]{1,0:T(8,128)(2,1)} %param.8) | copy-start | bytes 1572868
  2.9 4.8 %collective-permute-start = (bf16[272,256]{1,0:T(8,128)(2,1)}, bf16[272,256]{1,0:T(8,128)(2,1)S(1)}, u32[]{:S(2)}, u32[]{:S(2)}) collective-permute-start(bf16[272,256]{1,0:T(8,128)(2,1)} %stage.1), channel_id=1, source_target_pairs={{0,16},{16,0},{32,48},{48,32},{64,80},{80,64},{96,112},{112,96},{1... | collective-permute-start | bytes 417800 | tf_op jit(solution)/shard_map/ppermute | solution.py:351
  8.7 10.0 %collective-permute-start.1 = (bf16[2,272,256]{2,1,0:T(8,128)(2,1)S(1)}, bf16[2,272,256]{2,1,0:T(8,128)(2,1)S(1)}, u32[]{:S(2)}, u32[]{:S(2)}) collective-permute-start(bf16[2,272,256]{2,1,0:T(8,128)(2,1)S(1)} %pad_maximum_fusion.own_ref), channel_id=1, source_target_pairs={{0,32},{1,225},{2,34},{3,227},{4,36},{5,229},{6,38},{7,231},{8,40}... | collective-permute-start | bytes 835592 | tf_op jit(solution)/shard_map/ppermute | solution.py:363
  18.7 30.9 %copy-start.1 = (bf16[2,272,256]{2,1,0:T(8,128)(2,1)}, bf16[2,272,256]{2,1,0:T(8,128)(2,1)S(1)}, u32[]{:S(2)}) copy-start(bf16[2,272,256]{2,1,0:T(8,128)(2,1)S(1)} %collective-permute-done.1.refs_0_) | copy-start | bytes 835588
  18.7 11.0 %collective-permute-start.2 = (bf16[2,272,256]{2,1,0:T(8,128)(2,1)S(1)}, bf16[2,272,256]{2,1,0:T(8,128)(2,1)S(1)}, u32[]{:S(2)}, u32[]{:S(2)}) collective-permute-start(bf16[2,272,256]{2,1,0:T(8,128)(2,1)S(1)} %collective-permute-done.1.refs_0_), channel_id=1, source_target_pairs={{0,32},{1,225},{2,34},{3,227},{4,36},{5,229},{6,38},{7,231},{8,40}... | collective-permute-start | bytes 835592 | tf_op jit(solution)/shard_map/ppermute | solution.py:364
  22.6 18.4 %all-to-all-start.1 = ((bf16[16,16,1024]{2,0,1:T(8,128)(2,1)}), bf16[16,16,1024]{2,0,1:T(8,128)(2,1)S(1)}, u32[]{:S(2)}, u32[]{:S(2)}) async-start(bf16[16,16,1024]{2,0,1:T(8,128)(2,1)} %bitcast.24), calls=%async_computation.1 | async-start | bytes 1048576 | tf_op jit(solution)/shard_map/all_to_all | solution.py:370
  29.7 2.8 %collective-permute-start.6 = (bf16[2,272,256]{2,1,0:T(8,128)(2,1)S(1)}, bf16[2,272,256]{2,1,0:T(8,128)(2,1)S(1)}, u32[]{:S(2)}, u32[]{:S(2)}) collective-permute-start(bf16[2,272,256]{2,1,0:T(8,128)(2,1)S(1)} %collective-permute-done.2.refs_1_), channel_id=1, source_target_pairs={{0,1},{1,0},{2,3},{3,2},{4,5},{5,4},{6,7},{7,6},{8,9},{9,8},{10,11... | collective-permute-start | bytes 835592 | tf_op jit(solution)/shard_map/ppermute | solution.py:369
  32.5 49.2 %copy-start.3 = (bf16[2,272,256]{2,1,0:T(8,128)(2,1)}, bf16[2,272,256]{2,1,0:T(8,128)(2,1)S(1)}, u32[]{:S(2)}) copy-start(bf16[2,272,256]{2,1,0:T(8,128)(2,1)S(1)} %collective-permute-done.6.refs_5_) | copy-start | bytes 835588
  41.0 48.2 %all-to-all-start = ((bf16[16,32,1024]{2,1,0:T(8,128)(2,1)}), bf16[16,32,1024]{2,1,0:T(8,128)(2,1)S(1)}, u32[]{:S(2)}, u32[]{:S(2)}) async-start(bf16[16,32,1024]{2,1,0:T(8,128)(2,1)} %bitcast.30), calls=%async_computation | async-start | bytes 2097152 | tf_op jit(solution)/shard_map/all_to_all | solution.py:379
  46.9 42.3 %copy-start.13 = (s32[4096]{0:T(1024)S(1)}, s32[4096]{0:T(1024)}, u32[]{:S(2)}) copy-start(s32[4096]{0:T(1024)} %seg_ref.1) | copy-start | bytes 49156
  46.9 42.3 %copy-start.14 = (s32[32,32]{1,0:T(8,128)S(1)}, s32[32,32]{1,0:T(8,128)}, u32[]{:S(2)}) copy-start(s32[32,32]{1,0:T(8,128)} %allow_ref.1) | copy-start | bytes 12292
  46.9 28.3 %collective-permute-start.3 = (bf16[2,272,256]{2,1,0:T(8,128)(2,1)S(1)}, bf16[2,272,256]{2,1,0:T(8,128)(2,1)S(1)}, u32[]{:S(2)}, u32[]{:S(2)}) collective-permute-start(bf16[2,272,256]{2,1,0:T(8,128)(2,1)S(1)} %collective-permute-done.2.refs_1_), channel_id=1, source_target_pairs={{0,32},{1,225},{2,34},{3,227},{4,36},{5,229},{6,38},{7,231},{8,40}... | collective-permute-start | bytes 835592 | tf_op jit(solution)/shard_map/ppermute | solution.py:365
  49.6 31.4 %collective-permute-start.5 = (bf16[2,272,256]{2,1,0:T(8,128)(2,1)S(1)}, bf16[2,272,256]{2,1,0:T(8,128)(2,1)S(1)}, u32[]{:S(2)}, u32[]{:S(2)}) collective-permute-start(bf16[2,272,256]{2,1,0:T(8,128)(2,1)S(1)} %collective-permute-done.1.refs_0_), channel_id=1, source_target_pairs={{0,1},{1,0},{2,3},{3,2},{4,5},{5,4},{6,7},{7,6},{8,9},{9,8},{10,11... | collective-permute-start | bytes 835592 | tf_op jit(solution)/shard_map/ppermute | solution.py:369
  50.4 28.8 %collective-permute-start.4 = (bf16[272,256]{1,0:T(8,128)(2,1)S(1)}, bf16[272,256]{1,0:T(8,128)(2,1)S(1)}, u32[]{:S(2)}, u32[]{:S(2)}) collective-permute-start(bf16[272,256]{1,0:T(8,128)(2,1)S(1)} %dynamic-slice_bitcast_fusion), channel_id=1, source_target_pairs={{0,64},{1,193},{2,66},{3,195},{4,68},{5,197},{6,70},{7,199},{8,72}... | collective-permute-start | bytes 417800 | tf_op jit(solution)/shard_map/ppermute | solution.py:367
  75.2 6.5 %collective-permute-start.7 = (bf16[2,272,256]{2,1,0:T(8,128)(2,1)S(1)}, bf16[2,272,256]{2,1,0:T(8,128)(2,1)}, u32[]{:S(2)}, u32[]{:S(2)}) collective-permute-start(bf16[2,272,256]{2,1,0:T(8,128)(2,1)S(1)} %collective-permute-done.3.refs_2_), channel_id=1, source_target_pairs={{0,1},{1,0},{2,3},{3,2},{4,5},{5,4},{6,7},{7,6},{8,9},{9,8},{10,11... | collective-permute-start | bytes 835592 | tf_op jit(solution)/shard_map/ppermute | solution.py:369
  76.8 0.7 copy-start.5
  79.2 2.6 %collective-permute-start.8 = (bf16[272,256]{1,0:T(8,128)(2,1)S(1)}, bf16[272,256]{1,0:T(8,128)(2,1)}, u32[]{:S(2)}, u32[]{:S(2)}) collective-permute-start(bf16[272,256]{1,0:T(8,128)(2,1)S(1)} %collective-permute-done.4.refs_3_), channel_id=1, source_target_pairs={{0,1},{1,0},{2,3},{3,2},{4,5},{5,4},{6,7},{7,6},{8,9},{9,8},{10,11... | collective-permute-start | bytes 417800 | tf_op jit(solution)/shard_map/ppermute | solution.py:369
  80.3 0.6 copy-start.11
  81.0 0.7 copy-start.7
  81.7 1.0 copy-start.2
  82.7 1.0 copy-start.4
  83.6 1.0 copy-start.6
  84.6 1.0 copy-start.8
  85.5 0.9 copy-start.12
  88.5 0.7 copy-start.9
  89.2 1.0 copy-start.10
  97.1 1.1 copy-start
  98.1 0.5 copy-start.15
  98.7 2.1 %collective-permute-start.9 = (bf16[2560,128]{1,0:T(8,128)(2,1)S(1)}, bf16[2560,128]{1,0:T(8,128)(2,1)S(1)}, u32[]{:S(2)}, u32[]{:S(2)}) collective-permute-start(bf16[2560,128]{1,0:T(8,128)(2,1)S(1)} %get-tuple-element.15), channel_id=1, source_target_pairs={{0,1},{1,0},{2,3},{3,2},{4,5},{5,4},{6,7},{7,6},{8,9},{9,8},{10,11... | collective-permute-start | bytes 1966088 | tf_op jit(solution)/shard_map/ppermute | solution.py:394
  100.8 0.8 copy-start.16

commit v5 on v4

--- a/solution.py
+++ b/solution.py
@@ -366,7 +366,6 @@
     half = lax.dynamic_index_in_dim(second, tp_index % 2, 0, keepdims=False)
     fourth = lax.ppermute(half, ("ctx", "tp"), around(2))
     mine = [first, second, third, fourth]
-    theirs = [lax.ppermute(piece, "tp", swap) for piece in mine]
     g_local = lax.all_to_all(out_grad, "tp", split_axis=1, concat_axis=0, tiled=True)
     q_send = pl.pallas_call(
         pack_kernel,
@@ -375,7 +374,8 @@
         out_shape=jax.ShapeDtypeStruct((SHARDS * SLOTS, width), BF16),
         name="pack",
     )(place.reshape(1, TOK), queries)
-    q_send, theirs[1] = lax.optimization_barrier((q_send, theirs[1]))
+    q_send, *mine = lax.optimization_barrier((q_send, *mine))
+    theirs = [lax.ppermute(piece, "tp", swap) for piece in mine]
     q_recv = lax.all_to_all(q_send, "ctx", split_axis=0, concat_axis=0, tiled=True)
     kv_window, unpack = pl.pallas_call(
         permute_kernel,

time: 178 us -> 155 us (0.87); the launches traced: 176 us -> 156 us
  waiting for transfers between devices: 40.7 us -> 26.3 us
  blocking collectives: 71.3 us -> 64 us
  starting transfers between devices: 33.6 us -> 35.4 us
    ppermute x1, waiting for transfers between devices: 22.4 us -> 0.01 us  [on_device(): third = lax.ppermute(second, ('ctx', 'tp'), around(1))]
    all_to_all x1, waiting for transfers between devices: 0.01 us -> 11.8 us  [on_device(): lax.all_to_all(q_send, 'ctx', split_axis=0, concat_axis=0, tiled=True)]
    all_to_all x1, blocking collectives: 57.7 us -> 48.4 us  [on_device(): lax.all_to_all(part.reshape(SHARDS, TOK, HEAD_SIZE), 'ctx', split_axis=0,...]
    all_to_all x1, waiting for transfers between devices: 8.47 us -> 2.14 us  [on_device(): lax.all_to_all(out_grad, 'tp', split_axis=1, concat_axis=0, tiled=True)]
    ppermute x1, starting transfers between devices: 0.04 us -> 4.7 us  [on_device(): recv = lax.ppermute(send, 'tp', swap)]
    all_to_all x1, blocking collectives: 13.7 us -> 15.6 us  [on_device(): lax.all_to_all(owned.reshape(tp_size, TOK // tp_size, HEAD_SIZE), 'tp', s...]
  transfers between devices with their start and end apart: 12 -> 12, of which waited for: 6 -> 7; matrix products, arithmetic and copies ran while one was open for 1% -> 1% of each run, Pallas kernels for 3% -> 3%
where the time goes in v5:
time: 155 us; the launch traced here: 156 us
  blocking collectives  64 us (41%)
  starting transfers between devices  35.4 us (23%)
  waiting for transfers between devices  26.3 us (17%)
  Pallas kernels  16.6 us (11%)
  local copies, waits for them, and re-layouts  11.7 us (8%)
    all_to_all x1, blocking collectives, on_device(): lax.all_to_all(part.reshape(SHARDS, TOK, HEAD_SIZE), 'ctx', split_axis=0,...  48.4 us
    all_to_all x1, blocking collectives, on_device(): lax.all_to_all(owned.reshape(tp_size, TOK // tp_size, HEAD_SIZE), 'tp', s...  15.6 us
    all_to_all x1, waiting for transfers between devices, on_device(): lax.all_to_all(q_send, 'ctx', split_axis=0, concat_axis=0, tiled=True)  11.8 us
    unnamed x36, local copies, waits for them, and re-layouts  10.2 us
    all_to_all x1, starting transfers between devices, on_device(): lax.all_to_all(out_grad, 'tp', split_axis=1, concat_axis=0, tiled=True)  7.06 us
    pallas_call x1, Pallas kernels, call_attention(): pl.pallas_call(attention_kernel, in_specs=[SMEM, SMEM, SMEM] + [VMEM] * 5...  6.9 us
    ppermute x1, starting transfers between devices, on_device(): first = lax.ppermute(own, ('ctx', 'tp'), around(1))  6.54 us
    all_to_all x1, starting transfers between devices, on_device(): lax.all_to_all(q_send, 'ctx', split_axis=0, concat_axis=0, tiled=True)  6.03 us
  transfers between devices with their start and end apart: 12, of which 7 were waited for; matrix products, arithmetic and copies ran while one was open for 1% of the time, Pallas kernels for 3%

profile of v5, /device:TPU:1, one launch (start us, length us, event | category | flops | bytes accessed | tf_op | source)
XLA Modules:
  0.0 155.9 jit_solution(6529428130082627802)
XLA Ops:
  0.6 2.3 %stage.1 = bf16[272,256]{1,0:T(8,128)(2,1)} custom-call(s32[1,256]{1,0:T(1,128)} %bitcast.37, bf16[2,256,1024]{2,1,0:T(8,128)(2,1)} %kv_ref.1), custom_call_target="tpu_custom_call" | custom-call | tf_op jit(solution)/shard_map/stage/pallas_call | solution.py:343
  2.9 2.1 %collective-permute-start = (bf16[272,256]{1,0:T(8,128)(2,1)}, bf16[272,256]{1,0:T(8,128)(2,1)S(1)}, u32[]{:S(2)}, u32[]{:S(2)}) collective-permute-start(bf16[272,256]{1,0:T(8,128)(2,1)} %stage.1), channel_id=1, source_target_pairs={{0,16},{16,0},{32,48},{48,32},{64,80},{80,64},{96,112},{112,96},{1... | collective-permute-start | bytes 417800 | tf_op jit(solution)/shard_map/ppermute | solution.py:351
  5.1 2.7 %collective-permute-done = bf16[272,256]{1,0:T(8,128)(2,1)S(1)} collective-permute-done((bf16[272,256]{1,0:T(8,128)(2,1)}, bf16[272,256]{1,0:T(8,128)(2,1)S(1)}, u32[]{:S(2)}, u32[]{:S(2)}) %collective-permute-start) | collective-permute-done | bytes 139296 | tf_op jit(solution)/shard_map/ppermute | solution.py:351
  7.7 0.9 pad_maximum_fusion.own_ref
  8.7 6.5 %collective-permute-start.1 = (bf16[2,272,256]{2,1,0:T(8,128)(2,1)S(1)}, bf16[2,272,256]{2,1,0:T(8,128)(2,1)S(1)}, u32[]{:S(2)}, u32[]{:S(2)}) collective-permute-start(bf16[2,272,256]{2,1,0:T(8,128)(2,1)S(1)} %pad_maximum_fusion.own_ref), channel_id=1, source_target_pairs={{0,32},{1,225},{2,34},{3,227},{4,36},{5,229},{6,38},{7,231},{8,40}... | collective-permute-start | bytes 835592 | tf_op jit(solution)/shard_map/ppermute | solution.py:363
  15.2 3.5 %collective-permute-done.1.refs_0_ = bf16[2,272,256]{2,1,0:T(8,128)(2,1)S(1)} collective-permute-done((bf16[2,272,256]{2,1,0:T(8,128)(2,1)S(1)}, bf16[2,272,256]{2,1,0:T(8,128)(2,1)S(1)}, u32[]{:S(2)}, u32[]{:S(2)}) %collective-permute-start.1) | collective-permute-done | bytes 278560 | tf_op jit(solution)/shard_map/ppermute | solution.py:363
  18.7 3.1 %collective-permute-start.2 = (bf16[2,272,256]{2,1,0:T(8,128)(2,1)S(1)}, bf16[2,272,256]{2,1,0:T(8,128)(2,1)S(1)}, u32[]{:S(2)}, u32[]{:S(2)}) collective-permute-start(bf16[2,272,256]{2,1,0:T(8,128)(2,1)S(1)} %collective-permute-done.1.refs_0_), channel_id=1, source_target_pairs={{0,32},{1,225},{2,34},{3,227},{4,36},{5,229},{6,38},{7,231},{8,40}... | collective-permute-start | bytes 835592 | tf_op jit(solution)/shard_map/ppermute | solution.py:364
  21.8 0.8 copy.16
  22.6 7.1 %all-to-all-start.1 = ((bf16[16,16,1024]{2,0,1:T(8,128)(2,1)}), bf16[16,16,1024]{2,0,1:T(8,128)(2,1)S(1)}, u32[]{:S(2)}, u32[]{:S(2)}) async-start(bf16[16,16,1024]{2,0,1:T(8,128)(2,1)} %bitcast.24), calls=%async_computation.1 | async-start | bytes 1048576 | tf_op jit(solution)/shard_map/all_to_all | solution.py:369
  29.7 0.0 collective-permute-done.2.refs_1_
  29.7 2.7 %collective-permute-start.3 = (bf16[2,272,256]{2,1,0:T(8,128)(2,1)S(1)}, bf16[2,272,256]{2,1,0:T(8,128)(2,1)S(1)}, u32[]{:S(2)}, u32[]{:S(2)}) collective-permute-start(bf16[2,272,256]{2,1,0:T(8,128)(2,1)S(1)} %collective-permute-done.2.refs_1_), channel_id=1, source_target_pairs={{0,32},{1,225},{2,34},{3,227},{4,36},{5,229},{6,38},{7,231},{8,40}... | collective-permute-start | bytes 835592 | tf_op jit(solution)/shard_map/ppermute | solution.py:365
  32.4 1.1 collective-permute-start.4
  33.4 2.6 %pack.1 = bf16[512,1024]{1,0:T(8,128)(2,1)} custom-call(s32[1,256]{1,0:T(1,128)} %bitcast.38, bf16[256,1024]{1,0:T(8,128)(2,1)} %rows_ref.1), custom_call_target="tpu_custom_call" | custom-call | tf_op jit(solution)/shard_map/pack/pallas_call | solution.py:370
  36.1 2.8 %collective-permute-done.4.refs_3_ = bf16[272,256]{1,0:T(8,128)(2,1)S(1)} collective-permute-done((bf16[272,256]{1,0:T(8,128)(2,1)S(1)}, bf16[272,256]{1,0:T(8,128)(2,1)S(1)}, u32[]{:S(2)}, u32[]{:S(2)}) %collective-permute-start.4) | collective-permute-done | bytes 139296 | tf_op jit(solution)/shard_map/ppermute | solution.py:367
  38.9 0.0 collective-permute-done.3.refs_2_
  38.9 2.1 %all-to-all-done.1 = bf16[16,16,1024]{2,0,1:T(8,128)(2,1)S(1)} async-done(((bf16[16,16,1024]{2,0,1:T(8,128)(2,1)}), bf16[16,16,1024]{2,0,1:T(8,128)(2,1)S(1)}, u32[]{:S(2)}, u32[]{:S(2)}) %all-to-all-start.1) | async-done | bytes 524320 | tf_op jit(solution)/shard_map/all_to_all | solution.py:369
  41.0 6.0 %all-to-all-start = ((bf16[16,32,1024]{2,1,0:T(8,128)(2,1)}), bf16[16,32,1024]{2,1,0:T(8,128)(2,1)S(1)}, u32[]{:S(2)}, u32[]{:S(2)}) async-start(bf16[16,32,1024]{2,1,0:T(8,128)(2,1)} %bitcast.30), calls=%async_computation | async-start | bytes 2097152 | tf_op jit(solution)/shard_map/all_to_all | solution.py:379
  47.0 1.5 collective-permute-start.5
  48.6 0.1 collective-permute-start.6
  48.7 0.4 collective-permute-start.7
  49.1 0.1 collective-permute-start.8
  49.2 0.1 pad_add_fusion.info_ref
  49.3 1.6 %collective-permute-done.8.refs_7_ = bf16[272,256]{1,0:T(8,128)(2,1)} collective-permute-done((bf16[272,256]{1,0:T(8,128)(2,1)S(1)}, bf16[272,256]{1,0:T(8,128)(2,1)}, u32[]{:S(2)}, u32[]{:S(2)}) %collective-permute-start.8) | collective-permute-done | bytes 139296 | tf_op jit(solution)/shard_map/ppermute | solution.py:378
  50.9 0.0 collective-permute-done.5.refs_4_
  50.9 0.7 copy-done.5
  51.6 0.7 copy-done.7
  52.3 0.0 collective-permute-done.7.refs_6_
  52.3 1.0 copy-done.2
  53.3 1.0 copy-done.4
  54.2 1.0 copy-done.6
  55.2 1.0 copy-done.8
  56.2 0.9 copy-done.12
  57.1 2.0 %permute.1 = (bf16[2560,256]{1,0:T(8,128)(2,1)S(1)}, bf16[512,256]{1,0:T(8,128)(2,1)S(1)}) custom-call(s32[2]{0:T(128)S(1)} %pad_add_fusion.info_ref, bf16[2,272,256]{2,1,0:T(8,128)(2,1)S(1)} %pad_maximum_fusion.own_ref, bf16[2,272,256]{2,1,0:T(8,128)(2,1)S(1)} %copy-done.2, bf16[2,272,256]{2,1,0:T(8,128)(2,1)S(1)} %collective-permute-done.2.refs_1_, ...), custom_call_target="tpu_custom_call" | custom-call | tf_op jit(solution)/shard_map/permute/pallas_call | solution.py:380
  59.1 0.0 copy-start.9
  59.1 0.7 copy-done.9
  59.8 11.8 %all-to-all-done = bf16[16,32,1024]{2,1,0:T(8,128)(2,1)S(1)} async-done(((bf16[16,32,1024]{2,1,0:T(8,128)(2,1)}), bf16[16,32,1024]{2,1,0:T(8,128)(2,1)S(1)}, u32[]{:S(2)}, u32[]{:S(2)}) %all-to-all-start) | async-done | bytes 1048608 | tf_op jit(solution)/shard_map/all_to_all | solution.py:379
  71.6 0.9 copy-done.10
  72.6 6.9 %attention.1 = (bf16[256,1024]{1,0:T(8,128)(2,1)}, f32[2560,128]{1,0:T(8,128)S(1)}, bf16[2560,128]{1,0:T(8,128)(2,1)S(1)}) custom-call(s32[2]{0:T(128)S(1)} %pad_add_fusion.info_ref, s32[4096]{0:T(1024)S(1)} %copy-done.13, s32[32,32]{1,0:T(8,128)S(1)} %copy-done.14, s32[32,128]{1,0:T(8,128)S(1)} %bitcast.28, bf16[512,256]{1,0:T(8,128)(2,1)S(1)} %copy-done.10, ...), custom_call_target="tpu_custom_call" | custom-call | tf_op jit(solution)/shard_map/attention/pallas_call | solution.py:304
  79.5 1.1 copy-done
  80.6 0.5 copy-done.15
  81.1 4.7 %collective-permute-start.9 = (bf16[2560,128]{1,0:T(8,128)(2,1)S(1)}, bf16[2560,128]{1,0:T(8,128)(2,1)S(1)}, u32[]{:S(2)}, u32[]{:S(2)}) collective-permute-start(bf16[2560,128]{1,0:T(8,128)(2,1)S(1)} %get-tuple-element.21), channel_id=1, source_target_pairs={{0,1},{1,0},{2,3},{3,2},{4,5},{5,4},{6,7},{7,6},{8,9},{9,8},{10,11... | collective-permute-start | bytes 1966088 | tf_op jit(solution)/shard_map/ppermute | solution.py:394
  85.8 1.7 %collective-permute-done.9.recv_ref = bf16[2560,128]{1,0:T(8,128)(2,1)S(1)} collective-permute-done((bf16[2560,128]{1,0:T(8,128)(2,1)S(1)}, bf16[2560,128]{1,0:T(8,128)(2,1)S(1)}, u32[]{:S(2)}, u32[]{:S(2)}) %collective-permute-start.9) | collective-permute-done | bytes 655392 | tf_op jit(solution)/shard_map/ppermute | solution.py:394
  87.5 0.8 copy-done.16
  88.4 2.7 %merge.1 = bf16[4096,128]{1,0:T(8,128)(2,1)} custom-call(s32[2]{0:T(128)} %copy-done.15, f32[2560,128]{1,0:T(8,128)} %copy-done, bf16[2560,128]{1,0:T(8,128)(2,1)} %copy-done.16), custom_call_target="tpu_custom_call" | custom-call | tf_op jit(solution)/shard_map/merge/pallas_call | solution.py:395
  91.1 48.4 %all_to_all.40 = bf16[16,256,128]{2,1,0:T(8,128)(2,1)S(1)} all-to-all(bf16[16,256,128]{2,1,0:T(8,128)(2,1)} %bitcast.29), channel_id=1, replica_groups=mesh['ctx'=16,'tp'=16] {'ctx'}, dimensions={0} | all-to-all | bytes 2097152 | tf_op jit(solution)/shard_map/all_to_all | solution.py:402
  139.5 0.1 reduce_sum.12
  139.6 15.6 %all_to_all.41 = bf16[16,16,128]{2,1,0:T(8,128)(2,1)S(1)} all-to-all(bf16[16,16,128]{2,1,0:T(8,128)(2,1)S(1)} %bitcast.33), channel_id=1, replica_groups=mesh['ctx'=16,'tp'=16] {'tp'}, dimensions={0} | all-to-all | bytes 131072 | tf_op jit(solution)/shard_map/all_to_all | solution.py:406
  155.2 0.6 copy.17
  (25 shorter events, 0.1 us)
Async XLA Ops:
  0.6 21.2 %copy-start.17 = (bf16[16,16384]{1,0:T(8,128)(2,1)S(1)}, bf16[16,16384]{1,0:T(8,128)(2,1)}, u32[]{:S(2)}) copy-start(bf16[16,16384]{1,0:T(8,128)(2,1)} %param.8) | copy-start | bytes 1572868
  2.9 4.8 %collective-permute-start = (bf16[272,256]{1,0:T(8,128)(2,1)}, bf16[272,256]{1,0:T(8,128)(2,1)S(1)}, u32[]{:S(2)}, u32[]{:S(2)}) collective-permute-start(bf16[272,256]{1,0:T(8,128)(2,1)} %stage.1), channel_id=1, source_target_pairs={{0,16},{16,0},{32,48},{48,32},{64,80},{80,64},{96,112},{112,96},{1... | collective-permute-start | bytes 417800 | tf_op jit(solution)/shard_map/ppermute | solution.py:351
  8.7 10.0 %collective-permute-start.1 = (bf16[2,272,256]{2,1,0:T(8,128)(2,1)S(1)}, bf16[2,272,256]{2,1,0:T(8,128)(2,1)S(1)}, u32[]{:S(2)}, u32[]{:S(2)}) collective-permute-start(bf16[2,272,256]{2,1,0:T(8,128)(2,1)S(1)} %pad_maximum_fusion.own_ref), channel_id=1, source_target_pairs={{0,32},{1,225},{2,34},{3,227},{4,36},{5,229},{6,38},{7,231},{8,40}... | collective-permute-start | bytes 835592 | tf_op jit(solution)/shard_map/ppermute | solution.py:363
  18.7 28.4 %copy-start.1 = (bf16[2,272,256]{2,1,0:T(8,128)(2,1)}, bf16[2,272,256]{2,1,0:T(8,128)(2,1)S(1)}, u32[]{:S(2)}) copy-start(bf16[2,272,256]{2,1,0:T(8,128)(2,1)S(1)} %collective-permute-done.1.refs_0_) | copy-start | bytes 835588
  18.7 11.0 %collective-permute-start.2 = (bf16[2,272,256]{2,1,0:T(8,128)(2,1)S(1)}, bf16[2,272,256]{2,1,0:T(8,128)(2,1)S(1)}, u32[]{:S(2)}, u32[]{:S(2)}) collective-permute-start(bf16[2,272,256]{2,1,0:T(8,128)(2,1)S(1)} %collective-permute-done.1.refs_0_), channel_id=1, source_target_pairs={{0,32},{1,225},{2,34},{3,227},{4,36},{5,229},{6,38},{7,231},{8,40}... | collective-permute-start | bytes 835592 | tf_op jit(solution)/shard_map/ppermute | solution.py:364
  22.6 18.4 %all-to-all-start.1 = ((bf16[16,16,1024]{2,0,1:T(8,128)(2,1)}), bf16[16,16,1024]{2,0,1:T(8,128)(2,1)S(1)}, u32[]{:S(2)}, u32[]{:S(2)}) async-start(bf16[16,16,1024]{2,0,1:T(8,128)(2,1)} %bitcast.24), calls=%async_computation.1 | async-start | bytes 1048576 | tf_op jit(solution)/shard_map/all_to_all | solution.py:369
  29.7 9.1 %collective-permute-start.3 = (bf16[2,272,256]{2,1,0:T(8,128)(2,1)S(1)}, bf16[2,272,256]{2,1,0:T(8,128)(2,1)S(1)}, u32[]{:S(2)}, u32[]{:S(2)}) collective-permute-start(bf16[2,272,256]{2,1,0:T(8,128)(2,1)S(1)} %collective-permute-done.2.refs_1_), channel_id=1, source_target_pairs={{0,32},{1,225},{2,34},{3,227},{4,36},{5,229},{6,38},{7,231},{8,40}... | collective-permute-start | bytes 835592 | tf_op jit(solution)/shard_map/ppermute | solution.py:365
  32.4 6.5 %collective-permute-start.4 = (bf16[272,256]{1,0:T(8,128)(2,1)S(1)}, bf16[272,256]{1,0:T(8,128)(2,1)S(1)}, u32[]{:S(2)}, u32[]{:S(2)}) collective-permute-start(bf16[272,256]{1,0:T(8,128)(2,1)S(1)} %dynamic-slice_bitcast_fusion), channel_id=1, source_target_pairs={{0,64},{1,193},{2,66},{3,195},{4,68},{5,197},{6,70},{7,199},{8,72}... | collective-permute-start | bytes 417800 | tf_op jit(solution)/shard_map/ppermute | solution.py:367
  38.8 12.8 %copy-start.11 = (bf16[272,256]{1,0:T(8,128)(2,1)}, bf16[272,256]{1,0:T(8,128)(2,1)S(1)}, u32[]{:S(2)}) copy-start(bf16[272,256]{1,0:T(8,128)(2,1)S(1)} %collective-permute-done.4.refs_3_) | copy-start | bytes 417796
  38.9 12.8 %copy-start.3 = (bf16[2,272,256]{2,1,0:T(8,128)(2,1)}, bf16[2,272,256]{2,1,0:T(8,128)(2,1)S(1)}, u32[]{:S(2)}) copy-start(bf16[2,272,256]{2,1,0:T(8,128)(2,1)S(1)} %collective-permute-done.3.refs_2_) | copy-start | bytes 835588
  41.0 30.6 %copy-start.13 = (s32[4096]{0:T(1024)S(1)}, s32[4096]{0:T(1024)}, u32[]{:S(2)}) copy-start(s32[4096]{0:T(1024)} %seg_ref.1) | copy-start | bytes 49156
  41.0 30.6 %copy-start.14 = (s32[32,32]{1,0:T(8,128)S(1)}, s32[32,32]{1,0:T(8,128)}, u32[]{:S(2)}) copy-start(s32[32,32]{1,0:T(8,128)} %allow_ref.1) | copy-start | bytes 12292
  41.0 30.6 %all-to-all-start = ((bf16[16,32,1024]{2,1,0:T(8,128)(2,1)}), bf16[16,32,1024]{2,1,0:T(8,128)(2,1)S(1)}, u32[]{:S(2)}, u32[]{:S(2)}) async-start(bf16[16,32,1024]{2,1,0:T(8,128)(2,1)} %bitcast.30), calls=%async_computation | async-start | bytes 2097152 | tf_op jit(solution)/shard_map/all_to_all | solution.py:379
  47.0 3.9 %collective-permute-start.5 = (bf16[2,272,256]{2,1,0:T(8,128)(2,1)S(1)}, bf16[2,272,256]{2,1,0:T(8,128)(2,1)S(1)}, u32[]{:S(2)}, u32[]{:S(2)}) collective-permute-start(bf16[2,272,256]{2,1,0:T(8,128)(2,1)S(1)} %collective-permute-done.1.refs_0_), channel_id=1, source_target_pairs={{0,1},{1,0},{2,3},{3,2},{4,5},{5,4},{6,7},{7,6},{8,9},{9,8},{10,11... | collective-permute-start | bytes 835592 | tf_op jit(solution)/shard_map/ppermute | solution.py:378
  48.6 3.0 %collective-permute-start.6 = (bf16[2,272,256]{2,1,0:T(8,128)(2,1)S(1)}, bf16[2,272,256]{2,1,0:T(8,128)(2,1)S(1)}, u32[]{:S(2)}, u32[]{:S(2)}) collective-permute-start(bf16[2,272,256]{2,1,0:T(8,128)(2,1)S(1)} %collective-permute-done.2.refs_1_), channel_id=1, source_target_pairs={{0,1},{1,0},{2,3},{3,2},{4,5},{5,4},{6,7},{7,6},{8,9},{9,8},{10,11... | collective-permute-start | bytes 835592 | tf_op jit(solution)/shard_map/ppermute | solution.py:378
  48.7 3.6 %collective-permute-start.7 = (bf16[2,272,256]{2,1,0:T(8,128)(2,1)S(1)}, bf16[2,272,256]{2,1,0:T(8,128)(2,1)}, u32[]{:S(2)}, u32[]{:S(2)}) collective-permute-start(bf16[2,272,256]{2,1,0:T(8,128)(2,1)S(1)} %collective-permute-done.3.refs_2_), channel_id=1, source_target_pairs={{0,1},{1,0},{2,3},{3,2},{4,5},{5,4},{6,7},{7,6},{8,9},{9,8},{10,11... | collective-permute-start | bytes 835592 | tf_op jit(solution)/shard_map/ppermute | solution.py:378
  49.1 1.8 %collective-permute-start.8 = (bf16[272,256]{1,0:T(8,128)(2,1)S(1)}, bf16[272,256]{1,0:T(8,128)(2,1)}, u32[]{:S(2)}, u32[]{:S(2)}) collective-permute-start(bf16[272,256]{1,0:T(8,128)(2,1)S(1)} %collective-permute-done.4.refs_3_), channel_id=1, source_target_pairs={{0,1},{1,0},{2,3},{3,2},{4,5},{5,4},{6,7},{7,6},{8,9},{9,8},{10,11... | collective-permute-start | bytes 417800 | tf_op jit(solution)/shard_map/ppermute | solution.py:378
  50.9 0.7 copy-start.5
  51.6 0.7 copy-start.7
  52.3 1.0 copy-start.2
  53.3 1.0 copy-start.4
  54.2 1.0 copy-start.6
  55.2 1.0 copy-start.8
  56.2 0.9 copy-start.12
  59.1 0.7 copy-start.9
  71.6 1.0 copy-start.10
  79.5 1.1 copy-start
  80.6 0.5 copy-start.15
  81.1 6.4 %collective-permute-start.9 = (bf16[2560,128]{1,0:T(8,128)(2,1)S(1)}, bf16[2560,128]{1,0:T(8,128)(2,1)S(1)}, u32[]{:S(2)}, u32[]{:S(2)}) collective-permute-start(bf16[2560,128]{1,0:T(8,128)(2,1)S(1)} %get-tuple-element.21), channel_id=1, source_target_pairs={{0,1},{1,0},{2,3},{3,2},{4,5},{5,4},{6,7},{7,6},{8,9},{9,8},{10,11... | collective-permute-start | bytes 1966088 | tf_op jit(solution)/shard_map/ppermute | solution.py:394
  87.5 0.8 copy-start.16

commit v6 on v5

v6 whole, which is shorter than its diff:
```python
import functools
import math

import jax
import jax.numpy as jnp
from jax import lax
from jax.experimental import pallas as pl
from jax.experimental.pallas import tpu as pltpu
from jax.sharding import PartitionSpec as P

QUERY_HEAD_COUNT = 128
KEY_VALUE_HEADS = 8
HEAD_SIZE = 128
BLK = 128
TOK = 256
SHARDS = 16
SLOTS = 32
META = 16
Z_CHIPS = SHARDS // 2
RING = Z_CHIPS // 2
DOC_MOST = 2304
BACK = -(-DOC_MOST // TOK)
WINDOW = BACK + 1
BLOCKS_BACK = -(-DOC_MOST // BLK)
WIDE = 4
NARROW = 2
MOST_BLOCKS = WIDE * -(-(BLOCKS_BACK + 1) // WIDE)
LOCAL_HEADS = 8
LANES = LOCAL_HEADS * BLK
NEG_FILL = -1e30
SCALE = 1.0 / math.sqrt(HEAD_SIZE)
EXP2_SCALE = SCALE * math.log2(math.e)
F32 = jnp.float32
BF16 = jnp.bfloat16


def iota(shape, dim):
    return lax.broadcasted_iota(jnp.int32, shape, dim)


def dot(a, b):
    return jnp.dot(a, b, preferred_element_type=F32)


def ranks_within(member):
    earlier = (iota((TOK, TOK), 0) < iota((TOK, TOK), 1)).astype(F32).astype(BF16)
    counts = dot(member.astype(F32).astype(BF16), earlier)
    return jnp.where(member, counts, -1.0)


def pack_kernel(place_ref, rows_ref, out_ref):
    owner = place_ref[...] >> 8
    rank = ranks_within(owner == iota((SHARDS, TOK), 0))
    slot = iota((SLOTS, TOK), 0).astype(F32)
    picks = jnp.concatenate(
        [(rank[s : s + 1, :] == slot).astype(F32) for s in range(SHARDS)], axis=0
    ).astype(BF16)
    for first in range(0, rows_ref.shape[1], 256):
        cols = pl.ds(first, 256)
        out_ref[:, cols] = dot(picks, rows_ref[:, cols]).astype(BF16)


def stage_kernel(place_ref, kv_ref, out_ref, arrived):
    cols = pl.ds(pl.multiple_of((lax.axis_index("tp") // 2) * HEAD_SIZE, HEAD_SIZE), HEAD_SIZE)
    copies = [
        pltpu.make_async_copy(
            kv_ref.at[i, :, cols],
            out_ref.at[pl.ds(0, TOK), pl.ds(i * HEAD_SIZE, HEAD_SIZE)],
            arrived.at[i],
        )
        for i in range(2)
    ]
    for copy in copies:
        copy.start()
    place = place_ref[...]
    row = iota((META, TOK), 0)
    owner = jnp.broadcast_to((place >> 8).astype(F32), (META, TOK))
    within = jnp.broadcast_to((place & (TOK - 1)).astype(F32), (META, TOK))
    meta = jnp.where(row == 0, owner, jnp.where(row == 1, within, 0.0))
    out_ref[TOK:, :] = meta.astype(BF16)
    for copy in copies:
        copy.wait()


def permute_kernel(info_ref, grad_ref, own_ref, *refs):
    mine, theirs = refs[:RING], refs[RING : 2 * RING]
    out_ref, unpack_ref, gr_ref, gt_ref, slots_s = refs[2 * RING :]
    shard = info_ref[0]
    core = info_ref[1]
    base = jnp.maximum(shard - BACK, 0)
    z, x = shard // 2, shard % 2
    sources = [(own_ref.at[j], shard ^ j) for j in range(2)]
    for refs_k, side in ((mine, core), (theirs, 1 - core)):
        for k in range(1, RING):
            far = (z + k * (2 * side - 1) + Z_CHIPS) % Z_CHIPS
            sources += [(refs_k[k - 1].at[j], 2 * far + (x ^ j)) for j in range(2)]
        far = (z + RING) % Z_CHIPS
        sources += [(refs_k[RING - 1], 2 * far + (x ^ side))]
    owners = jnp.concatenate([ref[TOK : TOK + 1, :].astype(F32) for ref, _ in sources], axis=0)
    within = jnp.concatenate([ref[TOK + 1 : TOK + 2, :].astype(F32) for ref, _ in sources], axis=0)
    rank = ranks_within(owners == shard.astype(F32))
    slot = iota((SLOTS, TOK), 0).astype(F32)
    lane = iota((SLOTS, TOK), 1).astype(F32)
    for i, (_, source) in enumerate(sources):
        hit = rank[i : i + 1, :] == slot
        landing = jnp.sum(jnp.where(hit, within[i : i + 1, :] + 1.0, 0.0), axis=1, keepdims=True)
        rows = pl.ds(pl.multiple_of(source * SLOTS, SLOTS), SLOTS)
        slots_s[rows, :] = (landing == lane + 1.0).astype(F32)
    unpack_ref[...] = slots_s[...].T.astype(BF16)
    for half in range(2):
        for h in range(LOCAL_HEADS):
            block = grad_ref[half * BLK : (half + 1) * BLK, h * HEAD_SIZE : (h + 1) * HEAD_SIZE]
            gr_ref[half, h * BLK : (h + 1) * BLK, :] = block
            gt_ref[half, :, h * BLK : (h + 1) * BLK] = block.astype(F32).T.astype(BF16)

    def one_shard(i, carry):
        rows = iota((TOK, TOK), 0).astype(F32)
        goal = jnp.where(owners == (base + i).astype(F32), within, -1.0)
        total = jnp.zeros((TOK, 2 * HEAD_SIZE), F32)
        for n, (ref, _) in enumerate(sources):
            picks = (goal[n : n + 1, :] == rows).astype(F32).astype(BF16)
            total = total + dot(picks, ref[:TOK, :])
        out_ref[pl.ds(pl.multiple_of(i * TOK, TOK), TOK), :] = total.astype(BF16)
        return carry

    lax.fori_loop(0, shard - base + 1, one_shard, 0)


def visible_blocks(qb, seg_ref, allow_ref, on_block):
    q_first = seg_ref[qb * BLK]

    def scan(kb, count):
        seen = jnp.logical_and(seg_ref[kb * BLK + BLK - 1] >= q_first, allow_ref[qb, kb] != 0)

        @pl.when(seen)
        def _():
            on_block(kb, count)

        return count + seen.astype(jnp.int32)

    count = lax.fori_loop(jnp.maximum(qb - BLOCKS_BACK, 0), qb + 1, scan, 0)
    wide = (count + 1) // WIDE
    narrow = (count + WIDE - 1) // WIDE - wide
    return count, wide, narrow


def block_rows(n, blocks=1):
    return pl.ds(pl.multiple_of(n * BLK, BLK), blocks * BLK)


def attention_kernel(
    info_ref,
    seg_ref,
    allow_ref,
    segv_ref,
    unpack_ref,
    recv_ref,
    gr_ref,
    gt_ref,
    kv_ref,
    keep_ref,
    send_ref,
    sg_ref,
    qr_s,
    qt_s,
    k_s,
    v_s,
    bias_s,
    e_s,
    dp_s,
    top_s,
    acc_s,
    sg_s,
    list_s,
    sent,
):
    shard = info_ref[0]
    core = info_ref[1]
    base = jnp.maximum(shard - BACK, 0)
    acc_s[...] = jnp.zeros_like(acc_s)

    def query_block(half, carry):
        qb = shard * 2 + half
        q_seg = segv_ref[pl.ds(qb, 1), :]
        q_last = seg_ref[qb * BLK + BLK - 1]

        def on_block(kb, count):
            list_s[count] = kb - 2 * base
            src = block_rows(kb - 2 * base)
            dst = block_rows(count)
            k_s[dst, :] = kv_ref[src, :HEAD_SIZE]
            v_s[dst, :] = kv_ref[src, HEAD_SIZE:]
            whole = jnp.logical_and(kb < qb, seg_ref[kb * BLK] == q_last)

            @pl.when(whole)
            def _():
                bias_s[dst, :] = jnp.zeros((BLK, BLK), F32)

            @pl.when(jnp.logical_not(whole))
            def _():
                k_seg = jnp.broadcast_to(segv_ref[pl.ds(kb, 1), :].astype(F32), (BLK, BLK)).T
                k_pos = kb * BLK + iota((BLK, BLK), 0)
                q_pos = qb * BLK + iota((BLK, BLK), 1)
                ok = (k_seg == q_seg.astype(F32)) & (k_pos <= q_pos)
                bias_s[dst, :] = jnp.where(ok, 0.0, NEG_FILL)

        count, wide, narrow = visible_blocks(qb, seg_ref, allow_ref, on_block)

        def fill(n, c):
            list_s[n] = 2 * WINDOW
            dst = block_rows(n)
            k_s[dst, :] = jnp.zeros((BLK, HEAD_SIZE), BF16)
            v_s[dst, :] = jnp.zeros((BLK, HEAD_SIZE), BF16)
            bias_s[dst, :] = jnp.full((BLK, BLK), NEG_FILL, F32)
            return c

        lax.fori_loop(count, wide * WIDE + narrow * NARROW, fill, 0)
        picks = unpack_ref[block_rows(half), :]
        for pair in range(LOCAL_HEADS // 2):
            q_two = dot(picks, recv_ref[:, pair * 256 : (pair + 1) * 256])
            for i in range(2):
                mine = slice((2 * pair + i) * BLK, (2 * pair + i + 1) * BLK)
                q_one = q_two[:, i * HEAD_SIZE : (i + 1) * HEAD_SIZE]
                qr_s[mine, :] = q_one.astype(BF16)
                qt_s[:, mine] = q_one.T.astype(BF16)

        def first_pass(start, blocks, slot, state):
            top, total, weighed = state
            rows = block_rows(start, blocks)
            scores = dot(k_s[rows, :], qt_s[...])
            scores = scores + jnp.concatenate([bias_s[rows, :]] * LOCAL_HEADS, axis=1)
            new_top = jnp.maximum(top, jnp.max(scores, axis=0, keepdims=True))
            factor = jnp.exp2((top - new_top) * EXP2_SCALE)
            e = jnp.exp2((scores - new_top) * EXP2_SCALE)
            dp = dot(v_s[rows, :], gt_ref[half])
            e_s[rows, :] = e
            dp_s[rows, :] = dp
            top_s[slot] = new_top
            total = total * factor + jnp.sum(e.reshape(-1, 8, LANES), axis=0)
            weighed = weighed * factor + jnp.sum((e * dp).reshape(-1, 8, LANES), axis=0)
            return (new_top, total, weighed)

        state = (
            jnp.full((1, LANES), NEG_FILL, F32),
            jnp.zeros((8, LANES), F32),
            jnp.zeros((8, LANES), F32),
        )
        state = lax.fori_loop(
            0, wide, lambda n, st: first_pass(n * WIDE, WIDE, n, st), state
        )
        top, total, weighed = lax.fori_loop(
            0, narrow, lambda n, st: first_pass(wide * WIDE, NARROW, wide, st), state
        )
        inverse = 1.0 / jnp.sum(total, axis=0, keepdims=True)
        out_dot = jnp.sum(weighed, axis=0, keepdims=True) * inverse

        def copy_out(start, blocks, buffer):
            return pltpu.make_async_copy(
                sg_s.at[buffer, pl.ds(0, blocks * BLK), :],
                sg_ref.at[half, block_rows(start, blocks), :],
                sent.at[buffer],
            )

        def second_pass(start, blocks, slot, buffer):
            rows = block_rows(start, blocks)
            factor = jnp.exp2((top_s[slot] - top) * EXP2_SCALE) * inverse
            weights = e_s[rows, :] * factor
            score_grad = (weights * (dp_s[rows, :] - out_dot)).astype(BF16)
            sg_s[buffer, : blocks * BLK, :] = score_grad
            copy_out(start, blocks, buffer).start()
            value_terms = dot(weights.astype(BF16), gr_ref[half])
            key_terms = dot(score_grad, qr_s[...])
            for n in range(blocks):
                dst = block_rows(list_s[start + n])
                acc_s[0, dst, :] += key_terms[n * BLK : (n + 1) * BLK, :]
                acc_s[1, dst, :] += value_terms[n * BLK : (n + 1) * BLK, :]

        def wide_step(n, c):
            @pl.when(n >= 2)
            def _():
                copy_out((n - 2) * WIDE, WIDE, n % 2).wait()

            second_pass(n * WIDE, WIDE, n, n % 2)
            return c

        lax.fori_loop(0, wide, wide_step, 0)

        @pl.when(narrow > 0)
        def _():
            second_pass(wide * WIDE, NARROW, wide, 2)
            copy_out(wide * WIDE, NARROW, 2).wait()

        for late in (1, 2):

            @pl.when(wide >= late)
            def _():
                copy_out((wide - late) * WIDE, WIDE, (wide - late) % 2).wait()

        return carry

    lax.fori_loop(0, 2, query_block, 0)
    rows = slice(0, WINDOW * TOK)

    @pl.when(core == 0)
    def _():
        keep_ref[...] = (acc_s[0, rows, :] * SCALE).astype(BF16)
        send_ref[...] = acc_s[1, rows, :].astype(BF16)

    @pl.when(core == 1)
    def _():
        keep_ref[...] = acc_s[1, rows, :].astype(BF16)
        send_ref[...] = (acc_s[0, rows, :] * SCALE).astype(BF16)


def query_grad_kernel(
    info_ref, seg_ref, allow_ref, kv_ref, sg_ref, dq_ref, kt_s, dqt_s, sg_s, arrived
):
    shard = info_ref[0]
    base = jnp.maximum(shard - BACK, 0)

    def query_block(half, carry):
        def on_block(kb, count):
            lanes = block_rows(count % NARROW)
            k_blk = kv_ref[block_rows(kb - 2 * base), :HEAD_SIZE]
            kt_s[count // NARROW, :, lanes] = k_blk.astype(F32).T.astype(BF16)

        count, wide, narrow = visible_blocks(shard * 2 + half, seg_ref, allow_ref, on_block)
        steps = wide * (WIDE // NARROW) + narrow

        def fill(n, c):
            lanes = block_rows(n % NARROW)
            kt_s[n // NARROW, :, lanes] = jnp.zeros((HEAD_SIZE, BLK), BF16)
            return c

        lax.fori_loop(count, steps * NARROW, fill, 0)

        def fetch(step):
            return pltpu.make_async_copy(
                sg_ref.at[half, block_rows(step * NARROW, NARROW), :],
                sg_s.at[step % 2],
                arrived.at[step % 2],
            )

        fetch(0).start()
        dqt_s[...] = jnp.zeros_like(dqt_s)

        def one_step(step, c):
            @pl.when(step + 1 < steps)
            def _():
                fetch(step + 1).start()

            fetch(step).wait()
            dqt_s[...] += dot(kt_s[step], sg_s[step % 2])
            return c

        lax.fori_loop(0, steps, one_step, 0)
        for h in range(LOCAL_HEADS):
            block = dqt_s[:, h * BLK : (h + 1) * BLK] * SCALE
            dq_ref[block_rows(half), h * HEAD_SIZE : (h + 1) * HEAD_SIZE] = block.T.astype(BF16)
        return carry

    lax.fori_loop(0, 2, query_block, 0)


def merge_kernel(info_ref, keep_ref, recv_ref, out_ref):
    base = jnp.maximum(info_ref[0] - BACK, 0)
    out_ref[...] = jnp.zeros_like(out_ref)
    rows = pl.ds(pl.multiple_of(base * TOK, TOK), WINDOW * TOK)
    out_ref[rows, :] = (keep_ref[...].astype(F32) + recv_ref[...].astype(F32)).astype(BF16)


VMEM = pl.BlockSpec(memory_space=pltpu.VMEM)
SMEM = pl.BlockSpec(memory_space=pltpu.SMEM)


ANY = pl.BlockSpec(memory_space=pl.ANY)


def call_permute(info, grad, own, mine, theirs):
    return pl.pallas_call(
        permute_kernel,
        in_specs=[SMEM] + [VMEM] * (2 * RING + 2),
        out_specs=[VMEM] * 4,
        out_shape=[
            jax.ShapeDtypeStruct((WINDOW * TOK, 2 * HEAD_SIZE), BF16),
            jax.ShapeDtypeStruct((TOK, SHARDS * SLOTS), BF16),
            jax.ShapeDtypeStruct((2, LANES, HEAD_SIZE), BF16),
            jax.ShapeDtypeStruct((2, HEAD_SIZE, LANES), BF16),
        ],
        scratch_shapes=[pltpu.VMEM((SHARDS * SLOTS, TOK), F32)],
        compiler_params=pltpu.CompilerParams(vmem_limit_bytes=32 * 2**20),
        name="permute",
    )(info, grad, own, *mine, *theirs)


def call_attention(info, segments, allow, unpack, q_recv, gr, gt, kv_window):
    return pl.pallas_call(
        attention_kernel,
        in_specs=[SMEM, SMEM, SMEM] + [VMEM] * 6,
        out_specs=[VMEM, VMEM, ANY],
        out_shape=[
            jax.ShapeDtypeStruct((WINDOW * TOK, HEAD_SIZE), BF16),
            jax.ShapeDtypeStruct((WINDOW * TOK, HEAD_SIZE), BF16),
            jax.ShapeDtypeStruct((2, MOST_BLOCKS * BLK, LANES), BF16),
        ],
        scratch_shapes=[
            pltpu.VMEM((LANES, HEAD_SIZE), BF16),
            pltpu.VMEM((HEAD_SIZE, LANES), BF16),
            pltpu.VMEM((MOST_BLOCKS * BLK, HEAD_SIZE), BF16),
            pltpu.VMEM((MOST_BLOCKS * BLK, HEAD_SIZE), BF16),
            pltpu.VMEM((MOST_BLOCKS * BLK, BLK), F32),
            pltpu.VMEM((MOST_BLOCKS * BLK, LANES), F32),
            pltpu.VMEM((MOST_BLOCKS * BLK, LANES), F32),
            pltpu.VMEM((MOST_BLOCKS // WIDE + 1, 1, LANES), F32),
            pltpu.VMEM((2, WINDOW * TOK + BLK, HEAD_SIZE), F32),
            pltpu.VMEM((3, WIDE * BLK, LANES), BF16),
            pltpu.SMEM((MOST_BLOCKS,), jnp.int32),
            pltpu.SemaphoreType.DMA((3,)),
        ],
        compiler_params=pltpu.CompilerParams(vmem_limit_bytes=48 * 2**20),
        name="attention",
    )(info, segments, allow, segments.reshape(-1, BLK), unpack, q_recv, gr, gt, kv_window)


def call_query_grad(info, segments, allow, kv_window, score_grad):
    return pl.pallas_call(
        query_grad_kernel,
        in_specs=[SMEM, SMEM, SMEM, VMEM, ANY],
        out_specs=VMEM,
        out_shape=jax.ShapeDtypeStruct((TOK, LOCAL_HEADS * HEAD_SIZE), BF16),
        scratch_shapes=[
            pltpu.VMEM((MOST_BLOCKS // NARROW, HEAD_SIZE, NARROW * BLK), BF16),
            pltpu.VMEM((HEAD_SIZE, LANES), F32),
            pltpu.VMEM((2, NARROW * BLK, LANES), BF16),
            pltpu.SemaphoreType.DMA((2,)),
        ],
        compiler_params=pltpu.CompilerParams(vmem_limit_bytes=32 * 2**20),
        cost_estimate=pl.CostEstimate(
            flops=2 * TOK * 2048 * LANES, bytes_accessed=12 * 2**20, transcendentals=0
        ),
        name="query_grad",
    )(info, segments, allow, kv_window, score_grad)


def on_device(queries, keys_values, out_grad, place, segments, allow):
    tp_index = lax.axis_index("tp")
    ctx_index = lax.axis_index("ctx")
    tp_size = lax.axis_size("tp")
    width = LOCAL_HEADS * HEAD_SIZE
    info = jnp.stack([ctx_index, tp_index % 2]).astype(jnp.int32)
    staged = pl.pallas_call(
        stage_kernel,
        in_specs=[VMEM, pl.BlockSpec(memory_space=pl.ANY)],
        out_specs=VMEM,
        out_shape=jax.ShapeDtypeStruct((TOK + META, 2 * HEAD_SIZE), BF16),
        scratch_shapes=[pltpu.SemaphoreType.DMA((2,))],
        name="stage",
    )(place.reshape(1, TOK), keys_values)
    beside = lax.ppermute(staged, "ctx", [(k, k ^ 1) for k in range(SHARDS)])
    own = jnp.stack([staged, beside])

    def around(hops):
        pairs = []
        for k in range(SHARDS * tp_size):
            ctx, tp = k // tp_size, k % tp_size
            far = (ctx + (2 * hops if tp % 2 == 0 else -2 * hops)) % SHARDS
            pairs.append((k, far * tp_size + tp))
        return pairs

    swap = [(k, k ^ 1) for k in range(tp_size)]
    first = lax.ppermute(own, ("ctx", "tp"), around(1))
    second = lax.ppermute(first, ("ctx", "tp"), around(1))
    third = lax.ppermute(second, ("ctx", "tp"), around(1))
    half = lax.dynamic_index_in_dim(second, tp_index % 2, 0, keepdims=False)
    fourth = lax.ppermute(half, ("ctx", "tp"), around(2))
    mine = [first, second, third, fourth]
    g_local = lax.all_to_all(out_grad, "tp", split_axis=1, concat_axis=0, tiled=True)
    q_send = pl.pallas_call(
        pack_kernel,
        in_specs=[VMEM, VMEM],
        out_specs=VMEM,
        out_shape=jax.ShapeDtypeStruct((SHARDS * SLOTS, width), BF16),
        name="pack",
    )(place.reshape(1, TOK), queries)
    q_send, *mine = lax.optimization_barrier((q_send, *mine))
    theirs = [lax.ppermute(piece, "tp", swap) for piece in mine]
    q_recv = lax.all_to_all(q_send, "ctx", split_axis=0, concat_axis=0, tiled=True)
    kv_window, unpack, gr, gt = call_permute(info, g_local, own, mine, theirs)
    keep, send, score_grad = call_attention(
        info, segments, allow, unpack, q_recv, gr, gt, kv_window
    )
    recv = lax.ppermute(send, "tp", swap)
    part = pl.pallas_call(
        merge_kernel,
        in_specs=[SMEM, VMEM, VMEM],
        out_specs=VMEM,
        out_shape=jax.ShapeDtypeStruct((SHARDS * TOK, HEAD_SIZE), BF16),
        name="merge",
    )(info, keep, recv)
    part, score_grad = lax.optimization_barrier((part, score_grad))
    parts = lax.all_to_all(
        part.reshape(SHARDS, TOK, HEAD_SIZE), "ctx", split_axis=0, concat_axis=0, tiled=True
    )
    grad_q = call_query_grad(info, segments, allow, kv_window, score_grad)
    owned = jnp.sum(parts.astype(F32), axis=0).astype(BF16)
    heads = lax.all_to_all(
        owned.reshape(tp_size, TOK // tp_size, HEAD_SIZE),
        "tp",
        split_axis=0,
        concat_axis=0,
        tiled=True,
    )
    key_value_gradient = (
        heads.reshape(KEY_VALUE_HEADS, 2, TOK // tp_size, HEAD_SIZE)
        .transpose(1, 2, 0, 3)
        .reshape(2, TOK // tp_size, KEY_VALUE_HEADS * HEAD_SIZE)
    )
    return (grad_q, key_value_gradient)


def solution(mesh):
    in_specs = (P("ctx", "tp"), P(None, "ctx", None), P(("ctx", "tp"), None), P("ctx"), P(), P())
    out_specs = (P("ctx", "tp"), P(None, ("ctx", "tp"), None))
    return jax.shard_map(
        on_device, mesh=mesh, in_specs=in_specs, out_specs=out_specs, check_vma=False
    )
```

time: 155 us -> 154 us (level); the launches traced: 156 us -> 151 us
  blocking collectives: 64 us -> 41.2 us
  local copies, waits for them, and re-layouts: 11.7 us -> 20.9 us
  starting transfers between devices: 35.4 us -> 43.7 us
  Pallas kernels: 16.6 us -> 18.6 us
  waiting for transfers between devices: 26.3 us -> 24.5 us
    all_to_all x1 -> x0, blocking collectives: 15.6 us -> none  [on_device(): lax.all_to_all(owned.reshape(tp_size, TOK // tp_size, HEAD_SIZE), 'tp', s...]
    all_to_all x0 -> x1, starting transfers between devices: none -> 8.45 us  [on_device(): lax.all_to_all(owned.reshape(tp_size, TOK // tp_size, HEAD_SIZE), 'tp', s...]
    unnamed x36 -> x46, local copies, waits for them, and re-layouts: 10.2 us -> 18.4 us
    all_to_all x1, blocking collectives: 48.4 us -> 41.2 us  [on_device(): lax.all_to_all(part.reshape(SHARDS, TOK, HEAD_SIZE), 'ctx', split_axis=0,...]
    pallas_call x2 -> x3, Pallas kernels: 8.92 us -> 11.2 us  [the longest x1 5.79 us: call_attention(): pl.pallas_call(attention_kernel, in_specs=[SMEM, SMEM, SMEM] + [VMEM] * 6...]
    all_to_all x1, waiting for transfers between devices: 11.8 us -> 10 us  [on_device(): lax.all_to_all(q_send, 'ctx', split_axis=0, concat_axis=0, tiled=True)]
  transfers between devices with their start and end apart: 12 -> 13, of which waited for: 7 -> 7; matrix products, arithmetic and copies ran while one was open for 1% -> 1% of each run, Pallas kernels for 3% -> 5%
where the time goes in v6:
time: 154 us; the launch traced here: 151 us
  starting transfers between devices  43.7 us (28%)
  blocking collectives  41.2 us (27%)
  waiting for transfers between devices  24.5 us (16%)
  local copies, waits for them, and re-layouts  20.9 us (14%)
  Pallas kernels  18.6 us (12%)
  other arithmetic  1.78 us (1%)
    all_to_all x1, blocking collectives, on_device(): lax.all_to_all(part.reshape(SHARDS, TOK, HEAD_SIZE), 'ctx', split_axis=0,...  41.2 us
    unnamed x46, local copies, waits for them, and re-layouts  18.4 us
    all_to_all x1, waiting for transfers between devices, on_device(): lax.all_to_all(q_send, 'ctx', split_axis=0, concat_axis=0, tiled=True)  10 us
    all_to_all x1, starting transfers between devices, on_device(): lax.all_to_all(owned.reshape(tp_size, TOK // tp_size, HEAD_SIZE), 'tp', s...  8.45 us
    all_to_all x1, starting transfers between devices, on_device(): lax.all_to_all(out_grad, 'tp', split_axis=1, concat_axis=0, tiled=True)  7.06 us
    ppermute x1, starting transfers between devices, on_device(): first = lax.ppermute(own, ('ctx', 'tp'), around(1))  6.54 us
    all_to_all x1, starting transfers between devices, on_device(): lax.all_to_all(q_send, 'ctx', split_axis=0, concat_axis=0, tiled=True)  5.9 us
    pallas_call x1, Pallas kernels, call_attention(): pl.pallas_call(attention_kernel, in_specs=[SMEM, SMEM, SMEM] + [VMEM] * 6...  5.79 us
  transfers between devices with their start and end apart: 13, of which 7 were waited for; matrix products, arithmetic and copies ran while one was open for 1% of the time, Pallas kernels for 5%

profile of v6, /device:TPU:1, one launch (start us, length us, event | category | flops | bytes accessed | tf_op | source)
XLA Modules:
  0.0 151.4 jit_solution(4623693466530753805)
XLA Ops:
  0.7 2.2 %stage.1 = bf16[272,256]{1,0:T(8,128)(2,1)} custom-call(s32[1,256]{1,0:T(1,128)} %bitcast.36, bf16[2,256,1024]{2,1,0:T(8,128)(2,1)} %kv_ref.1), custom_call_target="tpu_custom_call" | custom-call | tf_op jit(solution)/shard_map/stage/pallas_call | solution.py:451
  2.9 2.1 %collective-permute-start = (bf16[272,256]{1,0:T(8,128)(2,1)}, bf16[272,256]{1,0:T(8,128)(2,1)S(1)}, u32[]{:S(2)}, u32[]{:S(2)}) collective-permute-start(bf16[272,256]{1,0:T(8,128)(2,1)} %stage.1), channel_id=1, source_target_pairs={{0,16},{16,0},{32,48},{48,32},{64,80},{80,64},{96,112},{112,96},{1... | collective-permute-start | bytes 417800 | tf_op jit(solution)/shard_map/ppermute | solution.py:459
  5.0 2.7 %collective-permute-done = bf16[272,256]{1,0:T(8,128)(2,1)S(1)} collective-permute-done((bf16[272,256]{1,0:T(8,128)(2,1)}, bf16[272,256]{1,0:T(8,128)(2,1)S(1)}, u32[]{:S(2)}, u32[]{:S(2)}) %collective-permute-start) | collective-permute-done | bytes 139296 | tf_op jit(solution)/shard_map/ppermute | solution.py:459
  7.7 0.9 pad_maximum_fusion.own_ref
  8.6 6.5 %collective-permute-start.1 = (bf16[2,272,256]{2,1,0:T(8,128)(2,1)S(1)}, bf16[2,272,256]{2,1,0:T(8,128)(2,1)S(1)}, u32[]{:S(2)}, u32[]{:S(2)}) collective-permute-start(bf16[2,272,256]{2,1,0:T(8,128)(2,1)S(1)} %pad_maximum_fusion.own_ref), channel_id=1, source_target_pairs={{0,32},{1,225},{2,34},{3,227},{4,36},{5,229},{6,38},{7,231},{8,40}... | collective-permute-start | bytes 835592 | tf_op jit(solution)/shard_map/ppermute | solution.py:471
  15.2 3.5 %collective-permute-done.1.refs_0_ = bf16[2,272,256]{2,1,0:T(8,128)(2,1)S(1)} collective-permute-done((bf16[2,272,256]{2,1,0:T(8,128)(2,1)S(1)}, bf16[2,272,256]{2,1,0:T(8,128)(2,1)S(1)}, u32[]{:S(2)}, u32[]{:S(2)}) %collective-permute-start.1) | collective-permute-done | bytes 278560 | tf_op jit(solution)/shard_map/ppermute | solution.py:471
  18.7 3.1 %collective-permute-start.2 = (bf16[2,272,256]{2,1,0:T(8,128)(2,1)S(1)}, bf16[2,272,256]{2,1,0:T(8,128)(2,1)S(1)}, u32[]{:S(2)}, u32[]{:S(2)}) collective-permute-start(bf16[2,272,256]{2,1,0:T(8,128)(2,1)S(1)} %collective-permute-done.1.refs_0_), channel_id=1, source_target_pairs={{0,32},{1,225},{2,34},{3,227},{4,36},{5,229},{6,38},{7,231},{8,40}... | collective-permute-start | bytes 835592 | tf_op jit(solution)/shard_map/ppermute | solution.py:472
  21.8 1.9 %copy.16 = bf16[2,16,8,1024]{3,2,0,1:T(8,128)(2,1)} copy(bf16[2,16,8,1024]{3,2,1,0:T(8,128)(2,1)} %bitcast.32) | data formatting | bytes 1048576 | tf_op jit(solution)/shard_map/all_to_all | solution.py:477
  23.6 7.1 %all-to-all-start = ((bf16[16,16,1024]{2,0,1:T(8,128)(2,1)}), bf16[16,16,1024]{2,0,1:T(8,128)(2,1)S(1)}, u32[]{:S(2)}, u32[]{:S(2)}) async-start(bf16[16,16,1024]{2,0,1:T(8,128)(2,1)} %bitcast.24), calls=%async_computation | async-start | bytes 1048576 | tf_op jit(solution)/shard_map/all_to_all | solution.py:477
  30.7 2.7 %collective-permute-start.3 = (bf16[2,272,256]{2,1,0:T(8,128)(2,1)S(1)}, bf16[2,272,256]{2,1,0:T(8,128)(2,1)S(1)}, u32[]{:S(2)}, u32[]{:S(2)}) collective-permute-start(bf16[2,272,256]{2,1,0:T(8,128)(2,1)S(1)} %collective-permute-done.2.refs_1_), channel_id=1, source_target_pairs={{0,32},{1,225},{2,34},{3,227},{4,36},{5,229},{6,38},{7,231},{8,40}... | collective-permute-start | bytes 835592 | tf_op jit(solution)/shard_map/ppermute | solution.py:473
  33.4 1.1 collective-permute-start.4
  34.4 2.6 %pack.1 = bf16[512,1024]{1,0:T(8,128)(2,1)} custom-call(s32[1,256]{1,0:T(1,128)} %bitcast.37, bf16[256,1024]{1,0:T(8,128)(2,1)} %rows_ref.1), custom_call_target="tpu_custom_call" | custom-call | tf_op jit(solution)/shard_map/pack/pallas_call | solution.py:478
  37.0 2.8 %collective-permute-done.4.refs_3_ = bf16[272,256]{1,0:T(8,128)(2,1)S(1)} collective-permute-done((bf16[272,256]{1,0:T(8,128)(2,1)S(1)}, bf16[272,256]{1,0:T(8,128)(2,1)S(1)}, u32[]{:S(2)}, u32[]{:S(2)}) %collective-permute-start.4) | collective-permute-done | bytes 139296 | tf_op jit(solution)/shard_map/ppermute | solution.py:475
  39.9 2.1 %all-to-all-done = bf16[16,16,1024]{2,0,1:T(8,128)(2,1)S(1)} async-done(((bf16[16,16,1024]{2,0,1:T(8,128)(2,1)}), bf16[16,16,1024]{2,0,1:T(8,128)(2,1)S(1)}, u32[]{:S(2)}, u32[]{:S(2)}) %all-to-all-start) | async-done | bytes 524320 | tf_op jit(solution)/shard_map/all_to_all | solution.py:477
  42.0 5.9 %all-to-all-start.1 = ((bf16[16,32,1024]{2,1,0:T(8,128)(2,1)}), bf16[16,32,1024]{2,1,0:T(8,128)(2,1)S(1)}, u32[]{:S(2)}, u32[]{:S(2)}) async-start(bf16[16,32,1024]{2,1,0:T(8,128)(2,1)} %bitcast.30), calls=%async_computation.1 | async-start | bytes 2097152 | tf_op jit(solution)/shard_map/all_to_all | solution.py:487
  47.9 1.5 %collective-permute-start.5 = (bf16[2,272,256]{2,1,0:T(8,128)(2,1)S(1)}, bf16[2,272,256]{2,1,0:T(8,128)(2,1)S(1)}, u32[]{:S(2)}, u32[]{:S(2)}) collective-permute-start(bf16[2,272,256]{2,1,0:T(8,128)(2,1)S(1)} %collective-permute-done.1.refs_0_), channel_id=1, source_target_pairs={{0,1},{1,0},{2,3},{3,2},{4,5},{5,4},{6,7},{7,6},{8,9},{9,8},{10,11... | collective-permute-start | bytes 835592 | tf_op jit(solution)/shard_map/ppermute | solution.py:486
  49.4 0.1 collective-permute-start.6
  49.5 0.4 collective-permute-start.7
  50.1 1.6 %collective-permute-done.8.refs_7_ = bf16[272,256]{1,0:T(8,128)(2,1)} collective-permute-done((bf16[272,256]{1,0:T(8,128)(2,1)S(1)}, bf16[272,256]{1,0:T(8,128)(2,1)}, u32[]{:S(2)}, u32[]{:S(2)}) %collective-permute-start.8) | collective-permute-done | bytes 139296 | tf_op jit(solution)/shard_map/ppermute | solution.py:486
  51.8 0.7 copy-done.10
  52.5 0.7 copy-done.12
  53.2 0.9 copy-done.7
  54.2 1.0 copy-done.9
  55.1 1.0 copy-done.11
  56.1 1.0 copy-done.13
  57.0 0.9 copy-done.18
  57.9 2.2 %permute.1 = (bf16[2560,256]{1,0:T(8,128)(2,1)S(1)}, bf16[256,512]{1,0:T(8,128)(2,1)S(1)}, bf16[2,1024,128]{2,1,0:T(8,128)(2,1)S(1)}, bf16[2,128,1024]{2,1,0:T(8,128)(2,1)S(1)}) custom-call(s32[2]{0:T(128)S(1)} %pad_add_fusion.info_ref, bf16[256,1024]{1,0:T(8,128)(2,1)S(1)} %bitcast.27, bf16[2,272,256]{2,1,0:T(8,128)(2,1)S(1)} %pad_maximum_fusion.own_ref, ...), custom_call_target="tpu_custom_call" | custom-call | tf_op jit(solution)/shard_map/permute/pallas_call | solution.py:380
  60.2 0.8 copy-done.2
  61.0 0.8 copy-done.4
  61.8 0.7 copy-done.14
  62.5 10.0 %all-to-all-done.1 = bf16[16,32,1024]{2,1,0:T(8,128)(2,1)S(1)} async-done(((bf16[16,32,1024]{2,1,0:T(8,128)(2,1)}), bf16[16,32,1024]{2,1,0:T(8,128)(2,1)S(1)}, u32[]{:S(2)}, u32[]{:S(2)}) %all-to-all-start.1) | async-done | bytes 1048608 | tf_op jit(solution)/shard_map/all_to_all | solution.py:487
  72.5 1.0 copy-done.3
  73.6 1.0 copy-done.5
  74.6 0.9 copy-done.15
  75.5 5.8 %attention.1 = (bf16[2560,128]{1,0:T(8,128)(2,1)S(1)}, bf16[2560,128]{1,0:T(8,128)(2,1)S(1)}, bf16[2,2560,1024]{2,1,0:T(8,128)(2,1)}) custom-call(s32[2]{0:T(128)S(1)} %pad_add_fusion.info_ref, s32[4096]{0:T(1024)S(1)} %copy-done.16, s32[32,32]{1,0:T(8,128)S(1)} %copy-done.19, s32[32,128]{1,0:T(8,128)S(1)} %bitcast.28, bf16[256,512]{1,0:T(8,128)(2,1)S(1)} %copy-done.15, ...), custom_call_target="tpu_custom_call" | custom-call | tf_op jit(solution)/shard_map/attention/pallas_call | solution.py:397
  81.4 0.8 copy-done.1
  82.2 0.5 copy-done.20
  82.7 4.7 %collective-permute-start.9 = (bf16[2560,128]{1,0:T(8,128)(2,1)S(1)}, bf16[2560,128]{1,0:T(8,128)(2,1)S(1)}, u32[]{:S(2)}, u32[]{:S(2)}) collective-permute-start(bf16[2560,128]{1,0:T(8,128)(2,1)S(1)} %get-tuple-element.26), channel_id=1, source_target_pairs={{0,1},{1,0},{2,3},{3,2},{4,5},{5,4},{6,7},{7,6},{8,9},{9,8},{10,11... | collective-permute-start | bytes 1966088 | tf_op jit(solution)/shard_map/ppermute | solution.py:492
  87.4 1.7 %collective-permute-done.9.recv_ref = bf16[2560,128]{1,0:T(8,128)(2,1)S(1)} collective-permute-done((bf16[2560,128]{1,0:T(8,128)(2,1)S(1)}, bf16[2560,128]{1,0:T(8,128)(2,1)S(1)}, u32[]{:S(2)}, u32[]{:S(2)}) %collective-permute-start.9) | collective-permute-done | bytes 655392 | tf_op jit(solution)/shard_map/ppermute | solution.py:492
  89.1 0.9 copy-done.22
  90.0 2.5 %merge.1 = bf16[4096,128]{1,0:T(8,128)(2,1)} custom-call(s32[2]{0:T(128)} %copy-done.20, bf16[2560,128]{1,0:T(8,128)(2,1)} %copy-done.1, bf16[2560,128]{1,0:T(8,128)(2,1)} %copy-done.22), custom_call_target="tpu_custom_call" | custom-call | tf_op jit(solution)/shard_map/merge/pallas_call | solution.py:493
  92.6 41.2 %all_to_all.40 = bf16[16,256,128]{2,1,0:T(8,128)(2,1)S(1)} all-to-all(bf16[16,256,128]{2,1,0:T(8,128)(2,1)} %bitcast.29), channel_id=1, replica_groups=mesh['ctx'=16,'tp'=16] {'ctx'}, dimensions={0} | all-to-all | bytes 2097152 | tf_op jit(solution)/shard_map/all_to_all | solution.py:501
  133.7 0.8 reduce_sum.12
  134.5 8.4 %all-to-all-start.3 = ((bf16[16,16,128]{2,1,0:T(8,128)(2,1)}), bf16[16,16,128]{2,1,0:T(8,128)(2,1)S(1)}, u32[]{:S(2)}, u32[]{:S(2)}) async-start(bf16[16,16,128]{2,1,0:T(8,128)(2,1)} %bitcast.12), calls=%async_computation.3 | async-start | bytes 131072 | tf_op jit(solution)/shard_map/all_to_all | solution.py:506
  142.9 4.0 %copy-done = bf16[2,2560,1024]{2,1,0:T(8,128)(2,1)S(1)} copy-done((bf16[2,2560,1024]{2,1,0:T(8,128)(2,1)S(1)}, bf16[2,2560,1024]{2,1,0:T(8,128)(2,1)}, u32[]{:S(2)}) %copy-start) | copy-done | bytes 10485784
  146.9 0.7 copy-done.21
  147.6 3.2 %query_grad.1 = bf16[256,1024]{1,0:T(8,128)(2,1)} custom-call(s32[2]{0:T(128)S(1)} %copy-done.21, s32[4096]{0:T(1024)S(1)} %copy-done.16, s32[32,32]{1,0:T(8,128)S(1)} %copy-done.19, bf16[2560,256]{1,0:T(8,128)(2,1)S(1)} %get-tuple-element.20.kv_ref, bf16[2,2560,1024]{2,1,0:T(8,128)(2,1)S(1)} %copy-done), custom_call_target="tpu_custom_call" | custom-call | flops 1073741824 | bytes 12582912 | tf_op jit(solution)/shard_map/query_grad/pallas_call | solution.py:426
  150.8 0.6 copy.17
  (37 shorter events, 0.3 us)
Async XLA Ops:
  0.6 71.9 %copy-start.19 = (s32[32,32]{1,0:T(8,128)S(1)}, s32[32,32]{1,0:T(8,128)}, u32[]{:S(2)}) copy-start(s32[32,32]{1,0:T(8,128)} %allow_ref.3) | copy-start | bytes 12292
  0.6 71.9 %copy-start.16 = (s32[4096]{0:T(1024)S(1)}, s32[4096]{0:T(1024)}, u32[]{:S(2)}) copy-start(s32[4096]{0:T(1024)} %seg_ref.3) | copy-start | bytes 49156
  2.9 4.8 %collective-permute-start = (bf16[272,256]{1,0:T(8,128)(2,1)}, bf16[272,256]{1,0:T(8,128)(2,1)S(1)}, u32[]{:S(2)}, u32[]{:S(2)}) collective-permute-start(bf16[272,256]{1,0:T(8,128)(2,1)} %stage.1), channel_id=1, source_target_pairs={{0,16},{16,0},{32,48},{48,32},{64,80},{80,64},{96,112},{112,96},{1... | collective-permute-start | bytes 417800 | tf_op jit(solution)/shard_map/ppermute | solution.py:459
  8.6 10.0 %collective-permute-start.1 = (bf16[2,272,256]{2,1,0:T(8,128)(2,1)S(1)}, bf16[2,272,256]{2,1,0:T(8,128)(2,1)S(1)}, u32[]{:S(2)}, u32[]{:S(2)}) collective-permute-start(bf16[2,272,256]{2,1,0:T(8,128)(2,1)S(1)} %pad_maximum_fusion.own_ref), channel_id=1, source_target_pairs={{0,32},{1,225},{2,34},{3,227},{4,36},{5,229},{6,38},{7,231},{8,40}... | collective-permute-start | bytes 835592 | tf_op jit(solution)/shard_map/ppermute | solution.py:471
  18.6 34.5 %copy-start.6 = (bf16[2,272,256]{2,1,0:T(8,128)(2,1)}, bf16[2,272,256]{2,1,0:T(8,128)(2,1)S(1)}, u32[]{:S(2)}) copy-start(bf16[2,272,256]{2,1,0:T(8,128)(2,1)S(1)} %collective-permute-done.1.refs_0_) | copy-start | bytes 835588
  18.7 12.1 %collective-permute-start.2 = (bf16[2,272,256]{2,1,0:T(8,128)(2,1)S(1)}, bf16[2,272,256]{2,1,0:T(8,128)(2,1)S(1)}, u32[]{:S(2)}, u32[]{:S(2)}) collective-permute-start(bf16[2,272,256]{2,1,0:T(8,128)(2,1)S(1)} %collective-permute-done.1.refs_0_), channel_id=1, source_target_pairs={{0,32},{1,225},{2,34},{3,227},{4,36},{5,229},{6,38},{7,231},{8,40}... | collective-permute-start | bytes 835592 | tf_op jit(solution)/shard_map/ppermute | solution.py:472
  23.6 18.4 %all-to-all-start = ((bf16[16,16,1024]{2,0,1:T(8,128)(2,1)}), bf16[16,16,1024]{2,0,1:T(8,128)(2,1)S(1)}, u32[]{:S(2)}, u32[]{:S(2)}) async-start(bf16[16,16,1024]{2,0,1:T(8,128)(2,1)} %bitcast.24), calls=%async_computation | async-start | bytes 1048576 | tf_op jit(solution)/shard_map/all_to_all | solution.py:477
  30.7 9.1 %collective-permute-start.3 = (bf16[2,272,256]{2,1,0:T(8,128)(2,1)S(1)}, bf16[2,272,256]{2,1,0:T(8,128)(2,1)S(1)}, u32[]{:S(2)}, u32[]{:S(2)}) collective-permute-start(bf16[2,272,256]{2,1,0:T(8,128)(2,1)S(1)} %collective-permute-done.2.refs_1_), channel_id=1, source_target_pairs={{0,32},{1,225},{2,34},{3,227},{4,36},{5,229},{6,38},{7,231},{8,40}... | collective-permute-start | bytes 835592 | tf_op jit(solution)/shard_map/ppermute | solution.py:473
  33.4 6.5 %collective-permute-start.4 = (bf16[272,256]{1,0:T(8,128)(2,1)S(1)}, bf16[272,256]{1,0:T(8,128)(2,1)S(1)}, u32[]{:S(2)}, u32[]{:S(2)}) collective-permute-start(bf16[272,256]{1,0:T(8,128)(2,1)S(1)} %dynamic-slice_bitcast_fusion), channel_id=1, source_target_pairs={{0,64},{1,193},{2,66},{3,195},{4,68},{5,197},{6,70},{7,199},{8,72}... | collective-permute-start | bytes 417800 | tf_op jit(solution)/shard_map/ppermute | solution.py:475
  39.8 13.3 %copy-start.17 = (bf16[272,256]{1,0:T(8,128)(2,1)}, bf16[272,256]{1,0:T(8,128)(2,1)S(1)}, u32[]{:S(2)}) copy-start(bf16[272,256]{1,0:T(8,128)(2,1)S(1)} %collective-permute-done.4.refs_3_) | copy-start | bytes 417796
  39.9 13.3 %copy-start.8 = (bf16[2,272,256]{2,1,0:T(8,128)(2,1)}, bf16[2,272,256]{2,1,0:T(8,128)(2,1)S(1)}, u32[]{:S(2)}) copy-start(bf16[2,272,256]{2,1,0:T(8,128)(2,1)S(1)} %collective-permute-done.3.refs_2_) | copy-start | bytes 835588
  42.0 30.5 %all-to-all-start.1 = ((bf16[16,32,1024]{2,1,0:T(8,128)(2,1)}), bf16[16,32,1024]{2,1,0:T(8,128)(2,1)S(1)}, u32[]{:S(2)}, u32[]{:S(2)}) async-start(bf16[16,32,1024]{2,1,0:T(8,128)(2,1)} %bitcast.30), calls=%async_computation.1 | async-start | bytes 2097152 | tf_op jit(solution)/shard_map/all_to_all | solution.py:487
  47.9 3.9 %collective-permute-start.5 = (bf16[2,272,256]{2,1,0:T(8,128)(2,1)S(1)}, bf16[2,272,256]{2,1,0:T(8,128)(2,1)S(1)}, u32[]{:S(2)}, u32[]{:S(2)}) collective-permute-start(bf16[2,272,256]{2,1,0:T(8,128)(2,1)S(1)} %collective-permute-done.1.refs_0_), channel_id=1, source_target_pairs={{0,1},{1,0},{2,3},{3,2},{4,5},{5,4},{6,7},{7,6},{8,9},{9,8},{10,11... | collective-permute-start | bytes 835592 | tf_op jit(solution)/shard_map/ppermute | solution.py:486
  49.4 3.0 %collective-permute-start.6 = (bf16[2,272,256]{2,1,0:T(8,128)(2,1)S(1)}, bf16[2,272,256]{2,1,0:T(8,128)(2,1)S(1)}, u32[]{:S(2)}, u32[]{:S(2)}) collective-permute-start(bf16[2,272,256]{2,1,0:T(8,128)(2,1)S(1)} %collective-permute-done.2.refs_1_), channel_id=1, source_target_pairs={{0,1},{1,0},{2,3},{3,2},{4,5},{5,4},{6,7},{7,6},{8,9},{9,8},{10,11... | collective-permute-start | bytes 835592 | tf_op jit(solution)/shard_map/ppermute | solution.py:486
  49.5 3.6 %collective-permute-start.7 = (bf16[2,272,256]{2,1,0:T(8,128)(2,1)S(1)}, bf16[2,272,256]{2,1,0:T(8,128)(2,1)}, u32[]{:S(2)}, u32[]{:S(2)}) collective-permute-start(bf16[2,272,256]{2,1,0:T(8,128)(2,1)S(1)} %collective-permute-done.3.refs_2_), channel_id=1, source_target_pairs={{0,1},{1,0},{2,3},{3,2},{4,5},{5,4},{6,7},{7,6},{8,9},{9,8},{10,11... | collective-permute-start | bytes 835592 | tf_op jit(solution)/shard_map/ppermute | solution.py:486
  49.9 1.8 %collective-permute-start.8 = (bf16[272,256]{1,0:T(8,128)(2,1)S(1)}, bf16[272,256]{1,0:T(8,128)(2,1)}, u32[]{:S(2)}, u32[]{:S(2)}) collective-permute-start(bf16[272,256]{1,0:T(8,128)(2,1)S(1)} %collective-permute-done.4.refs_3_), channel_id=1, source_target_pairs={{0,1},{1,0},{2,3},{3,2},{4,5},{5,4},{6,7},{7,6},{8,9},{9,8},{10,11... | collective-permute-start | bytes 417800 | tf_op jit(solution)/shard_map/ppermute | solution.py:486
  51.8 0.7 copy-start.10
  52.5 0.7 copy-start.12
  53.2 1.0 copy-start.7
  54.2 1.0 copy-start.9
  55.1 1.0 copy-start.11
  56.1 1.0 copy-start.13
  57.0 0.9 copy-start.18
  60.2 0.8 copy-start.2
  61.0 0.8 copy-start.4
  61.8 0.7 copy-start.14
  72.5 1.0 copy-start.3
  73.6 1.0 copy-start.5
  74.6 0.9 copy-start.15
  81.3 0.8 copy-start.1
  82.2 0.5 copy-start.20
  82.7 6.4 %collective-permute-start.9 = (bf16[2560,128]{1,0:T(8,128)(2,1)S(1)}, bf16[2560,128]{1,0:T(8,128)(2,1)S(1)}, u32[]{:S(2)}, u32[]{:S(2)}) collective-permute-start(bf16[2560,128]{1,0:T(8,128)(2,1)S(1)} %get-tuple-element.26), channel_id=1, source_target_pairs={{0,1},{1,0},{2,3},{3,2},{4,5},{5,4},{6,7},{7,6},{8,9},{9,8},{10,11... | collective-permute-start | bytes 1966088 | tf_op jit(solution)/shard_map/ppermute | solution.py:492
  89.1 0.9 copy-start.22
  134.5 16.3 %all-to-all-start.3 = ((bf16[16,16,128]{2,1,0:T(8,128)(2,1)}), bf16[16,16,128]{2,1,0:T(8,128)(2,1)S(1)}, u32[]{:S(2)}, u32[]{:S(2)}) async-start(bf16[16,16,128]{2,1,0:T(8,128)(2,1)} %bitcast.12), calls=%async_computation.3 | async-start | bytes 131072 | tf_op jit(solution)/shard_map/all_to_all | solution.py:506
  142.9 4.0 %copy-start = (bf16[2,2560,1024]{2,1,0:T(8,128)(2,1)S(1)}, bf16[2,2560,1024]{2,1,0:T(8,128)(2,1)}, u32[]{:S(2)}) copy-start(bf16[2,2560,1024]{2,1,0:T(8,128)(2,1)} %get-tuple-element.28.sg_ref) | copy-start | bytes 31457284
  146.9 0.7 copy-start.21

commit v7 on v6

--- a/solution.py
+++ b/solution.py
@@ -28,6 +28,7 @@
 LOCAL_HEADS = 8
 LANES = LOCAL_HEADS * BLK
 NEG_FILL = -1e30
+VMEM_LIMIT = 60 * 2**20
 SCALE = 1.0 / math.sqrt(HEAD_SIZE)
 EXP2_SCALE = SCALE * math.log2(math.e)
 F32 = jnp.float32
@@ -82,9 +83,24 @@
         copy.wait()
 
 
-def permute_kernel(info_ref, grad_ref, own_ref, *refs):
-    mine, theirs = refs[:RING], refs[RING : 2 * RING]
-    out_ref, unpack_ref, gr_ref, gt_ref, slots_s = refs[2 * RING :]
+def fetch_all(sources, buffers, arrived):
+    copies = [
+        pltpu.make_async_copy(source, buffer, arrived.at[i])
+        for i, (source, buffer) in enumerate(zip(sources, buffers))
+    ]
+    for copy in copies:
+        copy.start()
+    return copies
+
+
+def permute_kernel(info_ref, *refs):
+    count = 2 * RING + 2
+    out_ref, unpack_ref, gr_ref, gt_ref, slots_s = refs[count : count + 5]
+    grad_ref, own_ref = refs[count + 5 : count + 7]
+    mine = refs[count + 7 : count + 7 + RING]
+    theirs = refs[count + 7 + RING : count + 7 + 2 * RING]
+    for copy in fetch_all(refs[:count], refs[count + 5 : -1], refs[-1]):
+        copy.wait()
     shard = info_ref[0]
     core = info_ref[1]
     base = jnp.maximum(shard - BACK, 0)
@@ -153,11 +169,11 @@
     seg_ref,
     allow_ref,
     segv_ref,
-    unpack_ref,
-    recv_ref,
-    gr_ref,
-    gt_ref,
-    kv_ref,
+    unpack_in,
+    recv_in,
+    gr_in,
+    gt_in,
+    kv_in,
     keep_ref,
     send_ref,
     sg_ref,
@@ -173,11 +189,23 @@
     sg_s,
     list_s,
     sent,
+    kv_ref,
+    unpack_ref,
+    recv_ref,
+    gr_ref,
+    gt_ref,
+    arrived,
 ):
     shard = info_ref[0]
     core = info_ref[1]
     base = jnp.maximum(shard - BACK, 0)
+    copies = fetch_all(
+        (kv_in, unpack_in, recv_in, gr_in, gt_in),
+        (kv_ref, unpack_ref, recv_ref, gr_ref, gt_ref),
+        arrived,
+    )
     acc_s[...] = jnp.zeros_like(acc_s)
+    copies[0].wait()
 
     def query_block(half, carry):
         qb = shard * 2 + half
@@ -215,6 +243,12 @@
             return c
 
         lax.fori_loop(count, wide * WIDE + narrow * NARROW, fill, 0)
+
+        @pl.when(half == 0)
+        def _():
+            for copy in copies[1:]:
+                copy.wait()
+
         picks = unpack_ref[block_rows(half), :]
         for pair in range(LOCAL_HEADS // 2):
             q_two = dot(picks, recv_ref[:, pair * 256 : (pair + 1) * 256])
@@ -313,10 +347,13 @@
 
 
 def query_grad_kernel(
-    info_ref, seg_ref, allow_ref, kv_ref, sg_ref, dq_ref, kt_s, dqt_s, sg_s, arrived
+    info_ref, seg_ref, allow_ref, kv_in, sg_ref, dq_ref, kt_s, dqt_s, sg_s, arrived, kv_ref, kv_sem
 ):
     shard = info_ref[0]
     base = jnp.maximum(shard - BACK, 0)
+    copy = pltpu.make_async_copy(kv_in, kv_ref, kv_sem)
+    copy.start()
+    copy.wait()
 
     def query_block(half, carry):
         def on_block(kb, count):
@@ -362,11 +399,26 @@
     lax.fori_loop(0, 2, query_block, 0)
 
 
-def merge_kernel(info_ref, keep_ref, recv_ref, out_ref):
+def merge_kernel(info_ref, keep_in, recv_in, out_ref, keep_s, recv_s, sum_s, zero_s, sems):
     base = jnp.maximum(info_ref[0] - BACK, 0)
-    out_ref[...] = jnp.zeros_like(out_ref)
+    loads = fetch_all((keep_in, recv_in), (keep_s, recv_s), sems)
+    zero_s[...] = jnp.zeros_like(zero_s)
+    stores = []
+    for i in range(SHARDS - WINDOW):
+        n = jnp.where(i < base, i, i + WINDOW)
+        rows = pl.ds(pl.multiple_of(n * TOK, TOK), TOK)
+        stores.append(pltpu.make_async_copy(zero_s, out_ref.at[rows, :], sems.at[2 + i]))
+    for store in stores:
+        store.start()
+    for load in loads:
+        load.wait()
+    sum_s[...] = (keep_s[...].astype(F32) + recv_s[...].astype(F32)).astype(BF16)
     rows = pl.ds(pl.multiple_of(base * TOK, TOK), WINDOW * TOK)
-    out_ref[rows, :] = (keep_ref[...].astype(F32) + recv_ref[...].astype(F32)).astype(BF16)
+    window = pltpu.make_async_copy(sum_s, out_ref.at[rows, :], sems.at[2 + SHARDS - WINDOW])
+    window.start()
+    for store in stores:
+        store.wait()
+    window.wait()
 
 
 VMEM = pl.BlockSpec(memory_space=pltpu.VMEM)
@@ -379,7 +431,7 @@
 def call_permute(info, grad, own, mine, theirs):
     return pl.pallas_call(
         permute_kernel,
-        in_specs=[SMEM] + [VMEM] * (2 * RING + 2),
+        in_specs=[SMEM] + [ANY] * (2 * RING + 2),
         out_specs=[VMEM] * 4,
         out_shape=[
             jax.ShapeDtypeStruct((WINDOW * TOK, 2 * HEAD_SIZE), BF16),
@@ -387,8 +439,10 @@
             jax.ShapeDtypeStruct((2, LANES, HEAD_SIZE), BF16),
             jax.ShapeDtypeStruct((2, HEAD_SIZE, LANES), BF16),
         ],
-        scratch_shapes=[pltpu.VMEM((SHARDS * SLOTS, TOK), F32)],
-        compiler_params=pltpu.CompilerParams(vmem_limit_bytes=32 * 2**20),
+        scratch_shapes=[pltpu.VMEM((SHARDS * SLOTS, TOK), F32)]
+        + [pltpu.VMEM(x.shape, x.dtype) for x in (grad, own, *mine, *theirs)]
+        + [pltpu.SemaphoreType.DMA((2 * RING + 2,))],
+        compiler_params=pltpu.CompilerParams(vmem_limit_bytes=VMEM_LIMIT),
         name="permute",
     )(info, grad, own, *mine, *theirs)
 
@@ -396,7 +450,7 @@
 def call_attention(info, segments, allow, unpack, q_recv, gr, gt, kv_window):
     return pl.pallas_call(
         attention_kernel,
-        in_specs=[SMEM, SMEM, SMEM] + [VMEM] * 6,
+        in_specs=[SMEM, SMEM, SMEM, VMEM] + [ANY] * 5,
         out_specs=[VMEM, VMEM, ANY],
         out_shape=[
             jax.ShapeDtypeStruct((WINDOW * TOK, HEAD_SIZE), BF16),
@@ -416,8 +470,10 @@
             pltpu.VMEM((3, WIDE * BLK, LANES), BF16),
             pltpu.SMEM((MOST_BLOCKS,), jnp.int32),
             pltpu.SemaphoreType.DMA((3,)),
-        ],
-        compiler_params=pltpu.CompilerParams(vmem_limit_bytes=48 * 2**20),
+        ]
+        + [pltpu.VMEM(x.shape, x.dtype) for x in (kv_window, unpack, q_recv, gr, gt)]
+        + [pltpu.SemaphoreType.DMA((5,))],
+        compiler_params=pltpu.CompilerParams(vmem_limit_bytes=VMEM_LIMIT),
         name="attention",
     )(info, segments, allow, segments.reshape(-1, BLK), unpack, q_recv, gr, gt, kv_window)
 
@@ -425,7 +481,7 @@
 def call_query_grad(info, segments, allow, kv_window, score_grad):
     return pl.pallas_call(
         query_grad_kernel,
-        in_specs=[SMEM, SMEM, SMEM, VMEM, ANY],
+        in_specs=[SMEM, SMEM, SMEM, ANY, ANY],
         out_specs=VMEM,
         out_shape=jax.ShapeDtypeStruct((TOK, LOCAL_HEADS * HEAD_SIZE), BF16),
         scratch_shapes=[
@@ -433,8 +489,10 @@
             pltpu.VMEM((HEAD_SIZE, LANES), F32),
             pltpu.VMEM((2, NARROW * BLK, LANES), BF16),
             pltpu.SemaphoreType.DMA((2,)),
+            pltpu.VMEM(kv_window.shape, BF16),
+            pltpu.SemaphoreType.DMA(()),
         ],
-        compiler_params=pltpu.CompilerParams(vmem_limit_bytes=32 * 2**20),
+        compiler_params=pltpu.CompilerParams(vmem_limit_bytes=VMEM_LIMIT),
         cost_estimate=pl.CostEstimate(
             flops=2 * TOK * 2048 * LANES, bytes_accessed=12 * 2**20, transcendentals=0
         ),
@@ -492,9 +550,15 @@
     recv = lax.ppermute(send, "tp", swap)
     part = pl.pallas_call(
         merge_kernel,
-        in_specs=[SMEM, VMEM, VMEM],
-        out_specs=VMEM,
+        in_specs=[SMEM, ANY, ANY],
+        out_specs=ANY,
         out_shape=jax.ShapeDtypeStruct((SHARDS * TOK, HEAD_SIZE), BF16),
+        scratch_shapes=[pltpu.VMEM((WINDOW * TOK, HEAD_SIZE), BF16)] * 3
+        + [
+            pltpu.VMEM((TOK, HEAD_SIZE), BF16),
+            pltpu.SemaphoreType.DMA((3 + SHARDS - WINDOW,)),
+        ],
+        compiler_params=pltpu.CompilerParams(vmem_limit_bytes=VMEM_LIMIT),
         name="merge",
     )(info, keep, recv)
     part, score_grad = lax.optimization_barrier((part, score_grad))
@@ -503,6 +567,7 @@
     )
     grad_q = call_query_grad(info, segments, allow, kv_window, score_grad)
     owned = jnp.sum(parts.astype(F32), axis=0).astype(BF16)
+    owned, grad_q = lax.optimization_barrier((owned, grad_q))
     heads = lax.all_to_all(
         owned.reshape(tp_size, TOK // tp_size, HEAD_SIZE),
         "tp",

time: 154 us -> 152 us (0.987)
  blocking collectives: 41.2 us -> 17.7 us
  waiting for transfers between devices: 24.5 us -> 47.8 us
  local copies, waits for them, and re-layouts: 20.9 us -> 5.23 us
  Pallas kernels: 18.6 us -> 28.4 us
  starting transfers between devices: 43.7 us -> 49.1 us
    all_to_all x1, blocking collectives: 41.2 us -> 17.7 us  [on_device(): lax.all_to_all(owned.reshape(tp_size, TOK // tp_size, HEAD_SIZE), 'tp', s...]
    all_to_all x1, waiting for transfers between devices: 0.01 us -> 19.1 us  [on_device(): lax.all_to_all(part.reshape(SHARDS, TOK, HEAD_SIZE), 'ctx', split_axis=0,...]
    unnamed x46 -> x22, local copies, waits for them, and re-layouts: 18.4 us -> 2.7 us
    pallas_call x4, Pallas kernels: 13.8 us -> 23.5 us  [the longest x1 8.68 us: call_attention(): pl.pallas_call(attention_kernel, in_specs=[SMEM, SMEM, SMEM, VMEM] + [ANY...]
    all_to_all x1, starting transfers between devices: 8.45 us -> 13.6 us  [on_device(): lax.all_to_all(part.reshape(SHARDS, TOK, HEAD_SIZE), 'ctx', split_axis=0,...]
    all_to_all x1, waiting for transfers between devices: 10 us -> 14.4 us  [on_device(): lax.all_to_all(q_send, 'ctx', split_axis=0, concat_axis=0, tiled=True)]
  transfers between devices with their start and end apart: 13 -> 13, of which waited for: 7 -> 8; matrix products, arithmetic and copies ran while one was open for 1% -> 2% of each run, Pallas kernels for 5% -> 10%
where the time goes in v7:
time: 152 us; the launch traced here: 151 us
  starting transfers between devices  49.1 us (32%)
  waiting for transfers between devices  47.8 us (31%)
  Pallas kernels  28.4 us (19%)
  blocking collectives  17.7 us (12%)
  local copies, waits for them, and re-layouts  5.23 us (3%)
  other arithmetic  1.64 us (1%)
    all_to_all x1, waiting for transfers between devices, on_device(): lax.all_to_all(part.reshape(SHARDS, TOK, HEAD_SIZE), 'ctx', split_axis=0,...  19.1 us
    all_to_all x1, blocking collectives, on_device(): lax.all_to_all(owned.reshape(tp_size, TOK // tp_size, HEAD_SIZE), 'tp', s...  17.7 us
    all_to_all x1, waiting for transfers between devices, on_device(): lax.all_to_all(q_send, 'ctx', split_axis=0, concat_axis=0, tiled=True)  14.4 us
    all_to_all x1, starting transfers between devices, on_device(): lax.all_to_all(part.reshape(SHARDS, TOK, HEAD_SIZE), 'ctx', split_axis=0,...  13.6 us
    pallas_call x1, Pallas kernels, call_attention(): pl.pallas_call(attention_kernel, in_specs=[SMEM, SMEM, SMEM, VMEM] + [ANY...  8.68 us
    all_to_all x1, starting transfers between devices, on_device(): lax.all_to_all(out_grad, 'tp', split_axis=1, concat_axis=0, tiled=True)  7.06 us
    pallas_call x1, Pallas kernels, call_query_grad(): pl.pallas_call(query_grad_kernel, in_specs=[SMEM, SMEM, SMEM, ANY, ANY],...  6.54 us
    ppermute x1, starting transfers between devices, on_device(): first = lax.ppermute(own, ('ctx', 'tp'), around(1))  6.54 us
  transfers between devices with their start and end apart: 13, of which 8 were waited for; matrix products, arithmetic and copies ran while one was open for 2% of the time, Pallas kernels for 10%

profile of v7, /device:TPU:1, one launch (start us, length us, event | category | flops | bytes accessed | tf_op | source)
XLA Modules:
  0.0 150.6 jit_solution(9596963595293564479)
XLA Ops:
  0.6 2.2 %stage.1 = bf16[272,256]{1,0:T(8,128)(2,1)} custom-call(s32[1,256]{1,0:T(1,128)} %bitcast.37, bf16[2,256,1024]{2,1,0:T(8,128)(2,1)} %kv_ref.1), custom_call_target="tpu_custom_call" | custom-call | tf_op jit(solution)/shard_map/stage/pallas_call | solution.py:509
  2.9 2.1 %collective-permute-start = (bf16[272,256]{1,0:T(8,128)(2,1)}, bf16[272,256]{1,0:T(8,128)(2,1)S(1)}, u32[]{:S(2)}, u32[]{:S(2)}) collective-permute-start(bf16[272,256]{1,0:T(8,128)(2,1)} %stage.1), channel_id=1, source_target_pairs={{0,16},{16,0},{32,48},{48,32},{64,80},{80,64},{96,112},{112,96},{1... | collective-permute-start | bytes 417800 | tf_op jit(solution)/shard_map/ppermute | solution.py:517
  5.0 2.7 %collective-permute-done = bf16[272,256]{1,0:T(8,128)(2,1)S(1)} collective-permute-done((bf16[272,256]{1,0:T(8,128)(2,1)}, bf16[272,256]{1,0:T(8,128)(2,1)S(1)}, u32[]{:S(2)}, u32[]{:S(2)}) %collective-permute-start) | collective-permute-done | bytes 139296 | tf_op jit(solution)/shard_map/ppermute | solution.py:517
  7.7 0.9 pad_maximum_fusion.refs_1_
  8.6 0.0 copy-start.2
  8.6 6.5 %collective-permute-start.1 = (bf16[2,272,256]{2,1,0:T(8,128)(2,1)S(1)}, bf16[2,272,256]{2,1,0:T(8,128)(2,1)S(1)}, u32[]{:S(2)}, u32[]{:S(2)}) collective-permute-start(bf16[2,272,256]{2,1,0:T(8,128)(2,1)S(1)} %pad_maximum_fusion.refs_1_), channel_id=1, source_target_pairs={{0,32},{1,225},{2,34},{3,227},{4,36},{5,229},{6,38},{7,231},{8,40}... | collective-permute-start | bytes 835592 | tf_op jit(solution)/shard_map/ppermute | solution.py:529
  15.1 3.5 %collective-permute-done.1.refs_2_ = bf16[2,272,256]{2,1,0:T(8,128)(2,1)S(1)} collective-permute-done((bf16[2,272,256]{2,1,0:T(8,128)(2,1)S(1)}, bf16[2,272,256]{2,1,0:T(8,128)(2,1)S(1)}, u32[]{:S(2)}, u32[]{:S(2)}) %collective-permute-start.1) | collective-permute-done | bytes 278560 | tf_op jit(solution)/shard_map/ppermute | solution.py:529
  18.6 3.1 %collective-permute-start.2 = (bf16[2,272,256]{2,1,0:T(8,128)(2,1)S(1)}, bf16[2,272,256]{2,1,0:T(8,128)(2,1)S(1)}, u32[]{:S(2)}, u32[]{:S(2)}) collective-permute-start(bf16[2,272,256]{2,1,0:T(8,128)(2,1)S(1)} %collective-permute-done.1.refs_2_), channel_id=1, source_target_pairs={{0,32},{1,225},{2,34},{3,227},{4,36},{5,229},{6,38},{7,231},{8,40}... | collective-permute-start | bytes 835592 | tf_op jit(solution)/shard_map/ppermute | solution.py:530
  21.7 1.9 %copy.16 = bf16[2,16,8,1024]{3,2,0,1:T(8,128)(2,1)} copy(bf16[2,16,8,1024]{3,2,1,0:T(8,128)(2,1)} %bitcast.31) | data formatting | bytes 1048576 | tf_op jit(solution)/shard_map/all_to_all | solution.py:535
  23.6 7.1 %all-to-all-start = ((bf16[16,16,1024]{2,0,1:T(8,128)(2,1)}), bf16[16,16,1024]{2,0,1:T(8,128)(2,1)S(1)}, u32[]{:S(2)}, u32[]{:S(2)}) async-start(bf16[16,16,1024]{2,0,1:T(8,128)(2,1)} %bitcast.24), calls=%async_computation | async-start | bytes 1048576 | tf_op jit(solution)/shard_map/all_to_all | solution.py:535
  30.7 0.0 collective-permute-done.2.refs_3_
  30.7 0.0 copy-start.4
  30.7 2.7 %collective-permute-start.3 = (bf16[2,272,256]{2,1,0:T(8,128)(2,1)S(1)}, bf16[2,272,256]{2,1,0:T(8,128)(2,1)S(1)}, u32[]{:S(2)}, u32[]{:S(2)}) collective-permute-start(bf16[2,272,256]{2,1,0:T(8,128)(2,1)S(1)} %collective-permute-done.2.refs_3_), channel_id=1, source_target_pairs={{0,32},{1,225},{2,34},{3,227},{4,36},{5,229},{6,38},{7,231},{8,40}... | collective-permute-start | bytes 835592 | tf_op jit(solution)/shard_map/ppermute | solution.py:531
  33.4 1.1 collective-permute-start.4
  34.4 2.7 %pack.1 = bf16[512,1024]{1,0:T(8,128)(2,1)} custom-call(s32[1,256]{1,0:T(1,128)} %bitcast.38, bf16[256,1024]{1,0:T(8,128)(2,1)} %rows_ref.1), custom_call_target="tpu_custom_call" | custom-call | tf_op jit(solution)/shard_map/pack/pallas_call | solution.py:536
  37.1 2.7 %collective-permute-done.4.refs_5_ = bf16[272,256]{1,0:T(8,128)(2,1)S(1)} collective-permute-done((bf16[272,256]{1,0:T(8,128)(2,1)S(1)}, bf16[272,256]{1,0:T(8,128)(2,1)S(1)}, u32[]{:S(2)}, u32[]{:S(2)}) %collective-permute-start.4) | collective-permute-done | bytes 139296 | tf_op jit(solution)/shard_map/ppermute | solution.py:533
  39.8 0.0 collective-permute-done.3.refs_4_
  39.8 2.1 %all-to-all-done = bf16[16,16,1024]{2,0,1:T(8,128)(2,1)S(1)} async-done(((bf16[16,16,1024]{2,0,1:T(8,128)(2,1)}), bf16[16,16,1024]{2,0,1:T(8,128)(2,1)S(1)}, u32[]{:S(2)}, u32[]{:S(2)}) %all-to-all-start) | async-done | bytes 524320 | tf_op jit(solution)/shard_map/all_to_all | solution.py:535
  42.0 0.0 copy-done.10
  42.0 5.9 %all-to-all-start.1 = ((bf16[16,32,1024]{2,1,0:T(8,128)(2,1)}), bf16[16,32,1024]{2,1,0:T(8,128)(2,1)S(1)}, u32[]{:S(2)}, u32[]{:S(2)}) async-start(bf16[16,32,1024]{2,1,0:T(8,128)(2,1)} %bitcast.27), calls=%async_computation.1 | async-start | bytes 2097152 | tf_op jit(solution)/shard_map/all_to_all | solution.py:545
  47.9 1.6 %collective-permute-start.5 = (bf16[2,272,256]{2,1,0:T(8,128)(2,1)S(1)}, bf16[2,272,256]{2,1,0:T(8,128)(2,1)S(1)}, u32[]{:S(2)}, u32[]{:S(2)}) collective-permute-start(bf16[2,272,256]{2,1,0:T(8,128)(2,1)S(1)} %collective-permute-done.1.refs_2_), channel_id=1, source_target_pairs={{0,1},{1,0},{2,3},{3,2},{4,5},{5,4},{6,7},{7,6},{8,9},{9,8},{10,11... | collective-permute-start | bytes 835592 | tf_op jit(solution)/shard_map/ppermute | solution.py:544
  49.5 0.1 collective-permute-start.6
  49.6 0.4 collective-permute-start.7
  50.0 0.1 collective-permute-start.8
  50.1 0.6 pad_add_fusion.info_ref
  50.6 1.3 collective-permute-done.8.refs_9_
  52.0 0.0 collective-permute-done.5.refs_6_
  52.0 0.0 collective-permute-done.6.refs_7_
  52.0 0.0 copy-start.8
  52.0 0.0 collective-permute-done.7.refs_8_
  52.0 0.0 copy-start.9
  52.0 0.6 copy-done.7
  52.7 0.1 copy-done.8
  52.8 0.1 copy-done.9
  52.9 5.2 %permute.1 = (bf16[2560,256]{1,0:T(8,128)(2,1)}, bf16[256,512]{1,0:T(8,128)(2,1)}, bf16[2,1024,128]{2,1,0:T(8,128)(2,1)}, bf16[2,128,1024]{2,1,0:T(8,128)(2,1)}) custom-call(s32[2]{0:T(128)} %pad_add_fusion.info_ref, bf16[256,1024]{1,0:T(8,128)(2,1)} %bitcast.29, bf16[2,272,256]{2,1,0:T(8,128)(2,1)} %copy-done.2, bf16[2,272,256]{2,1,0:T(8,128)(2,1)} %copy-done.5, ...), custom_call_target="tpu_custom_call" | custom-call | tf_op jit(solution)/shard_map/permute/pallas_call | solution.py:432
  58.0 14.4 %all-to-all-done.1 = bf16[16,32,1024]{2,1,0:T(8,128)(2,1)S(1)} async-done(((bf16[16,32,1024]{2,1,0:T(8,128)(2,1)}), bf16[16,32,1024]{2,1,0:T(8,128)(2,1)S(1)}, u32[]{:S(2)}, u32[]{:S(2)}) %all-to-all-start.1) | async-done | bytes 1048608 | tf_op jit(solution)/shard_map/all_to_all | solution.py:545
  72.4 1.0 copy-done
  73.5 8.7 %attention.1 = (bf16[2560,128]{1,0:T(8,128)(2,1)}, bf16[2560,128]{1,0:T(8,128)(2,1)}, bf16[2,2560,1024]{2,1,0:T(8,128)(2,1)}) custom-call(s32[2]{0:T(128)} %pad_add_fusion.info_ref, s32[4096]{0:T(1024)} %seg_ref.3, s32[32,32]{1,0:T(8,128)} %allow_ref.3, s32[32,128]{1,0:T(8,128)} %bitcast.34, bf16[256,512]{1,0:T(8,128)(2,1)} %get-tuple-element.22.unpack_in, ...), custom_call_target="tpu_custom_call" | custom-call | tf_op jit(solution)/shard_map/attention/pallas_call | solution.py:451
  82.1 4.8 %collective-permute-start.9 = (bf16[2560,128]{1,0:T(8,128)(2,1)}, bf16[2560,128]{1,0:T(8,128)(2,1)S(1)}, u32[]{:S(2)}, u32[]{:S(2)}) collective-permute-start(bf16[2560,128]{1,0:T(8,128)(2,1)} %get-tuple-element.28), channel_id=1, source_target_pairs={{0,1},{1,0},{2,3},{3,2},{4,5},{5,4},{6,7},{7,6},{8,9},{9,8},{10,11... | collective-permute-start | bytes 1966088 | tf_op jit(solution)/shard_map/ppermute | solution.py:550
  87.0 1.9 %collective-permute-done.9.recv_in = bf16[2560,128]{1,0:T(8,128)(2,1)S(1)} collective-permute-done((bf16[2560,128]{1,0:T(8,128)(2,1)}, bf16[2560,128]{1,0:T(8,128)(2,1)S(1)}, u32[]{:S(2)}, u32[]{:S(2)}) %collective-permute-start.9) | collective-permute-done | bytes 655392 | tf_op jit(solution)/shard_map/ppermute | solution.py:550
  88.9 0.8 copy-done.3
  89.7 3.2 %merge.1 = bf16[4096,128]{1,0:T(8,128)(2,1)} custom-call(s32[2]{0:T(128)} %pad_add_fusion.info_ref, bf16[2560,128]{1,0:T(8,128)(2,1)} %get-tuple-element.27.keep_in, bf16[2560,128]{1,0:T(8,128)(2,1)} %copy-done.3), custom_call_target="tpu_custom_call" | custom-call | tf_op jit(solution)/shard_map/merge/pallas_call | solution.py:551
  92.9 13.6 %all-to-all-start.2 = ((bf16[16,256,128]{2,1,0:T(8,128)(2,1)}), bf16[16,256,128]{2,1,0:T(8,128)(2,1)S(1)}, u32[]{:S(2)}, u32[]{:S(2)}) async-start(bf16[16,256,128]{2,1,0:T(8,128)(2,1)} %bitcast.26), calls=%async_computation.2 | async-start | bytes 2097152 | tf_op jit(solution)/shard_map/all_to_all | solution.py:565
  106.5 6.5 %query_grad.1 = bf16[256,1024]{1,0:T(8,128)(2,1)} custom-call(s32[2]{0:T(128)} %pad_add_fusion.info_ref, s32[4096]{0:T(1024)} %seg_ref.3, s32[32,32]{1,0:T(8,128)} %allow_ref.3, bf16[2560,256]{1,0:T(8,128)(2,1)} %get-tuple-element.26.kv_in, bf16[2,2560,1024]{2,1,0:T(8,128)(2,1)} %get-tuple-element.31.sg_ref), custom_call_target="tpu_custom_call" | custom-call | flops 1073741824 | bytes 12582912 | tf_op jit(solution)/shard_map/query_grad/pallas_call | solution.py:482
  113.1 19.1 %all-to-all-done.2 = bf16[16,256,128]{2,1,0:T(8,128)(2,1)S(1)} async-done(((bf16[16,256,128]{2,1,0:T(8,128)(2,1)}), bf16[16,256,128]{2,1,0:T(8,128)(2,1)S(1)}, u32[]{:S(2)}, u32[]{:S(2)}) %all-to-all-start.2) | async-done | bytes 1048608 | tf_op jit(solution)/shard_map/all_to_all | solution.py:565
  132.2 0.1 reduce_sum.12
  132.4 17.7 %all_to_all.40 = bf16[16,16,128]{2,1,0:T(8,128)(2,1)S(1)} all-to-all(bf16[16,16,128]{2,1,0:T(8,128)(2,1)S(1)} %bitcast.32), channel_id=1, replica_groups=mesh['ctx'=16,'tp'=16] {'tp'}, dimensions={0} | all-to-all | bytes 131072 | tf_op jit(solution)/shard_map/all_to_all | solution.py:571
  150.0 0.6 copy.17
  (13 shorter events, 0.0 us)
Async XLA Ops:
  2.9 4.8 %collective-permute-start = (bf16[272,256]{1,0:T(8,128)(2,1)}, bf16[272,256]{1,0:T(8,128)(2,1)S(1)}, u32[]{:S(2)}, u32[]{:S(2)}) collective-permute-start(bf16[272,256]{1,0:T(8,128)(2,1)} %stage.1), channel_id=1, source_target_pairs={{0,16},{16,0},{32,48},{48,32},{64,80},{80,64},{96,112},{112,96},{1... | collective-permute-start | bytes 417800 | tf_op jit(solution)/shard_map/ppermute | solution.py:517
  8.6 43.4 %copy-start.2 = (bf16[2,272,256]{2,1,0:T(8,128)(2,1)}, bf16[2,272,256]{2,1,0:T(8,128)(2,1)S(1)}, u32[]{:S(2)}) copy-start(bf16[2,272,256]{2,1,0:T(8,128)(2,1)S(1)} %pad_maximum_fusion.refs_1_) | copy-start | bytes 835588
  8.6 10.0 %collective-permute-start.1 = (bf16[2,272,256]{2,1,0:T(8,128)(2,1)S(1)}, bf16[2,272,256]{2,1,0:T(8,128)(2,1)S(1)}, u32[]{:S(2)}, u32[]{:S(2)}) collective-permute-start(bf16[2,272,256]{2,1,0:T(8,128)(2,1)S(1)} %pad_maximum_fusion.refs_1_), channel_id=1, source_target_pairs={{0,32},{1,225},{2,34},{3,227},{4,36},{5,229},{6,38},{7,231},{8,40}... | collective-permute-start | bytes 835592 | tf_op jit(solution)/shard_map/ppermute | solution.py:529
  18.6 33.4 %copy-start.5 = (bf16[2,272,256]{2,1,0:T(8,128)(2,1)}, bf16[2,272,256]{2,1,0:T(8,128)(2,1)S(1)}, u32[]{:S(2)}) copy-start(bf16[2,272,256]{2,1,0:T(8,128)(2,1)S(1)} %collective-permute-done.1.refs_2_) | copy-start | bytes 835588
  18.6 12.1 %collective-permute-start.2 = (bf16[2,272,256]{2,1,0:T(8,128)(2,1)S(1)}, bf16[2,272,256]{2,1,0:T(8,128)(2,1)S(1)}, u32[]{:S(2)}, u32[]{:S(2)}) collective-permute-start(bf16[2,272,256]{2,1,0:T(8,128)(2,1)S(1)} %collective-permute-done.1.refs_2_), channel_id=1, source_target_pairs={{0,32},{1,225},{2,34},{3,227},{4,36},{5,229},{6,38},{7,231},{8,40}... | collective-permute-start | bytes 835592 | tf_op jit(solution)/shard_map/ppermute | solution.py:530
  23.6 18.4 %all-to-all-start = ((bf16[16,16,1024]{2,0,1:T(8,128)(2,1)}), bf16[16,16,1024]{2,0,1:T(8,128)(2,1)S(1)}, u32[]{:S(2)}, u32[]{:S(2)}) async-start(bf16[16,16,1024]{2,0,1:T(8,128)(2,1)} %bitcast.24), calls=%async_computation | async-start | bytes 1048576 | tf_op jit(solution)/shard_map/all_to_all | solution.py:535
  30.7 21.3 %copy-start.4 = (bf16[2,272,256]{2,1,0:T(8,128)(2,1)}, bf16[2,272,256]{2,1,0:T(8,128)(2,1)S(1)}, u32[]{:S(2)}) copy-start(bf16[2,272,256]{2,1,0:T(8,128)(2,1)S(1)} %collective-permute-done.2.refs_3_) | copy-start | bytes 835588
  30.7 9.1 %collective-permute-start.3 = (bf16[2,272,256]{2,1,0:T(8,128)(2,1)S(1)}, bf16[2,272,256]{2,1,0:T(8,128)(2,1)S(1)}, u32[]{:S(2)}, u32[]{:S(2)}) collective-permute-start(bf16[2,272,256]{2,1,0:T(8,128)(2,1)S(1)} %collective-permute-done.2.refs_3_), channel_id=1, source_target_pairs={{0,32},{1,225},{2,34},{3,227},{4,36},{5,229},{6,38},{7,231},{8,40}... | collective-permute-start | bytes 835592 | tf_op jit(solution)/shard_map/ppermute | solution.py:531
  33.4 6.5 %collective-permute-start.4 = (bf16[272,256]{1,0:T(8,128)(2,1)S(1)}, bf16[272,256]{1,0:T(8,128)(2,1)S(1)}, u32[]{:S(2)}, u32[]{:S(2)}) collective-permute-start(bf16[272,256]{1,0:T(8,128)(2,1)S(1)} %dynamic-slice_bitcast_fusion), channel_id=1, source_target_pairs={{0,64},{1,193},{2,66},{3,195},{4,68},{5,197},{6,70},{7,199},{8,72}... | collective-permute-start | bytes 417800 | tf_op jit(solution)/shard_map/ppermute | solution.py:533
  39.8 2.1 %copy-start.10 = (bf16[272,256]{1,0:T(8,128)(2,1)}, bf16[272,256]{1,0:T(8,128)(2,1)S(1)}, u32[]{:S(2)}) copy-start(bf16[272,256]{1,0:T(8,128)(2,1)S(1)} %collective-permute-done.4.refs_5_) | copy-start | bytes 417796
  39.8 12.2 %copy-start.6 = (bf16[2,272,256]{2,1,0:T(8,128)(2,1)}, bf16[2,272,256]{2,1,0:T(8,128)(2,1)S(1)}, u32[]{:S(2)}) copy-start(bf16[2,272,256]{2,1,0:T(8,128)(2,1)S(1)} %collective-permute-done.3.refs_4_) | copy-start | bytes 835588
  42.0 10.1 %copy-start.1 = (bf16[16,16,1024]{2,0,1:T(8,128)(2,1)}, bf16[16,16,1024]{2,0,1:T(8,128)(2,1)S(1)}, u32[]{:S(2)}) copy-start(bf16[16,16,1024]{2,0,1:T(8,128)(2,1)S(1)} %all-to-all-done) | copy-start | bytes 1572868
  42.0 30.5 %all-to-all-start.1 = ((bf16[16,32,1024]{2,1,0:T(8,128)(2,1)}), bf16[16,32,1024]{2,1,0:T(8,128)(2,1)S(1)}, u32[]{:S(2)}, u32[]{:S(2)}) async-start(bf16[16,32,1024]{2,1,0:T(8,128)(2,1)} %bitcast.27), calls=%async_computation.1 | async-start | bytes 2097152 | tf_op jit(solution)/shard_map/all_to_all | solution.py:545
  47.9 4.1 %collective-permute-start.5 = (bf16[2,272,256]{2,1,0:T(8,128)(2,1)S(1)}, bf16[2,272,256]{2,1,0:T(8,128)(2,1)S(1)}, u32[]{:S(2)}, u32[]{:S(2)}) collective-permute-start(bf16[2,272,256]{2,1,0:T(8,128)(2,1)S(1)} %collective-permute-done.1.refs_2_), channel_id=1, source_target_pairs={{0,1},{1,0},{2,3},{3,2},{4,5},{5,4},{6,7},{7,6},{8,9},{9,8},{10,11... | collective-permute-start | bytes 835592 | tf_op jit(solution)/shard_map/ppermute | solution.py:544
  49.5 2.5 %collective-permute-start.6 = (bf16[2,272,256]{2,1,0:T(8,128)(2,1)S(1)}, bf16[2,272,256]{2,1,0:T(8,128)(2,1)S(1)}, u32[]{:S(2)}, u32[]{:S(2)}) collective-permute-start(bf16[2,272,256]{2,1,0:T(8,128)(2,1)S(1)} %collective-permute-done.2.refs_3_), channel_id=1, source_target_pairs={{0,1},{1,0},{2,3},{3,2},{4,5},{5,4},{6,7},{7,6},{8,9},{9,8},{10,11... | collective-permute-start | bytes 835592 | tf_op jit(solution)/shard_map/ppermute | solution.py:544
  49.6 2.4 %collective-permute-start.7 = (bf16[2,272,256]{2,1,0:T(8,128)(2,1)S(1)}, bf16[2,272,256]{2,1,0:T(8,128)(2,1)S(1)}, u32[]{:S(2)}, u32[]{:S(2)}) collective-permute-start(bf16[2,272,256]{2,1,0:T(8,128)(2,1)S(1)} %collective-permute-done.3.refs_4_), channel_id=1, source_target_pairs={{0,1},{1,0},{2,3},{3,2},{4,5},{5,4},{6,7},{7,6},{8,9},{9,8},{10,11... | collective-permute-start | bytes 835592 | tf_op jit(solution)/shard_map/ppermute | solution.py:544
  50.0 2.0 %collective-permute-start.8 = (bf16[272,256]{1,0:T(8,128)(2,1)}, bf16[272,256]{1,0:T(8,128)(2,1)}, u32[]{:S(2)}, u32[]{:S(2)}) collective-permute-start(bf16[272,256]{1,0:T(8,128)(2,1)} %copy-done.10), channel_id=1, source_target_pairs={{0,1},{1,0},{2,3},{3,2},{4,5},{5,4},{6,7},{7,6},{8,9},{9,8},{10,11... | collective-permute-start | bytes 417800 | tf_op jit(solution)/shard_map/ppermute | solution.py:544
  52.0 0.7 copy-start.7
  52.0 0.8 copy-start.8
  52.0 0.9 copy-start.9
  72.4 1.0 copy-start
  82.1 6.8 %collective-permute-start.9 = (bf16[2560,128]{1,0:T(8,128)(2,1)}, bf16[2560,128]{1,0:T(8,128)(2,1)S(1)}, u32[]{:S(2)}, u32[]{:S(2)}) collective-permute-start(bf16[2560,128]{1,0:T(8,128)(2,1)} %get-tuple-element.28), channel_id=1, source_target_pairs={{0,1},{1,0},{2,3},{3,2},{4,5},{5,4},{6,7},{7,6},{8,9},{9,8},{10,11... | collective-permute-start | bytes 1966088 | tf_op jit(solution)/shard_map/ppermute | solution.py:550
  88.9 0.8 copy-start.3
  92.9 39.3 %all-to-all-start.2 = ((bf16[16,256,128]{2,1,0:T(8,128)(2,1)}), bf16[16,256,128]{2,1,0:T(8,128)(2,1)S(1)}, u32[]{:S(2)}, u32[]{:S(2)}) async-start(bf16[16,256,128]{2,1,0:T(8,128)(2,1)} %bitcast.26), calls=%async_computation.2 | async-start | bytes 2097152 | tf_op jit(solution)/shard_map/all_to_all | solution.py:565

commit v8 on v7

--- a/solution.py
+++ b/solution.py
@@ -6,6 +6,7 @@
 from jax import lax
 from jax.experimental import pallas as pl
 from jax.experimental.pallas import tpu as pltpu
+from jax.sharding import Mesh
 from jax.sharding import PartitionSpec as P
 
 QUERY_HEAD_COUNT = 128
@@ -158,6 +159,11 @@
     wide = (count + 1) // WIDE
     narrow = (count + WIDE - 1) // WIDE - wide
     return count, wide, narrow
+
+
+def parity_block(kb):
+    shard = kb // 2
+    return ((shard % 2) * Z_CHIPS + shard // 2) * 2 + kb % 2
 
 
 def block_rows(n, blocks=1):
@@ -213,7 +219,7 @@
         q_last = seg_ref[qb * BLK + BLK - 1]
 
         def on_block(kb, count):
-            list_s[count] = kb - 2 * base
+            list_s[count] = parity_block(kb)
             src = block_rows(kb - 2 * base)
             dst = block_rows(count)
             k_s[dst, :] = kv_ref[src, :HEAD_SIZE]
@@ -235,7 +241,7 @@
         count, wide, narrow = visible_blocks(qb, seg_ref, allow_ref, on_block)
 
         def fill(n, c):
-            list_s[n] = 2 * WINDOW
+            list_s[n] = 2 * SHARDS
             dst = block_rows(n)
             k_s[dst, :] = jnp.zeros((BLK, HEAD_SIZE), BF16)
             v_s[dst, :] = jnp.zeros((BLK, HEAD_SIZE), BF16)
@@ -333,7 +339,7 @@
         return carry
 
     lax.fori_loop(0, 2, query_block, 0)
-    rows = slice(0, WINDOW * TOK)
+    rows = slice(0, SHARDS * TOK)
 
     @pl.when(core == 0)
     def _():
@@ -399,39 +405,18 @@
     lax.fori_loop(0, 2, query_block, 0)
 
 
-def merge_kernel(info_ref, keep_in, recv_in, out_ref, keep_s, recv_s, sum_s, zero_s, sems):
-    base = jnp.maximum(info_ref[0] - BACK, 0)
-    loads = fetch_all((keep_in, recv_in), (keep_s, recv_s), sems)
-    zero_s[...] = jnp.zeros_like(zero_s)
-    stores = []
-    for i in range(SHARDS - WINDOW):
-        n = jnp.where(i < base, i, i + WINDOW)
-        rows = pl.ds(pl.multiple_of(n * TOK, TOK), TOK)
-        stores.append(pltpu.make_async_copy(zero_s, out_ref.at[rows, :], sems.at[2 + i]))
-    for store in stores:
-        store.start()
-    for load in loads:
-        load.wait()
-    sum_s[...] = (keep_s[...].astype(F32) + recv_s[...].astype(F32)).astype(BF16)
-    rows = pl.ds(pl.multiple_of(base * TOK, TOK), WINDOW * TOK)
-    window = pltpu.make_async_copy(sum_s, out_ref.at[rows, :], sems.at[2 + SHARDS - WINDOW])
-    window.start()
-    for store in stores:
-        store.wait()
-    window.wait()
-
-
 VMEM = pl.BlockSpec(memory_space=pltpu.VMEM)
 SMEM = pl.BlockSpec(memory_space=pltpu.SMEM)
 
 
 ANY = pl.BlockSpec(memory_space=pl.ANY)
+HBM = pl.BlockSpec(memory_space=pltpu.HBM)
 
 
 def call_permute(info, grad, own, mine, theirs):
     return pl.pallas_call(
         permute_kernel,
-        in_specs=[SMEM] + [ANY] * (2 * RING + 2),
+        in_specs=[SMEM] + [HBM] * (2 * RING + 2),
         out_specs=[VMEM] * 4,
         out_shape=[
             jax.ShapeDtypeStruct((WINDOW * TOK, 2 * HEAD_SIZE), BF16),
@@ -450,11 +435,11 @@
 def call_attention(info, segments, allow, unpack, q_recv, gr, gt, kv_window):
     return pl.pallas_call(
         attention_kernel,
-        in_specs=[SMEM, SMEM, SMEM, VMEM] + [ANY] * 5,
-        out_specs=[VMEM, VMEM, ANY],
+        in_specs=[SMEM, SMEM, SMEM, VMEM] + [HBM] * 5,
+        out_specs=[VMEM, VMEM, HBM],
         out_shape=[
-            jax.ShapeDtypeStruct((WINDOW * TOK, HEAD_SIZE), BF16),
-            jax.ShapeDtypeStruct((WINDOW * TOK, HEAD_SIZE), BF16),
+            jax.ShapeDtypeStruct((SHARDS * TOK, HEAD_SIZE), BF16),
+            jax.ShapeDtypeStruct((SHARDS * TOK, HEAD_SIZE), BF16),
             jax.ShapeDtypeStruct((2, MOST_BLOCKS * BLK, LANES), BF16),
         ],
         scratch_shapes=[
@@ -466,7 +451,7 @@
             pltpu.VMEM((MOST_BLOCKS * BLK, LANES), F32),
             pltpu.VMEM((MOST_BLOCKS * BLK, LANES), F32),
             pltpu.VMEM((MOST_BLOCKS // WIDE + 1, 1, LANES), F32),
-            pltpu.VMEM((2, WINDOW * TOK + BLK, HEAD_SIZE), F32),
+            pltpu.VMEM((2, SHARDS * TOK + BLK, HEAD_SIZE), F32),
             pltpu.VMEM((3, WIDE * BLK, LANES), BF16),
             pltpu.SMEM((MOST_BLOCKS,), jnp.int32),
             pltpu.SemaphoreType.DMA((3,)),
@@ -481,7 +466,7 @@
 def call_query_grad(info, segments, allow, kv_window, score_grad):
     return pl.pallas_call(
         query_grad_kernel,
-        in_specs=[SMEM, SMEM, SMEM, ANY, ANY],
+        in_specs=[SMEM, SMEM, SMEM, HBM, HBM],
         out_specs=VMEM,
         out_shape=jax.ShapeDtypeStruct((TOK, LOCAL_HEADS * HEAD_SIZE), BF16),
         scratch_shapes=[
@@ -502,7 +487,7 @@
 
 def on_device(queries, keys_values, out_grad, place, segments, allow):
     tp_index = lax.axis_index("tp")
-    ctx_index = lax.axis_index("ctx")
+    ctx_index = lax.axis_index(("z", "x"))
     tp_size = lax.axis_size("tp")
     width = LOCAL_HEADS * HEAD_SIZE
     info = jnp.stack([ctx_index, tp_index % 2]).astype(jnp.int32)
@@ -514,7 +499,7 @@
         scratch_shapes=[pltpu.SemaphoreType.DMA((2,))],
         name="stage",
     )(place.reshape(1, TOK), keys_values)
-    beside = lax.ppermute(staged, "ctx", [(k, k ^ 1) for k in range(SHARDS)])
+    beside = lax.ppermute(staged, "x", [(0, 1), (1, 0)])
     own = jnp.stack([staged, beside])
 
     def around(hops):
@@ -526,11 +511,11 @@
         return pairs
 
     swap = [(k, k ^ 1) for k in range(tp_size)]
-    first = lax.ppermute(own, ("ctx", "tp"), around(1))
-    second = lax.ppermute(first, ("ctx", "tp"), around(1))
-    third = lax.ppermute(second, ("ctx", "tp"), around(1))
+    first = lax.ppermute(own, ("z", "x", "tp"), around(1))
+    second = lax.ppermute(first, ("z", "x", "tp"), around(1))
+    third = lax.ppermute(second, ("z", "x", "tp"), around(1))
     half = lax.dynamic_index_in_dim(second, tp_index % 2, 0, keepdims=False)
-    fourth = lax.ppermute(half, ("ctx", "tp"), around(2))
+    fourth = lax.ppermute(half, ("z", "x", "tp"), around(2))
     mine = [first, second, third, fourth]
     g_local = lax.all_to_all(out_grad, "tp", split_axis=1, concat_axis=0, tiled=True)
     q_send = pl.pallas_call(
@@ -542,29 +527,26 @@
     )(place.reshape(1, TOK), queries)
     q_send, *mine = lax.optimization_barrier((q_send, *mine))
     theirs = [lax.ppermute(piece, "tp", swap) for piece in mine]
-    q_recv = lax.all_to_all(q_send, "ctx", split_axis=0, concat_axis=0, tiled=True)
+    q_recv = lax.all_to_all(q_send, ("z", "x"), split_axis=0, concat_axis=0, tiled=True)
     kv_window, unpack, gr, gt = call_permute(info, g_local, own, mine, theirs)
     keep, send, score_grad = call_attention(
         info, segments, allow, unpack, q_recv, gr, gt, kv_window
     )
     recv = lax.ppermute(send, "tp", swap)
-    part = pl.pallas_call(
-        merge_kernel,
-        in_specs=[SMEM, ANY, ANY],
-        out_specs=ANY,
-        out_shape=jax.ShapeDtypeStruct((SHARDS * TOK, HEAD_SIZE), BF16),
-        scratch_shapes=[pltpu.VMEM((WINDOW * TOK, HEAD_SIZE), BF16)] * 3
-        + [
-            pltpu.VMEM((TOK, HEAD_SIZE), BF16),
-            pltpu.SemaphoreType.DMA((3 + SHARDS - WINDOW,)),
-        ],
-        compiler_params=pltpu.CompilerParams(vmem_limit_bytes=VMEM_LIMIT),
-        name="merge",
-    )(info, keep, recv)
+    halves = (2, Z_CHIPS, TOK, HEAD_SIZE)
+    x_index = lax.axis_index("x")
+
+    def summed(parity):
+        terms = [
+            lax.dynamic_index_in_dim(term.reshape(halves), parity, 0, keepdims=False)
+            for term in (keep, recv)
+        ]
+        return (terms[0].astype(F32) + terms[1].astype(F32)).astype(BF16)
+
+    beside = lax.ppermute(summed(1 - x_index), "x", [(0, 1), (1, 0)])
+    part = (summed(x_index).astype(F32) + beside.astype(F32)).astype(BF16)
     part, score_grad = lax.optimization_barrier((part, score_grad))
-    parts = lax.all_to_all(
-        part.reshape(SHARDS, TOK, HEAD_SIZE), "ctx", split_axis=0, concat_axis=0, tiled=True
-    )
+    parts = lax.all_to_all(part, "z", split_axis=0, concat_axis=0, tiled=True)
     grad_q = call_query_grad(info, segments, allow, kv_window, score_grad)
     owned = jnp.sum(parts.astype(F32), axis=0).astype(BF16)
     owned, grad_q = lax.optimization_barrier((owned, grad_q))
@@ -584,8 +566,11 @@
 
 
 def solution(mesh):
-    in_specs = (P("ctx", "tp"), P(None, "ctx", None), P(("ctx", "tp"), None), P("ctx"), P(), P())
-    out_specs = (P("ctx", "tp"), P(None, ("ctx", "tp"), None))
+    tp_size = mesh.shape["tp"]
+    split = Mesh(mesh.devices.reshape(Z_CHIPS, 2, tp_size), ("z", "x", "tp"))
+    ctx = ("z", "x")
+    in_specs = (P(ctx, "tp"), P(None, ctx, None), P((*ctx, "tp"), None), P(ctx), P(), P())
+    out_specs = (P(ctx, "tp"), P(None, (*ctx, "tp"), None))
     return jax.shard_map(
-        on_device, mesh=mesh, in_specs=in_specs, out_specs=out_specs, check_vma=False
+        on_device, mesh=split, in_specs=in_specs, out_specs=out_specs, check_vma=False
     )

time: 152 us -> 154 us (1.013)
  other arithmetic: 1.64 us -> 4.91 us
  waiting for transfers between devices: 47.8 us -> 50.9 us
  Pallas kernels: 28.4 us -> 25.6 us
  blocking collectives: 17.7 us -> 15.7 us
  starting transfers between devices: 49.1 us -> 50.8 us
    ppermute x5 -> x6, waiting for transfers between devices: 8.9 us -> 20.7 us  [the longest x1 11.8 us: on_device(): beside = lax.ppermute(summed(1 - x_index), 'x', [(0, 1), (1, 0)])]
    all_to_all x2, waiting for transfers between devices: 33.5 us -> 24.3 us  [the longest x1 14.4 us: on_device(): lax.all_to_all(q_send, ('z', 'x'), split_axis=0, concat_axis=0, tiled=True)]
    convert_element_type x0 -> x2, other arithmetic: none -> 3.26 us  [the longest x1 2.08 us: on_device(): part = (summed(x_index).astype(F32) + beside.astype(F32)).astype(BF16)]
    pallas_call x4 -> x3, Pallas kernels: 23.5 us -> 20.7 us  [the longest x1 9.06 us: call_attention(): pl.pallas_call(attention_kernel, in_specs=[SMEM, SMEM, SMEM, VMEM] + [HBM...]
    all_to_all x1, blocking collectives: 17.7 us -> 15.7 us  [on_device(): lax.all_to_all(owned.reshape(tp_size, TOK // tp_size, HEAD_SIZE), 'tp', s...]
    ppermute x5 -> x6, starting transfers between devices: 15.5 us -> 16.9 us  [the longest x1 6.54 us: on_device(): first = lax.ppermute(own, ('z', 'x', 'tp'), around(1))]
  transfers between devices with their start and end apart: 13 -> 14, of which waited for: 8 -> 9; matrix products, arithmetic and copies ran while one was open for 2% -> 2% of each run, Pallas kernels for 10% -> 9%
where the time goes in v8:
time: 154 us; the launch traced here: 153 us
  waiting for transfers between devices  50.9 us (33%)
  starting transfers between devices  50.8 us (33%)
  Pallas kernels  25.6 us (17%)
  blocking collectives  15.7 us (10%)
  other arithmetic  4.91 us (3%)
  local copies, waits for them, and re-layouts  4.36 us (3%)
    all_to_all x1, blocking collectives, on_device(): lax.all_to_all(owned.reshape(tp_size, TOK // tp_size, HEAD_SIZE), 'tp', s...  15.7 us
    all_to_all x1, waiting for transfers between devices, on_device(): lax.all_to_all(q_send, ('z', 'x'), split_axis=0, concat_axis=0, tiled=True)  14.4 us
    all_to_all x1, starting transfers between devices, on_device(): parts = lax.all_to_all(part, 'z', split_axis=0, concat_axis=0, tiled=True)  14 us
    ppermute x1, waiting for transfers between devices, on_device(): beside = lax.ppermute(summed(1 - x_index), 'x', [(0, 1), (1, 0)])  11.8 us
    all_to_all x1, waiting for transfers between devices, on_device(): parts = lax.all_to_all(part, 'z', split_axis=0, concat_axis=0, tiled=True)  9.88 us
    pallas_call x1, Pallas kernels, call_attention(): pl.pallas_call(attention_kernel, in_specs=[SMEM, SMEM, SMEM, VMEM] + [HBM...  9.06 us
    all_to_all x1, starting transfers between devices, on_device(): lax.all_to_all(out_grad, 'tp', split_axis=1, concat_axis=0, tiled=True)  7.06 us
    ppermute x1, starting transfers between devices, on_device(): first = lax.ppermute(own, ('z', 'x', 'tp'), around(1))  6.54 us
  transfers between devices with their start and end apart: 14, of which 9 were waited for; matrix products, arithmetic and copies ran while one was open for 2% of the time, Pallas kernels for 9%

profile of v8, /device:TPU:1, one launch (start us, length us, event | category | flops | bytes accessed | tf_op | source)
XLA Modules:
  0.0 153.1 jit_solution(17139714097392405879)
XLA Ops:
  0.6 2.2 %stage.1 = bf16[272,256]{1,0:T(8,128)(2,1)} custom-call(s32[1,256]{1,0:T(1,128)} %bitcast.48, bf16[2,256,1024]{2,1,0:T(8,128)(2,1)} %kv_ref.1), custom_call_target="tpu_custom_call" | custom-call | tf_op jit(solution)/shard_map/stage/pallas_call | solution.py:494
  2.9 2.1 %collective-permute-start = (bf16[272,256]{1,0:T(8,128)(2,1)}, bf16[272,256]{1,0:T(8,128)(2,1)S(1)}, u32[]{:S(2)}, u32[]{:S(2)}) collective-permute-start(bf16[272,256]{1,0:T(8,128)(2,1)} %stage.1), channel_id=1, source_target_pairs={{0,16},{16,0},{1,17},{17,1},{2,18},{18,2},{3,19},{19,3},{4,20},{20... | collective-permute-start | bytes 417800 | tf_op jit(solution)/shard_map/ppermute | solution.py:502
  5.0 2.7 %collective-permute-done = bf16[272,256]{1,0:T(8,128)(2,1)S(1)} collective-permute-done((bf16[272,256]{1,0:T(8,128)(2,1)}, bf16[272,256]{1,0:T(8,128)(2,1)S(1)}, u32[]{:S(2)}, u32[]{:S(2)}) %collective-permute-start) | collective-permute-done | bytes 139296 | tf_op jit(solution)/shard_map/ppermute | solution.py:502
  7.7 0.9 pad_maximum_fusion.refs_1_
  8.6 0.0 copy-start.2
  8.6 6.5 %collective-permute-start.1 = (bf16[2,272,256]{2,1,0:T(8,128)(2,1)S(1)}, bf16[2,272,256]{2,1,0:T(8,128)(2,1)S(1)}, u32[]{:S(2)}, u32[]{:S(2)}) collective-permute-start(bf16[2,272,256]{2,1,0:T(8,128)(2,1)S(1)} %pad_maximum_fusion.refs_1_), channel_id=1, source_target_pairs={{0,32},{1,225},{2,34},{3,227},{4,36},{5,229},{6,38},{7,231},{8,40}... | collective-permute-start | bytes 835592 | tf_op jit(solution)/shard_map/ppermute | solution.py:514
  15.1 3.5 %collective-permute-done.1.refs_2_ = bf16[2,272,256]{2,1,0:T(8,128)(2,1)S(1)} collective-permute-done((bf16[2,272,256]{2,1,0:T(8,128)(2,1)S(1)}, bf16[2,272,256]{2,1,0:T(8,128)(2,1)S(1)}, u32[]{:S(2)}, u32[]{:S(2)}) %collective-permute-start.1) | collective-permute-done | bytes 278560 | tf_op jit(solution)/shard_map/ppermute | solution.py:514
  18.6 3.1 %collective-permute-start.2 = (bf16[2,272,256]{2,1,0:T(8,128)(2,1)S(1)}, bf16[2,272,256]{2,1,0:T(8,128)(2,1)S(1)}, u32[]{:S(2)}, u32[]{:S(2)}) collective-permute-start(bf16[2,272,256]{2,1,0:T(8,128)(2,1)S(1)} %collective-permute-done.1.refs_2_), channel_id=1, source_target_pairs={{0,32},{1,225},{2,34},{3,227},{4,36},{5,229},{6,38},{7,231},{8,40}... | collective-permute-start | bytes 835592 | tf_op jit(solution)/shard_map/ppermute | solution.py:515
  21.7 1.9 %copy.16 = bf16[2,16,8,1024]{3,2,0,1:T(8,128)(2,1)} copy(bf16[2,16,8,1024]{3,2,1,0:T(8,128)(2,1)} %bitcast.42) | data formatting | bytes 1048576 | tf_op jit(solution)/shard_map/all_to_all | solution.py:520
  23.6 7.1 %all-to-all-start = ((bf16[16,16,1024]{2,0,1:T(8,128)(2,1)}), bf16[16,16,1024]{2,0,1:T(8,128)(2,1)S(1)}, u32[]{:S(2)}, u32[]{:S(2)}) async-start(bf16[16,16,1024]{2,0,1:T(8,128)(2,1)} %bitcast.32), calls=%async_computation | async-start | bytes 1048576 | tf_op jit(solution)/shard_map/all_to_all | solution.py:520
  30.7 0.0 collective-permute-done.2.refs_3_
  30.7 0.0 copy-start.3
  30.7 2.7 %collective-permute-start.3 = (bf16[2,272,256]{2,1,0:T(8,128)(2,1)S(1)}, bf16[2,272,256]{2,1,0:T(8,128)(2,1)S(1)}, u32[]{:S(2)}, u32[]{:S(2)}) collective-permute-start(bf16[2,272,256]{2,1,0:T(8,128)(2,1)S(1)} %collective-permute-done.2.refs_3_), channel_id=1, source_target_pairs={{0,32},{1,225},{2,34},{3,227},{4,36},{5,229},{6,38},{7,231},{8,40}... | collective-permute-start | bytes 835592 | tf_op jit(solution)/shard_map/ppermute | solution.py:516
  33.4 1.1 collective-permute-start.4
  34.4 2.7 %pack.1 = bf16[512,1024]{1,0:T(8,128)(2,1)} custom-call(s32[1,256]{1,0:T(1,128)} %bitcast.49, bf16[256,1024]{1,0:T(8,128)(2,1)} %rows_ref.1), custom_call_target="tpu_custom_call" | custom-call | tf_op jit(solution)/shard_map/pack/pallas_call | solution.py:521
  37.1 2.7 %collective-permute-done.4.refs_5_ = bf16[272,256]{1,0:T(8,128)(2,1)S(1)} collective-permute-done((bf16[272,256]{1,0:T(8,128)(2,1)S(1)}, bf16[272,256]{1,0:T(8,128)(2,1)S(1)}, u32[]{:S(2)}, u32[]{:S(2)}) %collective-permute-start.4) | collective-permute-done | bytes 139296 | tf_op jit(solution)/shard_map/ppermute | solution.py:518
  39.8 0.0 collective-permute-done.3.refs_4_
  39.8 2.1 %all-to-all-done = bf16[16,16,1024]{2,0,1:T(8,128)(2,1)S(1)} async-done(((bf16[16,16,1024]{2,0,1:T(8,128)(2,1)}), bf16[16,16,1024]{2,0,1:T(8,128)(2,1)S(1)}, u32[]{:S(2)}, u32[]{:S(2)}) %all-to-all-start) | async-done | bytes 524320 | tf_op jit(solution)/shard_map/all_to_all | solution.py:520
  42.0 0.0 copy-done.9
  42.0 5.9 %all-to-all-start.1 = ((bf16[16,32,1024]{2,1,0:T(8,128)(2,1)}), bf16[16,32,1024]{2,1,0:T(8,128)(2,1)S(1)}, u32[]{:S(2)}, u32[]{:S(2)}) async-start(bf16[16,32,1024]{2,1,0:T(8,128)(2,1)} %bitcast.34), calls=%async_computation.1 | async-start | bytes 2097152 | tf_op jit(solution)/shard_map/all_to_all | solution.py:530
  47.9 1.6 %collective-permute-start.5 = (bf16[2,272,256]{2,1,0:T(8,128)(2,1)S(1)}, bf16[2,272,256]{2,1,0:T(8,128)(2,1)S(1)}, u32[]{:S(2)}, u32[]{:S(2)}) collective-permute-start(bf16[2,272,256]{2,1,0:T(8,128)(2,1)S(1)} %collective-permute-done.1.refs_2_), channel_id=1, source_target_pairs={{0,1},{1,0},{2,3},{3,2},{4,5},{5,4},{6,7},{7,6},{8,9},{9,8},{10,11... | collective-permute-start | bytes 835592 | tf_op jit(solution)/shard_map/ppermute | solution.py:529
  49.5 0.1 collective-permute-start.6
  49.6 0.4 collective-permute-start.7
  50.0 0.1 collective-permute-start.8
  50.1 0.6 pad_add_fusion.info_ref
  50.7 1.2 collective-permute-done.8.refs_9_
  52.0 0.0 collective-permute-done.5.refs_6_
  52.0 0.0 collective-permute-done.6.refs_7_
  52.0 0.0 collective-permute-done.7.refs_8_
  52.0 0.6 copy-done.6
  52.7 0.1 copy-done.7
  52.8 0.1 copy-done.8
  52.9 5.1 %permute.1 = (bf16[2560,256]{1,0:T(8,128)(2,1)}, bf16[256,512]{1,0:T(8,128)(2,1)}, bf16[2,1024,128]{2,1,0:T(8,128)(2,1)}, bf16[2,128,1024]{2,1,0:T(8,128)(2,1)}) custom-call(s32[2]{0:T(128)} %pad_add_fusion.info_ref, bf16[256,1024]{1,0:T(8,128)(2,1)} %bitcast.36, bf16[2,272,256]{2,1,0:T(8,128)(2,1)} %copy-done.2, bf16[2,272,256]{2,1,0:T(8,128)(2,1)} %copy-done.4, ...), custom_call_target="tpu_custom_call" | custom-call | tf_op jit(solution)/shard_map/permute/pallas_call | solution.py:417
  58.0 14.4 %all-to-all-done.1 = bf16[16,32,1024]{2,1,0:T(8,128)(2,1)S(1)} async-done(((bf16[16,32,1024]{2,1,0:T(8,128)(2,1)}), bf16[16,32,1024]{2,1,0:T(8,128)(2,1)S(1)}, u32[]{:S(2)}, u32[]{:S(2)}) %all-to-all-start.1) | async-done | bytes 1048608 | tf_op jit(solution)/shard_map/all_to_all | solution.py:530
  72.4 1.0 copy-done
  73.4 9.1 %attention.1 = (bf16[4096,128]{1,0:T(8,128)(2,1)}, bf16[4096,128]{1,0:T(8,128)(2,1)}, bf16[2,2560,1024]{2,1,0:T(8,128)(2,1)}) custom-call(s32[2]{0:T(128)} %pad_add_fusion.info_ref, s32[4096]{0:T(1024)} %seg_ref.3, s32[32,32]{1,0:T(8,128)} %allow_ref.3, s32[32,128]{1,0:T(8,128)} %bitcast.45, bf16[256,512]{1,0:T(8,128)(2,1)} %get-tuple-element.22.unpack_in, ...), custom_call_target="tpu_custom_call" | custom-call | tf_op jit(solution)/shard_map/attention/pallas_call | solution.py:436
  82.5 4.8 %collective-permute-start.9 = (bf16[4096,128]{1,0:T(8,128)(2,1)}, bf16[4096,128]{1,0:T(8,128)(2,1)S(1)}, u32[]{:S(2)}, u32[]{:S(2)}) collective-permute-start(bf16[4096,128]{1,0:T(8,128)(2,1)} %get-tuple-element.28), channel_id=1, source_target_pairs={{0,1},{1,0},{2,3},{3,2},{4,5},{5,4},{6,7},{7,6},{8,9},{9,8},{10,11... | collective-permute-start | bytes 3145736 | tf_op jit(solution)/shard_map/ppermute | solution.py:535
  87.3 2.5 %collective-permute-done.9 = bf16[4096,128]{1,0:T(8,128)(2,1)S(1)} collective-permute-done((bf16[4096,128]{1,0:T(8,128)(2,1)}, bf16[4096,128]{1,0:T(8,128)(2,1)S(1)}, u32[]{:S(2)}, u32[]{:S(2)}) %collective-permute-start.9) | collective-permute-done | bytes 1048608 | tf_op jit(solution)/shard_map/ppermute | solution.py:535
  89.8 1.2 fusion.2
  91.0 1.4 collective-permute-start.10
  92.4 11.8 %collective-permute-done.10 = bf16[8,256,128]{2,1,0:T(8,128)(2,1)S(1)} collective-permute-done((bf16[8,256,128]{2,1,0:T(8,128)(2,1)S(1)}, bf16[8,256,128]{2,1,0:T(8,128)(2,1)S(1)}, u32[]{:S(2)}, u32[]{:S(2)}) %collective-permute-start.10) | collective-permute-done | bytes 524320 | tf_op jit(solution)/shard_map/ppermute | solution.py:546
  104.2 2.1 %fusion = bf16[8,256,128]{2,1,0:T(8,128)(2,1)} fusion(bf16[8,256,128]{2,1,0:T(8,128)(2,1)S(1)} %collective-permute-done.10, bf16[2,8,256,128]{3,2,1,0:T(8,128)(2,1)S(1)} %bitcast.40, s32[]{:T(128)S(6)} %select_n.24, bf16[2,8,256,128]{3,2,1,0:T(8,128)(2,1)} %bitcast.38), kind=kLoop, calls=%fused_computation.1 | loop fusion | flops 2097152 | bytes 2097156 | tf_op jit(solution)/shard_map/convert_element_type | solution.py:547
  106.3 14.0 %all-to-all-start.2 = ((bf16[8,256,128]{2,1,0:T(8,128)(2,1)}), bf16[8,256,128]{2,1,0:T(8,128)(2,1)S(1)}, u32[]{:S(2)}, u32[]{:S(2)}) async-start(bf16[8,256,128]{2,1,0:T(8,128)(2,1)} %fusion), calls=%async_computation.2 | async-start | bytes 1048576 | tf_op jit(solution)/shard_map/all_to_all | solution.py:549
  120.3 6.5 %query_grad.1 = bf16[256,1024]{1,0:T(8,128)(2,1)} custom-call(s32[2]{0:T(128)} %pad_add_fusion.info_ref, s32[4096]{0:T(1024)} %seg_ref.3, s32[32,32]{1,0:T(8,128)} %allow_ref.3, bf16[2560,256]{1,0:T(8,128)(2,1)} %get-tuple-element.26.kv_in, bf16[2,2560,1024]{2,1,0:T(8,128)(2,1)} %get-tuple-element.31.sg_ref), custom_call_target="tpu_custom_call" | custom-call | flops 1073741824 | bytes 12582912 | tf_op jit(solution)/shard_map/query_grad/pallas_call | solution.py:467
  126.8 9.9 %all-to-all-done.2 = bf16[8,256,128]{2,1,0:T(8,128)(2,1)S(1)} async-done(((bf16[8,256,128]{2,1,0:T(8,128)(2,1)}), bf16[8,256,128]{2,1,0:T(8,128)(2,1)S(1)}, u32[]{:S(2)}, u32[]{:S(2)}) %all-to-all-start.2) | async-done | bytes 524320 | tf_op jit(solution)/shard_map/all_to_all | solution.py:549
  136.7 0.1 reduce_sum.12
  136.8 15.7 %all_to_all.40 = bf16[16,16,128]{2,1,0:T(8,128)(2,1)S(1)} all-to-all(bf16[16,16,128]{2,1,0:T(8,128)(2,1)S(1)} %bitcast.44), channel_id=1, replica_groups=mesh['z'=8,'x'=2,'tp'=16] {'tp'}, dimensions={0} | all-to-all | bytes 131072 | tf_op jit(solution)/shard_map/all_to_all | solution.py:553
  152.5 0.6 copy.17
  (14 shorter events, 0.0 us)
Async XLA Ops:
  2.9 4.8 %collective-permute-start = (bf16[272,256]{1,0:T(8,128)(2,1)}, bf16[272,256]{1,0:T(8,128)(2,1)S(1)}, u32[]{:S(2)}, u32[]{:S(2)}) collective-permute-start(bf16[272,256]{1,0:T(8,128)(2,1)} %stage.1), channel_id=1, source_target_pairs={{0,16},{16,0},{1,17},{17,1},{2,18},{18,2},{3,19},{19,3},{4,20},{20... | collective-permute-start | bytes 417800 | tf_op jit(solution)/shard_map/ppermute | solution.py:502
  8.6 43.4 %copy-start.2 = (bf16[2,272,256]{2,1,0:T(8,128)(2,1)}, bf16[2,272,256]{2,1,0:T(8,128)(2,1)S(1)}, u32[]{:S(2)}) copy-start(bf16[2,272,256]{2,1,0:T(8,128)(2,1)S(1)} %pad_maximum_fusion.refs_1_) | copy-start | bytes 835588
  8.6 10.0 %collective-permute-start.1 = (bf16[2,272,256]{2,1,0:T(8,128)(2,1)S(1)}, bf16[2,272,256]{2,1,0:T(8,128)(2,1)S(1)}, u32[]{:S(2)}, u32[]{:S(2)}) collective-permute-start(bf16[2,272,256]{2,1,0:T(8,128)(2,1)S(1)} %pad_maximum_fusion.refs_1_), channel_id=1, source_target_pairs={{0,32},{1,225},{2,34},{3,227},{4,36},{5,229},{6,38},{7,231},{8,40}... | collective-permute-start | bytes 835592 | tf_op jit(solution)/shard_map/ppermute | solution.py:514
  18.6 33.4 %copy-start.4 = (bf16[2,272,256]{2,1,0:T(8,128)(2,1)}, bf16[2,272,256]{2,1,0:T(8,128)(2,1)S(1)}, u32[]{:S(2)}) copy-start(bf16[2,272,256]{2,1,0:T(8,128)(2,1)S(1)} %collective-permute-done.1.refs_2_) | copy-start | bytes 835588
  18.6 12.1 %collective-permute-start.2 = (bf16[2,272,256]{2,1,0:T(8,128)(2,1)S(1)}, bf16[2,272,256]{2,1,0:T(8,128)(2,1)S(1)}, u32[]{:S(2)}, u32[]{:S(2)}) collective-permute-start(bf16[2,272,256]{2,1,0:T(8,128)(2,1)S(1)} %collective-permute-done.1.refs_2_), channel_id=1, source_target_pairs={{0,32},{1,225},{2,34},{3,227},{4,36},{5,229},{6,38},{7,231},{8,40}... | collective-permute-start | bytes 835592 | tf_op jit(solution)/shard_map/ppermute | solution.py:515
  23.6 18.4 %all-to-all-start = ((bf16[16,16,1024]{2,0,1:T(8,128)(2,1)}), bf16[16,16,1024]{2,0,1:T(8,128)(2,1)S(1)}, u32[]{:S(2)}, u32[]{:S(2)}) async-start(bf16[16,16,1024]{2,0,1:T(8,128)(2,1)} %bitcast.32), calls=%async_computation | async-start | bytes 1048576 | tf_op jit(solution)/shard_map/all_to_all | solution.py:520
  30.7 21.3 %copy-start.3 = (bf16[2,272,256]{2,1,0:T(8,128)(2,1)}, bf16[2,272,256]{2,1,0:T(8,128)(2,1)S(1)}, u32[]{:S(2)}) copy-start(bf16[2,272,256]{2,1,0:T(8,128)(2,1)S(1)} %collective-permute-done.2.refs_3_) | copy-start | bytes 835588
  30.7 9.1 %collective-permute-start.3 = (bf16[2,272,256]{2,1,0:T(8,128)(2,1)S(1)}, bf16[2,272,256]{2,1,0:T(8,128)(2,1)S(1)}, u32[]{:S(2)}, u32[]{:S(2)}) collective-permute-start(bf16[2,272,256]{2,1,0:T(8,128)(2,1)S(1)} %collective-permute-done.2.refs_3_), channel_id=1, source_target_pairs={{0,32},{1,225},{2,34},{3,227},{4,36},{5,229},{6,38},{7,231},{8,40}... | collective-permute-start | bytes 835592 | tf_op jit(solution)/shard_map/ppermute | solution.py:516
  33.4 6.5 %collective-permute-start.4 = (bf16[272,256]{1,0:T(8,128)(2,1)S(1)}, bf16[272,256]{1,0:T(8,128)(2,1)S(1)}, u32[]{:S(2)}, u32[]{:S(2)}) collective-permute-start(bf16[272,256]{1,0:T(8,128)(2,1)S(1)} %dynamic-slice_bitcast_fusion), channel_id=1, source_target_pairs={{0,64},{1,193},{2,66},{3,195},{4,68},{5,197},{6,70},{7,199},{8,72}... | collective-permute-start | bytes 417800 | tf_op jit(solution)/shard_map/ppermute | solution.py:518
  39.8 2.1 %copy-start.9 = (bf16[272,256]{1,0:T(8,128)(2,1)}, bf16[272,256]{1,0:T(8,128)(2,1)S(1)}, u32[]{:S(2)}) copy-start(bf16[272,256]{1,0:T(8,128)(2,1)S(1)} %collective-permute-done.4.refs_5_) | copy-start | bytes 417796
  39.8 12.2 %copy-start.5 = (bf16[2,272,256]{2,1,0:T(8,128)(2,1)}, bf16[2,272,256]{2,1,0:T(8,128)(2,1)S(1)}, u32[]{:S(2)}) copy-start(bf16[2,272,256]{2,1,0:T(8,128)(2,1)S(1)} %collective-permute-done.3.refs_4_) | copy-start | bytes 835588
  42.0 10.1 %copy-start.1 = (bf16[16,16,1024]{2,0,1:T(8,128)(2,1)}, bf16[16,16,1024]{2,0,1:T(8,128)(2,1)S(1)}, u32[]{:S(2)}) copy-start(bf16[16,16,1024]{2,0,1:T(8,128)(2,1)S(1)} %all-to-all-done) | copy-start | bytes 1572868
  42.0 30.5 %all-to-all-start.1 = ((bf16[16,32,1024]{2,1,0:T(8,128)(2,1)}), bf16[16,32,1024]{2,1,0:T(8,128)(2,1)S(1)}, u32[]{:S(2)}, u32[]{:S(2)}) async-start(bf16[16,32,1024]{2,1,0:T(8,128)(2,1)} %bitcast.34), calls=%async_computation.1 | async-start | bytes 2097152 | tf_op jit(solution)/shard_map/all_to_all | solution.py:530
  47.9 4.1 %collective-permute-start.5 = (bf16[2,272,256]{2,1,0:T(8,128)(2,1)S(1)}, bf16[2,272,256]{2,1,0:T(8,128)(2,1)S(1)}, u32[]{:S(2)}, u32[]{:S(2)}) collective-permute-start(bf16[2,272,256]{2,1,0:T(8,128)(2,1)S(1)} %collective-permute-done.1.refs_2_), channel_id=1, source_target_pairs={{0,1},{1,0},{2,3},{3,2},{4,5},{5,4},{6,7},{7,6},{8,9},{9,8},{10,11... | collective-permute-start | bytes 835592 | tf_op jit(solution)/shard_map/ppermute | solution.py:529
  49.5 2.5 %collective-permute-start.6 = (bf16[2,272,256]{2,1,0:T(8,128)(2,1)S(1)}, bf16[2,272,256]{2,1,0:T(8,128)(2,1)S(1)}, u32[]{:S(2)}, u32[]{:S(2)}) collective-permute-start(bf16[2,272,256]{2,1,0:T(8,128)(2,1)S(1)} %collective-permute-done.2.refs_3_), channel_id=1, source_target_pairs={{0,1},{1,0},{2,3},{3,2},{4,5},{5,4},{6,7},{7,6},{8,9},{9,8},{10,11... | collective-permute-start | bytes 835592 | tf_op jit(solution)/shard_map/ppermute | solution.py:529
  49.6 2.4 %collective-permute-start.7 = (bf16[2,272,256]{2,1,0:T(8,128)(2,1)S(1)}, bf16[2,272,256]{2,1,0:T(8,128)(2,1)S(1)}, u32[]{:S(2)}, u32[]{:S(2)}) collective-permute-start(bf16[2,272,256]{2,1,0:T(8,128)(2,1)S(1)} %collective-permute-done.3.refs_4_), channel_id=1, source_target_pairs={{0,1},{1,0},{2,3},{3,2},{4,5},{5,4},{6,7},{7,6},{8,9},{9,8},{10,11... | collective-permute-start | bytes 835592 | tf_op jit(solution)/shard_map/ppermute | solution.py:529
  50.0 2.0 %collective-permute-start.8 = (bf16[272,256]{1,0:T(8,128)(2,1)}, bf16[272,256]{1,0:T(8,128)(2,1)}, u32[]{:S(2)}, u32[]{:S(2)}) collective-permute-start(bf16[272,256]{1,0:T(8,128)(2,1)} %copy-done.9), channel_id=1, source_target_pairs={{0,1},{1,0},{2,3},{3,2},{4,5},{5,4},{6,7},{7,6},{8,9},{9,8},{10,11... | collective-permute-start | bytes 417800 | tf_op jit(solution)/shard_map/ppermute | solution.py:529
  52.0 0.7 copy-start.6
  52.0 0.8 copy-start.7
  52.0 0.9 copy-start.8
  72.4 1.0 copy-start
  82.5 7.3 %collective-permute-start.9 = (bf16[4096,128]{1,0:T(8,128)(2,1)}, bf16[4096,128]{1,0:T(8,128)(2,1)S(1)}, u32[]{:S(2)}, u32[]{:S(2)}) collective-permute-start(bf16[4096,128]{1,0:T(8,128)(2,1)} %get-tuple-element.28), channel_id=1, source_target_pairs={{0,1},{1,0},{2,3},{3,2},{4,5},{5,4},{6,7},{7,6},{8,9},{9,8},{10,11... | collective-permute-start | bytes 3145736 | tf_op jit(solution)/shard_map/ppermute | solution.py:535
  91.0 13.2 %collective-permute-start.10 = (bf16[8,256,128]{2,1,0:T(8,128)(2,1)S(1)}, bf16[8,256,128]{2,1,0:T(8,128)(2,1)S(1)}, u32[]{:S(2)}, u32[]{:S(2)}) collective-permute-start(bf16[8,256,128]{2,1,0:T(8,128)(2,1)S(1)} %fusion.2), channel_id=1, source_target_pairs={{0,16},{16,0},{1,17},{17,1},{2,18},{18,2},{3,19},{19,3},{4,20},{20... | collective-permute-start | bytes 1572872 | tf_op jit(solution)/shard_map/ppermute | solution.py:546
  106.3 30.4 %all-to-all-start.2 = ((bf16[8,256,128]{2,1,0:T(8,128)(2,1)}), bf16[8,256,128]{2,1,0:T(8,128)(2,1)S(1)}, u32[]{:S(2)}, u32[]{:S(2)}) async-start(bf16[8,256,128]{2,1,0:T(8,128)(2,1)} %fusion), calls=%async_computation.2 | async-start | bytes 1048576 | tf_op jit(solution)/shard_map/all_to_all | solution.py:549

commit v9 on v8

--- a/solution.py
+++ b/solution.py
@@ -20,6 +20,8 @@
 Z_CHIPS = SHARDS // 2
 RING = Z_CHIPS // 2
 DOC_MOST = 2304
+Z_BACK = -(-DOC_MOST // (2 * TOK))
+Z_SPAN = min(Z_BACK + 1, Z_CHIPS)
 BACK = -(-DOC_MOST // TOK)
 WINDOW = BACK + 1
 BLOCKS_BACK = -(-DOC_MOST // BLK)
@@ -359,6 +361,26 @@
     base = jnp.maximum(shard - BACK, 0)
     copy = pltpu.make_async_copy(kv_in, kv_ref, kv_sem)
     copy.start()
+
+    def fetch(half, step):
+        rows = block_rows(step * NARROW, NARROW)
+        return pltpu.make_async_copy(
+            sg_ref.at[half, rows, :], sg_s.at[half, rows, :], arrived.at[half, step]
+        )
+
+    def steps_of(half):
+        nothing = lambda kb, count: None
+        count, wide, narrow = visible_blocks(shard * 2 + half, seg_ref, allow_ref, nothing)
+        return wide * (WIDE // NARROW) + narrow
+
+    def start_fetch(half, c):
+        def one(step, c2):
+            fetch(half, step).start()
+            return c2
+
+        return lax.fori_loop(0, steps_of(half), one, c)
+
+    lax.fori_loop(0, 2, start_fetch, 0)
     copy.wait()
 
     def query_block(half, carry):
@@ -376,24 +398,11 @@
             return c
 
         lax.fori_loop(count, steps * NARROW, fill, 0)
-
-        def fetch(step):
-            return pltpu.make_async_copy(
-                sg_ref.at[half, block_rows(step * NARROW, NARROW), :],
-                sg_s.at[step % 2],
-                arrived.at[step % 2],
-            )
-
-        fetch(0).start()
         dqt_s[...] = jnp.zeros_like(dqt_s)
 
         def one_step(step, c):
-            @pl.when(step + 1 < steps)
-            def _():
-                fetch(step + 1).start()
-
-            fetch(step).wait()
-            dqt_s[...] += dot(kt_s[step], sg_s[step % 2])
+            fetch(half, step).wait()
+            dqt_s[...] += dot(kt_s[step], sg_s[half, block_rows(step * NARROW, NARROW), :])
             return c
 
         lax.fori_loop(0, steps, one_step, 0)
@@ -407,8 +416,6 @@
 
 VMEM = pl.BlockSpec(memory_space=pltpu.VMEM)
 SMEM = pl.BlockSpec(memory_space=pltpu.SMEM)
-
-
 ANY = pl.BlockSpec(memory_space=pl.ANY)
 HBM = pl.BlockSpec(memory_space=pltpu.HBM)
 
@@ -472,8 +479,8 @@
         scratch_shapes=[
             pltpu.VMEM((MOST_BLOCKS // NARROW, HEAD_SIZE, NARROW * BLK), BF16),
             pltpu.VMEM((HEAD_SIZE, LANES), F32),
-            pltpu.VMEM((2, NARROW * BLK, LANES), BF16),
-            pltpu.SemaphoreType.DMA((2,)),
+            pltpu.VMEM((2, MOST_BLOCKS * BLK, LANES), BF16),
+            pltpu.SemaphoreType.DMA((2, MOST_BLOCKS // NARROW)),
             pltpu.VMEM(kv_window.shape, BF16),
             pltpu.SemaphoreType.DMA(()),
         ],
@@ -501,6 +508,8 @@
     )(place.reshape(1, TOK), keys_values)
     beside = lax.ppermute(staged, "x", [(0, 1), (1, 0)])
     own = jnp.stack([staged, beside])
+    g_send = out_grad.reshape(-1, tp_size, width).transpose(1, 0, 2)
+    own, g_send = lax.optimization_barrier((own, g_send))
 
     def around(hops):
         pairs = []
@@ -517,7 +526,8 @@
     half = lax.dynamic_index_in_dim(second, tp_index % 2, 0, keepdims=False)
     fourth = lax.ppermute(half, ("z", "x", "tp"), around(2))
     mine = [first, second, third, fourth]
-    g_local = lax.all_to_all(out_grad, "tp", split_axis=1, concat_axis=0, tiled=True)
+    g_local = lax.all_to_all(g_send, "tp", split_axis=0, concat_axis=0, tiled=True)
+    g_local = g_local.reshape(TOK, width)
     q_send = pl.pallas_call(
         pack_kernel,
         in_specs=[VMEM, VMEM],
@@ -543,9 +553,14 @@
         ]
         return (terms[0].astype(F32) + terms[1].astype(F32)).astype(BF16)
 
-    beside = lax.ppermute(summed(1 - x_index), "x", [(0, 1), (1, 0)])
-    part = (summed(x_index).astype(F32) + beside.astype(F32)).astype(BF16)
-    part, score_grad = lax.optimization_barrier((part, score_grad))
+    z_first = jnp.clip(ctx_index // 2 - Z_BACK, 0, Z_CHIPS - Z_SPAN)
+    to_send = lax.dynamic_slice_in_dim(summed(1 - x_index), z_first, Z_SPAN, 0)
+    to_send, score_grad = lax.optimization_barrier((to_send, score_grad))
+    beside_part = lax.ppermute(to_send, "x", [(0, 1), (1, 0)])
+    spare = Z_CHIPS - Z_SPAN
+    wide = jnp.pad(beside_part, ((spare, spare), (0, 0), (0, 0)))
+    placed = lax.dynamic_slice_in_dim(wide, spare - z_first, Z_CHIPS, 0)
+    part = (summed(x_index).astype(F32) + placed.astype(F32)).astype(BF16)
     parts = lax.all_to_all(part, "z", split_axis=0, concat_axis=0, tiled=True)
     grad_q = call_query_grad(info, segments, allow, kv_window, score_grad)
     owned = jnp.sum(parts.astype(F32), axis=0).astype(BF16)

time: 154 us -> 147 us (0.955)
  waiting for transfers between devices: 50.9 us -> 48 us
  starting transfers between devices: 50.8 us -> 48.4 us
  Pallas kernels: 25.6 us -> 23.8 us
    ppermute x1, waiting for transfers between devices: 11.8 us -> 9.03 us  [on_device(): beside_part = lax.ppermute(to_send, 'x', [(0, 1), (1, 0)])]
    all_to_all x1, starting transfers between devices: 14 us -> 11.5 us  [on_device(): parts = lax.all_to_all(part, 'z', split_axis=0, concat_axis=0, tiled=True)]
    ppermute x1, waiting for transfers between devices: 2.66 us -> 0.78 us  [on_device(): beside = lax.ppermute(staged, 'x', [(0, 1), (1, 0)])]
    all_to_all x1 -> x0, local copies, waits for them, and re-layouts: 1.88 us -> none  [on_device(): lax.all_to_all(out_grad, 'tp', split_axis=1, concat_axis=0, tiled=True)]
    reshape x0 -> x1, local copies, waits for them, and re-layouts: none -> 1.88 us  [on_device(): g_send = out_grad.reshape(-1, tp_size, width).transpose(1, 0, 2)]
    all_to_all x1, waiting for transfers between devices: 9.88 us -> 11.7 us  [on_device(): parts = lax.all_to_all(part, 'z', split_axis=0, concat_axis=0, tiled=True)]
    pallas_call x1, Pallas kernels: 6.53 us -> 4.69 us  [call_query_grad(): pl.pallas_call(query_grad_kernel, in_specs=[SMEM, SMEM, SMEM, HBM, HBM],...]
    convert_element_type x2 -> x1, other arithmetic: 3.26 us -> 2.1 us  [on_device(): part = (summed(x_index).astype(F32) + placed.astype(F32)).astype(BF16)]
where the time goes in v9:
time: 147 us; the launch traced here: 146 us
  starting transfers between devices  48.4 us (33%)
  waiting for transfers between devices  48 us (33%)
  Pallas kernels  23.8 us (16%)
  blocking collectives  15.6 us (11%)
  other arithmetic  4.85 us (3%)
  local copies, waits for them, and re-layouts  4.38 us (3%)
    all_to_all x1, blocking collectives, on_device(): lax.all_to_all(owned.reshape(tp_size, TOK // tp_size, HEAD_SIZE), 'tp', s...  15.6 us
    all_to_all x1, waiting for transfers between devices, on_device(): lax.all_to_all(q_send, ('z', 'x'), split_axis=0, concat_axis=0, tiled=True)  14.3 us
    all_to_all x1, waiting for transfers between devices, on_device(): parts = lax.all_to_all(part, 'z', split_axis=0, concat_axis=0, tiled=True)  11.7 us
    all_to_all x1, starting transfers between devices, on_device(): parts = lax.all_to_all(part, 'z', split_axis=0, concat_axis=0, tiled=True)  11.5 us
    pallas_call x1, Pallas kernels, call_attention(): pl.pallas_call(attention_kernel, in_specs=[SMEM, SMEM, SMEM, VMEM] + [HBM...  9.08 us
    ppermute x1, waiting for transfers between devices, on_device(): beside_part = lax.ppermute(to_send, 'x', [(0, 1), (1, 0)])  9.03 us
    all_to_all x1, starting transfers between devices, on_device(): lax.all_to_all(g_send, 'tp', split_axis=0, concat_axis=0, tiled=True)  7.06 us
    ppermute x1, starting transfers between devices, on_device(): first = lax.ppermute(own, ('z', 'x', 'tp'), around(1))  6.54 us
  transfers between devices with their start and end apart: 14, of which 9 were waited for; matrix products, arithmetic and copies ran while one was open for 2% of the time, Pallas kernels for 9%

profile of v9, /device:TPU:1, one launch (start us, length us, event | category | flops | bytes accessed | tf_op | source)
XLA Modules:
  0.0 145.9 jit_solution(8264640873718001440)
XLA Ops:
  0.6 2.2 %stage.1 = bf16[272,256]{1,0:T(8,128)(2,1)} custom-call(s32[1,256]{1,0:T(1,128)} %bitcast.49, bf16[2,256,1024]{2,1,0:T(8,128)(2,1)} %kv_ref.1), custom_call_target="tpu_custom_call" | custom-call | tf_op jit(solution)/shard_map/stage/pallas_call | solution.py:501
  2.9 2.1 %collective-permute-start = (bf16[272,256]{1,0:T(8,128)(2,1)}, bf16[272,256]{1,0:T(8,128)(2,1)S(1)}, u32[]{:S(2)}, u32[]{:S(2)}) collective-permute-start(bf16[272,256]{1,0:T(8,128)(2,1)} %stage.1), channel_id=1, source_target_pairs={{0,16},{16,0},{1,17},{17,1},{2,18},{18,2},{3,19},{19,3},{4,20},{20... | collective-permute-start | bytes 417800 | tf_op jit(solution)/shard_map/ppermute | solution.py:509
  5.0 1.9 %copy.16 = bf16[2,16,8,1024]{3,2,0,1:T(8,128)(2,1)} copy(bf16[2,16,8,1024]{3,2,1,0:T(8,128)(2,1)} %bitcast.43) | data formatting | bytes 1048576 | tf_op jit(solution)/shard_map/reshape | solution.py:511
  6.9 0.8 collective-permute-done
  7.6 0.9 pad_maximum_fusion.refs_1_
  8.6 6.5 %collective-permute-start.1 = (bf16[2,272,256]{2,1,0:T(8,128)(2,1)S(1)}, bf16[2,272,256]{2,1,0:T(8,128)(2,1)S(1)}, u32[]{:S(2)}, u32[]{:S(2)}) collective-permute-start(bf16[2,272,256]{2,1,0:T(8,128)(2,1)S(1)} %pad_maximum_fusion.refs_1_), channel_id=1, source_target_pairs={{0,32},{1,225},{2,34},{3,227},{4,36},{5,229},{6,38},{7,231},{8,40}... | collective-permute-start | bytes 835592 | tf_op jit(solution)/shard_map/ppermute | solution.py:523
  15.1 3.5 %collective-permute-done.1.refs_2_ = bf16[2,272,256]{2,1,0:T(8,128)(2,1)S(1)} collective-permute-done((bf16[2,272,256]{2,1,0:T(8,128)(2,1)S(1)}, bf16[2,272,256]{2,1,0:T(8,128)(2,1)S(1)}, u32[]{:S(2)}, u32[]{:S(2)}) %collective-permute-start.1) | collective-permute-done | bytes 278560 | tf_op jit(solution)/shard_map/ppermute | solution.py:523
  18.6 3.1 %collective-permute-start.2 = (bf16[2,272,256]{2,1,0:T(8,128)(2,1)S(1)}, bf16[2,272,256]{2,1,0:T(8,128)(2,1)S(1)}, u32[]{:S(2)}, u32[]{:S(2)}) collective-permute-start(bf16[2,272,256]{2,1,0:T(8,128)(2,1)S(1)} %collective-permute-done.1.refs_2_), channel_id=1, source_target_pairs={{0,32},{1,225},{2,34},{3,227},{4,36},{5,229},{6,38},{7,231},{8,40}... | collective-permute-start | bytes 835592 | tf_op jit(solution)/shard_map/ppermute | solution.py:524
  21.7 7.1 %all-to-all-start = ((bf16[16,16,1024]{2,1,0:T(8,128)(2,1)}), bf16[16,16,1024]{2,1,0:T(8,128)(2,1)S(1)}, u32[]{:S(2)}, u32[]{:S(2)}) async-start(bf16[16,16,1024]{2,1,0:T(8,128)(2,1)} %bitcast.33), calls=%async_computation | async-start | bytes 1048576 | tf_op jit(solution)/shard_map/all_to_all | solution.py:529
  28.8 0.0 collective-permute-done.2.refs_3_
  28.8 0.0 copy-start.3
  28.8 2.7 %collective-permute-start.3 = (bf16[2,272,256]{2,1,0:T(8,128)(2,1)S(1)}, bf16[2,272,256]{2,1,0:T(8,128)(2,1)S(1)}, u32[]{:S(2)}, u32[]{:S(2)}) collective-permute-start(bf16[2,272,256]{2,1,0:T(8,128)(2,1)S(1)} %collective-permute-done.2.refs_3_), channel_id=1, source_target_pairs={{0,32},{1,225},{2,34},{3,227},{4,36},{5,229},{6,38},{7,231},{8,40}... | collective-permute-start | bytes 835592 | tf_op jit(solution)/shard_map/ppermute | solution.py:525
  31.5 1.1 collective-permute-start.4
  32.5 2.7 %pack.1 = bf16[512,1024]{1,0:T(8,128)(2,1)} custom-call(s32[1,256]{1,0:T(1,128)} %bitcast.50, bf16[256,1024]{1,0:T(8,128)(2,1)} %rows_ref.1), custom_call_target="tpu_custom_call" | custom-call | tf_op jit(solution)/shard_map/pack/pallas_call | solution.py:531
  35.2 2.7 %collective-permute-done.4.refs_5_ = bf16[272,256]{1,0:T(8,128)(2,1)S(1)} collective-permute-done((bf16[272,256]{1,0:T(8,128)(2,1)S(1)}, bf16[272,256]{1,0:T(8,128)(2,1)S(1)}, u32[]{:S(2)}, u32[]{:S(2)}) %collective-permute-start.4) | collective-permute-done | bytes 139296 | tf_op jit(solution)/shard_map/ppermute | solution.py:527
  38.0 0.0 collective-permute-done.3.refs_4_
  38.0 2.1 %all-to-all-done = bf16[16,16,1024]{2,1,0:T(8,128)(2,1)S(1)} async-done(((bf16[16,16,1024]{2,1,0:T(8,128)(2,1)}), bf16[16,16,1024]{2,1,0:T(8,128)(2,1)S(1)}, u32[]{:S(2)}, u32[]{:S(2)}) %all-to-all-start) | async-done | bytes 524320 | tf_op jit(solution)/shard_map/all_to_all | solution.py:529
  40.1 0.0 copy-done.9
  40.1 5.9 %all-to-all-start.1 = ((bf16[16,32,1024]{2,1,0:T(8,128)(2,1)}), bf16[16,32,1024]{2,1,0:T(8,128)(2,1)S(1)}, u32[]{:S(2)}, u32[]{:S(2)}) async-start(bf16[16,32,1024]{2,1,0:T(8,128)(2,1)} %bitcast.35), calls=%async_computation.1 | async-start | bytes 2097152 | tf_op jit(solution)/shard_map/all_to_all | solution.py:540
  46.0 1.6 %collective-permute-start.5 = (bf16[2,272,256]{2,1,0:T(8,128)(2,1)S(1)}, bf16[2,272,256]{2,1,0:T(8,128)(2,1)S(1)}, u32[]{:S(2)}, u32[]{:S(2)}) collective-permute-start(bf16[2,272,256]{2,1,0:T(8,128)(2,1)S(1)} %collective-permute-done.1.refs_2_), channel_id=1, source_target_pairs={{0,1},{1,0},{2,3},{3,2},{4,5},{5,4},{6,7},{7,6},{8,9},{9,8},{10,11... | collective-permute-start | bytes 835592 | tf_op jit(solution)/shard_map/ppermute | solution.py:539
  47.6 0.1 collective-permute-start.6
  47.7 0.4 collective-permute-start.7
  48.1 0.1 collective-permute-start.8
  48.2 0.6 pad_add_fusion.info_ref
  48.9 1.2 collective-permute-done.8.refs_9_
  50.1 0.0 collective-permute-done.5.refs_6_
  50.1 0.0 collective-permute-done.6.refs_7_
  50.1 0.0 copy-start.7
  50.2 0.0 collective-permute-done.7.refs_8_
  50.2 0.6 copy-done.6
  50.9 0.1 copy-done.7
  51.0 0.1 copy-done.8
  51.1 5.1 %permute.1 = (bf16[2560,256]{1,0:T(8,128)(2,1)}, bf16[256,512]{1,0:T(8,128)(2,1)}, bf16[2,1024,128]{2,1,0:T(8,128)(2,1)}, bf16[2,128,1024]{2,1,0:T(8,128)(2,1)}) custom-call(s32[2]{0:T(128)} %pad_add_fusion.info_ref, bf16[256,1024]{1,0:T(8,128)(2,1)} %bitcast.37, bf16[2,272,256]{2,1,0:T(8,128)(2,1)} %copy-done.2, bf16[2,272,256]{2,1,0:T(8,128)(2,1)} %copy-done.4, ...), custom_call_target="tpu_custom_call" | custom-call | tf_op jit(solution)/shard_map/permute/pallas_call | solution.py:424
  56.2 14.3 %all-to-all-done.1 = bf16[16,32,1024]{2,1,0:T(8,128)(2,1)S(1)} async-done(((bf16[16,32,1024]{2,1,0:T(8,128)(2,1)}), bf16[16,32,1024]{2,1,0:T(8,128)(2,1)S(1)}, u32[]{:S(2)}, u32[]{:S(2)}) %all-to-all-start.1) | async-done | bytes 1048608 | tf_op jit(solution)/shard_map/all_to_all | solution.py:540
  70.5 1.0 copy-done
  71.5 9.1 %attention.1 = (bf16[4096,128]{1,0:T(8,128)(2,1)}, bf16[4096,128]{1,0:T(8,128)(2,1)}, bf16[2,2560,1024]{2,1,0:T(8,128)(2,1)}) custom-call(s32[2]{0:T(128)} %pad_add_fusion.info_ref, s32[4096]{0:T(1024)} %seg_ref.3, s32[32,32]{1,0:T(8,128)} %allow_ref.3, s32[32,128]{1,0:T(8,128)} %bitcast.46, bf16[256,512]{1,0:T(8,128)(2,1)} %get-tuple-element.26.unpack_in, ...), custom_call_target="tpu_custom_call" | custom-call | tf_op jit(solution)/shard_map/attention/pallas_call | solution.py:443
  80.6 4.9 %collective-permute-start.9 = (bf16[4096,128]{1,0:T(8,128)(2,1)}, bf16[4096,128]{1,0:T(8,128)(2,1)S(1)}, u32[]{:S(2)}, u32[]{:S(2)}) collective-permute-start(bf16[4096,128]{1,0:T(8,128)(2,1)} %get-tuple-element.32), channel_id=1, source_target_pairs={{0,1},{1,0},{2,3},{3,2},{4,5},{5,4},{6,7},{7,6},{8,9},{9,8},{10,11... | collective-permute-start | bytes 3145736 | tf_op jit(solution)/shard_map/ppermute | solution.py:545
  85.5 2.5 %collective-permute-done.9 = bf16[4096,128]{1,0:T(8,128)(2,1)S(1)} collective-permute-done((bf16[4096,128]{1,0:T(8,128)(2,1)}, bf16[4096,128]{1,0:T(8,128)(2,1)S(1)}, u32[]{:S(2)}, u32[]{:S(2)}) %collective-permute-start.9) | collective-permute-done | bytes 1048608 | tf_op jit(solution)/shard_map/ppermute | solution.py:545
  88.0 1.1 fusion.2
  89.1 1.4 collective-permute-start.10
  90.5 9.0 %collective-permute-done.10 = bf16[6,256,128]{2,1,0:T(8,128)(2,1)S(1)} collective-permute-done((bf16[6,256,128]{2,1,0:T(8,128)(2,1)S(1)}, bf16[6,256,128]{2,1,0:T(8,128)(2,1)S(1)}, u32[]{:S(2)}, u32[]{:S(2)}) %collective-permute-start.10) | collective-permute-done | bytes 393248 | tf_op jit(solution)/shard_map/ppermute | solution.py:559
  99.5 2.1 %fusion = bf16[8,256,128]{2,1,0:T(8,128)(2,1)} fusion(s32[]{:T(128)S(6)} %select_n.35, bf16[6,256,128]{2,1,0:T(8,128)(2,1)S(1)} %collective-permute-done.10, bf16[2,8,256,128]{3,2,1,0:T(8,128)(2,1)S(1)} %bitcast.41, s32[]{:T(128)S(6)} %select_n.32, bf16[2,8,256,128]{3,2,1,0:T(8,128)(2,1)} %bitcast.39), kind=kLoop, calls=%fused_computation.1 | loop fusion | flops 2097152 | bytes 1966088 | tf_op jit(solution)/shard_map/convert_element_type | solution.py:563
  101.6 11.5 %all-to-all-start.2 = ((bf16[8,256,128]{2,1,0:T(8,128)(2,1)}), bf16[8,256,128]{2,1,0:T(8,128)(2,1)S(1)}, u32[]{:S(2)}, u32[]{:S(2)}) async-start(bf16[8,256,128]{2,1,0:T(8,128)(2,1)} %fusion), calls=%async_computation.2 | async-start | bytes 1048576 | tf_op jit(solution)/shard_map/all_to_all | solution.py:564
  113.1 4.7 %query_grad.1 = bf16[256,1024]{1,0:T(8,128)(2,1)} custom-call(s32[2]{0:T(128)} %pad_add_fusion.info_ref, s32[4096]{0:T(1024)} %seg_ref.3, s32[32,32]{1,0:T(8,128)} %allow_ref.3, bf16[2560,256]{1,0:T(8,128)(2,1)} %get-tuple-element.30.kv_in, bf16[2,2560,1024]{2,1,0:T(8,128)(2,1)} %get-tuple-element.35.sg_ref), custom_call_target="tpu_custom_call" | custom-call | flops 1073741824 | bytes 12582912 | tf_op jit(solution)/shard_map/query_grad/pallas_call | solution.py:474
  117.8 11.7 %all-to-all-done.2 = bf16[8,256,128]{2,1,0:T(8,128)(2,1)S(1)} async-done(((bf16[8,256,128]{2,1,0:T(8,128)(2,1)}), bf16[8,256,128]{2,1,0:T(8,128)(2,1)S(1)}, u32[]{:S(2)}, u32[]{:S(2)}) %all-to-all-start.2) | async-done | bytes 524320 | tf_op jit(solution)/shard_map/all_to_all | solution.py:564
  129.5 0.1 reduce_sum.12
  129.6 15.6 %all_to_all.26 = bf16[16,16,128]{2,1,0:T(8,128)(2,1)S(1)} all-to-all(bf16[16,16,128]{2,1,0:T(8,128)(2,1)S(1)} %bitcast.45), channel_id=1, replica_groups=mesh['z'=8,'x'=2,'tp'=16] {'tp'}, dimensions={0} | all-to-all | bytes 131072 | tf_op jit(solution)/shard_map/all_to_all | solution.py:568
  145.2 0.6 copy.17
  (14 shorter events, 0.0 us)
Async XLA Ops:
  2.9 4.8 %collective-permute-start = (bf16[272,256]{1,0:T(8,128)(2,1)}, bf16[272,256]{1,0:T(8,128)(2,1)S(1)}, u32[]{:S(2)}, u32[]{:S(2)}) collective-permute-start(bf16[272,256]{1,0:T(8,128)(2,1)} %stage.1), channel_id=1, source_target_pairs={{0,16},{16,0},{1,17},{17,1},{2,18},{18,2},{3,19},{19,3},{4,20},{20... | collective-permute-start | bytes 417800 | tf_op jit(solution)/shard_map/ppermute | solution.py:509
  8.6 41.6 %copy-start.2 = (bf16[2,272,256]{2,1,0:T(8,128)(2,1)}, bf16[2,272,256]{2,1,0:T(8,128)(2,1)S(1)}, u32[]{:S(2)}) copy-start(bf16[2,272,256]{2,1,0:T(8,128)(2,1)S(1)} %pad_maximum_fusion.refs_1_) | copy-start | bytes 835588
  8.6 10.0 %collective-permute-start.1 = (bf16[2,272,256]{2,1,0:T(8,128)(2,1)S(1)}, bf16[2,272,256]{2,1,0:T(8,128)(2,1)S(1)}, u32[]{:S(2)}, u32[]{:S(2)}) collective-permute-start(bf16[2,272,256]{2,1,0:T(8,128)(2,1)S(1)} %pad_maximum_fusion.refs_1_), channel_id=1, source_target_pairs={{0,32},{1,225},{2,34},{3,227},{4,36},{5,229},{6,38},{7,231},{8,40}... | collective-permute-start | bytes 835592 | tf_op jit(solution)/shard_map/ppermute | solution.py:523
  18.6 31.6 %copy-start.4 = (bf16[2,272,256]{2,1,0:T(8,128)(2,1)}, bf16[2,272,256]{2,1,0:T(8,128)(2,1)S(1)}, u32[]{:S(2)}) copy-start(bf16[2,272,256]{2,1,0:T(8,128)(2,1)S(1)} %collective-permute-done.1.refs_2_) | copy-start | bytes 835588
  18.6 10.2 %collective-permute-start.2 = (bf16[2,272,256]{2,1,0:T(8,128)(2,1)S(1)}, bf16[2,272,256]{2,1,0:T(8,128)(2,1)S(1)}, u32[]{:S(2)}, u32[]{:S(2)}) collective-permute-start(bf16[2,272,256]{2,1,0:T(8,128)(2,1)S(1)} %collective-permute-done.1.refs_2_), channel_id=1, source_target_pairs={{0,32},{1,225},{2,34},{3,227},{4,36},{5,229},{6,38},{7,231},{8,40}... | collective-permute-start | bytes 835592 | tf_op jit(solution)/shard_map/ppermute | solution.py:524
  21.7 18.4 %all-to-all-start = ((bf16[16,16,1024]{2,1,0:T(8,128)(2,1)}), bf16[16,16,1024]{2,1,0:T(8,128)(2,1)S(1)}, u32[]{:S(2)}, u32[]{:S(2)}) async-start(bf16[16,16,1024]{2,1,0:T(8,128)(2,1)} %bitcast.33), calls=%async_computation | async-start | bytes 1048576 | tf_op jit(solution)/shard_map/all_to_all | solution.py:529
  28.8 21.4 %copy-start.3 = (bf16[2,272,256]{2,1,0:T(8,128)(2,1)}, bf16[2,272,256]{2,1,0:T(8,128)(2,1)S(1)}, u32[]{:S(2)}) copy-start(bf16[2,272,256]{2,1,0:T(8,128)(2,1)S(1)} %collective-permute-done.2.refs_3_) | copy-start | bytes 835588
  28.8 9.1 %collective-permute-start.3 = (bf16[2,272,256]{2,1,0:T(8,128)(2,1)S(1)}, bf16[2,272,256]{2,1,0:T(8,128)(2,1)S(1)}, u32[]{:S(2)}, u32[]{:S(2)}) collective-permute-start(bf16[2,272,256]{2,1,0:T(8,128)(2,1)S(1)} %collective-permute-done.2.refs_3_), channel_id=1, source_target_pairs={{0,32},{1,225},{2,34},{3,227},{4,36},{5,229},{6,38},{7,231},{8,40}... | collective-permute-start | bytes 835592 | tf_op jit(solution)/shard_map/ppermute | solution.py:525
  31.5 6.5 %collective-permute-start.4 = (bf16[272,256]{1,0:T(8,128)(2,1)S(1)}, bf16[272,256]{1,0:T(8,128)(2,1)S(1)}, u32[]{:S(2)}, u32[]{:S(2)}) collective-permute-start(bf16[272,256]{1,0:T(8,128)(2,1)S(1)} %dynamic-slice_bitcast_fusion), channel_id=1, source_target_pairs={{0,64},{1,193},{2,66},{3,195},{4,68},{5,197},{6,70},{7,199},{8,72}... | collective-permute-start | bytes 417800 | tf_op jit(solution)/shard_map/ppermute | solution.py:527
  38.0 2.1 %copy-start.9 = (bf16[272,256]{1,0:T(8,128)(2,1)}, bf16[272,256]{1,0:T(8,128)(2,1)S(1)}, u32[]{:S(2)}) copy-start(bf16[272,256]{1,0:T(8,128)(2,1)S(1)} %collective-permute-done.4.refs_5_) | copy-start | bytes 417796
  38.0 12.2 %copy-start.5 = (bf16[2,272,256]{2,1,0:T(8,128)(2,1)}, bf16[2,272,256]{2,1,0:T(8,128)(2,1)S(1)}, u32[]{:S(2)}) copy-start(bf16[2,272,256]{2,1,0:T(8,128)(2,1)S(1)} %collective-permute-done.3.refs_4_) | copy-start | bytes 835588
  40.1 10.1 %copy-start.1 = (bf16[16,16,1024]{2,1,0:T(8,128)(2,1)}, bf16[16,16,1024]{2,1,0:T(8,128)(2,1)S(1)}, u32[]{:S(2)}) copy-start(bf16[16,16,1024]{2,1,0:T(8,128)(2,1)S(1)} %all-to-all-done) | copy-start | bytes 1572868
  40.1 30.4 %all-to-all-start.1 = ((bf16[16,32,1024]{2,1,0:T(8,128)(2,1)}), bf16[16,32,1024]{2,1,0:T(8,128)(2,1)S(1)}, u32[]{:S(2)}, u32[]{:S(2)}) async-start(bf16[16,32,1024]{2,1,0:T(8,128)(2,1)} %bitcast.35), calls=%async_computation.1 | async-start | bytes 2097152 | tf_op jit(solution)/shard_map/all_to_all | solution.py:540
  46.0 4.1 %collective-permute-start.5 = (bf16[2,272,256]{2,1,0:T(8,128)(2,1)S(1)}, bf16[2,272,256]{2,1,0:T(8,128)(2,1)S(1)}, u32[]{:S(2)}, u32[]{:S(2)}) collective-permute-start(bf16[2,272,256]{2,1,0:T(8,128)(2,1)S(1)} %collective-permute-done.1.refs_2_), channel_id=1, source_target_pairs={{0,1},{1,0},{2,3},{3,2},{4,5},{5,4},{6,7},{7,6},{8,9},{9,8},{10,11... | collective-permute-start | bytes 835592 | tf_op jit(solution)/shard_map/ppermute | solution.py:539
  47.6 2.5 %collective-permute-start.6 = (bf16[2,272,256]{2,1,0:T(8,128)(2,1)S(1)}, bf16[2,272,256]{2,1,0:T(8,128)(2,1)S(1)}, u32[]{:S(2)}, u32[]{:S(2)}) collective-permute-start(bf16[2,272,256]{2,1,0:T(8,128)(2,1)S(1)} %collective-permute-done.2.refs_3_), channel_id=1, source_target_pairs={{0,1},{1,0},{2,3},{3,2},{4,5},{5,4},{6,7},{7,6},{8,9},{9,8},{10,11... | collective-permute-start | bytes 835592 | tf_op jit(solution)/shard_map/ppermute | solution.py:539
  47.7 2.4 %collective-permute-start.7 = (bf16[2,272,256]{2,1,0:T(8,128)(2,1)S(1)}, bf16[2,272,256]{2,1,0:T(8,128)(2,1)S(1)}, u32[]{:S(2)}, u32[]{:S(2)}) collective-permute-start(bf16[2,272,256]{2,1,0:T(8,128)(2,1)S(1)} %collective-permute-done.3.refs_4_), channel_id=1, source_target_pairs={{0,1},{1,0},{2,3},{3,2},{4,5},{5,4},{6,7},{7,6},{8,9},{9,8},{10,11... | collective-permute-start | bytes 835592 | tf_op jit(solution)/shard_map/ppermute | solution.py:539
  48.1 2.0 %collective-permute-start.8 = (bf16[272,256]{1,0:T(8,128)(2,1)}, bf16[272,256]{1,0:T(8,128)(2,1)}, u32[]{:S(2)}, u32[]{:S(2)}) collective-permute-start(bf16[272,256]{1,0:T(8,128)(2,1)} %copy-done.9), channel_id=1, source_target_pairs={{0,1},{1,0},{2,3},{3,2},{4,5},{5,4},{6,7},{7,6},{8,9},{9,8},{10,11... | collective-permute-start | bytes 417800 | tf_op jit(solution)/shard_map/ppermute | solution.py:539
  50.1 0.7 copy-start.6
  50.1 0.8 copy-start.7
  50.2 0.9 copy-start.8
  70.5 1.0 copy-start
  80.6 7.4 %collective-permute-start.9 = (bf16[4096,128]{1,0:T(8,128)(2,1)}, bf16[4096,128]{1,0:T(8,128)(2,1)S(1)}, u32[]{:S(2)}, u32[]{:S(2)}) collective-permute-start(bf16[4096,128]{1,0:T(8,128)(2,1)} %get-tuple-element.32), channel_id=1, source_target_pairs={{0,1},{1,0},{2,3},{3,2},{4,5},{5,4},{6,7},{7,6},{8,9},{9,8},{10,11... | collective-permute-start | bytes 3145736 | tf_op jit(solution)/shard_map/ppermute | solution.py:545
  89.1 10.4 %collective-permute-start.10 = (bf16[6,256,128]{2,1,0:T(8,128)(2,1)S(1)}, bf16[6,256,128]{2,1,0:T(8,128)(2,1)S(1)}, u32[]{:S(2)}, u32[]{:S(2)}) collective-permute-start(bf16[6,256,128]{2,1,0:T(8,128)(2,1)S(1)} %fusion.2), channel_id=1, source_target_pairs={{0,16},{16,0},{1,17},{17,1},{2,18},{18,2},{3,19},{19,3},{4,20},{20... | collective-permute-start | bytes 1179656 | tf_op jit(solution)/shard_map/ppermute | solution.py:559
  101.6 27.9 %all-to-all-start.2 = ((bf16[8,256,128]{2,1,0:T(8,128)(2,1)}), bf16[8,256,128]{2,1,0:T(8,128)(2,1)S(1)}, u32[]{:S(2)}, u32[]{:S(2)}) async-start(bf16[8,256,128]{2,1,0:T(8,128)(2,1)} %fusion), calls=%async_computation.2 | async-start | bytes 1048576 | tf_op jit(solution)/shard_map/all_to_all | solution.py:564

commit v10 on v9

--- a/solution.py
+++ b/solution.py
@@ -20,8 +20,6 @@
 Z_CHIPS = SHARDS // 2
 RING = Z_CHIPS // 2
 DOC_MOST = 2304
-Z_BACK = -(-DOC_MOST // (2 * TOK))
-Z_SPAN = min(Z_BACK + 1, Z_CHIPS)
 BACK = -(-DOC_MOST // TOK)
 WINDOW = BACK + 1
 BLOCKS_BACK = -(-DOC_MOST // BLK)
@@ -161,11 +159,6 @@
     wide = (count + 1) // WIDE
     narrow = (count + WIDE - 1) // WIDE - wide
     return count, wide, narrow
-
-
-def parity_block(kb):
-    shard = kb // 2
-    return ((shard % 2) * Z_CHIPS + shard // 2) * 2 + kb % 2
 
 
 def block_rows(n, blocks=1):
@@ -221,7 +214,7 @@
         q_last = seg_ref[qb * BLK + BLK - 1]
 
         def on_block(kb, count):
-            list_s[count] = parity_block(kb)
+            list_s[count] = kb
             src = block_rows(kb - 2 * base)
             dst = block_rows(count)
             k_s[dst, :] = kv_ref[src, :HEAD_SIZE]
@@ -543,39 +536,24 @@
         info, segments, allow, unpack, q_recv, gr, gt, kv_window
     )
     recv = lax.ppermute(send, "tp", swap)
-    halves = (2, Z_CHIPS, TOK, HEAD_SIZE)
-    x_index = lax.axis_index("x")
-
-    def summed(parity):
-        terms = [
-            lax.dynamic_index_in_dim(term.reshape(halves), parity, 0, keepdims=False)
-            for term in (keep, recv)
-        ]
-        return (terms[0].astype(F32) + terms[1].astype(F32)).astype(BF16)
-
-    z_first = jnp.clip(ctx_index // 2 - Z_BACK, 0, Z_CHIPS - Z_SPAN)
-    to_send = lax.dynamic_slice_in_dim(summed(1 - x_index), z_first, Z_SPAN, 0)
-    to_send, score_grad = lax.optimization_barrier((to_send, score_grad))
-    beside_part = lax.ppermute(to_send, "x", [(0, 1), (1, 0)])
-    spare = Z_CHIPS - Z_SPAN
-    wide = jnp.pad(beside_part, ((spare, spare), (0, 0), (0, 0)))
-    placed = lax.dynamic_slice_in_dim(wide, spare - z_first, Z_CHIPS, 0)
-    part = (summed(x_index).astype(F32) + placed.astype(F32)).astype(BF16)
-    parts = lax.all_to_all(part, "z", split_axis=0, concat_axis=0, tiled=True)
-    grad_q = call_query_grad(info, segments, allow, kv_window, score_grad)
-    owned = jnp.sum(parts.astype(F32), axis=0).astype(BF16)
-    owned, grad_q = lax.optimization_barrier((owned, grad_q))
-    heads = lax.all_to_all(
-        owned.reshape(tp_size, TOK // tp_size, HEAD_SIZE),
-        "tp",
+    part = (keep.astype(F32) + recv.astype(F32)).astype(BF16)
+    part, score_grad = lax.optimization_barrier((part, score_grad))
+    rows = TOK // tp_size
+    parts = lax.all_to_all(
+        part.reshape(SHARDS * tp_size, rows, HEAD_SIZE),
+        ("z", "x", "tp"),
         split_axis=0,
         concat_axis=0,
         tiled=True,
     )
+    grad_q = call_query_grad(info, segments, allow, kv_window, score_grad)
+    parts, grad_q = lax.optimization_barrier((parts, grad_q))
+    heads = jnp.sum(parts.reshape(SHARDS, tp_size, rows, HEAD_SIZE).astype(F32), axis=0)
     key_value_gradient = (
-        heads.reshape(KEY_VALUE_HEADS, 2, TOK // tp_size, HEAD_SIZE)
+        heads.astype(BF16)
+        .reshape(KEY_VALUE_HEADS, 2, rows, HEAD_SIZE)
         .transpose(1, 2, 0, 3)
-        .reshape(2, TOK // tp_size, KEY_VALUE_HEADS * HEAD_SIZE)
+        .reshape(2, rows, KEY_VALUE_HEADS * HEAD_SIZE)
     )
     return (grad_q, key_value_gradient)
 

time: 147 us -> 142 us (0.966)
  blocking collectives: 15.6 us -> 0 us
  waiting for transfers between devices: 48 us -> 54.8 us
  starting transfers between devices: 48.4 us -> 54.1 us
    all_to_all x1, waiting for transfers between devices: 11.7 us -> 27.5 us  [on_device(): lax.all_to_all(part.reshape(SHARDS * tp_size, rows, HEAD_SIZE), ('z', 'x'...]
    all_to_all x1 -> x0, blocking collectives: 15.6 us -> none  [on_device(): lax.all_to_all(owned.reshape(tp_size, TOK // tp_size, HEAD_SIZE), 'tp', s...]
    ppermute x1 -> x0, waiting for transfers between devices: 9.03 us -> none  [on_device(): beside_part = lax.ppermute(to_send, 'x', [(0, 1), (1, 0)])]
    all_to_all x1, starting transfers between devices: 11.5 us -> 18.6 us  [on_device(): lax.all_to_all(part.reshape(SHARDS * tp_size, rows, HEAD_SIZE), ('z', 'x'...]
  transfers between devices with their start and end apart: 14 -> 13, of which waited for: 9 -> 8; matrix products, arithmetic and copies ran while one was open for 2% -> 2% of each run, Pallas kernels for 9% -> 9%
where the time goes in v10:
time: 142 us
  waiting for transfers between devices  54.8 us (39%)
  starting transfers between devices  54.1 us (38%)
  Pallas kernels  23.7 us (17%)
  local copies, waits for them, and re-layouts  4.41 us (3%)
  other arithmetic  4.19 us (3%)
    all_to_all x1, waiting for transfers between devices, on_device(): lax.all_to_all(part.reshape(SHARDS * tp_size, rows, HEAD_SIZE), ('z', 'x'...  27.5 us
    all_to_all x1, starting transfers between devices, on_device(): lax.all_to_all(part.reshape(SHARDS * tp_size, rows, HEAD_SIZE), ('z', 'x'...  18.6 us
    all_to_all x1, waiting for transfers between devices, on_device(): lax.all_to_all(q_send, ('z', 'x'), split_axis=0, concat_axis=0, tiled=True)  14.8 us
    pallas_call x1, Pallas kernels, call_attention(): pl.pallas_call(attention_kernel, in_specs=[SMEM, SMEM, SMEM, VMEM] + [HBM...  9.04 us
    all_to_all x1, starting transfers between devices, on_device(): lax.all_to_all(g_send, 'tp', split_axis=0, concat_axis=0, tiled=True)  7.06 us
    ppermute x1, starting transfers between devices, on_device(): first = lax.ppermute(own, ('z', 'x', 'tp'), around(1))  6.54 us
    all_to_all x1, starting transfers between devices, on_device(): lax.all_to_all(q_send, ('z', 'x'), split_axis=0, concat_axis=0, tiled=True)  5.9 us
    pallas_call x1, Pallas kernels, call_permute(): pl.pallas_call(permute_kernel, in_specs=[SMEM] + [HBM] * (2 * RING + 2),...  5.12 us
  transfers between devices with their start and end apart: 13, of which 8 were waited for; matrix products, arithmetic and copies ran while one was open for 2% of the time, Pallas kernels for 9%

profile of v10, /device:TPU:1, one launch (start us, length us, event | category | flops | bytes accessed | tf_op | source)
XLA Modules:
  0.0 142.0 jit_solution(12126040702513149050)
XLA Ops:
  0.6 2.2 %stage.1 = bf16[272,256]{1,0:T(8,128)(2,1)} custom-call(s32[1,256]{1,0:T(1,128)} %bitcast.37, bf16[2,256,1024]{2,1,0:T(8,128)(2,1)} %kv_ref.1), custom_call_target="tpu_custom_call" | custom-call | tf_op jit(solution)/shard_map/stage/pallas_call | solution.py:494
  2.9 2.1 %collective-permute-start = (bf16[272,256]{1,0:T(8,128)(2,1)}, bf16[272,256]{1,0:T(8,128)(2,1)S(1)}, u32[]{:S(2)}, u32[]{:S(2)}) collective-permute-start(bf16[272,256]{1,0:T(8,128)(2,1)} %stage.1), channel_id=1, source_target_pairs={{0,16},{16,0},{1,17},{17,1},{2,18},{18,2},{3,19},{19,3},{4,20},{20... | collective-permute-start | bytes 417800 | tf_op jit(solution)/shard_map/ppermute | solution.py:502
  5.0 1.9 %copy.16 = bf16[2,16,8,1024]{3,2,0,1:T(8,128)(2,1)} copy(bf16[2,16,8,1024]{3,2,1,0:T(8,128)(2,1)} %bitcast.32) | data formatting | bytes 1048576 | tf_op jit(solution)/shard_map/reshape | solution.py:504
  6.9 0.8 collective-permute-done
  7.6 0.9 pad_maximum_fusion.refs_1_
  8.6 0.0 copy-start.2
  8.6 6.5 %collective-permute-start.1 = (bf16[2,272,256]{2,1,0:T(8,128)(2,1)S(1)}, bf16[2,272,256]{2,1,0:T(8,128)(2,1)S(1)}, u32[]{:S(2)}, u32[]{:S(2)}) collective-permute-start(bf16[2,272,256]{2,1,0:T(8,128)(2,1)S(1)} %pad_maximum_fusion.refs_1_), channel_id=1, source_target_pairs={{0,32},{1,225},{2,34},{3,227},{4,36},{5,229},{6,38},{7,231},{8,40}... | collective-permute-start | bytes 835592 | tf_op jit(solution)/shard_map/ppermute | solution.py:516
  15.1 3.5 %collective-permute-done.1.refs_2_ = bf16[2,272,256]{2,1,0:T(8,128)(2,1)S(1)} collective-permute-done((bf16[2,272,256]{2,1,0:T(8,128)(2,1)S(1)}, bf16[2,272,256]{2,1,0:T(8,128)(2,1)S(1)}, u32[]{:S(2)}, u32[]{:S(2)}) %collective-permute-start.1) | collective-permute-done | bytes 278560 | tf_op jit(solution)/shard_map/ppermute | solution.py:516
  18.6 3.1 %collective-permute-start.2 = (bf16[2,272,256]{2,1,0:T(8,128)(2,1)S(1)}, bf16[2,272,256]{2,1,0:T(8,128)(2,1)S(1)}, u32[]{:S(2)}, u32[]{:S(2)}) collective-permute-start(bf16[2,272,256]{2,1,0:T(8,128)(2,1)S(1)} %collective-permute-done.1.refs_2_), channel_id=1, source_target_pairs={{0,32},{1,225},{2,34},{3,227},{4,36},{5,229},{6,38},{7,231},{8,40}... | collective-permute-start | bytes 835592 | tf_op jit(solution)/shard_map/ppermute | solution.py:517
  21.7 7.1 %all-to-all-start = ((bf16[16,16,1024]{2,1,0:T(8,128)(2,1)}), bf16[16,16,1024]{2,1,0:T(8,128)(2,1)S(1)}, u32[]{:S(2)}, u32[]{:S(2)}) async-start(bf16[16,16,1024]{2,1,0:T(8,128)(2,1)} %bitcast.25), calls=%async_computation | async-start | bytes 1048576 | tf_op jit(solution)/shard_map/all_to_all | solution.py:522
  28.8 0.0 collective-permute-done.2.refs_3_
  28.8 0.0 copy-start.3
  28.8 2.7 %collective-permute-start.3 = (bf16[2,272,256]{2,1,0:T(8,128)(2,1)S(1)}, bf16[2,272,256]{2,1,0:T(8,128)(2,1)S(1)}, u32[]{:S(2)}, u32[]{:S(2)}) collective-permute-start(bf16[2,272,256]{2,1,0:T(8,128)(2,1)S(1)} %collective-permute-done.2.refs_3_), channel_id=1, source_target_pairs={{0,32},{1,225},{2,34},{3,227},{4,36},{5,229},{6,38},{7,231},{8,40}... | collective-permute-start | bytes 835592 | tf_op jit(solution)/shard_map/ppermute | solution.py:518
  31.5 1.1 collective-permute-start.4
  32.5 2.7 %pack.1 = bf16[512,1024]{1,0:T(8,128)(2,1)} custom-call(s32[1,256]{1,0:T(1,128)} %bitcast.38, bf16[256,1024]{1,0:T(8,128)(2,1)} %rows_ref.1), custom_call_target="tpu_custom_call" | custom-call | tf_op jit(solution)/shard_map/pack/pallas_call | solution.py:524
  35.2 2.7 %collective-permute-done.4.refs_5_ = bf16[272,256]{1,0:T(8,128)(2,1)S(1)} collective-permute-done((bf16[272,256]{1,0:T(8,128)(2,1)S(1)}, bf16[272,256]{1,0:T(8,128)(2,1)S(1)}, u32[]{:S(2)}, u32[]{:S(2)}) %collective-permute-start.4) | collective-permute-done | bytes 139296 | tf_op jit(solution)/shard_map/ppermute | solution.py:520
  38.0 0.0 collective-permute-done.3.refs_4_
  38.0 2.1 %all-to-all-done = bf16[16,16,1024]{2,1,0:T(8,128)(2,1)S(1)} async-done(((bf16[16,16,1024]{2,1,0:T(8,128)(2,1)}), bf16[16,16,1024]{2,1,0:T(8,128)(2,1)S(1)}, u32[]{:S(2)}, u32[]{:S(2)}) %all-to-all-start) | async-done | bytes 524320 | tf_op jit(solution)/shard_map/all_to_all | solution.py:522
  40.1 5.9 %all-to-all-start.1 = ((bf16[16,32,1024]{2,1,0:T(8,128)(2,1)}), bf16[16,32,1024]{2,1,0:T(8,128)(2,1)S(1)}, u32[]{:S(2)}, u32[]{:S(2)}) async-start(bf16[16,32,1024]{2,1,0:T(8,128)(2,1)} %bitcast.27), calls=%async_computation.1 | async-start | bytes 2097152 | tf_op jit(solution)/shard_map/all_to_all | solution.py:533
  46.0 0.0 copy-done.4
  46.0 1.5 %collective-permute-start.5 = (bf16[2,272,256]{2,1,0:T(8,128)(2,1)S(1)}, bf16[2,272,256]{2,1,0:T(8,128)(2,1)S(1)}, u32[]{:S(2)}, u32[]{:S(2)}) collective-permute-start(bf16[2,272,256]{2,1,0:T(8,128)(2,1)S(1)} %collective-permute-done.1.refs_2_), channel_id=1, source_target_pairs={{0,1},{1,0},{2,3},{3,2},{4,5},{5,4},{6,7},{7,6},{8,9},{9,8},{10,11... | collective-permute-start | bytes 835592 | tf_op jit(solution)/shard_map/ppermute | solution.py:532
  47.6 0.1 collective-permute-start.6
  47.7 0.4 collective-permute-start.7
  48.1 0.1 collective-permute-start.8
  48.2 0.6 pad_add_fusion.info_ref
  48.8 0.9 collective-permute-done.8.refs_9_
  49.7 0.0 collective-permute-done.5.refs_6_
  49.7 0.0 collective-permute-done.6.refs_7_
  49.8 0.0 collective-permute-done.7.refs_8_
  49.8 0.0 copy-start.8
  49.8 0.0 copy-done.3
  49.8 0.0 copy-done.9
  49.8 0.6 copy-done.10
  50.4 0.1 copy-done.6
  50.5 0.1 copy-done.7
  50.6 0.1 copy-done.8
  50.7 5.1 %permute.1 = (bf16[2560,256]{1,0:T(8,128)(2,1)}, bf16[256,512]{1,0:T(8,128)(2,1)}, bf16[2,1024,128]{2,1,0:T(8,128)(2,1)}, bf16[2,128,1024]{2,1,0:T(8,128)(2,1)}) custom-call(s32[2]{0:T(128)} %pad_add_fusion.info_ref, bf16[256,1024]{1,0:T(8,128)(2,1)} %bitcast.30, bf16[2,272,256]{2,1,0:T(8,128)(2,1)} %copy-done.2, bf16[2,272,256]{2,1,0:T(8,128)(2,1)} %copy-done.4, ...), custom_call_target="tpu_custom_call" | custom-call | tf_op jit(solution)/shard_map/permute/pallas_call | solution.py:417
  55.8 14.8 %all-to-all-done.1 = bf16[16,32,1024]{2,1,0:T(8,128)(2,1)S(1)} async-done(((bf16[16,32,1024]{2,1,0:T(8,128)(2,1)}), bf16[16,32,1024]{2,1,0:T(8,128)(2,1)S(1)}, u32[]{:S(2)}, u32[]{:S(2)}) %all-to-all-start.1) | async-done | bytes 1048608 | tf_op jit(solution)/shard_map/all_to_all | solution.py:533
  70.6 1.0 copy-done
  71.6 9.0 %attention.1 = (bf16[4096,128]{1,0:T(8,128)(2,1)}, bf16[4096,128]{1,0:T(8,128)(2,1)}, bf16[2,2560,1024]{2,1,0:T(8,128)(2,1)}) custom-call(s32[2]{0:T(128)} %pad_add_fusion.info_ref, s32[4096]{0:T(1024)} %seg_ref.3, s32[32,32]{1,0:T(8,128)} %allow_ref.3, s32[32,128]{1,0:T(8,128)} %bitcast.34, bf16[256,512]{1,0:T(8,128)(2,1)} %get-tuple-element.26.unpack_in, ...), custom_call_target="tpu_custom_call" | custom-call | tf_op jit(solution)/shard_map/attention/pallas_call | solution.py:436
  80.6 5.0 %collective-permute-start.9 = (bf16[4096,128]{1,0:T(8,128)(2,1)}, bf16[4096,128]{1,0:T(8,128)(2,1)S(1)}, u32[]{:S(2)}, u32[]{:S(2)}) collective-permute-start(bf16[4096,128]{1,0:T(8,128)(2,1)} %get-tuple-element.32), channel_id=1, source_target_pairs={{0,1},{1,0},{2,3},{3,2},{4,5},{5,4},{6,7},{7,6},{8,9},{9,8},{10,11... | collective-permute-start | bytes 3145736 | tf_op jit(solution)/shard_map/ppermute | solution.py:538
  85.6 2.5 %collective-permute-done.9 = bf16[4096,128]{1,0:T(8,128)(2,1)S(1)} collective-permute-done((bf16[4096,128]{1,0:T(8,128)(2,1)}, bf16[4096,128]{1,0:T(8,128)(2,1)S(1)}, u32[]{:S(2)}, u32[]{:S(2)}) %collective-permute-start.9) | collective-permute-done | bytes 1048608 | tf_op jit(solution)/shard_map/ppermute | solution.py:538
  88.1 2.5 %add_convert_fusion = bf16[4096,128]{1,0:T(8,128)(2,1)} fusion(bf16[4096,128]{1,0:T(8,128)(2,1)S(1)} %collective-permute-done.9, bf16[4096,128]{1,0:T(8,128)(2,1)} %get-tuple-element.31), kind=kLoop, calls=%fused_computation | loop fusion | flops 2097152 | bytes 3145728 | tf_op jit(solution)/shard_map/convert_element_type | solution.py:539
  90.6 18.6 %all-to-all-start.2 = ((bf16[256,16,128]{2,1,0:T(8,128)(2,1)}), bf16[256,16,128]{2,1,0:T(8,128)(2,1)S(1)}, u32[]{:S(2)}, u32[]{:S(2)}) async-start(bf16[256,16,128]{2,1,0:T(8,128)(2,1)} %bitcast.11), calls=%async_computation.2 | async-start | bytes 2097152 | tf_op jit(solution)/shard_map/all_to_all | solution.py:542
  109.1 4.6 %query_grad.1 = bf16[256,1024]{1,0:T(8,128)(2,1)} custom-call(s32[2]{0:T(128)} %pad_add_fusion.info_ref, s32[4096]{0:T(1024)} %seg_ref.3, s32[32,32]{1,0:T(8,128)} %allow_ref.3, bf16[2560,256]{1,0:T(8,128)(2,1)} %get-tuple-element.30.kv_in, bf16[2,2560,1024]{2,1,0:T(8,128)(2,1)} %get-tuple-element.35.sg_ref), custom_call_target="tpu_custom_call" | custom-call | flops 1073741824 | bytes 12582912 | tf_op jit(solution)/shard_map/query_grad/pallas_call | solution.py:467
  113.7 27.5 %all-to-all-done.2 = bf16[256,16,128]{2,1,0:T(8,128)(2,1)S(1)} async-done(((bf16[256,16,128]{2,1,0:T(8,128)(2,1)}), bf16[256,16,128]{2,1,0:T(8,128)(2,1)S(1)}, u32[]{:S(2)}, u32[]{:S(2)}) %all-to-all-start.2) | async-done | bytes 1048608 | tf_op jit(solution)/shard_map/all_to_all | solution.py:542
  141.2 0.1 reduce_sum.12
  141.4 0.6 copy.17
  (12 shorter events, 0.0 us)
Async XLA Ops:
  2.9 4.8 %collective-permute-start = (bf16[272,256]{1,0:T(8,128)(2,1)}, bf16[272,256]{1,0:T(8,128)(2,1)S(1)}, u32[]{:S(2)}, u32[]{:S(2)}) collective-permute-start(bf16[272,256]{1,0:T(8,128)(2,1)} %stage.1), channel_id=1, source_target_pairs={{0,16},{16,0},{1,17},{17,1},{2,18},{18,2},{3,19},{19,3},{4,20},{20... | collective-permute-start | bytes 417800 | tf_op jit(solution)/shard_map/ppermute | solution.py:502
  8.6 31.5 %copy-start.2 = (bf16[2,272,256]{2,1,0:T(8,128)(2,1)}, bf16[2,272,256]{2,1,0:T(8,128)(2,1)S(1)}, u32[]{:S(2)}) copy-start(bf16[2,272,256]{2,1,0:T(8,128)(2,1)S(1)} %pad_maximum_fusion.refs_1_) | copy-start | bytes 835588
  8.6 10.0 %collective-permute-start.1 = (bf16[2,272,256]{2,1,0:T(8,128)(2,1)S(1)}, bf16[2,272,256]{2,1,0:T(8,128)(2,1)S(1)}, u32[]{:S(2)}, u32[]{:S(2)}) collective-permute-start(bf16[2,272,256]{2,1,0:T(8,128)(2,1)S(1)} %pad_maximum_fusion.refs_1_), channel_id=1, source_target_pairs={{0,32},{1,225},{2,34},{3,227},{4,36},{5,229},{6,38},{7,231},{8,40}... | collective-permute-start | bytes 835592 | tf_op jit(solution)/shard_map/ppermute | solution.py:516
  18.6 27.4 %copy-start.4 = (bf16[2,272,256]{2,1,0:T(8,128)(2,1)}, bf16[2,272,256]{2,1,0:T(8,128)(2,1)S(1)}, u32[]{:S(2)}) copy-start(bf16[2,272,256]{2,1,0:T(8,128)(2,1)S(1)} %collective-permute-done.1.refs_2_) | copy-start | bytes 835588
  18.6 10.2 %collective-permute-start.2 = (bf16[2,272,256]{2,1,0:T(8,128)(2,1)S(1)}, bf16[2,272,256]{2,1,0:T(8,128)(2,1)S(1)}, u32[]{:S(2)}, u32[]{:S(2)}) collective-permute-start(bf16[2,272,256]{2,1,0:T(8,128)(2,1)S(1)} %collective-permute-done.1.refs_2_), channel_id=1, source_target_pairs={{0,32},{1,225},{2,34},{3,227},{4,36},{5,229},{6,38},{7,231},{8,40}... | collective-permute-start | bytes 835592 | tf_op jit(solution)/shard_map/ppermute | solution.py:517
  21.7 18.4 %all-to-all-start = ((bf16[16,16,1024]{2,1,0:T(8,128)(2,1)}), bf16[16,16,1024]{2,1,0:T(8,128)(2,1)S(1)}, u32[]{:S(2)}, u32[]{:S(2)}) async-start(bf16[16,16,1024]{2,1,0:T(8,128)(2,1)} %bitcast.25), calls=%async_computation | async-start | bytes 1048576 | tf_op jit(solution)/shard_map/all_to_all | solution.py:522
  28.8 21.0 %copy-start.3 = (bf16[2,272,256]{2,1,0:T(8,128)(2,1)}, bf16[2,272,256]{2,1,0:T(8,128)(2,1)S(1)}, u32[]{:S(2)}) copy-start(bf16[2,272,256]{2,1,0:T(8,128)(2,1)S(1)} %collective-permute-done.2.refs_3_) | copy-start | bytes 835588
  28.8 9.1 %collective-permute-start.3 = (bf16[2,272,256]{2,1,0:T(8,128)(2,1)S(1)}, bf16[2,272,256]{2,1,0:T(8,128)(2,1)S(1)}, u32[]{:S(2)}, u32[]{:S(2)}) collective-permute-start(bf16[2,272,256]{2,1,0:T(8,128)(2,1)S(1)} %collective-permute-done.2.refs_3_), channel_id=1, source_target_pairs={{0,32},{1,225},{2,34},{3,227},{4,36},{5,229},{6,38},{7,231},{8,40}... | collective-permute-start | bytes 835592 | tf_op jit(solution)/shard_map/ppermute | solution.py:518
  31.5 6.5 %collective-permute-start.4 = (bf16[272,256]{1,0:T(8,128)(2,1)S(1)}, bf16[272,256]{1,0:T(8,128)(2,1)S(1)}, u32[]{:S(2)}, u32[]{:S(2)}) collective-permute-start(bf16[272,256]{1,0:T(8,128)(2,1)S(1)} %dynamic-slice_bitcast_fusion), channel_id=1, source_target_pairs={{0,64},{1,193},{2,66},{3,195},{4,68},{5,197},{6,70},{7,199},{8,72}... | collective-permute-start | bytes 417800 | tf_op jit(solution)/shard_map/ppermute | solution.py:520
  38.0 11.8 %copy-start.9 = (bf16[272,256]{1,0:T(8,128)(2,1)}, bf16[272,256]{1,0:T(8,128)(2,1)S(1)}, u32[]{:S(2)}) copy-start(bf16[272,256]{1,0:T(8,128)(2,1)S(1)} %collective-permute-done.4.refs_5_) | copy-start | bytes 417796
  38.0 11.8 %copy-start.5 = (bf16[2,272,256]{2,1,0:T(8,128)(2,1)}, bf16[2,272,256]{2,1,0:T(8,128)(2,1)S(1)}, u32[]{:S(2)}) copy-start(bf16[2,272,256]{2,1,0:T(8,128)(2,1)S(1)} %collective-permute-done.3.refs_4_) | copy-start | bytes 835588
  40.1 9.7 %copy-start.1 = (bf16[16,16,1024]{2,1,0:T(8,128)(2,1)}, bf16[16,16,1024]{2,1,0:T(8,128)(2,1)S(1)}, u32[]{:S(2)}) copy-start(bf16[16,16,1024]{2,1,0:T(8,128)(2,1)S(1)} %all-to-all-done) | copy-start | bytes 1572868
  40.1 30.5 %all-to-all-start.1 = ((bf16[16,32,1024]{2,1,0:T(8,128)(2,1)}), bf16[16,32,1024]{2,1,0:T(8,128)(2,1)S(1)}, u32[]{:S(2)}, u32[]{:S(2)}) async-start(bf16[16,32,1024]{2,1,0:T(8,128)(2,1)} %bitcast.27), calls=%async_computation.1 | async-start | bytes 2097152 | tf_op jit(solution)/shard_map/all_to_all | solution.py:533
  46.0 3.7 %collective-permute-start.5 = (bf16[2,272,256]{2,1,0:T(8,128)(2,1)S(1)}, bf16[2,272,256]{2,1,0:T(8,128)(2,1)S(1)}, u32[]{:S(2)}, u32[]{:S(2)}) collective-permute-start(bf16[2,272,256]{2,1,0:T(8,128)(2,1)S(1)} %collective-permute-done.1.refs_2_), channel_id=1, source_target_pairs={{0,1},{1,0},{2,3},{3,2},{4,5},{5,4},{6,7},{7,6},{8,9},{9,8},{10,11... | collective-permute-start | bytes 835592 | tf_op jit(solution)/shard_map/ppermute | solution.py:532
  47.6 2.2 %collective-permute-start.6 = (bf16[2,272,256]{2,1,0:T(8,128)(2,1)S(1)}, bf16[2,272,256]{2,1,0:T(8,128)(2,1)S(1)}, u32[]{:S(2)}, u32[]{:S(2)}) collective-permute-start(bf16[2,272,256]{2,1,0:T(8,128)(2,1)S(1)} %collective-permute-done.2.refs_3_), channel_id=1, source_target_pairs={{0,1},{1,0},{2,3},{3,2},{4,5},{5,4},{6,7},{7,6},{8,9},{9,8},{10,11... | collective-permute-start | bytes 835592 | tf_op jit(solution)/shard_map/ppermute | solution.py:532
  47.7 2.1 %collective-permute-start.7 = (bf16[2,272,256]{2,1,0:T(8,128)(2,1)S(1)}, bf16[2,272,256]{2,1,0:T(8,128)(2,1)S(1)}, u32[]{:S(2)}, u32[]{:S(2)}) collective-permute-start(bf16[2,272,256]{2,1,0:T(8,128)(2,1)S(1)} %collective-permute-done.3.refs_4_), channel_id=1, source_target_pairs={{0,1},{1,0},{2,3},{3,2},{4,5},{5,4},{6,7},{7,6},{8,9},{9,8},{10,11... | collective-permute-start | bytes 835592 | tf_op jit(solution)/shard_map/ppermute | solution.py:532
  48.1 1.7 %collective-permute-start.8 = (bf16[272,256]{1,0:T(8,128)(2,1)S(1)}, bf16[272,256]{1,0:T(8,128)(2,1)S(1)}, u32[]{:S(2)}, u32[]{:S(2)}) collective-permute-start(bf16[272,256]{1,0:T(8,128)(2,1)S(1)} %collective-permute-done.4.refs_5_), channel_id=1, source_target_pairs={{0,1},{1,0},{2,3},{3,2},{4,5},{5,4},{6,7},{7,6},{8,9},{9,8},{10,11... | collective-permute-start | bytes 417800 | tf_op jit(solution)/shard_map/ppermute | solution.py:532
  49.7 0.7 copy-start.10
  49.7 0.8 copy-start.6
  49.7 0.9 copy-start.7
  49.8 0.9 copy-start.8
  70.6 1.0 copy-start
  80.6 7.5 %collective-permute-start.9 = (bf16[4096,128]{1,0:T(8,128)(2,1)}, bf16[4096,128]{1,0:T(8,128)(2,1)S(1)}, u32[]{:S(2)}, u32[]{:S(2)}) collective-permute-start(bf16[4096,128]{1,0:T(8,128)(2,1)} %get-tuple-element.32), channel_id=1, source_target_pairs={{0,1},{1,0},{2,3},{3,2},{4,5},{5,4},{6,7},{7,6},{8,9},{9,8},{10,11... | collective-permute-start | bytes 3145736 | tf_op jit(solution)/shard_map/ppermute | solution.py:538
  90.6 50.7 %all-to-all-start.2 = ((bf16[256,16,128]{2,1,0:T(8,128)(2,1)}), bf16[256,16,128]{2,1,0:T(8,128)(2,1)S(1)}, u32[]{:S(2)}, u32[]{:S(2)}) async-start(bf16[256,16,128]{2,1,0:T(8,128)(2,1)} %bitcast.11), calls=%async_computation.2 | async-start | bytes 2097152 | tf_op jit(solution)/shard_map/all_to_all | solution.py:542

commit v11 on v10

--- a/solution.py
+++ b/solution.py
@@ -170,11 +170,11 @@
     seg_ref,
     allow_ref,
     segv_ref,
-    unpack_in,
-    recv_in,
-    gr_in,
-    gt_in,
-    kv_in,
+    unpack_ref,
+    recv_ref,
+    gr_ref,
+    gt_ref,
+    kv_ref,
     keep_ref,
     send_ref,
     sg_ref,
@@ -190,66 +190,16 @@
     sg_s,
     list_s,
     sent,
-    kv_ref,
-    unpack_ref,
-    recv_ref,
-    gr_ref,
-    gt_ref,
-    arrived,
 ):
     shard = info_ref[0]
     core = info_ref[1]
     base = jnp.maximum(shard - BACK, 0)
-    copies = fetch_all(
-        (kv_in, unpack_in, recv_in, gr_in, gt_in),
-        (kv_ref, unpack_ref, recv_ref, gr_ref, gt_ref),
-        arrived,
-    )
     acc_s[...] = jnp.zeros_like(acc_s)
-    copies[0].wait()
 
     def query_block(half, carry):
         qb = shard * 2 + half
         q_seg = segv_ref[pl.ds(qb, 1), :]
         q_last = seg_ref[qb * BLK + BLK - 1]
-
-        def on_block(kb, count):
-            list_s[count] = kb
-            src = block_rows(kb - 2 * base)
-            dst = block_rows(count)
-            k_s[dst, :] = kv_ref[src, :HEAD_SIZE]
-            v_s[dst, :] = kv_ref[src, HEAD_SIZE:]
-            whole = jnp.logical_and(kb < qb, seg_ref[kb * BLK] == q_last)
-
-            @pl.when(whole)
-            def _():
-                bias_s[dst, :] = jnp.zeros((BLK, BLK), F32)
-
-            @pl.when(jnp.logical_not(whole))
-            def _():
-                k_seg = jnp.broadcast_to(segv_ref[pl.ds(kb, 1), :].astype(F32), (BLK, BLK)).T
-                k_pos = kb * BLK + iota((BLK, BLK), 0)
-                q_pos = qb * BLK + iota((BLK, BLK), 1)
-                ok = (k_seg == q_seg.astype(F32)) & (k_pos <= q_pos)
-                bias_s[dst, :] = jnp.where(ok, 0.0, NEG_FILL)
-
-        count, wide, narrow = visible_blocks(qb, seg_ref, allow_ref, on_block)
-
-        def fill(n, c):
-            list_s[n] = 2 * SHARDS
-            dst = block_rows(n)
-            k_s[dst, :] = jnp.zeros((BLK, HEAD_SIZE), BF16)
-            v_s[dst, :] = jnp.zeros((BLK, HEAD_SIZE), BF16)
-            bias_s[dst, :] = jnp.full((BLK, BLK), NEG_FILL, F32)
-            return c
-
-        lax.fori_loop(count, wide * WIDE + narrow * NARROW, fill, 0)
-
-        @pl.when(half == 0)
-        def _():
-            for copy in copies[1:]:
-                copy.wait()
-
         picks = unpack_ref[block_rows(half), :]
         for pair in range(LOCAL_HEADS // 2):
             q_two = dot(picks, recv_ref[:, pair * 256 : (pair + 1) * 256])
@@ -258,6 +208,38 @@
                 q_one = q_two[:, i * HEAD_SIZE : (i + 1) * HEAD_SIZE]
                 qr_s[mine, :] = q_one.astype(BF16)
                 qt_s[:, mine] = q_one.T.astype(BF16)
+
+        def on_block(kb, count):
+            list_s[count] = kb
+            src = block_rows(kb - 2 * base)
+            dst = block_rows(count)
+            k_s[dst, :] = kv_ref[src, :HEAD_SIZE]
+            v_s[dst, :] = kv_ref[src, HEAD_SIZE:]
+            whole = jnp.logical_and(kb < qb, seg_ref[kb * BLK] == q_last)
+
+            @pl.when(whole)
+            def _():
+                bias_s[dst, :] = jnp.zeros((BLK, BLK), F32)
+
+            @pl.when(jnp.logical_not(whole))
+            def _():
+                k_seg = jnp.broadcast_to(segv_ref[pl.ds(kb, 1), :].astype(F32), (BLK, BLK)).T
+                k_pos = kb * BLK + iota((BLK, BLK), 0)
+                q_pos = qb * BLK + iota((BLK, BLK), 1)
+                ok = (k_seg == q_seg.astype(F32)) & (k_pos <= q_pos)
+                bias_s[dst, :] = jnp.where(ok, 0.0, NEG_FILL)
+
+        count, wide, narrow = visible_blocks(qb, seg_ref, allow_ref, on_block)
+
+        def fill(n, c):
+            list_s[n] = 2 * SHARDS
+            dst = block_rows(n)
+            k_s[dst, :] = jnp.zeros((BLK, HEAD_SIZE), BF16)
+            v_s[dst, :] = jnp.zeros((BLK, HEAD_SIZE), BF16)
+            bias_s[dst, :] = jnp.full((BLK, BLK), NEG_FILL, F32)
+            return c
+
+        lax.fori_loop(count, wide * WIDE + narrow * NARROW, fill, 0)
 
         def first_pass(start, blocks, slot, state):
             top, total, weighed = state
@@ -416,7 +398,7 @@
 def call_permute(info, grad, own, mine, theirs):
     return pl.pallas_call(
         permute_kernel,
-        in_specs=[SMEM] + [HBM] * (2 * RING + 2),
+        in_specs=[SMEM] + [ANY] * (2 * RING + 2),
         out_specs=[VMEM] * 4,
         out_shape=[
             jax.ShapeDtypeStruct((WINDOW * TOK, 2 * HEAD_SIZE), BF16),
@@ -427,7 +409,7 @@
         scratch_shapes=[pltpu.VMEM((SHARDS * SLOTS, TOK), F32)]
         + [pltpu.VMEM(x.shape, x.dtype) for x in (grad, own, *mine, *theirs)]
         + [pltpu.SemaphoreType.DMA((2 * RING + 2,))],
-        compiler_params=pltpu.CompilerParams(vmem_limit_bytes=VMEM_LIMIT),
+        compiler_params=pltpu.CompilerParams(vmem_limit_bytes=12 * 2**20),
         name="permute",
     )(info, grad, own, *mine, *theirs)
 
@@ -435,7 +417,7 @@
 def call_attention(info, segments, allow, unpack, q_recv, gr, gt, kv_window):
     return pl.pallas_call(
         attention_kernel,
-        in_specs=[SMEM, SMEM, SMEM, VMEM] + [HBM] * 5,
+        in_specs=[SMEM, SMEM, SMEM] + [VMEM] * 6,
         out_specs=[VMEM, VMEM, HBM],
         out_shape=[
             jax.ShapeDtypeStruct((SHARDS * TOK, HEAD_SIZE), BF16),
@@ -455,10 +437,8 @@
             pltpu.VMEM((3, WIDE * BLK, LANES), BF16),
             pltpu.SMEM((MOST_BLOCKS,), jnp.int32),
             pltpu.SemaphoreType.DMA((3,)),
-        ]
-        + [pltpu.VMEM(x.shape, x.dtype) for x in (kv_window, unpack, q_recv, gr, gt)]
-        + [pltpu.SemaphoreType.DMA((5,))],
-        compiler_params=pltpu.CompilerParams(vmem_limit_bytes=VMEM_LIMIT),
+        ],
+        compiler_params=pltpu.CompilerParams(vmem_limit_bytes=40 * 2**20),
         name="attention",
     )(info, segments, allow, segments.reshape(-1, BLK), unpack, q_recv, gr, gt, kv_window)
 

time: 142 us -> 140 us (0.986); the launches traced: 142 us -> 138 us
  local copies, waits for them, and re-layouts: 4.41 us -> 14.5 us
  waiting for transfers between devices: 54.8 us -> 49.5 us
  Pallas kernels: 23.7 us -> 18.8 us
  other arithmetic: 4.19 us -> 2.46 us
  starting transfers between devices: 54.1 us -> 52.4 us
    unnamed x22 -> x40, local copies, waits for them, and re-layouts: 1.88 us -> 12 us
    all_to_all x1, waiting for transfers between devices: 14.8 us -> 8.96 us  [on_device(): lax.all_to_all(q_send, ('z', 'x'), split_axis=0, concat_axis=0, tiled=True)]
    pallas_call x2, Pallas kernels: 14.2 us -> 9.24 us  [the longest x1 5.95 us: call_attention(): pl.pallas_call(attention_kernel, in_specs=[SMEM, SMEM, SMEM] + [VMEM] * 6...]
    all_to_all x1, starting transfers between devices: 18.6 us -> 17 us  [on_device(): lax.all_to_all(part.reshape(SHARDS * tp_size, rows, HEAD_SIZE), ('z', 'x'...]
  transfers between devices with their start and end apart: 13 -> 13, of which waited for: 8 -> 8; matrix products, arithmetic and copies ran while one was open for 2% -> 1% of each run, Pallas kernels for 9% -> 8%
where the time goes in v11:
time: 140 us; the launch traced here: 138 us
  starting transfers between devices  52.4 us (37%)
  waiting for transfers between devices  49.5 us (35%)
  Pallas kernels  18.8 us (13%)
  local copies, waits for them, and re-layouts  14.5 us (10%)
  other arithmetic  2.46 us (2%)
    all_to_all x1, waiting for transfers between devices, on_device(): lax.all_to_all(part.reshape(SHARDS * tp_size, rows, HEAD_SIZE), ('z', 'x'...  27.4 us
    all_to_all x1, starting transfers between devices, on_device(): lax.all_to_all(part.reshape(SHARDS * tp_size, rows, HEAD_SIZE), ('z', 'x'...  17 us
    unnamed x40, local copies, waits for them, and re-layouts  12 us
    all_to_all x1, waiting for transfers between devices, on_device(): lax.all_to_all(q_send, ('z', 'x'), split_axis=0, concat_axis=0, tiled=True)  8.96 us
    all_to_all x1, starting transfers between devices, on_device(): lax.all_to_all(g_send, 'tp', split_axis=0, concat_axis=0, tiled=True)  7.06 us
    ppermute x1, starting transfers between devices, on_device(): first = lax.ppermute(own, ('z', 'x', 'tp'), around(1))  6.54 us
    all_to_all x1, starting transfers between devices, on_device(): lax.all_to_all(q_send, ('z', 'x'), split_axis=0, concat_axis=0, tiled=True)  6.03 us
    pallas_call x1, Pallas kernels, call_attention(): pl.pallas_call(attention_kernel, in_specs=[SMEM, SMEM, SMEM] + [VMEM] * 6...  5.95 us
  transfers between devices with their start and end apart: 13, of which 8 were waited for; matrix products, arithmetic and copies ran while one was open for 1% of the time, Pallas kernels for 8%

profile of v11, /device:TPU:1, one launch (start us, length us, event | category | flops | bytes accessed | tf_op | source)
XLA Modules:
  0.0 138.4 jit_solution(16871346657853376409)
XLA Ops:
  0.6 2.2 %stage.1 = bf16[272,256]{1,0:T(8,128)(2,1)} custom-call(s32[1,256]{1,0:T(1,128)} %bitcast.37, bf16[2,256,1024]{2,1,0:T(8,128)(2,1)} %kv_ref.1), custom_call_target="tpu_custom_call" | custom-call | tf_op jit(solution)/shard_map/stage/pallas_call | solution.py:474
  2.9 2.1 %collective-permute-start = (bf16[272,256]{1,0:T(8,128)(2,1)}, bf16[272,256]{1,0:T(8,128)(2,1)S(1)}, u32[]{:S(2)}, u32[]{:S(2)}) collective-permute-start(bf16[272,256]{1,0:T(8,128)(2,1)} %stage.1), channel_id=1, source_target_pairs={{0,16},{16,0},{1,17},{17,1},{2,18},{18,2},{3,19},{19,3},{4,20},{20... | collective-permute-start | bytes 417800 | tf_op jit(solution)/shard_map/ppermute | solution.py:482
  5.0 1.9 %copy.16 = bf16[2,16,8,1024]{3,2,0,1:T(8,128)(2,1)} copy(bf16[2,16,8,1024]{3,2,1,0:T(8,128)(2,1)} %bitcast.33) | data formatting | bytes 1048576 | tf_op jit(solution)/shard_map/reshape | solution.py:484
  6.9 0.8 collective-permute-done
  7.6 0.9 pad_maximum_fusion.refs_1_
  8.6 6.5 %collective-permute-start.1 = (bf16[2,272,256]{2,1,0:T(8,128)(2,1)S(1)}, bf16[2,272,256]{2,1,0:T(8,128)(2,1)S(1)}, u32[]{:S(2)}, u32[]{:S(2)}) collective-permute-start(bf16[2,272,256]{2,1,0:T(8,128)(2,1)S(1)} %pad_maximum_fusion.refs_1_), channel_id=1, source_target_pairs={{0,32},{1,225},{2,34},{3,227},{4,36},{5,229},{6,38},{7,231},{8,40}... | collective-permute-start | bytes 835592 | tf_op jit(solution)/shard_map/ppermute | solution.py:496
  15.1 3.5 %collective-permute-done.1.refs_2_ = bf16[2,272,256]{2,1,0:T(8,128)(2,1)S(1)} collective-permute-done((bf16[2,272,256]{2,1,0:T(8,128)(2,1)S(1)}, bf16[2,272,256]{2,1,0:T(8,128)(2,1)S(1)}, u32[]{:S(2)}, u32[]{:S(2)}) %collective-permute-start.1) | collective-permute-done | bytes 278560 | tf_op jit(solution)/shard_map/ppermute | solution.py:496
  18.6 3.1 %collective-permute-start.2 = (bf16[2,272,256]{2,1,0:T(8,128)(2,1)S(1)}, bf16[2,272,256]{2,1,0:T(8,128)(2,1)S(1)}, u32[]{:S(2)}, u32[]{:S(2)}) collective-permute-start(bf16[2,272,256]{2,1,0:T(8,128)(2,1)S(1)} %collective-permute-done.1.refs_2_), channel_id=1, source_target_pairs={{0,32},{1,225},{2,34},{3,227},{4,36},{5,229},{6,38},{7,231},{8,40}... | collective-permute-start | bytes 835592 | tf_op jit(solution)/shard_map/ppermute | solution.py:497
  21.7 7.1 %all-to-all-start = ((bf16[16,16,1024]{2,1,0:T(8,128)(2,1)}), bf16[16,16,1024]{2,1,0:T(8,128)(2,1)S(1)}, u32[]{:S(2)}, u32[]{:S(2)}) async-start(bf16[16,16,1024]{2,1,0:T(8,128)(2,1)} %bitcast.25), calls=%async_computation | async-start | bytes 1048576 | tf_op jit(solution)/shard_map/all_to_all | solution.py:502
  28.8 2.7 %collective-permute-start.3 = (bf16[2,272,256]{2,1,0:T(8,128)(2,1)S(1)}, bf16[2,272,256]{2,1,0:T(8,128)(2,1)S(1)}, u32[]{:S(2)}, u32[]{:S(2)}) collective-permute-start(bf16[2,272,256]{2,1,0:T(8,128)(2,1)S(1)} %collective-permute-done.2.refs_3_), channel_id=1, source_target_pairs={{0,32},{1,225},{2,34},{3,227},{4,36},{5,229},{6,38},{7,231},{8,40}... | collective-permute-start | bytes 835592 | tf_op jit(solution)/shard_map/ppermute | solution.py:498
  31.5 1.1 collective-permute-start.4
  32.5 2.6 %pack.1 = bf16[512,1024]{1,0:T(8,128)(2,1)} custom-call(s32[1,256]{1,0:T(1,128)} %bitcast.38, bf16[256,1024]{1,0:T(8,128)(2,1)} %rows_ref.1), custom_call_target="tpu_custom_call" | custom-call | tf_op jit(solution)/shard_map/pack/pallas_call | solution.py:504
  35.1 2.8 %collective-permute-done.4.refs_5_ = bf16[272,256]{1,0:T(8,128)(2,1)S(1)} collective-permute-done((bf16[272,256]{1,0:T(8,128)(2,1)S(1)}, bf16[272,256]{1,0:T(8,128)(2,1)S(1)}, u32[]{:S(2)}, u32[]{:S(2)}) %collective-permute-start.4) | collective-permute-done | bytes 139296 | tf_op jit(solution)/shard_map/ppermute | solution.py:500
  37.9 2.1 %all-to-all-done = bf16[16,16,1024]{2,1,0:T(8,128)(2,1)S(1)} async-done(((bf16[16,16,1024]{2,1,0:T(8,128)(2,1)}), bf16[16,16,1024]{2,1,0:T(8,128)(2,1)S(1)}, u32[]{:S(2)}, u32[]{:S(2)}) %all-to-all-start) | async-done | bytes 524320 | tf_op jit(solution)/shard_map/all_to_all | solution.py:502
  40.1 6.0 %all-to-all-start.1 = ((bf16[16,32,1024]{2,1,0:T(8,128)(2,1)}), bf16[16,32,1024]{2,1,0:T(8,128)(2,1)S(1)}, u32[]{:S(2)}, u32[]{:S(2)}) async-start(bf16[16,32,1024]{2,1,0:T(8,128)(2,1)} %bitcast.30), calls=%async_computation.1 | async-start | bytes 2097152 | tf_op jit(solution)/shard_map/all_to_all | solution.py:513
  46.1 1.5 %collective-permute-start.5 = (bf16[2,272,256]{2,1,0:T(8,128)(2,1)S(1)}, bf16[2,272,256]{2,1,0:T(8,128)(2,1)S(1)}, u32[]{:S(2)}, u32[]{:S(2)}) collective-permute-start(bf16[2,272,256]{2,1,0:T(8,128)(2,1)S(1)} %collective-permute-done.1.refs_2_), channel_id=1, source_target_pairs={{0,1},{1,0},{2,3},{3,2},{4,5},{5,4},{6,7},{7,6},{8,9},{9,8},{10,11... | collective-permute-start | bytes 835592 | tf_op jit(solution)/shard_map/ppermute | solution.py:512
  47.7 0.1 collective-permute-start.6
  47.8 0.4 collective-permute-start.7
  48.2 0.1 collective-permute-start.8
  48.3 0.1 pad_add_fusion.info_ref
  48.3 1.6 %collective-permute-done.8.refs_9_ = bf16[272,256]{1,0:T(8,128)(2,1)} collective-permute-done((bf16[272,256]{1,0:T(8,128)(2,1)S(1)}, bf16[272,256]{1,0:T(8,128)(2,1)}, u32[]{:S(2)}, u32[]{:S(2)}) %collective-permute-start.8) | collective-permute-done | bytes 139296 | tf_op jit(solution)/shard_map/ppermute | solution.py:512
  50.0 0.7 copy-done.9
  50.7 0.7 copy-done.11
  51.4 0.9 copy-done.6
  52.4 1.0 copy-done.8
  53.3 1.0 copy-done.10
  54.3 1.0 copy-done.12
  55.2 0.9 copy-done.17
  56.1 3.3 %permute.1 = (bf16[2560,256]{1,0:T(8,128)(2,1)S(1)}, bf16[256,512]{1,0:T(8,128)(2,1)S(1)}, bf16[2,1024,128]{2,1,0:T(8,128)(2,1)S(1)}, bf16[2,128,1024]{2,1,0:T(8,128)(2,1)S(1)}) custom-call(s32[2]{0:T(128)S(1)} %pad_add_fusion.info_ref, bf16[256,1024]{1,0:T(8,128)(2,1)S(1)} %bitcast.28, bf16[2,272,256]{2,1,0:T(8,128)(2,1)S(1)} %pad_maximum_fusion.refs_1_, ...), custom_call_target="tpu_custom_call" | custom-call | tf_op jit(solution)/shard_map/permute/pallas_call | solution.py:399
  59.4 0.0 copy-start.1
  59.5 0.8 copy-done.1
  60.2 0.8 copy-done.3
  61.0 0.7 copy-done.13
  61.8 9.0 %all-to-all-done.1 = bf16[16,32,1024]{2,1,0:T(8,128)(2,1)S(1)} async-done(((bf16[16,32,1024]{2,1,0:T(8,128)(2,1)}), bf16[16,32,1024]{2,1,0:T(8,128)(2,1)S(1)}, u32[]{:S(2)}, u32[]{:S(2)}) %all-to-all-start.1) | async-done | bytes 1048608 | tf_op jit(solution)/shard_map/all_to_all | solution.py:513
  70.7 1.0 copy-done.2
  71.8 1.0 copy-done.4
  72.8 0.9 copy-done.14
  73.8 5.9 %attention.1 = (bf16[4096,128]{1,0:T(8,128)(2,1)S(1)}, bf16[4096,128]{1,0:T(8,128)(2,1)S(1)}, bf16[2,2560,1024]{2,1,0:T(8,128)(2,1)}) custom-call(s32[2]{0:T(128)S(1)} %pad_add_fusion.info_ref, s32[4096]{0:T(1024)S(1)} %copy-done.15, s32[32,32]{1,0:T(8,128)S(1)} %copy-done.18, s32[32,128]{1,0:T(8,128)S(1)} %bitcast.29, bf16[256,512]{1,0:T(8,128)(2,1)S(1)} %copy-done.14, ...), custom_call_target="tpu_custom_call" | custom-call | tf_op jit(solution)/shard_map/attention/pallas_call | solution.py:418
  79.7 0.0 copy-start.19
  79.7 0.5 copy-done.19
  80.2 4.7 %collective-permute-start.9 = (bf16[4096,128]{1,0:T(8,128)(2,1)S(1)}, bf16[4096,128]{1,0:T(8,128)(2,1)S(1)}, u32[]{:S(2)}, u32[]{:S(2)}) collective-permute-start(bf16[4096,128]{1,0:T(8,128)(2,1)S(1)} %get-tuple-element.32), channel_id=1, source_target_pairs={{0,1},{1,0},{2,3},{3,2},{4,5},{5,4},{6,7},{7,6},{8,9},{9,8},{10,11... | collective-permute-start | bytes 3145736 | tf_op jit(solution)/shard_map/ppermute | solution.py:518
  84.9 2.3 %collective-permute-done.9 = bf16[4096,128]{1,0:T(8,128)(2,1)S(1)} collective-permute-done((bf16[4096,128]{1,0:T(8,128)(2,1)S(1)}, bf16[4096,128]{1,0:T(8,128)(2,1)S(1)}, u32[]{:S(2)}, u32[]{:S(2)}) %collective-permute-start.9) | collective-permute-done | bytes 1048608 | tf_op jit(solution)/shard_map/ppermute | solution.py:518
  87.2 1.3 add_convert_fusion
  88.5 17.0 %all-to-all-start.2 = ((bf16[256,16,128]{2,1,0:T(8,128)(2,1)}), bf16[256,16,128]{2,1,0:T(8,128)(2,1)S(1)}, u32[]{:S(2)}, u32[]{:S(2)}) async-start(bf16[256,16,128]{2,1,0:T(8,128)(2,1)} %bitcast.11), calls=%async_computation.2 | async-start | bytes 2097152 | tf_op jit(solution)/shard_map/all_to_all | solution.py:522
  105.5 4.7 %query_grad.1 = bf16[256,1024]{1,0:T(8,128)(2,1)} custom-call(s32[2]{0:T(128)} %copy-done.19, s32[4096]{0:T(1024)} %seg_ref.3, s32[32,32]{1,0:T(8,128)} %allow_ref.3, bf16[2560,256]{1,0:T(8,128)(2,1)} %copy-done, bf16[2,2560,1024]{2,1,0:T(8,128)(2,1)} %get-tuple-element.35.sg_ref), custom_call_target="tpu_custom_call" | custom-call | flops 1073741824 | bytes 12582912 | tf_op jit(solution)/shard_map/query_grad/pallas_call | solution.py:447
  110.2 27.4 %all-to-all-done.2 = bf16[256,16,128]{2,1,0:T(8,128)(2,1)S(1)} async-done(((bf16[256,16,128]{2,1,0:T(8,128)(2,1)}), bf16[256,16,128]{2,1,0:T(8,128)(2,1)S(1)}, u32[]{:S(2)}, u32[]{:S(2)}) %all-to-all-start.2) | async-done | bytes 1048608 | tf_op jit(solution)/shard_map/all_to_all | solution.py:522
  137.6 0.1 reduce_sum.12
  137.7 0.6 copy.17
  (30 shorter events, 0.1 us)
Async XLA Ops:
  2.9 4.8 %collective-permute-start = (bf16[272,256]{1,0:T(8,128)(2,1)}, bf16[272,256]{1,0:T(8,128)(2,1)S(1)}, u32[]{:S(2)}, u32[]{:S(2)}) collective-permute-start(bf16[272,256]{1,0:T(8,128)(2,1)} %stage.1), channel_id=1, source_target_pairs={{0,16},{16,0},{1,17},{17,1},{2,18},{18,2},{3,19},{19,3},{4,20},{20... | collective-permute-start | bytes 417800 | tf_op jit(solution)/shard_map/ppermute | solution.py:482
  8.6 10.0 %collective-permute-start.1 = (bf16[2,272,256]{2,1,0:T(8,128)(2,1)S(1)}, bf16[2,272,256]{2,1,0:T(8,128)(2,1)S(1)}, u32[]{:S(2)}, u32[]{:S(2)}) collective-permute-start(bf16[2,272,256]{2,1,0:T(8,128)(2,1)S(1)} %pad_maximum_fusion.refs_1_), channel_id=1, source_target_pairs={{0,32},{1,225},{2,34},{3,227},{4,36},{5,229},{6,38},{7,231},{8,40}... | collective-permute-start | bytes 835592 | tf_op jit(solution)/shard_map/ppermute | solution.py:496
  18.6 27.5 %copy-start.5 = (bf16[2,272,256]{2,1,0:T(8,128)(2,1)}, bf16[2,272,256]{2,1,0:T(8,128)(2,1)S(1)}, u32[]{:S(2)}) copy-start(bf16[2,272,256]{2,1,0:T(8,128)(2,1)S(1)} %collective-permute-done.1.refs_2_) | copy-start | bytes 835588
  18.6 10.2 %collective-permute-start.2 = (bf16[2,272,256]{2,1,0:T(8,128)(2,1)S(1)}, bf16[2,272,256]{2,1,0:T(8,128)(2,1)S(1)}, u32[]{:S(2)}, u32[]{:S(2)}) collective-permute-start(bf16[2,272,256]{2,1,0:T(8,128)(2,1)S(1)} %collective-permute-done.1.refs_2_), channel_id=1, source_target_pairs={{0,32},{1,225},{2,34},{3,227},{4,36},{5,229},{6,38},{7,231},{8,40}... | collective-permute-start | bytes 835592 | tf_op jit(solution)/shard_map/ppermute | solution.py:497
  21.7 18.4 %all-to-all-start = ((bf16[16,16,1024]{2,1,0:T(8,128)(2,1)}), bf16[16,16,1024]{2,1,0:T(8,128)(2,1)S(1)}, u32[]{:S(2)}, u32[]{:S(2)}) async-start(bf16[16,16,1024]{2,1,0:T(8,128)(2,1)} %bitcast.25), calls=%async_computation | async-start | bytes 1048576 | tf_op jit(solution)/shard_map/all_to_all | solution.py:502
  28.8 9.1 %collective-permute-start.3 = (bf16[2,272,256]{2,1,0:T(8,128)(2,1)S(1)}, bf16[2,272,256]{2,1,0:T(8,128)(2,1)S(1)}, u32[]{:S(2)}, u32[]{:S(2)}) collective-permute-start(bf16[2,272,256]{2,1,0:T(8,128)(2,1)S(1)} %collective-permute-done.2.refs_3_), channel_id=1, source_target_pairs={{0,32},{1,225},{2,34},{3,227},{4,36},{5,229},{6,38},{7,231},{8,40}... | collective-permute-start | bytes 835592 | tf_op jit(solution)/shard_map/ppermute | solution.py:498
  31.5 6.5 %collective-permute-start.4 = (bf16[272,256]{1,0:T(8,128)(2,1)S(1)}, bf16[272,256]{1,0:T(8,128)(2,1)S(1)}, u32[]{:S(2)}, u32[]{:S(2)}) collective-permute-start(bf16[272,256]{1,0:T(8,128)(2,1)S(1)} %dynamic-slice_bitcast_fusion), channel_id=1, source_target_pairs={{0,64},{1,193},{2,66},{3,195},{4,68},{5,197},{6,70},{7,199},{8,72}... | collective-permute-start | bytes 417800 | tf_op jit(solution)/shard_map/ppermute | solution.py:500
  37.9 13.5 %copy-start.16 = (bf16[272,256]{1,0:T(8,128)(2,1)}, bf16[272,256]{1,0:T(8,128)(2,1)S(1)}, u32[]{:S(2)}) copy-start(bf16[272,256]{1,0:T(8,128)(2,1)S(1)} %collective-permute-done.4.refs_5_) | copy-start | bytes 417796
  37.9 13.5 %copy-start.7 = (bf16[2,272,256]{2,1,0:T(8,128)(2,1)}, bf16[2,272,256]{2,1,0:T(8,128)(2,1)S(1)}, u32[]{:S(2)}) copy-start(bf16[2,272,256]{2,1,0:T(8,128)(2,1)S(1)} %collective-permute-done.3.refs_4_) | copy-start | bytes 835588
  40.1 30.6 %copy-start.15 = (s32[4096]{0:T(1024)S(1)}, s32[4096]{0:T(1024)}, u32[]{:S(2)}) copy-start(s32[4096]{0:T(1024)} %seg_ref.3) | copy-start | bytes 49156
  40.1 30.6 %copy-start.18 = (s32[32,32]{1,0:T(8,128)S(1)}, s32[32,32]{1,0:T(8,128)}, u32[]{:S(2)}) copy-start(s32[32,32]{1,0:T(8,128)} %allow_ref.3) | copy-start | bytes 12292
  40.1 30.6 %all-to-all-start.1 = ((bf16[16,32,1024]{2,1,0:T(8,128)(2,1)}), bf16[16,32,1024]{2,1,0:T(8,128)(2,1)S(1)}, u32[]{:S(2)}, u32[]{:S(2)}) async-start(bf16[16,32,1024]{2,1,0:T(8,128)(2,1)} %bitcast.30), calls=%async_computation.1 | async-start | bytes 2097152 | tf_op jit(solution)/shard_map/all_to_all | solution.py:513
  46.1 3.9 %collective-permute-start.5 = (bf16[2,272,256]{2,1,0:T(8,128)(2,1)S(1)}, bf16[2,272,256]{2,1,0:T(8,128)(2,1)S(1)}, u32[]{:S(2)}, u32[]{:S(2)}) collective-permute-start(bf16[2,272,256]{2,1,0:T(8,128)(2,1)S(1)} %collective-permute-done.1.refs_2_), channel_id=1, source_target_pairs={{0,1},{1,0},{2,3},{3,2},{4,5},{5,4},{6,7},{7,6},{8,9},{9,8},{10,11... | collective-permute-start | bytes 835592 | tf_op jit(solution)/shard_map/ppermute | solution.py:512
  47.7 3.0 %collective-permute-start.6 = (bf16[2,272,256]{2,1,0:T(8,128)(2,1)S(1)}, bf16[2,272,256]{2,1,0:T(8,128)(2,1)S(1)}, u32[]{:S(2)}, u32[]{:S(2)}) collective-permute-start(bf16[2,272,256]{2,1,0:T(8,128)(2,1)S(1)} %collective-permute-done.2.refs_3_), channel_id=1, source_target_pairs={{0,1},{1,0},{2,3},{3,2},{4,5},{5,4},{6,7},{7,6},{8,9},{9,8},{10,11... | collective-permute-start | bytes 835592 | tf_op jit(solution)/shard_map/ppermute | solution.py:512
  47.8 3.6 %collective-permute-start.7 = (bf16[2,272,256]{2,1,0:T(8,128)(2,1)S(1)}, bf16[2,272,256]{2,1,0:T(8,128)(2,1)}, u32[]{:S(2)}, u32[]{:S(2)}) collective-permute-start(bf16[2,272,256]{2,1,0:T(8,128)(2,1)S(1)} %collective-permute-done.3.refs_4_), channel_id=1, source_target_pairs={{0,1},{1,0},{2,3},{3,2},{4,5},{5,4},{6,7},{7,6},{8,9},{9,8},{10,11... | collective-permute-start | bytes 835592 | tf_op jit(solution)/shard_map/ppermute | solution.py:512
  48.2 1.8 %collective-permute-start.8 = (bf16[272,256]{1,0:T(8,128)(2,1)S(1)}, bf16[272,256]{1,0:T(8,128)(2,1)}, u32[]{:S(2)}, u32[]{:S(2)}) collective-permute-start(bf16[272,256]{1,0:T(8,128)(2,1)S(1)} %collective-permute-done.4.refs_5_), channel_id=1, source_target_pairs={{0,1},{1,0},{2,3},{3,2},{4,5},{5,4},{6,7},{7,6},{8,9},{9,8},{10,11... | collective-permute-start | bytes 417800 | tf_op jit(solution)/shard_map/ppermute | solution.py:512
  50.0 0.7 copy-start.9
  50.7 0.7 copy-start.11
  51.4 1.0 copy-start.6
  52.4 1.0 copy-start.8
  53.3 1.0 copy-start.10
  54.3 1.0 copy-start.12
  55.2 0.9 copy-start.17
  59.4 0.8 copy-start.1
  60.2 0.8 copy-start.3
  61.0 0.7 copy-start.13
  61.8 26.8 %copy-start = (bf16[2560,256]{1,0:T(8,128)(2,1)}, bf16[2560,256]{1,0:T(8,128)(2,1)S(1)}, u32[]{:S(2)}) copy-start(bf16[2560,256]{1,0:T(8,128)(2,1)S(1)} %get-tuple-element.30.kv_ref.kv_in) | copy-start | bytes 3932164
  70.7 1.0 copy-start.2
  71.8 1.0 copy-start.4
  72.8 0.9 copy-start.14
  79.7 0.5 copy-start.19
  80.2 7.0 %collective-permute-start.9 = (bf16[4096,128]{1,0:T(8,128)(2,1)S(1)}, bf16[4096,128]{1,0:T(8,128)(2,1)S(1)}, u32[]{:S(2)}, u32[]{:S(2)}) collective-permute-start(bf16[4096,128]{1,0:T(8,128)(2,1)S(1)} %get-tuple-element.32), channel_id=1, source_target_pairs={{0,1},{1,0},{2,3},{3,2},{4,5},{5,4},{6,7},{7,6},{8,9},{9,8},{10,11... | collective-permute-start | bytes 3145736 | tf_op jit(solution)/shard_map/ppermute | solution.py:518
  88.5 49.1 %all-to-all-start.2 = ((bf16[256,16,128]{2,1,0:T(8,128)(2,1)}), bf16[256,16,128]{2,1,0:T(8,128)(2,1)S(1)}, u32[]{:S(2)}, u32[]{:S(2)}) async-start(bf16[256,16,128]{2,1,0:T(8,128)(2,1)} %bitcast.11), calls=%async_computation.2 | async-start | bytes 2097152 | tf_op jit(solution)/shard_map/all_to_all | solution.py:522

commit v12 on v11

--- a/solution.py
+++ b/solution.py
@@ -95,12 +95,11 @@
 
 
 def permute_kernel(info_ref, *refs):
-    count = 2 * RING + 2
-    out_ref, unpack_ref, gr_ref, gt_ref, slots_s = refs[count : count + 5]
-    grad_ref, own_ref = refs[count + 5 : count + 7]
-    mine = refs[count + 7 : count + 7 + RING]
-    theirs = refs[count + 7 + RING : count + 7 + 2 * RING]
-    for copy in fetch_all(refs[:count], refs[count + 5 : -1], refs[-1]):
+    count = 2 * RING + 1
+    out_ref, unpack_ref, slots_s = refs[count : count + 3]
+    buffers, arrived = refs[count + 3 : -1], refs[-1]
+    own_ref, mine, theirs = buffers[0], buffers[1 : 1 + RING], buffers[1 + RING :]
+    for copy in fetch_all(refs[:count], buffers, arrived):
         copy.wait()
     shard = info_ref[0]
     core = info_ref[1]
@@ -124,11 +123,6 @@
         rows = pl.ds(pl.multiple_of(source * SLOTS, SLOTS), SLOTS)
         slots_s[rows, :] = (landing == lane + 1.0).astype(F32)
     unpack_ref[...] = slots_s[...].T.astype(BF16)
-    for half in range(2):
-        for h in range(LOCAL_HEADS):
-            block = grad_ref[half * BLK : (half + 1) * BLK, h * HEAD_SIZE : (h + 1) * HEAD_SIZE]
-            gr_ref[half, h * BLK : (h + 1) * BLK, :] = block
-            gt_ref[half, :, h * BLK : (h + 1) * BLK] = block.astype(F32).T.astype(BF16)
 
     def one_shard(i, carry):
         rows = iota((TOK, TOK), 0).astype(F32)
@@ -172,14 +166,15 @@
     segv_ref,
     unpack_ref,
     recv_ref,
-    gr_ref,
-    gt_ref,
+    grad_ref,
     kv_ref,
     keep_ref,
     send_ref,
     sg_ref,
     qr_s,
     qt_s,
+    gr_s,
+    gt_s,
     k_s,
     v_s,
     bias_s,
@@ -208,6 +203,9 @@
                 q_one = q_two[:, i * HEAD_SIZE : (i + 1) * HEAD_SIZE]
                 qr_s[mine, :] = q_one.astype(BF16)
                 qt_s[:, mine] = q_one.T.astype(BF16)
+                g_one = grad_ref[block_rows(half), pl.ds((2 * pair + i) * HEAD_SIZE, HEAD_SIZE)]
+                gr_s[mine, :] = g_one
+                gt_s[:, mine] = g_one.astype(F32).T.astype(BF16)
 
         def on_block(kb, count):
             list_s[count] = kb
@@ -249,7 +247,7 @@
             new_top = jnp.maximum(top, jnp.max(scores, axis=0, keepdims=True))
             factor = jnp.exp2((top - new_top) * EXP2_SCALE)
             e = jnp.exp2((scores - new_top) * EXP2_SCALE)
-            dp = dot(v_s[rows, :], gt_ref[half])
+            dp = dot(v_s[rows, :], gt_s[...])
             e_s[rows, :] = e
             dp_s[rows, :] = dp
             top_s[slot] = new_top
@@ -285,7 +283,7 @@
             score_grad = (weights * (dp_s[rows, :] - out_dot)).astype(BF16)
             sg_s[buffer, : blocks * BLK, :] = score_grad
             copy_out(start, blocks, buffer).start()
-            value_terms = dot(weights.astype(BF16), gr_ref[half])
+            value_terms = dot(weights.astype(BF16), gr_s[...])
             key_terms = dot(score_grad, qr_s[...])
             for n in range(blocks):
                 dst = block_rows(list_s[start + n])
@@ -395,29 +393,27 @@
 HBM = pl.BlockSpec(memory_space=pltpu.HBM)
 
 
-def call_permute(info, grad, own, mine, theirs):
+def call_permute(info, own, mine, theirs):
     return pl.pallas_call(
         permute_kernel,
-        in_specs=[SMEM] + [ANY] * (2 * RING + 2),
-        out_specs=[VMEM] * 4,
+        in_specs=[SMEM] + [ANY] * (2 * RING + 1),
+        out_specs=[VMEM] * 2,
         out_shape=[
             jax.ShapeDtypeStruct((WINDOW * TOK, 2 * HEAD_SIZE), BF16),
             jax.ShapeDtypeStruct((TOK, SHARDS * SLOTS), BF16),
-            jax.ShapeDtypeStruct((2, LANES, HEAD_SIZE), BF16),
-            jax.ShapeDtypeStruct((2, HEAD_SIZE, LANES), BF16),
         ],
         scratch_shapes=[pltpu.VMEM((SHARDS * SLOTS, TOK), F32)]
-        + [pltpu.VMEM(x.shape, x.dtype) for x in (grad, own, *mine, *theirs)]
-        + [pltpu.SemaphoreType.DMA((2 * RING + 2,))],
+        + [pltpu.VMEM(x.shape, x.dtype) for x in (own, *mine, *theirs)]
+        + [pltpu.SemaphoreType.DMA((2 * RING + 1,))],
         compiler_params=pltpu.CompilerParams(vmem_limit_bytes=12 * 2**20),
         name="permute",
-    )(info, grad, own, *mine, *theirs)
-
-
-def call_attention(info, segments, allow, unpack, q_recv, gr, gt, kv_window):
+    )(info, own, *mine, *theirs)
+
+
+def call_attention(info, segments, allow, unpack, q_recv, grad, kv_window):
     return pl.pallas_call(
         attention_kernel,
-        in_specs=[SMEM, SMEM, SMEM] + [VMEM] * 6,
+        in_specs=[SMEM, SMEM, SMEM] + [VMEM] * 5,
         out_specs=[VMEM, VMEM, HBM],
         out_shape=[
             jax.ShapeDtypeStruct((SHARDS * TOK, HEAD_SIZE), BF16),
@@ -425,6 +421,8 @@
             jax.ShapeDtypeStruct((2, MOST_BLOCKS * BLK, LANES), BF16),
         ],
         scratch_shapes=[
+            pltpu.VMEM((LANES, HEAD_SIZE), BF16),
+            pltpu.VMEM((HEAD_SIZE, LANES), BF16),
             pltpu.VMEM((LANES, HEAD_SIZE), BF16),
             pltpu.VMEM((HEAD_SIZE, LANES), BF16),
             pltpu.VMEM((MOST_BLOCKS * BLK, HEAD_SIZE), BF16),
@@ -440,7 +438,7 @@
         ],
         compiler_params=pltpu.CompilerParams(vmem_limit_bytes=40 * 2**20),
         name="attention",
-    )(info, segments, allow, segments.reshape(-1, BLK), unpack, q_recv, gr, gt, kv_window)
+    )(info, segments, allow, segments.reshape(-1, BLK), unpack, q_recv, grad, kv_window)
 
 
 def call_query_grad(info, segments, allow, kv_window, score_grad):
@@ -511,13 +509,13 @@
     q_send, *mine = lax.optimization_barrier((q_send, *mine))
     theirs = [lax.ppermute(piece, "tp", swap) for piece in mine]
     q_recv = lax.all_to_all(q_send, ("z", "x"), split_axis=0, concat_axis=0, tiled=True)
-    kv_window, unpack, gr, gt = call_permute(info, g_local, own, mine, theirs)
+    kv_window, unpack = call_permute(info, own, mine, theirs)
     keep, send, score_grad = call_attention(
-        info, segments, allow, unpack, q_recv, gr, gt, kv_window
+        info, segments, allow, unpack, q_recv, g_local, kv_window
     )
     recv = lax.ppermute(send, "tp", swap)
     part = (keep.astype(F32) + recv.astype(F32)).astype(BF16)
-    part, score_grad = lax.optimization_barrier((part, score_grad))
+    part, score_grad, late_ctx = lax.optimization_barrier((part, score_grad, ctx_index))
     rows = TOK // tp_size
     parts = lax.all_to_all(
         part.reshape(SHARDS * tp_size, rows, HEAD_SIZE),
@@ -526,7 +524,8 @@
         concat_axis=0,
         tiled=True,
     )
-    grad_q = call_query_grad(info, segments, allow, kv_window, score_grad)
+    late_info = jnp.stack([late_ctx, late_ctx]).astype(jnp.int32)
+    grad_q = call_query_grad(late_info, segments, allow, kv_window, score_grad)
     parts, grad_q = lax.optimization_barrier((parts, grad_q))
     heads = jnp.sum(parts.reshape(SHARDS, tp_size, rows, HEAD_SIZE).astype(F32), axis=0)
     key_value_gradient = (

time: 140 us -> 139 us (level)
  local copies, waits for them, and re-layouts: 14.5 us -> 10.3 us
  starting transfers between devices: 52.4 us -> 53.9 us
    unnamed x40 -> x30, local copies, waits for them, and re-layouts: 12 us -> 7.81 us
    all_to_all x1, waiting for transfers between devices: 8.96 us -> 10.7 us  [on_device(): lax.all_to_all(q_send, ('z', 'x'), split_axis=0, concat_axis=0, tiled=True)]
    all_to_all x1, starting transfers between devices: 17 us -> 18.4 us  [on_device(): lax.all_to_all(part.reshape(SHARDS * tp_size, rows, HEAD_SIZE), ('z', 'x'...]
  transfers between devices with their start and end apart: 13 -> 13, of which waited for: 8 -> 8; matrix products, arithmetic and copies ran while one was open for 1% -> 2% of each run, Pallas kernels for 8% -> 8%
where the time goes in v12:
time: 139 us; the launch traced here: 137 us
  starting transfers between devices  53.9 us (39%)
  waiting for transfers between devices  50.5 us (36%)
  Pallas kernels  18.9 us (14%)
  local copies, waits for them, and re-layouts  10.3 us (7%)
  other arithmetic  3.12 us (2%)
    all_to_all x1, waiting for transfers between devices, on_device(): lax.all_to_all(part.reshape(SHARDS * tp_size, rows, HEAD_SIZE), ('z', 'x'...  26.7 us
    all_to_all x1, starting transfers between devices, on_device(): lax.all_to_all(part.reshape(SHARDS * tp_size, rows, HEAD_SIZE), ('z', 'x'...  18.4 us
    all_to_all x1, waiting for transfers between devices, on_device(): lax.all_to_all(q_send, ('z', 'x'), split_axis=0, concat_axis=0, tiled=True)  10.7 us
    unnamed x30, local copies, waits for them, and re-layouts  7.81 us
    all_to_all x1, starting transfers between devices, on_device(): lax.all_to_all(g_send, 'tp', split_axis=0, concat_axis=0, tiled=True)  7.06 us
    ppermute x1, starting transfers between devices, on_device(): first = lax.ppermute(own, ('z', 'x', 'tp'), around(1))  6.54 us
    pallas_call x1, Pallas kernels, call_attention(): pl.pallas_call(attention_kernel, in_specs=[SMEM, SMEM, SMEM] + [VMEM] * 5...  6.18 us
    all_to_all x1, starting transfers between devices, on_device(): lax.all_to_all(q_send, ('z', 'x'), split_axis=0, concat_axis=0, tiled=True)  6.03 us
  transfers between devices with their start and end apart: 13, of which 8 were waited for; matrix products, arithmetic and copies ran while one was open for 2% of the time, Pallas kernels for 8%

profile of v12, /device:TPU:1, one launch (start us, length us, event | category | flops | bytes accessed | tf_op | source)
XLA Modules:
  0.0 137.5 jit_solution(3715168933635873844)
XLA Ops:
  0.6 2.2 %stage.1 = bf16[272,256]{1,0:T(8,128)(2,1)} custom-call(s32[1,256]{1,0:T(1,128)} %bitcast.38, bf16[2,256,1024]{2,1,0:T(8,128)(2,1)} %kv_ref.1), custom_call_target="tpu_custom_call" | custom-call | tf_op jit(solution)/shard_map/stage/pallas_call | solution.py:472
  2.9 2.1 %collective-permute-start = (bf16[272,256]{1,0:T(8,128)(2,1)}, bf16[272,256]{1,0:T(8,128)(2,1)S(1)}, u32[]{:S(2)}, u32[]{:S(2)}) collective-permute-start(bf16[272,256]{1,0:T(8,128)(2,1)} %stage.1), channel_id=1, source_target_pairs={{0,16},{16,0},{1,17},{17,1},{2,18},{18,2},{3,19},{19,3},{4,20},{20... | collective-permute-start | bytes 417800 | tf_op jit(solution)/shard_map/ppermute | solution.py:480
  5.0 1.9 %copy.16 = bf16[2,16,8,1024]{3,2,0,1:T(8,128)(2,1)} copy(bf16[2,16,8,1024]{3,2,1,0:T(8,128)(2,1)} %bitcast.34) | data formatting | bytes 1048576 | tf_op jit(solution)/shard_map/reshape | solution.py:482
  6.9 0.8 collective-permute-done
  7.6 0.9 pad_maximum_fusion.refs_0_
  8.6 6.5 %collective-permute-start.1 = (bf16[2,272,256]{2,1,0:T(8,128)(2,1)S(1)}, bf16[2,272,256]{2,1,0:T(8,128)(2,1)S(1)}, u32[]{:S(2)}, u32[]{:S(2)}) collective-permute-start(bf16[2,272,256]{2,1,0:T(8,128)(2,1)S(1)} %pad_maximum_fusion.refs_0_), channel_id=1, source_target_pairs={{0,32},{1,225},{2,34},{3,227},{4,36},{5,229},{6,38},{7,231},{8,40}... | collective-permute-start | bytes 835592 | tf_op jit(solution)/shard_map/ppermute | solution.py:494
  15.1 3.5 %collective-permute-done.1.refs_1_ = bf16[2,272,256]{2,1,0:T(8,128)(2,1)S(1)} collective-permute-done((bf16[2,272,256]{2,1,0:T(8,128)(2,1)S(1)}, bf16[2,272,256]{2,1,0:T(8,128)(2,1)S(1)}, u32[]{:S(2)}, u32[]{:S(2)}) %collective-permute-start.1) | collective-permute-done | bytes 278560 | tf_op jit(solution)/shard_map/ppermute | solution.py:494
  18.6 3.1 %collective-permute-start.2 = (bf16[2,272,256]{2,1,0:T(8,128)(2,1)S(1)}, bf16[2,272,256]{2,1,0:T(8,128)(2,1)S(1)}, u32[]{:S(2)}, u32[]{:S(2)}) collective-permute-start(bf16[2,272,256]{2,1,0:T(8,128)(2,1)S(1)} %collective-permute-done.1.refs_1_), channel_id=1, source_target_pairs={{0,32},{1,225},{2,34},{3,227},{4,36},{5,229},{6,38},{7,231},{8,40}... | collective-permute-start | bytes 835592 | tf_op jit(solution)/shard_map/ppermute | solution.py:495
  21.7 7.1 %all-to-all-start.1 = ((bf16[16,16,1024]{2,1,0:T(8,128)(2,1)}), bf16[16,16,1024]{2,1,0:T(8,128)(2,1)S(1)}, u32[]{:S(2)}, u32[]{:S(2)}) async-start(bf16[16,16,1024]{2,1,0:T(8,128)(2,1)} %bitcast.26), calls=%async_computation.1 | async-start | bytes 1048576 | tf_op jit(solution)/shard_map/all_to_all | solution.py:500
  28.8 0.0 collective-permute-done.2.refs_2_
  28.8 2.7 %collective-permute-start.3 = (bf16[2,272,256]{2,1,0:T(8,128)(2,1)S(1)}, bf16[2,272,256]{2,1,0:T(8,128)(2,1)S(1)}, u32[]{:S(2)}, u32[]{:S(2)}) collective-permute-start(bf16[2,272,256]{2,1,0:T(8,128)(2,1)S(1)} %collective-permute-done.2.refs_2_), channel_id=1, source_target_pairs={{0,32},{1,225},{2,34},{3,227},{4,36},{5,229},{6,38},{7,231},{8,40}... | collective-permute-start | bytes 835592 | tf_op jit(solution)/shard_map/ppermute | solution.py:496
  31.5 1.1 collective-permute-start.4
  32.5 2.6 %pack.1 = bf16[512,1024]{1,0:T(8,128)(2,1)} custom-call(s32[1,256]{1,0:T(1,128)} %bitcast.39, bf16[256,1024]{1,0:T(8,128)(2,1)} %rows_ref.1), custom_call_target="tpu_custom_call" | custom-call | tf_op jit(solution)/shard_map/pack/pallas_call | solution.py:502
  35.2 2.8 %collective-permute-done.4.refs_4_ = bf16[272,256]{1,0:T(8,128)(2,1)S(1)} collective-permute-done((bf16[272,256]{1,0:T(8,128)(2,1)S(1)}, bf16[272,256]{1,0:T(8,128)(2,1)S(1)}, u32[]{:S(2)}, u32[]{:S(2)}) %collective-permute-start.4) | collective-permute-done | bytes 139296 | tf_op jit(solution)/shard_map/ppermute | solution.py:498
  37.9 0.0 collective-permute-done.3.refs_3_
  37.9 2.1 %all-to-all-done.1 = bf16[16,16,1024]{2,1,0:T(8,128)(2,1)S(1)} async-done(((bf16[16,16,1024]{2,1,0:T(8,128)(2,1)}), bf16[16,16,1024]{2,1,0:T(8,128)(2,1)S(1)}, u32[]{:S(2)}, u32[]{:S(2)}) %all-to-all-start.1) | async-done | bytes 524320 | tf_op jit(solution)/shard_map/all_to_all | solution.py:500
  40.1 6.0 %all-to-all-start = ((bf16[16,32,1024]{2,1,0:T(8,128)(2,1)}), bf16[16,32,1024]{2,1,0:T(8,128)(2,1)S(1)}, u32[]{:S(2)}, u32[]{:S(2)}) async-start(bf16[16,32,1024]{2,1,0:T(8,128)(2,1)} %bitcast.31), calls=%async_computation | async-start | bytes 2097152 | tf_op jit(solution)/shard_map/all_to_all | solution.py:511
  46.1 1.5 %collective-permute-start.5 = (bf16[2,272,256]{2,1,0:T(8,128)(2,1)S(1)}, bf16[2,272,256]{2,1,0:T(8,128)(2,1)S(1)}, u32[]{:S(2)}, u32[]{:S(2)}) collective-permute-start(bf16[2,272,256]{2,1,0:T(8,128)(2,1)S(1)} %collective-permute-done.1.refs_1_), channel_id=1, source_target_pairs={{0,1},{1,0},{2,3},{3,2},{4,5},{5,4},{6,7},{7,6},{8,9},{9,8},{10,11... | collective-permute-start | bytes 835592 | tf_op jit(solution)/shard_map/ppermute | solution.py:510
  47.7 0.1 collective-permute-start.6
  47.8 0.4 collective-permute-start.7
  48.2 0.1 collective-permute-start.8
  48.3 0.1 pad_add_fusion.info_ref
  48.4 1.6 %collective-permute-done.8.refs_8_ = bf16[272,256]{1,0:T(8,128)(2,1)} collective-permute-done((bf16[272,256]{1,0:T(8,128)(2,1)S(1)}, bf16[272,256]{1,0:T(8,128)(2,1)}, u32[]{:S(2)}, u32[]{:S(2)}) %collective-permute-start.8) | collective-permute-done | bytes 139296 | tf_op jit(solution)/shard_map/ppermute | solution.py:510
  50.0 0.0 collective-permute-done.5.refs_5_
  50.0 0.7 copy-done.5
  50.7 0.0 collective-permute-done.6.refs_6_
  50.7 0.7 copy-done.7
  51.4 0.0 collective-permute-done.7.refs_7_
  51.4 1.0 copy-done.2
  52.4 1.0 copy-done.4
  53.3 1.0 copy-done.6
  54.3 1.0 copy-done.8
  55.3 0.9 copy-done.13
  56.2 3.2 %permute.1 = (bf16[2560,256]{1,0:T(8,128)(2,1)S(1)}, bf16[256,512]{1,0:T(8,128)(2,1)S(1)}) custom-call(s32[2]{0:T(128)S(1)} %pad_add_fusion.info_ref, bf16[2,272,256]{2,1,0:T(8,128)(2,1)S(1)} %pad_maximum_fusion.refs_0_, bf16[2,272,256]{2,1,0:T(8,128)(2,1)S(1)} %copy-done.2, bf16[2,272,256]{2,1,0:T(8,128)(2,1)S(1)} %collective-permute-done.2.refs_2_, ...), custom_call_target="tpu_custom_call" | custom-call | tf_op jit(solution)/shard_map/permute/pallas_call | solution.py:397
  59.3 0.0 copy-start.9
  59.3 0.7 copy-done.9
  60.0 10.7 %all-to-all-done = bf16[16,32,1024]{2,1,0:T(8,128)(2,1)S(1)} async-done(((bf16[16,32,1024]{2,1,0:T(8,128)(2,1)}), bf16[16,32,1024]{2,1,0:T(8,128)(2,1)S(1)}, u32[]{:S(2)}, u32[]{:S(2)}) %all-to-all-start) | async-done | bytes 1048608 | tf_op jit(solution)/shard_map/all_to_all | solution.py:511
  70.7 0.9 copy-done.10
  71.7 6.2 %attention.1 = (bf16[4096,128]{1,0:T(8,128)(2,1)S(1)}, bf16[4096,128]{1,0:T(8,128)(2,1)S(1)}, bf16[2,2560,1024]{2,1,0:T(8,128)(2,1)}) custom-call(s32[2]{0:T(128)S(1)} %pad_add_fusion.info_ref, s32[4096]{0:T(1024)S(1)} %copy-done.11, s32[32,32]{1,0:T(8,128)S(1)} %copy-done.14, s32[32,128]{1,0:T(8,128)S(1)} %bitcast.30, bf16[256,512]{1,0:T(8,128)(2,1)S(1)} %copy-done.10, ...), custom_call_target="tpu_custom_call" | custom-call | tf_op jit(solution)/shard_map/attention/pallas_call | solution.py:414
  77.9 4.8 %collective-permute-start.9 = (bf16[4096,128]{1,0:T(8,128)(2,1)S(1)}, bf16[4096,128]{1,0:T(8,128)(2,1)S(1)}, u32[]{:S(2)}, u32[]{:S(2)}) collective-permute-start(bf16[4096,128]{1,0:T(8,128)(2,1)S(1)} %get-tuple-element.29), channel_id=1, source_target_pairs={{0,1},{1,0},{2,3},{3,2},{4,5},{5,4},{6,7},{7,6},{8,9},{9,8},{10,11... | collective-permute-start | bytes 3145736 | tf_op jit(solution)/shard_map/ppermute | solution.py:516
  82.7 2.3 %collective-permute-done.9 = bf16[4096,128]{1,0:T(8,128)(2,1)S(1)} collective-permute-done((bf16[4096,128]{1,0:T(8,128)(2,1)S(1)}, bf16[4096,128]{1,0:T(8,128)(2,1)S(1)}, u32[]{:S(2)}, u32[]{:S(2)}) %collective-permute-start.9) | collective-permute-done | bytes 1048608 | tf_op jit(solution)/shard_map/ppermute | solution.py:516
  84.9 1.3 add_convert_fusion
  86.2 18.4 %all-to-all-start.2 = ((bf16[256,16,128]{2,1,0:T(8,128)(2,1)}), bf16[256,16,128]{2,1,0:T(8,128)(2,1)S(1)}, u32[]{:S(2)}, u32[]{:S(2)}) async-start(bf16[256,16,128]{2,1,0:T(8,128)(2,1)} %bitcast.11), calls=%async_computation.2 | async-start | bytes 2097152 | tf_op jit(solution)/shard_map/all_to_all | solution.py:520
  104.6 0.7 pad_add_fusion.1.info_ref
  105.3 4.7 %query_grad.1 = bf16[256,1024]{1,0:T(8,128)(2,1)} custom-call(s32[2]{0:T(128)} %pad_add_fusion.1.info_ref, s32[4096]{0:T(1024)} %seg_ref.3, s32[32,32]{1,0:T(8,128)} %allow_ref.3, bf16[2560,256]{1,0:T(8,128)(2,1)} %copy-done, bf16[2,2560,1024]{2,1,0:T(8,128)(2,1)} %get-tuple-element.33.sg_ref), custom_call_target="tpu_custom_call" | custom-call | flops 1073741824 | bytes 12582912 | tf_op jit(solution)/shard_map/query_grad/pallas_call | solution.py:445
  110.0 26.7 %all-to-all-done.2 = bf16[256,16,128]{2,1,0:T(8,128)(2,1)S(1)} async-done(((bf16[256,16,128]{2,1,0:T(8,128)(2,1)}), bf16[256,16,128]{2,1,0:T(8,128)(2,1)S(1)}, u32[]{:S(2)}, u32[]{:S(2)}) %all-to-all-start.2) | async-done | bytes 1048608 | tf_op jit(solution)/shard_map/all_to_all | solution.py:520
  136.7 0.1 reduce_sum.12
  136.9 0.6 copy.17
  (21 shorter events, 0.0 us)
Async XLA Ops:
  2.9 4.8 %collective-permute-start = (bf16[272,256]{1,0:T(8,128)(2,1)}, bf16[272,256]{1,0:T(8,128)(2,1)S(1)}, u32[]{:S(2)}, u32[]{:S(2)}) collective-permute-start(bf16[272,256]{1,0:T(8,128)(2,1)} %stage.1), channel_id=1, source_target_pairs={{0,16},{16,0},{1,17},{17,1},{2,18},{18,2},{3,19},{19,3},{4,20},{20... | collective-permute-start | bytes 417800 | tf_op jit(solution)/shard_map/ppermute | solution.py:480
  8.6 10.0 %collective-permute-start.1 = (bf16[2,272,256]{2,1,0:T(8,128)(2,1)S(1)}, bf16[2,272,256]{2,1,0:T(8,128)(2,1)S(1)}, u32[]{:S(2)}, u32[]{:S(2)}) collective-permute-start(bf16[2,272,256]{2,1,0:T(8,128)(2,1)S(1)} %pad_maximum_fusion.refs_0_), channel_id=1, source_target_pairs={{0,32},{1,225},{2,34},{3,227},{4,36},{5,229},{6,38},{7,231},{8,40}... | collective-permute-start | bytes 835592 | tf_op jit(solution)/shard_map/ppermute | solution.py:494
  18.6 27.5 %copy-start.1 = (bf16[2,272,256]{2,1,0:T(8,128)(2,1)}, bf16[2,272,256]{2,1,0:T(8,128)(2,1)S(1)}, u32[]{:S(2)}) copy-start(bf16[2,272,256]{2,1,0:T(8,128)(2,1)S(1)} %collective-permute-done.1.refs_1_) | copy-start | bytes 835588
  18.6 10.2 %collective-permute-start.2 = (bf16[2,272,256]{2,1,0:T(8,128)(2,1)S(1)}, bf16[2,272,256]{2,1,0:T(8,128)(2,1)S(1)}, u32[]{:S(2)}, u32[]{:S(2)}) collective-permute-start(bf16[2,272,256]{2,1,0:T(8,128)(2,1)S(1)} %collective-permute-done.1.refs_1_), channel_id=1, source_target_pairs={{0,32},{1,225},{2,34},{3,227},{4,36},{5,229},{6,38},{7,231},{8,40}... | collective-permute-start | bytes 835592 | tf_op jit(solution)/shard_map/ppermute | solution.py:495
  21.7 18.4 %all-to-all-start.1 = ((bf16[16,16,1024]{2,1,0:T(8,128)(2,1)}), bf16[16,16,1024]{2,1,0:T(8,128)(2,1)S(1)}, u32[]{:S(2)}, u32[]{:S(2)}) async-start(bf16[16,16,1024]{2,1,0:T(8,128)(2,1)} %bitcast.26), calls=%async_computation.1 | async-start | bytes 1048576 | tf_op jit(solution)/shard_map/all_to_all | solution.py:500
  28.8 9.1 %collective-permute-start.3 = (bf16[2,272,256]{2,1,0:T(8,128)(2,1)S(1)}, bf16[2,272,256]{2,1,0:T(8,128)(2,1)S(1)}, u32[]{:S(2)}, u32[]{:S(2)}) collective-permute-start(bf16[2,272,256]{2,1,0:T(8,128)(2,1)S(1)} %collective-permute-done.2.refs_2_), channel_id=1, source_target_pairs={{0,32},{1,225},{2,34},{3,227},{4,36},{5,229},{6,38},{7,231},{8,40}... | collective-permute-start | bytes 835592 | tf_op jit(solution)/shard_map/ppermute | solution.py:496
  31.5 6.5 %collective-permute-start.4 = (bf16[272,256]{1,0:T(8,128)(2,1)S(1)}, bf16[272,256]{1,0:T(8,128)(2,1)S(1)}, u32[]{:S(2)}, u32[]{:S(2)}) collective-permute-start(bf16[272,256]{1,0:T(8,128)(2,1)S(1)} %dynamic-slice_bitcast_fusion), channel_id=1, source_target_pairs={{0,64},{1,193},{2,66},{3,195},{4,68},{5,197},{6,70},{7,199},{8,72}... | collective-permute-start | bytes 417800 | tf_op jit(solution)/shard_map/ppermute | solution.py:498
  37.9 12.8 %copy-start.12 = (bf16[272,256]{1,0:T(8,128)(2,1)}, bf16[272,256]{1,0:T(8,128)(2,1)S(1)}, u32[]{:S(2)}) copy-start(bf16[272,256]{1,0:T(8,128)(2,1)S(1)} %collective-permute-done.4.refs_4_) | copy-start | bytes 417796
  37.9 12.8 %copy-start.3 = (bf16[2,272,256]{2,1,0:T(8,128)(2,1)}, bf16[2,272,256]{2,1,0:T(8,128)(2,1)S(1)}, u32[]{:S(2)}) copy-start(bf16[2,272,256]{2,1,0:T(8,128)(2,1)S(1)} %collective-permute-done.3.refs_3_) | copy-start | bytes 835588
  40.1 30.6 %copy-start.11 = (s32[4096]{0:T(1024)S(1)}, s32[4096]{0:T(1024)}, u32[]{:S(2)}) copy-start(s32[4096]{0:T(1024)} %seg_ref.3) | copy-start | bytes 49156
  40.1 30.6 %copy-start.14 = (s32[32,32]{1,0:T(8,128)S(1)}, s32[32,32]{1,0:T(8,128)}, u32[]{:S(2)}) copy-start(s32[32,32]{1,0:T(8,128)} %allow_ref.3) | copy-start | bytes 12292
  40.1 30.6 %all-to-all-start = ((bf16[16,32,1024]{2,1,0:T(8,128)(2,1)}), bf16[16,32,1024]{2,1,0:T(8,128)(2,1)S(1)}, u32[]{:S(2)}, u32[]{:S(2)}) async-start(bf16[16,32,1024]{2,1,0:T(8,128)(2,1)} %bitcast.31), calls=%async_computation | async-start | bytes 2097152 | tf_op jit(solution)/shard_map/all_to_all | solution.py:511
  46.1 3.9 %collective-permute-start.5 = (bf16[2,272,256]{2,1,0:T(8,128)(2,1)S(1)}, bf16[2,272,256]{2,1,0:T(8,128)(2,1)S(1)}, u32[]{:S(2)}, u32[]{:S(2)}) collective-permute-start(bf16[2,272,256]{2,1,0:T(8,128)(2,1)S(1)} %collective-permute-done.1.refs_1_), channel_id=1, source_target_pairs={{0,1},{1,0},{2,3},{3,2},{4,5},{5,4},{6,7},{7,6},{8,9},{9,8},{10,11... | collective-permute-start | bytes 835592 | tf_op jit(solution)/shard_map/ppermute | solution.py:510
  47.7 3.0 %collective-permute-start.6 = (bf16[2,272,256]{2,1,0:T(8,128)(2,1)S(1)}, bf16[2,272,256]{2,1,0:T(8,128)(2,1)S(1)}, u32[]{:S(2)}, u32[]{:S(2)}) collective-permute-start(bf16[2,272,256]{2,1,0:T(8,128)(2,1)S(1)} %collective-permute-done.2.refs_2_), channel_id=1, source_target_pairs={{0,1},{1,0},{2,3},{3,2},{4,5},{5,4},{6,7},{7,6},{8,9},{9,8},{10,11... | collective-permute-start | bytes 835592 | tf_op jit(solution)/shard_map/ppermute | solution.py:510
  47.8 3.7 %collective-permute-start.7 = (bf16[2,272,256]{2,1,0:T(8,128)(2,1)S(1)}, bf16[2,272,256]{2,1,0:T(8,128)(2,1)}, u32[]{:S(2)}, u32[]{:S(2)}) collective-permute-start(bf16[2,272,256]{2,1,0:T(8,128)(2,1)S(1)} %collective-permute-done.3.refs_3_), channel_id=1, source_target_pairs={{0,1},{1,0},{2,3},{3,2},{4,5},{5,4},{6,7},{7,6},{8,9},{9,8},{10,11... | collective-permute-start | bytes 835592 | tf_op jit(solution)/shard_map/ppermute | solution.py:510
  48.2 1.8 %collective-permute-start.8 = (bf16[272,256]{1,0:T(8,128)(2,1)S(1)}, bf16[272,256]{1,0:T(8,128)(2,1)}, u32[]{:S(2)}, u32[]{:S(2)}) collective-permute-start(bf16[272,256]{1,0:T(8,128)(2,1)S(1)} %collective-permute-done.4.refs_4_), channel_id=1, source_target_pairs={{0,1},{1,0},{2,3},{3,2},{4,5},{5,4},{6,7},{7,6},{8,9},{9,8},{10,11... | collective-permute-start | bytes 417800 | tf_op jit(solution)/shard_map/ppermute | solution.py:510
  50.0 0.7 copy-start.5
  50.7 0.7 copy-start.7
  51.4 1.0 copy-start.2
  52.4 1.0 copy-start.4
  53.3 1.0 copy-start.6
  54.3 1.0 copy-start.8
  55.3 0.9 copy-start.13
  59.3 0.7 copy-start.9
  60.0 26.2 %copy-start = (bf16[2560,256]{1,0:T(8,128)(2,1)}, bf16[2560,256]{1,0:T(8,128)(2,1)S(1)}, u32[]{:S(2)}) copy-start(bf16[2560,256]{1,0:T(8,128)(2,1)S(1)} %get-tuple-element.27.kv_ref.kv_in) | copy-start | bytes 3932164
  70.7 1.0 copy-start.10
  77.9 7.1 %collective-permute-start.9 = (bf16[4096,128]{1,0:T(8,128)(2,1)S(1)}, bf16[4096,128]{1,0:T(8,128)(2,1)S(1)}, u32[]{:S(2)}, u32[]{:S(2)}) collective-permute-start(bf16[4096,128]{1,0:T(8,128)(2,1)S(1)} %get-tuple-element.29), channel_id=1, source_target_pairs={{0,1},{1,0},{2,3},{3,2},{4,5},{5,4},{6,7},{7,6},{8,9},{9,8},{10,11... | collective-permute-start | bytes 3145736 | tf_op jit(solution)/shard_map/ppermute | solution.py:516
  86.2 50.5 %all-to-all-start.2 = ((bf16[256,16,128]{2,1,0:T(8,128)(2,1)}), bf16[256,16,128]{2,1,0:T(8,128)(2,1)S(1)}, u32[]{:S(2)}, u32[]{:S(2)}) async-start(bf16[256,16,128]{2,1,0:T(8,128)(2,1)} %bitcast.11), calls=%async_computation.2 | async-start | bytes 2097152 | tf_op jit(solution)/shard_map/all_to_all | solution.py:520

commit v13 on v12

--- a/solution.py
+++ b/solution.py
@@ -23,11 +23,14 @@
 BACK = -(-DOC_MOST // TOK)
 WINDOW = BACK + 1
 BLOCKS_BACK = -(-DOC_MOST // BLK)
-WIDE = 4
+WIDE = 8
+MIDDLE = 4
 NARROW = 2
-MOST_BLOCKS = WIDE * -(-(BLOCKS_BACK + 1) // WIDE)
+MOST_BLOCKS = MIDDLE * -(-(BLOCKS_BACK + 1) // MIDDLE)
 LOCAL_HEADS = 8
 LANES = LOCAL_HEADS * BLK
+PICKS_FIRST = WINDOW * TOK
+PICKS_PARTS = SHARDS * SLOTS // (2 * HEAD_SIZE)
 NEG_FILL = -1e30
 VMEM_LIMIT = 60 * 2**20
 SCALE = 1.0 / math.sqrt(HEAD_SIZE)
@@ -96,8 +99,8 @@
 
 def permute_kernel(info_ref, *refs):
     count = 2 * RING + 1
-    out_ref, unpack_ref, slots_s = refs[count : count + 3]
-    buffers, arrived = refs[count + 3 : -1], refs[-1]
+    out_ref, slots_s = refs[count : count + 2]
+    buffers, arrived = refs[count + 2 : -1], refs[-1]
     own_ref, mine, theirs = buffers[0], buffers[1 : 1 + RING], buffers[1 + RING :]
     for copy in fetch_all(refs[:count], buffers, arrived):
         copy.wait()
@@ -122,7 +125,9 @@
         landing = jnp.sum(jnp.where(hit, within[i : i + 1, :] + 1.0, 0.0), axis=1, keepdims=True)
         rows = pl.ds(pl.multiple_of(source * SLOTS, SLOTS), SLOTS)
         slots_s[rows, :] = (landing == lane + 1.0).astype(F32)
-    unpack_ref[...] = slots_s[...].T.astype(BF16)
+    for j in range(PICKS_PARTS):
+        part = slots_s[j * TOK : (j + 1) * TOK, :].T.astype(BF16)
+        out_ref[PICKS_FIRST + j * TOK : PICKS_FIRST + (j + 1) * TOK, :] = part
 
     def one_shard(i, carry):
         rows = iota((TOK, TOK), 0).astype(F32)
@@ -150,9 +155,11 @@
         return count + seen.astype(jnp.int32)
 
     count = lax.fori_loop(jnp.maximum(qb - BLOCKS_BACK, 0), qb + 1, scan, 0)
-    wide = (count + 1) // WIDE
-    narrow = (count + WIDE - 1) // WIDE - wide
-    return count, wide, narrow
+    wide = count // WIDE
+    rest = count - wide * WIDE
+    middle = (rest + 1) // MIDDLE
+    narrow = (rest + MIDDLE - 1) // MIDDLE - middle
+    return count, wide, middle, narrow
 
 
 def block_rows(n, blocks=1):
@@ -164,7 +171,6 @@
     seg_ref,
     allow_ref,
     segv_ref,
-    unpack_ref,
     recv_ref,
     grad_ref,
     kv_ref,
@@ -195,7 +201,10 @@
         qb = shard * 2 + half
         q_seg = segv_ref[pl.ds(qb, 1), :]
         q_last = seg_ref[qb * BLK + BLK - 1]
-        picks = unpack_ref[block_rows(half), :]
+        picks = jnp.concatenate(
+            [kv_ref[block_rows(PICKS_FIRST // BLK + 2 * j + half), :] for j in range(PICKS_PARTS)],
+            axis=1,
+        )
         for pair in range(LOCAL_HEADS // 2):
             q_two = dot(picks, recv_ref[:, pair * 256 : (pair + 1) * 256])
             for i in range(2):
@@ -227,7 +236,9 @@
                 ok = (k_seg == q_seg.astype(F32)) & (k_pos <= q_pos)
                 bias_s[dst, :] = jnp.where(ok, 0.0, NEG_FILL)
 
-        count, wide, narrow = visible_blocks(qb, seg_ref, allow_ref, on_block)
+        count, wide, middle, narrow = visible_blocks(qb, seg_ref, allow_ref, on_block)
+        middle_first = wide * WIDE
+        narrow_first = middle_first + middle * MIDDLE
 
         def fill(n, c):
             list_s[n] = 2 * SHARDS
@@ -237,7 +248,7 @@
             bias_s[dst, :] = jnp.full((BLK, BLK), NEG_FILL, F32)
             return c
 
-        lax.fori_loop(count, wide * WIDE + narrow * NARROW, fill, 0)
+        lax.fori_loop(count, narrow_first + narrow * NARROW, fill, 0)
 
         def first_pass(start, blocks, slot, state):
             top, total, weighed = state
@@ -260,29 +271,33 @@
             jnp.zeros((8, LANES), F32),
             jnp.zeros((8, LANES), F32),
         )
+        state = lax.fori_loop(0, wide, lambda n, st: first_pass(n * WIDE, WIDE, n, st), state)
         state = lax.fori_loop(
-            0, wide, lambda n, st: first_pass(n * WIDE, WIDE, n, st), state
+            0,
+            middle,
+            lambda n, st: first_pass(middle_first + n * MIDDLE, MIDDLE, wide + n, st),
+            state,
         )
         top, total, weighed = lax.fori_loop(
-            0, narrow, lambda n, st: first_pass(wide * WIDE, NARROW, wide, st), state
+            0,
+            narrow,
+            lambda n, st: first_pass(narrow_first, NARROW, wide + middle, st),
+            state,
         )
         inverse = 1.0 / jnp.sum(total, axis=0, keepdims=True)
         out_dot = jnp.sum(weighed, axis=0, keepdims=True) * inverse
 
-        def copy_out(start, blocks, buffer):
-            return pltpu.make_async_copy(
-                sg_s.at[buffer, pl.ds(0, blocks * BLK), :],
-                sg_ref.at[half, block_rows(start, blocks), :],
-                sent.at[buffer],
-            )
-
-        def second_pass(start, blocks, slot, buffer):
+        def copy_out(start, blocks, slot):
+            rows = block_rows(start, blocks)
+            return pltpu.make_async_copy(sg_s.at[rows, :], sg_ref.at[half, rows, :], sent.at[slot])
+
+        def second_pass(start, blocks, slot):
             rows = block_rows(start, blocks)
             factor = jnp.exp2((top_s[slot] - top) * EXP2_SCALE) * inverse
             weights = e_s[rows, :] * factor
             score_grad = (weights * (dp_s[rows, :] - out_dot)).astype(BF16)
-            sg_s[buffer, : blocks * BLK, :] = score_grad
-            copy_out(start, blocks, buffer).start()
+            sg_s[rows, :] = score_grad
+            copy_out(start, blocks, slot).start()
             value_terms = dot(weights.astype(BF16), gr_s[...])
             key_terms = dot(score_grad, qr_s[...])
             for n in range(blocks):
@@ -290,27 +305,15 @@
                 acc_s[0, dst, :] += key_terms[n * BLK : (n + 1) * BLK, :]
                 acc_s[1, dst, :] += value_terms[n * BLK : (n + 1) * BLK, :]
 
-        def wide_step(n, c):
-            @pl.when(n >= 2)
-            def _():
-                copy_out((n - 2) * WIDE, WIDE, n % 2).wait()
-
-            second_pass(n * WIDE, WIDE, n, n % 2)
-            return c
-
-        lax.fori_loop(0, wide, wide_step, 0)
-
-        @pl.when(narrow > 0)
-        def _():
-            second_pass(wide * WIDE, NARROW, wide, 2)
-            copy_out(wide * WIDE, NARROW, 2).wait()
-
-        for late in (1, 2):
-
-            @pl.when(wide >= late)
-            def _():
-                copy_out((wide - late) * WIDE, WIDE, (wide - late) % 2).wait()
-
+        def finish(step, steps):
+            lax.fori_loop(0, steps, lambda n, c: step(n) or c, 0)
+
+        finish(lambda n: second_pass(n * WIDE, WIDE, n), wide)
+        finish(lambda n: second_pass(middle_first + n * MIDDLE, MIDDLE, wide + n), middle)
+        finish(lambda n: second_pass(narrow_first, NARROW, wide + middle), narrow)
+        finish(lambda n: copy_out(n * WIDE, WIDE, n).wait(), wide)
+        finish(lambda n: copy_out(middle_first + n * MIDDLE, MIDDLE, wide + n).wait(), middle)
+        finish(lambda n: copy_out(narrow_first, NARROW, wide + middle).wait(), narrow)
         return carry
 
     lax.fori_loop(0, 2, query_block, 0)
@@ -332,7 +335,7 @@
 ):
     shard = info_ref[0]
     base = jnp.maximum(shard - BACK, 0)
-    copy = pltpu.make_async_copy(kv_in, kv_ref, kv_sem)
+    copy = pltpu.make_async_copy(kv_in.at[pl.ds(0, PICKS_FIRST), :], kv_ref, kv_sem)
     copy.start()
 
     def fetch(half, step):
@@ -343,8 +346,8 @@
 
     def steps_of(half):
         nothing = lambda kb, count: None
-        count, wide, narrow = visible_blocks(shard * 2 + half, seg_ref, allow_ref, nothing)
-        return wide * (WIDE // NARROW) + narrow
+        count, *_ = visible_blocks(shard * 2 + half, seg_ref, allow_ref, nothing)
+        return (count + NARROW - 1) // NARROW
 
     def start_fetch(half, c):
         def one(step, c2):
@@ -362,8 +365,8 @@
             k_blk = kv_ref[block_rows(kb - 2 * base), :HEAD_SIZE]
             kt_s[count // NARROW, :, lanes] = k_blk.astype(F32).T.astype(BF16)
 
-        count, wide, narrow = visible_blocks(shard * 2 + half, seg_ref, allow_ref, on_block)
-        steps = wide * (WIDE // NARROW) + narrow
+        count, *_ = visible_blocks(shard * 2 + half, seg_ref, allow_ref, on_block)
+        steps = (count + NARROW - 1) // NARROW
 
         def fill(n, c):
             lanes = block_rows(n % NARROW)
@@ -397,11 +400,8 @@
     return pl.pallas_call(
         permute_kernel,
         in_specs=[SMEM] + [ANY] * (2 * RING + 1),
-        out_specs=[VMEM] * 2,
-        out_shape=[
-            jax.ShapeDtypeStruct((WINDOW * TOK, 2 * HEAD_SIZE), BF16),
-            jax.ShapeDtypeStruct((TOK, SHARDS * SLOTS), BF16),
-        ],
+        out_specs=VMEM,
+        out_shape=jax.ShapeDtypeStruct((PICKS_FIRST + PICKS_PARTS * TOK, 2 * HEAD_SIZE), BF16),
         scratch_shapes=[pltpu.VMEM((SHARDS * SLOTS, TOK), F32)]
         + [pltpu.VMEM(x.shape, x.dtype) for x in (own, *mine, *theirs)]
         + [pltpu.SemaphoreType.DMA((2 * RING + 1,))],
@@ -410,10 +410,10 @@
     )(info, own, *mine, *theirs)
 
 
-def call_attention(info, segments, allow, unpack, q_recv, grad, kv_window):
+def call_attention(info, segments, allow, q_recv, grad, kv_window):
     return pl.pallas_call(
         attention_kernel,
-        in_specs=[SMEM, SMEM, SMEM] + [VMEM] * 5,
+        in_specs=[SMEM, SMEM, SMEM] + [VMEM] * 4,
         out_specs=[VMEM, VMEM, HBM],
         out_shape=[
             jax.ShapeDtypeStruct((SHARDS * TOK, HEAD_SIZE), BF16),
@@ -430,15 +430,15 @@
             pltpu.VMEM((MOST_BLOCKS * BLK, BLK), F32),
             pltpu.VMEM((MOST_BLOCKS * BLK, LANES), F32),
             pltpu.VMEM((MOST_BLOCKS * BLK, LANES), F32),
-            pltpu.VMEM((MOST_BLOCKS // WIDE + 1, 1, LANES), F32),
+            pltpu.VMEM((MOST_BLOCKS // WIDE + 3, 1, LANES), F32),
             pltpu.VMEM((2, SHARDS * TOK + BLK, HEAD_SIZE), F32),
-            pltpu.VMEM((3, WIDE * BLK, LANES), BF16),
+            pltpu.VMEM((MOST_BLOCKS * BLK, LANES), BF16),
             pltpu.SMEM((MOST_BLOCKS,), jnp.int32),
-            pltpu.SemaphoreType.DMA((3,)),
+            pltpu.SemaphoreType.DMA((MOST_BLOCKS // WIDE + 3,)),
         ],
-        compiler_params=pltpu.CompilerParams(vmem_limit_bytes=40 * 2**20),
+        compiler_params=pltpu.CompilerParams(vmem_limit_bytes=48 * 2**20),
         name="attention",
-    )(info, segments, allow, segments.reshape(-1, BLK), unpack, q_recv, grad, kv_window)
+    )(info, segments, allow, segments.reshape(-1, BLK), q_recv, grad, kv_window)
 
 
 def call_query_grad(info, segments, allow, kv_window, score_grad):
@@ -452,7 +452,7 @@
             pltpu.VMEM((HEAD_SIZE, LANES), F32),
             pltpu.VMEM((2, MOST_BLOCKS * BLK, LANES), BF16),
             pltpu.SemaphoreType.DMA((2, MOST_BLOCKS // NARROW)),
-            pltpu.VMEM(kv_window.shape, BF16),
+            pltpu.VMEM((PICKS_FIRST, 2 * HEAD_SIZE), BF16),
             pltpu.SemaphoreType.DMA(()),
         ],
         compiler_params=pltpu.CompilerParams(vmem_limit_bytes=VMEM_LIMIT),
@@ -509,9 +509,9 @@
     q_send, *mine = lax.optimization_barrier((q_send, *mine))
     theirs = [lax.ppermute(piece, "tp", swap) for piece in mine]
     q_recv = lax.all_to_all(q_send, ("z", "x"), split_axis=0, concat_axis=0, tiled=True)
-    kv_window, unpack = call_permute(info, own, mine, theirs)
+    kv_window = call_permute(info, own, mine, theirs)
     keep, send, score_grad = call_attention(
-        info, segments, allow, unpack, q_recv, g_local, kv_window
+        info, segments, allow, q_recv, g_local, kv_window
     )
     recv = lax.ppermute(send, "tp", swap)
     part = (keep.astype(F32) + recv.astype(F32)).astype(BF16)

time: 139 us -> 134 us (0.964)
  starting transfers between devices: 53.9 us -> 49.6 us
    all_to_all x1, starting transfers between devices: 18.4 us -> 14.1 us  [on_device(): lax.all_to_all(part.reshape(SHARDS * tp_size, rows, HEAD_SIZE), ('z', 'x'...]
where the time goes in v13:
time: 134 us; the launch traced here: 132 us
  waiting for transfers between devices  50.2 us (37%)
  starting transfers between devices  49.6 us (37%)
  Pallas kernels  18.9 us (14%)
  local copies, waits for them, and re-layouts  9.65 us (7%)
  other arithmetic  3.07 us (2%)
    all_to_all x1, waiting for transfers between devices, on_device(): lax.all_to_all(part.reshape(SHARDS * tp_size, rows, HEAD_SIZE), ('z', 'x'...  26.9 us
    all_to_all x1, starting transfers between devices, on_device(): lax.all_to_all(part.reshape(SHARDS * tp_size, rows, HEAD_SIZE), ('z', 'x'...  14.1 us
    all_to_all x1, waiting for transfers between devices, on_device(): lax.all_to_all(q_send, ('z', 'x'), split_axis=0, concat_axis=0, tiled=True)  10.2 us
    unnamed x30, local copies, waits for them, and re-layouts  7.12 us
    all_to_all x1, starting transfers between devices, on_device(): lax.all_to_all(g_send, 'tp', split_axis=0, concat_axis=0, tiled=True)  7.06 us
    ppermute x1, starting transfers between devices, on_device(): first = lax.ppermute(own, ('z', 'x', 'tp'), around(1))  6.54 us
    pallas_call x1, Pallas kernels, call_attention(): pl.pallas_call(attention_kernel, in_specs=[SMEM, SMEM, SMEM] + [VMEM] * 4...  6.1 us
    all_to_all x1, starting transfers between devices, on_device(): lax.all_to_all(q_send, ('z', 'x'), split_axis=0, concat_axis=0, tiled=True)  6.03 us
  transfers between devices with their start and end apart: 13, of which 8 were waited for; matrix products, arithmetic and copies ran while one was open for 2% of the time, Pallas kernels for 8%

profile of v13, /device:TPU:1, one launch (start us, length us, event | category | flops | bytes accessed | tf_op | source)
XLA Modules:
  0.0 132.2 jit_solution(4826124061889383730)
XLA Ops:
  0.6 2.2 %stage.1 = bf16[272,256]{1,0:T(8,128)(2,1)} custom-call(s32[1,256]{1,0:T(1,128)} %bitcast.38, bf16[2,256,1024]{2,1,0:T(8,128)(2,1)} %kv_ref.1), custom_call_target="tpu_custom_call" | custom-call | tf_op jit(solution)/shard_map/stage/pallas_call | solution.py:472
  2.9 2.1 %collective-permute-start = (bf16[272,256]{1,0:T(8,128)(2,1)}, bf16[272,256]{1,0:T(8,128)(2,1)S(1)}, u32[]{:S(2)}, u32[]{:S(2)}) collective-permute-start(bf16[272,256]{1,0:T(8,128)(2,1)} %stage.1), channel_id=1, source_target_pairs={{0,16},{16,0},{1,17},{17,1},{2,18},{18,2},{3,19},{19,3},{4,20},{20... | collective-permute-start | bytes 417800 | tf_op jit(solution)/shard_map/ppermute | solution.py:480
  5.0 1.9 %copy.16 = bf16[2,16,8,1024]{3,2,0,1:T(8,128)(2,1)} copy(bf16[2,16,8,1024]{3,2,1,0:T(8,128)(2,1)} %bitcast.34) | data formatting | bytes 1048576 | tf_op jit(solution)/shard_map/reshape | solution.py:482
  6.9 0.8 collective-permute-done
  7.6 0.9 pad_maximum_fusion.refs_0_
  8.6 6.5 %collective-permute-start.1 = (bf16[2,272,256]{2,1,0:T(8,128)(2,1)S(1)}, bf16[2,272,256]{2,1,0:T(8,128)(2,1)S(1)}, u32[]{:S(2)}, u32[]{:S(2)}) collective-permute-start(bf16[2,272,256]{2,1,0:T(8,128)(2,1)S(1)} %pad_maximum_fusion.refs_0_), channel_id=1, source_target_pairs={{0,32},{1,225},{2,34},{3,227},{4,36},{5,229},{6,38},{7,231},{8,40}... | collective-permute-start | bytes 835592 | tf_op jit(solution)/shard_map/ppermute | solution.py:494
  15.1 3.5 %collective-permute-done.1.refs_1_ = bf16[2,272,256]{2,1,0:T(8,128)(2,1)S(1)} collective-permute-done((bf16[2,272,256]{2,1,0:T(8,128)(2,1)S(1)}, bf16[2,272,256]{2,1,0:T(8,128)(2,1)S(1)}, u32[]{:S(2)}, u32[]{:S(2)}) %collective-permute-start.1) | collective-permute-done | bytes 278560 | tf_op jit(solution)/shard_map/ppermute | solution.py:494
  18.6 3.1 %collective-permute-start.2 = (bf16[2,272,256]{2,1,0:T(8,128)(2,1)S(1)}, bf16[2,272,256]{2,1,0:T(8,128)(2,1)S(1)}, u32[]{:S(2)}, u32[]{:S(2)}) collective-permute-start(bf16[2,272,256]{2,1,0:T(8,128)(2,1)S(1)} %collective-permute-done.1.refs_1_), channel_id=1, source_target_pairs={{0,32},{1,225},{2,34},{3,227},{4,36},{5,229},{6,38},{7,231},{8,40}... | collective-permute-start | bytes 835592 | tf_op jit(solution)/shard_map/ppermute | solution.py:495
  21.7 7.1 %all-to-all-start.1 = ((bf16[16,16,1024]{2,1,0:T(8,128)(2,1)}), bf16[16,16,1024]{2,1,0:T(8,128)(2,1)S(1)}, u32[]{:S(2)}, u32[]{:S(2)}) async-start(bf16[16,16,1024]{2,1,0:T(8,128)(2,1)} %bitcast.26), calls=%async_computation.1 | async-start | bytes 1048576 | tf_op jit(solution)/shard_map/all_to_all | solution.py:500
  28.8 0.0 collective-permute-done.2.refs_2_
  28.8 2.7 %collective-permute-start.3 = (bf16[2,272,256]{2,1,0:T(8,128)(2,1)S(1)}, bf16[2,272,256]{2,1,0:T(8,128)(2,1)S(1)}, u32[]{:S(2)}, u32[]{:S(2)}) collective-permute-start(bf16[2,272,256]{2,1,0:T(8,128)(2,1)S(1)} %collective-permute-done.2.refs_2_), channel_id=1, source_target_pairs={{0,32},{1,225},{2,34},{3,227},{4,36},{5,229},{6,38},{7,231},{8,40}... | collective-permute-start | bytes 835592 | tf_op jit(solution)/shard_map/ppermute | solution.py:496
  31.5 1.1 collective-permute-start.4
  32.5 2.6 %pack.1 = bf16[512,1024]{1,0:T(8,128)(2,1)} custom-call(s32[1,256]{1,0:T(1,128)} %bitcast.39, bf16[256,1024]{1,0:T(8,128)(2,1)} %rows_ref.1), custom_call_target="tpu_custom_call" | custom-call | tf_op jit(solution)/shard_map/pack/pallas_call | solution.py:502
  35.2 2.8 %collective-permute-done.4.refs_4_ = bf16[272,256]{1,0:T(8,128)(2,1)S(1)} collective-permute-done((bf16[272,256]{1,0:T(8,128)(2,1)S(1)}, bf16[272,256]{1,0:T(8,128)(2,1)S(1)}, u32[]{:S(2)}, u32[]{:S(2)}) %collective-permute-start.4) | collective-permute-done | bytes 139296 | tf_op jit(solution)/shard_map/ppermute | solution.py:498
  37.9 0.0 collective-permute-done.3.refs_3_
  38.0 2.1 %all-to-all-done.1 = bf16[16,16,1024]{2,1,0:T(8,128)(2,1)S(1)} async-done(((bf16[16,16,1024]{2,1,0:T(8,128)(2,1)}), bf16[16,16,1024]{2,1,0:T(8,128)(2,1)S(1)}, u32[]{:S(2)}, u32[]{:S(2)}) %all-to-all-start.1) | async-done | bytes 524320 | tf_op jit(solution)/shard_map/all_to_all | solution.py:500
  40.1 6.0 %all-to-all-start = ((bf16[16,32,1024]{2,1,0:T(8,128)(2,1)}), bf16[16,32,1024]{2,1,0:T(8,128)(2,1)S(1)}, u32[]{:S(2)}, u32[]{:S(2)}) async-start(bf16[16,32,1024]{2,1,0:T(8,128)(2,1)} %bitcast.31), calls=%async_computation | async-start | bytes 2097152 | tf_op jit(solution)/shard_map/all_to_all | solution.py:511
  46.1 0.0 copy-start.11
  46.1 1.5 %collective-permute-start.5 = (bf16[2,272,256]{2,1,0:T(8,128)(2,1)S(1)}, bf16[2,272,256]{2,1,0:T(8,128)(2,1)S(1)}, u32[]{:S(2)}, u32[]{:S(2)}) collective-permute-start(bf16[2,272,256]{2,1,0:T(8,128)(2,1)S(1)} %collective-permute-done.1.refs_1_), channel_id=1, source_target_pairs={{0,1},{1,0},{2,3},{3,2},{4,5},{5,4},{6,7},{7,6},{8,9},{9,8},{10,11... | collective-permute-start | bytes 835592 | tf_op jit(solution)/shard_map/ppermute | solution.py:510
  47.7 0.1 collective-permute-start.6
  47.8 0.4 collective-permute-start.7
  48.2 0.1 collective-permute-start.8
  48.3 0.1 pad_add_fusion.info_ref
  48.4 1.6 %collective-permute-done.8.refs_8_ = bf16[272,256]{1,0:T(8,128)(2,1)} collective-permute-done((bf16[272,256]{1,0:T(8,128)(2,1)S(1)}, bf16[272,256]{1,0:T(8,128)(2,1)}, u32[]{:S(2)}, u32[]{:S(2)}) %collective-permute-start.8) | collective-permute-done | bytes 139296 | tf_op jit(solution)/shard_map/ppermute | solution.py:510
  50.0 0.0 collective-permute-done.5.refs_5_
  50.0 0.7 copy-done.7
  50.7 0.0 collective-permute-done.6.refs_6_
  50.7 0.7 copy-done.9
  51.4 0.0 collective-permute-done.7.refs_7_
  51.4 1.0 copy-done.2
  52.4 1.0 copy-done.4
  53.4 1.0 copy-done.6
  54.3 1.0 copy-done.8
  55.3 1.0 copy-done.10
  56.2 0.9 copy-done.13
  57.1 3.3 %permute.1.kv_ref.kv_in = bf16[3072,256]{1,0:T(8,128)(2,1)S(1)} custom-call(s32[2]{0:T(128)S(1)} %pad_add_fusion.info_ref, bf16[2,272,256]{2,1,0:T(8,128)(2,1)S(1)} %pad_maximum_fusion.refs_0_, bf16[2,272,256]{2,1,0:T(8,128)(2,1)S(1)} %copy-done.4, bf16[2,272,256]{2,1,0:T(8,128)(2,1)S(1)} %copy-done.2, bf16[2,272,256]{2,1,0:T(8,128)(2,1)S(1)} %copy-done.6, ...), custom_call_target="tpu_custom_call" | custom-call | tf_op jit(solution)/shard_map/permute/pallas_call | solution.py:400
  60.5 10.2 %all-to-all-done = bf16[16,32,1024]{2,1,0:T(8,128)(2,1)S(1)} async-done(((bf16[16,32,1024]{2,1,0:T(8,128)(2,1)}), bf16[16,32,1024]{2,1,0:T(8,128)(2,1)S(1)}, u32[]{:S(2)}, u32[]{:S(2)}) %all-to-all-start) | async-done | bytes 1048608 | tf_op jit(solution)/shard_map/all_to_all | solution.py:511
  70.7 6.1 %attention.1 = (bf16[4096,128]{1,0:T(8,128)(2,1)S(1)}, bf16[4096,128]{1,0:T(8,128)(2,1)S(1)}, bf16[2,2560,1024]{2,1,0:T(8,128)(2,1)}) custom-call(s32[2]{0:T(128)S(1)} %pad_add_fusion.info_ref, s32[4096]{0:T(1024)S(1)} %copy-done.11, s32[32,32]{1,0:T(8,128)S(1)} %copy-done.14, s32[32,128]{1,0:T(8,128)S(1)} %bitcast.30, bf16[512,1024]{1,0:T(8,128)(2,1)S(1)} %bitcast.28, ...), custom_call_target="tpu_custom_call" | custom-call | tf_op jit(solution)/shard_map/attention/pallas_call | solution.py:414
  76.8 4.8 %collective-permute-start.9 = (bf16[4096,128]{1,0:T(8,128)(2,1)S(1)}, bf16[4096,128]{1,0:T(8,128)(2,1)S(1)}, u32[]{:S(2)}, u32[]{:S(2)}) collective-permute-start(bf16[4096,128]{1,0:T(8,128)(2,1)S(1)} %get-tuple-element.25), channel_id=1, source_target_pairs={{0,1},{1,0},{2,3},{3,2},{4,5},{5,4},{6,7},{7,6},{8,9},{9,8},{10,11... | collective-permute-start | bytes 3145736 | tf_op jit(solution)/shard_map/ppermute | solution.py:516
  81.6 2.3 %collective-permute-done.9 = bf16[4096,128]{1,0:T(8,128)(2,1)S(1)} collective-permute-done((bf16[4096,128]{1,0:T(8,128)(2,1)S(1)}, bf16[4096,128]{1,0:T(8,128)(2,1)S(1)}, u32[]{:S(2)}, u32[]{:S(2)}) %collective-permute-start.9) | collective-permute-done | bytes 1048608 | tf_op jit(solution)/shard_map/ppermute | solution.py:516
  83.9 1.3 add_convert_fusion
  85.2 0.0 copy-done
  85.2 14.1 %all-to-all-start.2 = ((bf16[256,16,128]{2,1,0:T(8,128)(2,1)}), bf16[256,16,128]{2,1,0:T(8,128)(2,1)S(1)}, u32[]{:S(2)}, u32[]{:S(2)}) async-start(bf16[256,16,128]{2,1,0:T(8,128)(2,1)} %bitcast.11), calls=%async_computation.2 | async-start | bytes 2097152 | tf_op jit(solution)/shard_map/all_to_all | solution.py:520
  99.3 0.6 pad_add_fusion.1.info_ref
  99.9 4.6 %query_grad.1 = bf16[256,1024]{1,0:T(8,128)(2,1)} custom-call(s32[2]{0:T(128)} %pad_add_fusion.1.info_ref, s32[4096]{0:T(1024)} %seg_ref.3, s32[32,32]{1,0:T(8,128)} %allow_ref.3, bf16[3072,256]{1,0:T(8,128)(2,1)} %copy-done, bf16[2,2560,1024]{2,1,0:T(8,128)(2,1)} %get-tuple-element.29.sg_ref), custom_call_target="tpu_custom_call" | custom-call | flops 1073741824 | bytes 12582912 | tf_op jit(solution)/shard_map/query_grad/pallas_call | solution.py:445
  104.5 26.9 %all-to-all-done.2 = bf16[256,16,128]{2,1,0:T(8,128)(2,1)S(1)} async-done(((bf16[256,16,128]{2,1,0:T(8,128)(2,1)}), bf16[256,16,128]{2,1,0:T(8,128)(2,1)S(1)}, u32[]{:S(2)}, u32[]{:S(2)}) %all-to-all-start.2) | async-done | bytes 1048608 | tf_op jit(solution)/shard_map/all_to_all | solution.py:520
  131.4 0.1 reduce_sum.12
  131.5 0.6 copy.17
  (21 shorter events, 0.0 us)
Async XLA Ops:
  2.9 4.8 %collective-permute-start = (bf16[272,256]{1,0:T(8,128)(2,1)}, bf16[272,256]{1,0:T(8,128)(2,1)S(1)}, u32[]{:S(2)}, u32[]{:S(2)}) collective-permute-start(bf16[272,256]{1,0:T(8,128)(2,1)} %stage.1), channel_id=1, source_target_pairs={{0,16},{16,0},{1,17},{17,1},{2,18},{18,2},{3,19},{19,3},{4,20},{20... | collective-permute-start | bytes 417800 | tf_op jit(solution)/shard_map/ppermute | solution.py:480
  8.6 10.0 %collective-permute-start.1 = (bf16[2,272,256]{2,1,0:T(8,128)(2,1)S(1)}, bf16[2,272,256]{2,1,0:T(8,128)(2,1)S(1)}, u32[]{:S(2)}, u32[]{:S(2)}) collective-permute-start(bf16[2,272,256]{2,1,0:T(8,128)(2,1)S(1)} %pad_maximum_fusion.refs_0_), channel_id=1, source_target_pairs={{0,32},{1,225},{2,34},{3,227},{4,36},{5,229},{6,38},{7,231},{8,40}... | collective-permute-start | bytes 835592 | tf_op jit(solution)/shard_map/ppermute | solution.py:494
  18.6 27.5 %copy-start.3 = (bf16[2,272,256]{2,1,0:T(8,128)(2,1)}, bf16[2,272,256]{2,1,0:T(8,128)(2,1)S(1)}, u32[]{:S(2)}) copy-start(bf16[2,272,256]{2,1,0:T(8,128)(2,1)S(1)} %collective-permute-done.1.refs_1_) | copy-start | bytes 835588
  18.6 10.2 %collective-permute-start.2 = (bf16[2,272,256]{2,1,0:T(8,128)(2,1)S(1)}, bf16[2,272,256]{2,1,0:T(8,128)(2,1)S(1)}, u32[]{:S(2)}, u32[]{:S(2)}) collective-permute-start(bf16[2,272,256]{2,1,0:T(8,128)(2,1)S(1)} %collective-permute-done.1.refs_1_), channel_id=1, source_target_pairs={{0,32},{1,225},{2,34},{3,227},{4,36},{5,229},{6,38},{7,231},{8,40}... | collective-permute-start | bytes 835592 | tf_op jit(solution)/shard_map/ppermute | solution.py:495
  21.7 18.4 %all-to-all-start.1 = ((bf16[16,16,1024]{2,1,0:T(8,128)(2,1)}), bf16[16,16,1024]{2,1,0:T(8,128)(2,1)S(1)}, u32[]{:S(2)}, u32[]{:S(2)}) async-start(bf16[16,16,1024]{2,1,0:T(8,128)(2,1)} %bitcast.26), calls=%async_computation.1 | async-start | bytes 1048576 | tf_op jit(solution)/shard_map/all_to_all | solution.py:500
  28.8 21.9 %copy-start.1 = (bf16[2,272,256]{2,1,0:T(8,128)(2,1)}, bf16[2,272,256]{2,1,0:T(8,128)(2,1)S(1)}, u32[]{:S(2)}) copy-start(bf16[2,272,256]{2,1,0:T(8,128)(2,1)S(1)} %collective-permute-done.2.refs_2_) | copy-start | bytes 835588
  28.8 9.1 %collective-permute-start.3 = (bf16[2,272,256]{2,1,0:T(8,128)(2,1)S(1)}, bf16[2,272,256]{2,1,0:T(8,128)(2,1)S(1)}, u32[]{:S(2)}, u32[]{:S(2)}) collective-permute-start(bf16[2,272,256]{2,1,0:T(8,128)(2,1)S(1)} %collective-permute-done.2.refs_2_), channel_id=1, source_target_pairs={{0,32},{1,225},{2,34},{3,227},{4,36},{5,229},{6,38},{7,231},{8,40}... | collective-permute-start | bytes 835592 | tf_op jit(solution)/shard_map/ppermute | solution.py:496
  31.5 6.5 %collective-permute-start.4 = (bf16[272,256]{1,0:T(8,128)(2,1)S(1)}, bf16[272,256]{1,0:T(8,128)(2,1)S(1)}, u32[]{:S(2)}, u32[]{:S(2)}) collective-permute-start(bf16[272,256]{1,0:T(8,128)(2,1)S(1)} %dynamic-slice_bitcast_fusion), channel_id=1, source_target_pairs={{0,64},{1,193},{2,66},{3,195},{4,68},{5,197},{6,70},{7,199},{8,72}... | collective-permute-start | bytes 417800 | tf_op jit(solution)/shard_map/ppermute | solution.py:498
  37.9 12.8 %copy-start.12 = (bf16[272,256]{1,0:T(8,128)(2,1)}, bf16[272,256]{1,0:T(8,128)(2,1)S(1)}, u32[]{:S(2)}) copy-start(bf16[272,256]{1,0:T(8,128)(2,1)S(1)} %collective-permute-done.4.refs_4_) | copy-start | bytes 417796
  38.0 12.8 %copy-start.5 = (bf16[2,272,256]{2,1,0:T(8,128)(2,1)}, bf16[2,272,256]{2,1,0:T(8,128)(2,1)S(1)}, u32[]{:S(2)}) copy-start(bf16[2,272,256]{2,1,0:T(8,128)(2,1)S(1)} %collective-permute-done.3.refs_3_) | copy-start | bytes 835588
  40.1 30.6 %copy-start.14 = (s32[32,32]{1,0:T(8,128)S(1)}, s32[32,32]{1,0:T(8,128)}, u32[]{:S(2)}) copy-start(s32[32,32]{1,0:T(8,128)} %allow_ref.3) | copy-start | bytes 12292
  40.1 30.6 %all-to-all-start = ((bf16[16,32,1024]{2,1,0:T(8,128)(2,1)}), bf16[16,32,1024]{2,1,0:T(8,128)(2,1)S(1)}, u32[]{:S(2)}, u32[]{:S(2)}) async-start(bf16[16,32,1024]{2,1,0:T(8,128)(2,1)} %bitcast.31), calls=%async_computation | async-start | bytes 2097152 | tf_op jit(solution)/shard_map/all_to_all | solution.py:511
  46.1 24.6 %copy-start.11 = (s32[4096]{0:T(1024)S(1)}, s32[4096]{0:T(1024)}, u32[]{:S(2)}) copy-start(s32[4096]{0:T(1024)} %seg_ref.3) | copy-start | bytes 49156
  46.1 3.9 %collective-permute-start.5 = (bf16[2,272,256]{2,1,0:T(8,128)(2,1)S(1)}, bf16[2,272,256]{2,1,0:T(8,128)(2,1)S(1)}, u32[]{:S(2)}, u32[]{:S(2)}) collective-permute-start(bf16[2,272,256]{2,1,0:T(8,128)(2,1)S(1)} %collective-permute-done.1.refs_1_), channel_id=1, source_target_pairs={{0,1},{1,0},{2,3},{3,2},{4,5},{5,4},{6,7},{7,6},{8,9},{9,8},{10,11... | collective-permute-start | bytes 835592 | tf_op jit(solution)/shard_map/ppermute | solution.py:510
  47.7 3.0 %collective-permute-start.6 = (bf16[2,272,256]{2,1,0:T(8,128)(2,1)S(1)}, bf16[2,272,256]{2,1,0:T(8,128)(2,1)S(1)}, u32[]{:S(2)}, u32[]{:S(2)}) collective-permute-start(bf16[2,272,256]{2,1,0:T(8,128)(2,1)S(1)} %collective-permute-done.2.refs_2_), channel_id=1, source_target_pairs={{0,1},{1,0},{2,3},{3,2},{4,5},{5,4},{6,7},{7,6},{8,9},{9,8},{10,11... | collective-permute-start | bytes 835592 | tf_op jit(solution)/shard_map/ppermute | solution.py:510
  47.8 3.7 %collective-permute-start.7 = (bf16[2,272,256]{2,1,0:T(8,128)(2,1)S(1)}, bf16[2,272,256]{2,1,0:T(8,128)(2,1)}, u32[]{:S(2)}, u32[]{:S(2)}) collective-permute-start(bf16[2,272,256]{2,1,0:T(8,128)(2,1)S(1)} %collective-permute-done.3.refs_3_), channel_id=1, source_target_pairs={{0,1},{1,0},{2,3},{3,2},{4,5},{5,4},{6,7},{7,6},{8,9},{9,8},{10,11... | collective-permute-start | bytes 835592 | tf_op jit(solution)/shard_map/ppermute | solution.py:510
  48.2 1.8 %collective-permute-start.8 = (bf16[272,256]{1,0:T(8,128)(2,1)S(1)}, bf16[272,256]{1,0:T(8,128)(2,1)}, u32[]{:S(2)}, u32[]{:S(2)}) collective-permute-start(bf16[272,256]{1,0:T(8,128)(2,1)S(1)} %collective-permute-done.4.refs_4_), channel_id=1, source_target_pairs={{0,1},{1,0},{2,3},{3,2},{4,5},{5,4},{6,7},{7,6},{8,9},{9,8},{10,11... | collective-permute-start | bytes 417800 | tf_op jit(solution)/shard_map/ppermute | solution.py:510
  50.0 0.7 copy-start.7
  50.7 0.7 copy-start.9
  51.4 1.0 copy-start.2
  52.4 1.0 copy-start.4
  53.4 1.0 copy-start.6
  54.3 1.0 copy-start.8
  55.3 1.0 copy-start.10
  56.2 0.9 copy-start.13
  60.5 24.7 %copy-start = (bf16[3072,256]{1,0:T(8,128)(2,1)}, bf16[3072,256]{1,0:T(8,128)(2,1)S(1)}, u32[]{:S(2)}) copy-start(bf16[3072,256]{1,0:T(8,128)(2,1)S(1)} %permute.1.kv_ref.kv_in) | copy-start | bytes 4718596
  76.8 7.1 %collective-permute-start.9 = (bf16[4096,128]{1,0:T(8,128)(2,1)S(1)}, bf16[4096,128]{1,0:T(8,128)(2,1)S(1)}, u32[]{:S(2)}, u32[]{:S(2)}) collective-permute-start(bf16[4096,128]{1,0:T(8,128)(2,1)S(1)} %get-tuple-element.25), channel_id=1, source_target_pairs={{0,1},{1,0},{2,3},{3,2},{4,5},{5,4},{6,7},{7,6},{8,9},{9,8},{10,11... | collective-permute-start | bytes 3145736 | tf_op jit(solution)/shard_map/ppermute | solution.py:516
  85.2 46.1 %all-to-all-start.2 = ((bf16[256,16,128]{2,1,0:T(8,128)(2,1)}), bf16[256,16,128]{2,1,0:T(8,128)(2,1)S(1)}, u32[]{:S(2)}, u32[]{:S(2)}) async-start(bf16[256,16,128]{2,1,0:T(8,128)(2,1)} %bitcast.11), calls=%async_computation.2 | async-start | bytes 2097152 | tf_op jit(solution)/shard_map/all_to_all | solution.py:520

commit v14 on v13

--- a/solution.py
+++ b/solution.py
@@ -115,8 +115,9 @@
             sources += [(refs_k[k - 1].at[j], 2 * far + (x ^ j)) for j in range(2)]
         far = (z + RING) % Z_CHIPS
         sources += [(refs_k[RING - 1], 2 * far + (x ^ side))]
-    owners = jnp.concatenate([ref[TOK : TOK + 1, :].astype(F32) for ref, _ in sources], axis=0)
-    within = jnp.concatenate([ref[TOK + 1 : TOK + 2, :].astype(F32) for ref, _ in sources], axis=0)
+    notes = [ref[TOK : TOK + META, :].astype(F32) for ref, _ in sources]
+    owners = jnp.concatenate([note[:1, :] for note in notes], axis=0)
+    within = jnp.concatenate([note[1:2, :] for note in notes], axis=0)
     rank = ranks_within(owners == shard.astype(F32))
     slot = iota((SLOTS, TOK), 0).astype(F32)
     lane = iota((SLOTS, TOK), 1).astype(F32)
@@ -143,10 +144,10 @@
 
 
 def visible_blocks(qb, seg_ref, allow_ref, on_block):
-    q_first = seg_ref[qb * BLK]
+    q_first = seg_ref[0, qb]
 
     def scan(kb, count):
-        seen = jnp.logical_and(seg_ref[kb * BLK + BLK - 1] >= q_first, allow_ref[qb, kb] != 0)
+        seen = jnp.logical_and(seg_ref[1, kb] >= q_first, allow_ref[qb, kb] != 0)
 
         @pl.when(seen)
         def _():
@@ -200,7 +201,7 @@
     def query_block(half, carry):
         qb = shard * 2 + half
         q_seg = segv_ref[pl.ds(qb, 1), :]
-        q_last = seg_ref[qb * BLK + BLK - 1]
+        q_last = seg_ref[1, qb]
         picks = jnp.concatenate(
             [kv_ref[block_rows(PICKS_FIRST // BLK + 2 * j + half), :] for j in range(PICKS_PARTS)],
             axis=1,
@@ -222,7 +223,7 @@
             dst = block_rows(count)
             k_s[dst, :] = kv_ref[src, :HEAD_SIZE]
             v_s[dst, :] = kv_ref[src, HEAD_SIZE:]
-            whole = jnp.logical_and(kb < qb, seg_ref[kb * BLK] == q_last)
+            whole = jnp.logical_and(kb < qb, seg_ref[0, kb] == q_last)
 
             @pl.when(whole)
             def _():
@@ -410,7 +411,7 @@
     )(info, own, *mine, *theirs)
 
 
-def call_attention(info, segments, allow, q_recv, grad, kv_window):
+def call_attention(info, ends, segments, allow, q_recv, grad, kv_window):
     return pl.pallas_call(
         attention_kernel,
         in_specs=[SMEM, SMEM, SMEM] + [VMEM] * 4,
@@ -438,10 +439,10 @@
         ],
         compiler_params=pltpu.CompilerParams(vmem_limit_bytes=48 * 2**20),
         name="attention",
-    )(info, segments, allow, segments.reshape(-1, BLK), q_recv, grad, kv_window)
-
-
-def call_query_grad(info, segments, allow, kv_window, score_grad):
+    )(info, ends, allow, segments.reshape(-1, BLK), q_recv, grad, kv_window)
+
+
+def call_query_grad(info, ends, allow, kv_window, score_grad):
     return pl.pallas_call(
         query_grad_kernel,
         in_specs=[SMEM, SMEM, SMEM, HBM, HBM],
@@ -460,7 +461,7 @@
             flops=2 * TOK * 2048 * LANES, bytes_accessed=12 * 2**20, transcendentals=0
         ),
         name="query_grad",
-    )(info, segments, allow, kv_window, score_grad)
+    )(info, ends, allow, kv_window, score_grad)
 
 
 def on_device(queries, keys_values, out_grad, place, segments, allow):
@@ -509,9 +510,11 @@
     q_send, *mine = lax.optimization_barrier((q_send, *mine))
     theirs = [lax.ppermute(piece, "tp", swap) for piece in mine]
     q_recv = lax.all_to_all(q_send, ("z", "x"), split_axis=0, concat_axis=0, tiled=True)
+    blocks = segments.reshape(-1, BLK)
+    ends = jnp.stack([blocks[:, 0], blocks[:, BLK - 1]])
     kv_window = call_permute(info, own, mine, theirs)
     keep, send, score_grad = call_attention(
-        info, segments, allow, q_recv, g_local, kv_window
+        info, ends, segments, allow, q_recv, g_local, kv_window
     )
     recv = lax.ppermute(send, "tp", swap)
     part = (keep.astype(F32) + recv.astype(F32)).astype(BF16)
@@ -525,7 +528,7 @@
         tiled=True,
     )
     late_info = jnp.stack([late_ctx, late_ctx]).astype(jnp.int32)
-    grad_q = call_query_grad(late_info, segments, allow, kv_window, score_grad)
+    grad_q = call_query_grad(late_info, ends, allow, kv_window, score_grad)
     parts, grad_q = lax.optimization_barrier((parts, grad_q))
     heads = jnp.sum(parts.reshape(SHARDS, tp_size, rows, HEAD_SIZE).astype(F32), axis=0)
     key_value_gradient = (

time: 134 us -> 135 us (level); the launches traced: 132 us -> 135 us
  starting transfers between devices: 49.6 us -> 51.8 us
    all_to_all x1, starting transfers between devices: 14.1 us -> 16.4 us  [on_device(): lax.all_to_all(part.reshape(SHARDS * tp_size, rows, HEAD_SIZE), ('z', 'x'...]
    unnamed x30 -> x32, local copies, waits for them, and re-layouts: 7.12 us -> 7.68 us
where the time goes in v14:
time: 135 us
  starting transfers between devices  51.8 us (38%)
  waiting for transfers between devices  50.2 us (37%)
  Pallas kernels  18.5 us (14%)
  local copies, waits for them, and re-layouts  10.4 us (8%)
  other arithmetic  3.04 us (2%)
    all_to_all x1, waiting for transfers between devices, on_device(): lax.all_to_all(part.reshape(SHARDS * tp_size, rows, HEAD_SIZE), ('z', 'x'...  27.1 us
    all_to_all x1, starting transfers between devices, on_device(): lax.all_to_all(part.reshape(SHARDS * tp_size, rows, HEAD_SIZE), ('z', 'x'...  16.4 us
    all_to_all x1, waiting for transfers between devices, on_device(): lax.all_to_all(q_send, ('z', 'x'), split_axis=0, concat_axis=0, tiled=True)  10.4 us
    unnamed x32, local copies, waits for them, and re-layouts  7.68 us
    all_to_all x1, starting transfers between devices, on_device(): lax.all_to_all(g_send, 'tp', split_axis=0, concat_axis=0, tiled=True)  7.06 us
    ppermute x1, starting transfers between devices, on_device(): first = lax.ppermute(own, ('z', 'x', 'tp'), around(1))  6.54 us
    all_to_all x1, starting transfers between devices, on_device(): lax.all_to_all(q_send, ('z', 'x'), split_axis=0, concat_axis=0, tiled=True)  5.9 us
    pallas_call x1, Pallas kernels, call_attention(): pl.pallas_call(attention_kernel, in_specs=[SMEM, SMEM, SMEM] + [VMEM] * 4...  5.84 us
  transfers between devices with their start and end apart: 13, of which 8 were waited for; matrix products, arithmetic and copies ran while one was open for 2% of the time, Pallas kernels for 8%

profile of v14, /device:TPU:1, one launch (start us, length us, event | category | flops | bytes accessed | tf_op | source)
XLA Modules:
  0.0 134.6 jit_solution(4022362261196575640)
XLA Ops:
  0.6 2.2 %stage.1 = bf16[272,256]{1,0:T(8,128)(2,1)} custom-call(s32[1,256]{1,0:T(1,128)} %bitcast.41, bf16[2,256,1024]{2,1,0:T(8,128)(2,1)} %kv_ref.1), custom_call_target="tpu_custom_call" | custom-call | tf_op jit(solution)/shard_map/stage/pallas_call | solution.py:473
  2.9 2.1 %collective-permute-start = (bf16[272,256]{1,0:T(8,128)(2,1)}, bf16[272,256]{1,0:T(8,128)(2,1)S(1)}, u32[]{:S(2)}, u32[]{:S(2)}) collective-permute-start(bf16[272,256]{1,0:T(8,128)(2,1)} %stage.1), channel_id=1, source_target_pairs={{0,16},{16,0},{1,17},{17,1},{2,18},{18,2},{3,19},{19,3},{4,20},{20... | collective-permute-start | bytes 417800 | tf_op jit(solution)/shard_map/ppermute | solution.py:481
  5.0 1.9 %copy.16 = bf16[2,16,8,1024]{3,2,0,1:T(8,128)(2,1)} copy(bf16[2,16,8,1024]{3,2,1,0:T(8,128)(2,1)} %bitcast.37) | data formatting | bytes 1048576 | tf_op jit(solution)/shard_map/reshape | solution.py:483
  6.9 0.8 collective-permute-done
  7.7 0.9 pad_maximum_fusion.refs_0_
  8.6 6.5 %collective-permute-start.1 = (bf16[2,272,256]{2,1,0:T(8,128)(2,1)S(1)}, bf16[2,272,256]{2,1,0:T(8,128)(2,1)S(1)}, u32[]{:S(2)}, u32[]{:S(2)}) collective-permute-start(bf16[2,272,256]{2,1,0:T(8,128)(2,1)S(1)} %pad_maximum_fusion.refs_0_), channel_id=1, source_target_pairs={{0,32},{1,225},{2,34},{3,227},{4,36},{5,229},{6,38},{7,231},{8,40}... | collective-permute-start | bytes 835592 | tf_op jit(solution)/shard_map/ppermute | solution.py:495
  15.1 3.5 %collective-permute-done.1.refs_1_ = bf16[2,272,256]{2,1,0:T(8,128)(2,1)S(1)} collective-permute-done((bf16[2,272,256]{2,1,0:T(8,128)(2,1)S(1)}, bf16[2,272,256]{2,1,0:T(8,128)(2,1)S(1)}, u32[]{:S(2)}, u32[]{:S(2)}) %collective-permute-start.1) | collective-permute-done | bytes 278560 | tf_op jit(solution)/shard_map/ppermute | solution.py:495
  18.6 3.1 %collective-permute-start.2 = (bf16[2,272,256]{2,1,0:T(8,128)(2,1)S(1)}, bf16[2,272,256]{2,1,0:T(8,128)(2,1)S(1)}, u32[]{:S(2)}, u32[]{:S(2)}) collective-permute-start(bf16[2,272,256]{2,1,0:T(8,128)(2,1)S(1)} %collective-permute-done.1.refs_1_), channel_id=1, source_target_pairs={{0,32},{1,225},{2,34},{3,227},{4,36},{5,229},{6,38},{7,231},{8,40}... | collective-permute-start | bytes 835592 | tf_op jit(solution)/shard_map/ppermute | solution.py:496
  21.7 7.1 %all-to-all-start.1 = ((bf16[16,16,1024]{2,1,0:T(8,128)(2,1)}), bf16[16,16,1024]{2,1,0:T(8,128)(2,1)S(1)}, u32[]{:S(2)}, u32[]{:S(2)}) async-start(bf16[16,16,1024]{2,1,0:T(8,128)(2,1)} %bitcast.28), calls=%async_computation.1 | async-start | bytes 1048576 | tf_op jit(solution)/shard_map/all_to_all | solution.py:501
  28.8 0.0 collective-permute-done.2.refs_2_
  28.8 2.7 %collective-permute-start.3 = (bf16[2,272,256]{2,1,0:T(8,128)(2,1)S(1)}, bf16[2,272,256]{2,1,0:T(8,128)(2,1)S(1)}, u32[]{:S(2)}, u32[]{:S(2)}) collective-permute-start(bf16[2,272,256]{2,1,0:T(8,128)(2,1)S(1)} %collective-permute-done.2.refs_2_), channel_id=1, source_target_pairs={{0,32},{1,225},{2,34},{3,227},{4,36},{5,229},{6,38},{7,231},{8,40}... | collective-permute-start | bytes 835592 | tf_op jit(solution)/shard_map/ppermute | solution.py:497
  31.5 1.1 collective-permute-start.4
  32.6 2.6 %pack.1 = bf16[512,1024]{1,0:T(8,128)(2,1)} custom-call(s32[1,256]{1,0:T(1,128)} %bitcast.42, bf16[256,1024]{1,0:T(8,128)(2,1)} %rows_ref.1), custom_call_target="tpu_custom_call" | custom-call | tf_op jit(solution)/shard_map/pack/pallas_call | solution.py:503
  35.2 2.8 %collective-permute-done.4.refs_4_ = bf16[272,256]{1,0:T(8,128)(2,1)S(1)} collective-permute-done((bf16[272,256]{1,0:T(8,128)(2,1)S(1)}, bf16[272,256]{1,0:T(8,128)(2,1)S(1)}, u32[]{:S(2)}, u32[]{:S(2)}) %collective-permute-start.4) | collective-permute-done | bytes 139296 | tf_op jit(solution)/shard_map/ppermute | solution.py:499
  38.0 0.0 collective-permute-done.3.refs_3_
  38.0 2.1 %all-to-all-done.1 = bf16[16,16,1024]{2,1,0:T(8,128)(2,1)S(1)} async-done(((bf16[16,16,1024]{2,1,0:T(8,128)(2,1)}), bf16[16,16,1024]{2,1,0:T(8,128)(2,1)S(1)}, u32[]{:S(2)}, u32[]{:S(2)}) %all-to-all-start.1) | async-done | bytes 524320 | tf_op jit(solution)/shard_map/all_to_all | solution.py:501
  40.1 5.9 %all-to-all-start = ((bf16[16,32,1024]{2,1,0:T(8,128)(2,1)}), bf16[16,32,1024]{2,1,0:T(8,128)(2,1)S(1)}, u32[]{:S(2)}, u32[]{:S(2)}) async-start(bf16[16,32,1024]{2,1,0:T(8,128)(2,1)} %bitcast.34), calls=%async_computation | async-start | bytes 2097152 | tf_op jit(solution)/shard_map/all_to_all | solution.py:512
  46.0 0.0 copy-start.14
  46.0 1.5 %collective-permute-start.5 = (bf16[2,272,256]{2,1,0:T(8,128)(2,1)S(1)}, bf16[2,272,256]{2,1,0:T(8,128)(2,1)S(1)}, u32[]{:S(2)}, u32[]{:S(2)}) collective-permute-start(bf16[2,272,256]{2,1,0:T(8,128)(2,1)S(1)} %collective-permute-done.1.refs_1_), channel_id=1, source_target_pairs={{0,1},{1,0},{2,3},{3,2},{4,5},{5,4},{6,7},{7,6},{8,9},{9,8},{10,11... | collective-permute-start | bytes 835592 | tf_op jit(solution)/shard_map/ppermute | solution.py:511
  47.6 0.1 collective-permute-start.6
  47.7 0.4 collective-permute-start.7
  48.1 0.2 slice_reduce_fusion.1
  48.2 0.2 collective-permute-start.8
  48.4 0.1 pad_add_fusion.1.info_ref
  48.5 1.2 collective-permute-done.8.refs_8_
  49.7 0.0 collective-permute-done.5.refs_5_
  49.7 0.7 copy-done.7
  50.5 0.7 copy-done.9
  51.2 1.0 copy-done.2
  52.1 1.0 copy-done.4
  53.1 1.0 copy-done.6
  54.1 1.0 copy-done.8
  55.0 1.0 copy-done.10
  56.0 0.9 copy-done.13
  56.9 3.3 %permute.1.kv_ref.kv_in = bf16[3072,256]{1,0:T(8,128)(2,1)S(1)} custom-call(s32[2]{0:T(128)S(1)} %pad_add_fusion.1.info_ref, bf16[2,272,256]{2,1,0:T(8,128)(2,1)S(1)} %pad_maximum_fusion.refs_0_, bf16[2,272,256]{2,1,0:T(8,128)(2,1)S(1)} %copy-done.4, bf16[2,272,256]{2,1,0:T(8,128)(2,1)S(1)} %copy-done.2, bf16[2,272,256]{2,1,0:T(8,128)(2,1)S(1)} %copy-done.6, ...), custom_call_target="tpu_custom_call" | custom-call | tf_op jit(solution)/shard_map/permute/pallas_call | solution.py:401
  60.2 10.4 %all-to-all-done = bf16[16,32,1024]{2,1,0:T(8,128)(2,1)S(1)} async-done(((bf16[16,32,1024]{2,1,0:T(8,128)(2,1)}), bf16[16,32,1024]{2,1,0:T(8,128)(2,1)S(1)}, u32[]{:S(2)}, u32[]{:S(2)}) %all-to-all-start) | async-done | bytes 1048608 | tf_op jit(solution)/shard_map/all_to_all | solution.py:512
  70.6 5.8 %attention.1 = (bf16[4096,128]{1,0:T(8,128)(2,1)S(1)}, bf16[4096,128]{1,0:T(8,128)(2,1)S(1)}, bf16[2,2560,1024]{2,1,0:T(8,128)(2,1)}) custom-call(s32[2]{0:T(128)S(1)} %pad_add_fusion.1.info_ref, s32[2,32]{1,0:T(2,128)S(1)} %pad_add_fusion.seg_ref, s32[32,32]{1,0:T(8,128)S(1)} %copy-done.14, s32[32,128]{1,0:T(8,128)S(1)} %bitcast.33, ...), custom_call_target="tpu_custom_call" | custom-call | tf_op jit(solution)/shard_map/attention/pallas_call | solution.py:415
  76.4 0.0 copy-start.15
  76.5 0.6 copy-done.15
  77.0 4.7 %collective-permute-start.9 = (bf16[4096,128]{1,0:T(8,128)(2,1)S(1)}, bf16[4096,128]{1,0:T(8,128)(2,1)S(1)}, u32[]{:S(2)}, u32[]{:S(2)}) collective-permute-start(bf16[4096,128]{1,0:T(8,128)(2,1)S(1)} %get-tuple-element.25), channel_id=1, source_target_pairs={{0,1},{1,0},{2,3},{3,2},{4,5},{5,4},{6,7},{7,6},{8,9},{9,8},{10,11... | collective-permute-start | bytes 3145736 | tf_op jit(solution)/shard_map/ppermute | solution.py:519
  81.7 2.3 %collective-permute-done.9 = bf16[4096,128]{1,0:T(8,128)(2,1)S(1)} collective-permute-done((bf16[4096,128]{1,0:T(8,128)(2,1)S(1)}, bf16[4096,128]{1,0:T(8,128)(2,1)S(1)}, u32[]{:S(2)}, u32[]{:S(2)}) %collective-permute-start.9) | collective-permute-done | bytes 1048608 | tf_op jit(solution)/shard_map/ppermute | solution.py:519
  84.0 1.3 add_convert_fusion
  85.3 16.4 %all-to-all-start.2 = ((bf16[256,16,128]{2,1,0:T(8,128)(2,1)}), bf16[256,16,128]{2,1,0:T(8,128)(2,1)S(1)}, u32[]{:S(2)}, u32[]{:S(2)}) async-start(bf16[256,16,128]{2,1,0:T(8,128)(2,1)} %bitcast.11), calls=%async_computation.2 | async-start | bytes 2097152 | tf_op jit(solution)/shard_map/all_to_all | solution.py:523
  101.7 0.6 pad_add_fusion.2.info_ref
  102.3 4.4 %query_grad.1 = bf16[256,1024]{1,0:T(8,128)(2,1)} custom-call(s32[2]{0:T(128)} %pad_add_fusion.2.info_ref, s32[2,32]{1,0:T(2,128)} %copy-done.15, s32[32,32]{1,0:T(8,128)} %allow_ref.3, bf16[3072,256]{1,0:T(8,128)(2,1)} %copy-done, bf16[2,2560,1024]{2,1,0:T(8,128)(2,1)} %get-tuple-element.29.sg_ref), custom_call_target="tpu_custom_call" | custom-call | flops 1073741824 | bytes 12582912 | tf_op jit(solution)/shard_map/query_grad/pallas_call | solution.py:446
  106.7 27.1 %all-to-all-done.2 = bf16[256,16,128]{2,1,0:T(8,128)(2,1)S(1)} async-done(((bf16[256,16,128]{2,1,0:T(8,128)(2,1)}), bf16[256,16,128]{2,1,0:T(8,128)(2,1)S(1)}, u32[]{:S(2)}, u32[]{:S(2)}) %all-to-all-start.2) | async-done | bytes 1048608 | tf_op jit(solution)/shard_map/all_to_all | solution.py:523
  133.8 0.1 reduce_sum.12
  133.9 0.6 copy.17
  (25 shorter events, 0.1 us)
Async XLA Ops:
  2.9 4.8 %collective-permute-start = (bf16[272,256]{1,0:T(8,128)(2,1)}, bf16[272,256]{1,0:T(8,128)(2,1)S(1)}, u32[]{:S(2)}, u32[]{:S(2)}) collective-permute-start(bf16[272,256]{1,0:T(8,128)(2,1)} %stage.1), channel_id=1, source_target_pairs={{0,16},{16,0},{1,17},{17,1},{2,18},{18,2},{3,19},{19,3},{4,20},{20... | collective-permute-start | bytes 417800 | tf_op jit(solution)/shard_map/ppermute | solution.py:481
  8.6 10.0 %collective-permute-start.1 = (bf16[2,272,256]{2,1,0:T(8,128)(2,1)S(1)}, bf16[2,272,256]{2,1,0:T(8,128)(2,1)S(1)}, u32[]{:S(2)}, u32[]{:S(2)}) collective-permute-start(bf16[2,272,256]{2,1,0:T(8,128)(2,1)S(1)} %pad_maximum_fusion.refs_0_), channel_id=1, source_target_pairs={{0,32},{1,225},{2,34},{3,227},{4,36},{5,229},{6,38},{7,231},{8,40}... | collective-permute-start | bytes 835592 | tf_op jit(solution)/shard_map/ppermute | solution.py:495
  18.6 27.4 %copy-start.3 = (bf16[2,272,256]{2,1,0:T(8,128)(2,1)}, bf16[2,272,256]{2,1,0:T(8,128)(2,1)S(1)}, u32[]{:S(2)}) copy-start(bf16[2,272,256]{2,1,0:T(8,128)(2,1)S(1)} %collective-permute-done.1.refs_1_) | copy-start | bytes 835588
  18.6 10.2 %collective-permute-start.2 = (bf16[2,272,256]{2,1,0:T(8,128)(2,1)S(1)}, bf16[2,272,256]{2,1,0:T(8,128)(2,1)S(1)}, u32[]{:S(2)}, u32[]{:S(2)}) collective-permute-start(bf16[2,272,256]{2,1,0:T(8,128)(2,1)S(1)} %collective-permute-done.1.refs_1_), channel_id=1, source_target_pairs={{0,32},{1,225},{2,34},{3,227},{4,36},{5,229},{6,38},{7,231},{8,40}... | collective-permute-start | bytes 835592 | tf_op jit(solution)/shard_map/ppermute | solution.py:496
  21.7 18.4 %all-to-all-start.1 = ((bf16[16,16,1024]{2,1,0:T(8,128)(2,1)}), bf16[16,16,1024]{2,1,0:T(8,128)(2,1)S(1)}, u32[]{:S(2)}, u32[]{:S(2)}) async-start(bf16[16,16,1024]{2,1,0:T(8,128)(2,1)} %bitcast.28), calls=%async_computation.1 | async-start | bytes 1048576 | tf_op jit(solution)/shard_map/all_to_all | solution.py:501
  28.8 19.3 %copy-start.11 = (s32[4096]{0:T(1024)S(1)}, s32[4096]{0:T(1024)}, u32[]{:S(2)}) copy-start(s32[4096]{0:T(1024)} %param.10) | copy-start | bytes 49156
  28.8 21.6 %copy-start.1 = (bf16[2,272,256]{2,1,0:T(8,128)(2,1)}, bf16[2,272,256]{2,1,0:T(8,128)(2,1)S(1)}, u32[]{:S(2)}) copy-start(bf16[2,272,256]{2,1,0:T(8,128)(2,1)S(1)} %collective-permute-done.2.refs_2_) | copy-start | bytes 835588
  28.8 9.1 %collective-permute-start.3 = (bf16[2,272,256]{2,1,0:T(8,128)(2,1)S(1)}, bf16[2,272,256]{2,1,0:T(8,128)(2,1)S(1)}, u32[]{:S(2)}, u32[]{:S(2)}) collective-permute-start(bf16[2,272,256]{2,1,0:T(8,128)(2,1)S(1)} %collective-permute-done.2.refs_2_), channel_id=1, source_target_pairs={{0,32},{1,225},{2,34},{3,227},{4,36},{5,229},{6,38},{7,231},{8,40}... | collective-permute-start | bytes 835592 | tf_op jit(solution)/shard_map/ppermute | solution.py:497
  31.5 6.5 %collective-permute-start.4 = (bf16[272,256]{1,0:T(8,128)(2,1)S(1)}, bf16[272,256]{1,0:T(8,128)(2,1)S(1)}, u32[]{:S(2)}, u32[]{:S(2)}) collective-permute-start(bf16[272,256]{1,0:T(8,128)(2,1)S(1)} %dynamic-slice_bitcast_fusion), channel_id=1, source_target_pairs={{0,64},{1,193},{2,66},{3,195},{4,68},{5,197},{6,70},{7,199},{8,72}... | collective-permute-start | bytes 417800 | tf_op jit(solution)/shard_map/ppermute | solution.py:499
  38.0 12.5 %copy-start.12 = (bf16[272,256]{1,0:T(8,128)(2,1)}, bf16[272,256]{1,0:T(8,128)(2,1)S(1)}, u32[]{:S(2)}) copy-start(bf16[272,256]{1,0:T(8,128)(2,1)S(1)} %collective-permute-done.4.refs_4_) | copy-start | bytes 417796
  38.0 12.5 %copy-start.5 = (bf16[2,272,256]{2,1,0:T(8,128)(2,1)}, bf16[2,272,256]{2,1,0:T(8,128)(2,1)S(1)}, u32[]{:S(2)}) copy-start(bf16[2,272,256]{2,1,0:T(8,128)(2,1)S(1)} %collective-permute-done.3.refs_3_) | copy-start | bytes 835588
  40.1 30.5 %all-to-all-start = ((bf16[16,32,1024]{2,1,0:T(8,128)(2,1)}), bf16[16,32,1024]{2,1,0:T(8,128)(2,1)S(1)}, u32[]{:S(2)}, u32[]{:S(2)}) async-start(bf16[16,32,1024]{2,1,0:T(8,128)(2,1)} %bitcast.34), calls=%async_computation | async-start | bytes 2097152 | tf_op jit(solution)/shard_map/all_to_all | solution.py:512
  46.0 24.6 %copy-start.14 = (s32[32,32]{1,0:T(8,128)S(1)}, s32[32,32]{1,0:T(8,128)}, u32[]{:S(2)}) copy-start(s32[32,32]{1,0:T(8,128)} %allow_ref.3) | copy-start | bytes 12292
  46.0 3.7 %collective-permute-start.5 = (bf16[2,272,256]{2,1,0:T(8,128)(2,1)S(1)}, bf16[2,272,256]{2,1,0:T(8,128)(2,1)S(1)}, u32[]{:S(2)}, u32[]{:S(2)}) collective-permute-start(bf16[2,272,256]{2,1,0:T(8,128)(2,1)S(1)} %collective-permute-done.1.refs_1_), channel_id=1, source_target_pairs={{0,1},{1,0},{2,3},{3,2},{4,5},{5,4},{6,7},{7,6},{8,9},{9,8},{10,11... | collective-permute-start | bytes 835592 | tf_op jit(solution)/shard_map/ppermute | solution.py:511
  47.6 2.9 %collective-permute-start.6 = (bf16[2,272,256]{2,1,0:T(8,128)(2,1)S(1)}, bf16[2,272,256]{2,1,0:T(8,128)(2,1)S(1)}, u32[]{:S(2)}, u32[]{:S(2)}) collective-permute-start(bf16[2,272,256]{2,1,0:T(8,128)(2,1)S(1)} %collective-permute-done.2.refs_2_), channel_id=1, source_target_pairs={{0,1},{1,0},{2,3},{3,2},{4,5},{5,4},{6,7},{7,6},{8,9},{9,8},{10,11... | collective-permute-start | bytes 835592 | tf_op jit(solution)/shard_map/ppermute | solution.py:511
  47.7 3.5 %collective-permute-start.7 = (bf16[2,272,256]{2,1,0:T(8,128)(2,1)S(1)}, bf16[2,272,256]{2,1,0:T(8,128)(2,1)}, u32[]{:S(2)}, u32[]{:S(2)}) collective-permute-start(bf16[2,272,256]{2,1,0:T(8,128)(2,1)S(1)} %collective-permute-done.3.refs_3_), channel_id=1, source_target_pairs={{0,1},{1,0},{2,3},{3,2},{4,5},{5,4},{6,7},{7,6},{8,9},{9,8},{10,11... | collective-permute-start | bytes 835592 | tf_op jit(solution)/shard_map/ppermute | solution.py:511
  48.2 1.5 %collective-permute-start.8 = (bf16[272,256]{1,0:T(8,128)(2,1)S(1)}, bf16[272,256]{1,0:T(8,128)(2,1)S(1)}, u32[]{:S(2)}, u32[]{:S(2)}) collective-permute-start(bf16[272,256]{1,0:T(8,128)(2,1)S(1)} %collective-permute-done.4.refs_4_), channel_id=1, source_target_pairs={{0,1},{1,0},{2,3},{3,2},{4,5},{5,4},{6,7},{7,6},{8,9},{9,8},{10,11... | collective-permute-start | bytes 417800 | tf_op jit(solution)/shard_map/ppermute | solution.py:511
  49.7 0.7 copy-start.7
  50.5 0.7 copy-start.9
  51.2 1.0 copy-start.2
  52.1 1.0 copy-start.4
  53.1 1.0 copy-start.6
  54.1 1.0 copy-start.8
  55.0 1.0 copy-start.10
  56.0 0.9 copy-start.13
  60.2 25.1 %copy-start = (bf16[3072,256]{1,0:T(8,128)(2,1)}, bf16[3072,256]{1,0:T(8,128)(2,1)S(1)}, u32[]{:S(2)}) copy-start(bf16[3072,256]{1,0:T(8,128)(2,1)S(1)} %permute.1.kv_ref.kv_in) | copy-start | bytes 4718596
  76.4 0.6 copy-start.15
  77.0 7.0 %collective-permute-start.9 = (bf16[4096,128]{1,0:T(8,128)(2,1)S(1)}, bf16[4096,128]{1,0:T(8,128)(2,1)S(1)}, u32[]{:S(2)}, u32[]{:S(2)}) collective-permute-start(bf16[4096,128]{1,0:T(8,128)(2,1)S(1)} %get-tuple-element.25), channel_id=1, source_target_pairs={{0,1},{1,0},{2,3},{3,2},{4,5},{5,4},{6,7},{7,6},{8,9},{9,8},{10,11... | collective-permute-start | bytes 3145736 | tf_op jit(solution)/shard_map/ppermute | solution.py:519
  85.3 48.5 %all-to-all-start.2 = ((bf16[256,16,128]{2,1,0:T(8,128)(2,1)}), bf16[256,16,128]{2,1,0:T(8,128)(2,1)S(1)}, u32[]{:S(2)}, u32[]{:S(2)}) async-start(bf16[256,16,128]{2,1,0:T(8,128)(2,1)} %bitcast.11), calls=%async_computation.2 | async-start | bytes 2097152 | tf_op jit(solution)/shard_map/all_to_all | solution.py:523

commit v15 on v14

--- a/solution.py
+++ b/solution.py
@@ -464,6 +464,11 @@
     )(info, ends, allow, kv_window, score_grad)
 
 
+def block_ends(segments):
+    blocks = segments.reshape(-1, BLK)
+    return jnp.stack([blocks[:, 0], blocks[:, BLK - 1]])
+
+
 def on_device(queries, keys_values, out_grad, place, segments, allow):
     tp_index = lax.axis_index("tp")
     ctx_index = lax.axis_index(("z", "x"))
@@ -510,15 +515,16 @@
     q_send, *mine = lax.optimization_barrier((q_send, *mine))
     theirs = [lax.ppermute(piece, "tp", swap) for piece in mine]
     q_recv = lax.all_to_all(q_send, ("z", "x"), split_axis=0, concat_axis=0, tiled=True)
-    blocks = segments.reshape(-1, BLK)
-    ends = jnp.stack([blocks[:, 0], blocks[:, BLK - 1]])
+    ends = block_ends(segments)
     kv_window = call_permute(info, own, mine, theirs)
     keep, send, score_grad = call_attention(
         info, ends, segments, allow, q_recv, g_local, kv_window
     )
     recv = lax.ppermute(send, "tp", swap)
     part = (keep.astype(F32) + recv.astype(F32)).astype(BF16)
-    part, score_grad, late_ctx = lax.optimization_barrier((part, score_grad, ctx_index))
+    part, score_grad, late_ctx, late_segments = lax.optimization_barrier(
+        (part, score_grad, ctx_index, segments)
+    )
     rows = TOK // tp_size
     parts = lax.all_to_all(
         part.reshape(SHARDS * tp_size, rows, HEAD_SIZE),
@@ -528,7 +534,7 @@
         tiled=True,
     )
     late_info = jnp.stack([late_ctx, late_ctx]).astype(jnp.int32)
-    grad_q = call_query_grad(late_info, ends, allow, kv_window, score_grad)
+    grad_q = call_query_grad(late_info, block_ends(late_segments), allow, kv_window, score_grad)
     parts, grad_q = lax.optimization_barrier((parts, grad_q))
     heads = jnp.sum(parts.reshape(SHARDS, tp_size, rows, HEAD_SIZE).astype(F32), axis=0)
     key_value_gradient = (

time: 135 us -> 136 us (level)
  starting transfers between devices: 51.8 us -> 53.5 us
    all_to_all x1, starting transfers between devices: 16.4 us -> 18 us  [on_device(): lax.all_to_all(part.reshape(SHARDS * tp_size, rows, HEAD_SIZE), ('z', 'x'...]
    unnamed x32 -> x30, local copies, waits for them, and re-layouts: 7.68 us -> 7.12 us
  transfers between devices with their start and end apart: 13 -> 13, of which waited for: 8 -> 8; matrix products, arithmetic and copies ran while one was open for 2% -> 3% of each run, Pallas kernels for 8% -> 8%
where the time goes in v15:
time: 136 us
  starting transfers between devices  53.5 us (39%)
  waiting for transfers between devices  49.4 us (36%)
  Pallas kernels  18.5 us (14%)
  local copies, waits for them, and re-layouts  9.99 us (7%)
  other arithmetic  3.68 us (3%)
    all_to_all x1, waiting for transfers between devices, on_device(): lax.all_to_all(part.reshape(SHARDS * tp_size, rows, HEAD_SIZE), ('z', 'x'...  26.3 us
    all_to_all x1, starting transfers between devices, on_device(): lax.all_to_all(part.reshape(SHARDS * tp_size, rows, HEAD_SIZE), ('z', 'x'...  18 us
    all_to_all x1, waiting for transfers between devices, on_device(): lax.all_to_all(q_send, ('z', 'x'), split_axis=0, concat_axis=0, tiled=True)  10.4 us
    unnamed x30, local copies, waits for them, and re-layouts  7.12 us
    all_to_all x1, starting transfers between devices, on_device(): lax.all_to_all(g_send, 'tp', split_axis=0, concat_axis=0, tiled=True)  7.06 us
    ppermute x1, starting transfers between devices, on_device(): first = lax.ppermute(own, ('z', 'x', 'tp'), around(1))  6.54 us
    all_to_all x1, starting transfers between devices, on_device(): lax.all_to_all(q_send, ('z', 'x'), split_axis=0, concat_axis=0, tiled=True)  5.9 us
    pallas_call x1, Pallas kernels, call_attention(): pl.pallas_call(attention_kernel, in_specs=[SMEM, SMEM, SMEM] + [VMEM] * 4...  5.88 us
  transfers between devices with their start and end apart: 13, of which 8 were waited for; matrix products, arithmetic and copies ran while one was open for 3% of the time, Pallas kernels for 8%

profile of v15, /device:TPU:1, one launch (start us, length us, event | category | flops | bytes accessed | tf_op | source)
XLA Modules:
  0.0 135.8 jit_solution(2138775625448629894)
XLA Ops:
  0.6 2.2 %stage.1 = bf16[272,256]{1,0:T(8,128)(2,1)} custom-call(s32[1,256]{1,0:T(1,128)} %bitcast.45, bf16[2,256,1024]{2,1,0:T(8,128)(2,1)} %kv_ref.1), custom_call_target="tpu_custom_call" | custom-call | tf_op jit(solution)/shard_map/stage/pallas_call | solution.py:478
  2.9 2.1 %collective-permute-start = (bf16[272,256]{1,0:T(8,128)(2,1)}, bf16[272,256]{1,0:T(8,128)(2,1)S(1)}, u32[]{:S(2)}, u32[]{:S(2)}) collective-permute-start(bf16[272,256]{1,0:T(8,128)(2,1)} %stage.1), channel_id=1, source_target_pairs={{0,16},{16,0},{1,17},{17,1},{2,18},{18,2},{3,19},{19,3},{4,20},{20... | collective-permute-start | bytes 417800 | tf_op jit(solution)/shard_map/ppermute | solution.py:486
  5.0 1.9 %copy.16 = bf16[2,16,8,1024]{3,2,0,1:T(8,128)(2,1)} copy(bf16[2,16,8,1024]{3,2,1,0:T(8,128)(2,1)} %bitcast.41) | data formatting | bytes 1048576 | tf_op jit(solution)/shard_map/reshape | solution.py:488
  6.9 0.8 collective-permute-done
  7.6 0.9 pad_maximum_fusion.refs_0_
  8.6 6.5 %collective-permute-start.1 = (bf16[2,272,256]{2,1,0:T(8,128)(2,1)S(1)}, bf16[2,272,256]{2,1,0:T(8,128)(2,1)S(1)}, u32[]{:S(2)}, u32[]{:S(2)}) collective-permute-start(bf16[2,272,256]{2,1,0:T(8,128)(2,1)S(1)} %pad_maximum_fusion.refs_0_), channel_id=1, source_target_pairs={{0,32},{1,225},{2,34},{3,227},{4,36},{5,229},{6,38},{7,231},{8,40}... | collective-permute-start | bytes 835592 | tf_op jit(solution)/shard_map/ppermute | solution.py:500
  15.1 3.5 %collective-permute-done.1.refs_1_ = bf16[2,272,256]{2,1,0:T(8,128)(2,1)S(1)} collective-permute-done((bf16[2,272,256]{2,1,0:T(8,128)(2,1)S(1)}, bf16[2,272,256]{2,1,0:T(8,128)(2,1)S(1)}, u32[]{:S(2)}, u32[]{:S(2)}) %collective-permute-start.1) | collective-permute-done | bytes 278560 | tf_op jit(solution)/shard_map/ppermute | solution.py:500
  18.6 3.1 %collective-permute-start.2 = (bf16[2,272,256]{2,1,0:T(8,128)(2,1)S(1)}, bf16[2,272,256]{2,1,0:T(8,128)(2,1)S(1)}, u32[]{:S(2)}, u32[]{:S(2)}) collective-permute-start(bf16[2,272,256]{2,1,0:T(8,128)(2,1)S(1)} %collective-permute-done.1.refs_1_), channel_id=1, source_target_pairs={{0,32},{1,225},{2,34},{3,227},{4,36},{5,229},{6,38},{7,231},{8,40}... | collective-permute-start | bytes 835592 | tf_op jit(solution)/shard_map/ppermute | solution.py:501
  21.7 7.1 %all-to-all-start.1 = ((bf16[16,16,1024]{2,1,0:T(8,128)(2,1)}), bf16[16,16,1024]{2,1,0:T(8,128)(2,1)S(1)}, u32[]{:S(2)}, u32[]{:S(2)}) async-start(bf16[16,16,1024]{2,1,0:T(8,128)(2,1)} %bitcast.31), calls=%async_computation.1 | async-start | bytes 1048576 | tf_op jit(solution)/shard_map/all_to_all | solution.py:506
  28.8 0.0 collective-permute-done.2.refs_2_
  28.8 2.7 %collective-permute-start.3 = (bf16[2,272,256]{2,1,0:T(8,128)(2,1)S(1)}, bf16[2,272,256]{2,1,0:T(8,128)(2,1)S(1)}, u32[]{:S(2)}, u32[]{:S(2)}) collective-permute-start(bf16[2,272,256]{2,1,0:T(8,128)(2,1)S(1)} %collective-permute-done.2.refs_2_), channel_id=1, source_target_pairs={{0,32},{1,225},{2,34},{3,227},{4,36},{5,229},{6,38},{7,231},{8,40}... | collective-permute-start | bytes 835592 | tf_op jit(solution)/shard_map/ppermute | solution.py:502
  31.5 1.1 collective-permute-start.4
  32.5 2.6 %pack.1 = bf16[512,1024]{1,0:T(8,128)(2,1)} custom-call(s32[1,256]{1,0:T(1,128)} %bitcast.46, bf16[256,1024]{1,0:T(8,128)(2,1)} %rows_ref.1), custom_call_target="tpu_custom_call" | custom-call | tf_op jit(solution)/shard_map/pack/pallas_call | solution.py:508
  35.2 2.8 %collective-permute-done.4.refs_4_ = bf16[272,256]{1,0:T(8,128)(2,1)S(1)} collective-permute-done((bf16[272,256]{1,0:T(8,128)(2,1)S(1)}, bf16[272,256]{1,0:T(8,128)(2,1)S(1)}, u32[]{:S(2)}, u32[]{:S(2)}) %collective-permute-start.4) | collective-permute-done | bytes 139296 | tf_op jit(solution)/shard_map/ppermute | solution.py:504
  38.0 0.0 collective-permute-done.3.refs_3_
  38.0 2.1 %all-to-all-done.1 = bf16[16,16,1024]{2,1,0:T(8,128)(2,1)S(1)} async-done(((bf16[16,16,1024]{2,1,0:T(8,128)(2,1)}), bf16[16,16,1024]{2,1,0:T(8,128)(2,1)S(1)}, u32[]{:S(2)}, u32[]{:S(2)}) %all-to-all-start.1) | async-done | bytes 524320 | tf_op jit(solution)/shard_map/all_to_all | solution.py:506
  40.1 5.9 %all-to-all-start = ((bf16[16,32,1024]{2,1,0:T(8,128)(2,1)}), bf16[16,32,1024]{2,1,0:T(8,128)(2,1)S(1)}, u32[]{:S(2)}, u32[]{:S(2)}) async-start(bf16[16,32,1024]{2,1,0:T(8,128)(2,1)} %bitcast.38), calls=%async_computation | async-start | bytes 2097152 | tf_op jit(solution)/shard_map/all_to_all | solution.py:517
  46.0 0.0 copy-start.14
  46.0 1.5 %collective-permute-start.5 = (bf16[2,272,256]{2,1,0:T(8,128)(2,1)S(1)}, bf16[2,272,256]{2,1,0:T(8,128)(2,1)S(1)}, u32[]{:S(2)}, u32[]{:S(2)}) collective-permute-start(bf16[2,272,256]{2,1,0:T(8,128)(2,1)S(1)} %collective-permute-done.1.refs_1_), channel_id=1, source_target_pairs={{0,1},{1,0},{2,3},{3,2},{4,5},{5,4},{6,7},{7,6},{8,9},{9,8},{10,11... | collective-permute-start | bytes 835592 | tf_op jit(solution)/shard_map/ppermute | solution.py:516
  47.5 0.1 collective-permute-start.6
  47.6 0.4 collective-permute-start.7
  48.1 0.2 slice_reduce_fusion.3
  48.2 0.2 collective-permute-start.8
  48.4 0.1 pad_add_fusion.2.info_ref
  48.5 1.2 collective-permute-done.8.refs_8_
  49.7 0.7 copy-done.8
  50.4 0.0 collective-permute-done.6.refs_6_
  50.5 0.7 copy-done.10
  51.2 1.0 copy-done.2
  52.1 1.0 copy-done.5
  53.1 1.0 copy-done.7
  54.0 1.0 copy-done.9
  55.0 1.0 copy-done.11
  56.0 0.9 copy-done.13
  56.9 3.3 %permute.1.kv_ref.kv_in = bf16[3072,256]{1,0:T(8,128)(2,1)S(1)} custom-call(s32[2]{0:T(128)S(1)} %pad_add_fusion.2.info_ref, bf16[2,272,256]{2,1,0:T(8,128)(2,1)S(1)} %pad_maximum_fusion.refs_0_, bf16[2,272,256]{2,1,0:T(8,128)(2,1)S(1)} %copy-done.5, bf16[2,272,256]{2,1,0:T(8,128)(2,1)S(1)} %copy-done.2, bf16[2,272,256]{2,1,0:T(8,128)(2,1)S(1)} %copy-done.7, ...), custom_call_target="tpu_custom_call" | custom-call | tf_op jit(solution)/shard_map/permute/pallas_call | solution.py:401
  60.2 10.4 %all-to-all-done = bf16[16,32,1024]{2,1,0:T(8,128)(2,1)S(1)} async-done(((bf16[16,32,1024]{2,1,0:T(8,128)(2,1)}), bf16[16,32,1024]{2,1,0:T(8,128)(2,1)S(1)}, u32[]{:S(2)}, u32[]{:S(2)}) %all-to-all-start) | async-done | bytes 1048608 | tf_op jit(solution)/shard_map/all_to_all | solution.py:517
  70.6 5.9 %attention.1 = (bf16[4096,128]{1,0:T(8,128)(2,1)S(1)}, bf16[4096,128]{1,0:T(8,128)(2,1)S(1)}, bf16[2,2560,1024]{2,1,0:T(8,128)(2,1)}) custom-call(s32[2]{0:T(128)S(1)} %pad_add_fusion.2.info_ref, s32[2,32]{1,0:T(2,128)S(1)} %pad_add_fusion.seg_ref, s32[32,32]{1,0:T(8,128)S(1)} %copy-done.14, s32[32,128]{1,0:T(8,128)S(1)} %bitcast.36, ...), custom_call_target="tpu_custom_call" | custom-call | tf_op jit(solution)/shard_map/attention/pallas_call | solution.py:415
  76.5 4.8 %collective-permute-start.9 = (bf16[4096,128]{1,0:T(8,128)(2,1)S(1)}, bf16[4096,128]{1,0:T(8,128)(2,1)S(1)}, u32[]{:S(2)}, u32[]{:S(2)}) collective-permute-start(bf16[4096,128]{1,0:T(8,128)(2,1)S(1)} %get-tuple-element.26), channel_id=1, source_target_pairs={{0,1},{1,0},{2,3},{3,2},{4,5},{5,4},{6,7},{7,6},{8,9},{9,8},{10,11... | collective-permute-start | bytes 3145736 | tf_op jit(solution)/shard_map/ppermute | solution.py:523
  81.3 2.3 %collective-permute-done.9 = bf16[4096,128]{1,0:T(8,128)(2,1)S(1)} collective-permute-done((bf16[4096,128]{1,0:T(8,128)(2,1)S(1)}, bf16[4096,128]{1,0:T(8,128)(2,1)S(1)}, u32[]{:S(2)}, u32[]{:S(2)}) %collective-permute-start.9) | collective-permute-done | bytes 1048608 | tf_op jit(solution)/shard_map/ppermute | solution.py:523
  83.5 1.3 add_convert_fusion
  84.9 18.0 %all-to-all-start.2 = ((bf16[256,16,128]{2,1,0:T(8,128)(2,1)}), bf16[256,16,128]{2,1,0:T(8,128)(2,1)S(1)}, u32[]{:S(2)}, u32[]{:S(2)}) async-start(bf16[256,16,128]{2,1,0:T(8,128)(2,1)} %bitcast.11), calls=%async_computation.2 | async-start | bytes 2097152 | tf_op jit(solution)/shard_map/all_to_all | solution.py:529
  102.9 0.6 pad_add_fusion.3.info_ref
  103.5 0.2 slice_reduce_fusion.1
  103.7 0.6 pad_add_fusion.1.seg_ref
  104.3 4.4 %query_grad.1 = bf16[256,1024]{1,0:T(8,128)(2,1)} custom-call(s32[2]{0:T(128)} %pad_add_fusion.3.info_ref, s32[2,32]{1,0:T(2,128)} %pad_add_fusion.1.seg_ref, s32[32,32]{1,0:T(8,128)} %allow_ref.3, bf16[3072,256]{1,0:T(8,128)(2,1)} %copy-done, bf16[2,2560,1024]{2,1,0:T(8,128)(2,1)} %get-tuple-element.31.sg_ref), custom_call_target="tpu_custom_call" | custom-call | flops 1073741824 | bytes 12582912 | tf_op jit(solution)/shard_map/query_grad/pallas_call | solution.py:446
  108.7 26.3 %all-to-all-done.2 = bf16[256,16,128]{2,1,0:T(8,128)(2,1)S(1)} async-done(((bf16[256,16,128]{2,1,0:T(8,128)(2,1)}), bf16[256,16,128]{2,1,0:T(8,128)(2,1)S(1)}, u32[]{:S(2)}, u32[]{:S(2)}) %all-to-all-start.2) | async-done | bytes 1048608 | tf_op jit(solution)/shard_map/all_to_all | solution.py:529
  135.0 0.1 reduce_sum.12
  135.2 0.6 copy.17
  (25 shorter events, 0.1 us)
Async XLA Ops:
  2.9 4.8 %collective-permute-start = (bf16[272,256]{1,0:T(8,128)(2,1)}, bf16[272,256]{1,0:T(8,128)(2,1)S(1)}, u32[]{:S(2)}, u32[]{:S(2)}) collective-permute-start(bf16[272,256]{1,0:T(8,128)(2,1)} %stage.1), channel_id=1, source_target_pairs={{0,16},{16,0},{1,17},{17,1},{2,18},{18,2},{3,19},{19,3},{4,20},{20... | collective-permute-start | bytes 417800 | tf_op jit(solution)/shard_map/ppermute | solution.py:486
  8.6 10.0 %collective-permute-start.1 = (bf16[2,272,256]{2,1,0:T(8,128)(2,1)S(1)}, bf16[2,272,256]{2,1,0:T(8,128)(2,1)S(1)}, u32[]{:S(2)}, u32[]{:S(2)}) collective-permute-start(bf16[2,272,256]{2,1,0:T(8,128)(2,1)S(1)} %pad_maximum_fusion.refs_0_), channel_id=1, source_target_pairs={{0,32},{1,225},{2,34},{3,227},{4,36},{5,229},{6,38},{7,231},{8,40}... | collective-permute-start | bytes 835592 | tf_op jit(solution)/shard_map/ppermute | solution.py:500
  18.6 27.4 %copy-start.4 = (bf16[2,272,256]{2,1,0:T(8,128)(2,1)}, bf16[2,272,256]{2,1,0:T(8,128)(2,1)S(1)}, u32[]{:S(2)}) copy-start(bf16[2,272,256]{2,1,0:T(8,128)(2,1)S(1)} %collective-permute-done.1.refs_1_) | copy-start | bytes 835588
  18.6 10.2 %collective-permute-start.2 = (bf16[2,272,256]{2,1,0:T(8,128)(2,1)S(1)}, bf16[2,272,256]{2,1,0:T(8,128)(2,1)S(1)}, u32[]{:S(2)}, u32[]{:S(2)}) collective-permute-start(bf16[2,272,256]{2,1,0:T(8,128)(2,1)S(1)} %collective-permute-done.1.refs_1_), channel_id=1, source_target_pairs={{0,32},{1,225},{2,34},{3,227},{4,36},{5,229},{6,38},{7,231},{8,40}... | collective-permute-start | bytes 835592 | tf_op jit(solution)/shard_map/ppermute | solution.py:501
  21.7 18.4 %all-to-all-start.1 = ((bf16[16,16,1024]{2,1,0:T(8,128)(2,1)}), bf16[16,16,1024]{2,1,0:T(8,128)(2,1)S(1)}, u32[]{:S(2)}, u32[]{:S(2)}) async-start(bf16[16,16,1024]{2,1,0:T(8,128)(2,1)} %bitcast.31), calls=%async_computation.1 | async-start | bytes 1048576 | tf_op jit(solution)/shard_map/all_to_all | solution.py:506
  28.8 19.3 %copy-start.3 = (s32[4096]{0:T(1024)S(1)}, s32[4096]{0:T(1024)}, u32[]{:S(2)}) copy-start(s32[4096]{0:T(1024)} %param.10) | copy-start | bytes 49156
  28.8 21.6 %copy-start.1 = (bf16[2,272,256]{2,1,0:T(8,128)(2,1)}, bf16[2,272,256]{2,1,0:T(8,128)(2,1)S(1)}, u32[]{:S(2)}) copy-start(bf16[2,272,256]{2,1,0:T(8,128)(2,1)S(1)} %collective-permute-done.2.refs_2_) | copy-start | bytes 835588
  28.8 9.1 %collective-permute-start.3 = (bf16[2,272,256]{2,1,0:T(8,128)(2,1)S(1)}, bf16[2,272,256]{2,1,0:T(8,128)(2,1)S(1)}, u32[]{:S(2)}, u32[]{:S(2)}) collective-permute-start(bf16[2,272,256]{2,1,0:T(8,128)(2,1)S(1)} %collective-permute-done.2.refs_2_), channel_id=1, source_target_pairs={{0,32},{1,225},{2,34},{3,227},{4,36},{5,229},{6,38},{7,231},{8,40}... | collective-permute-start | bytes 835592 | tf_op jit(solution)/shard_map/ppermute | solution.py:502
  31.5 6.5 %collective-permute-start.4 = (bf16[272,256]{1,0:T(8,128)(2,1)S(1)}, bf16[272,256]{1,0:T(8,128)(2,1)S(1)}, u32[]{:S(2)}, u32[]{:S(2)}) collective-permute-start(bf16[272,256]{1,0:T(8,128)(2,1)S(1)} %dynamic-slice_bitcast_fusion), channel_id=1, source_target_pairs={{0,64},{1,193},{2,66},{3,195},{4,68},{5,197},{6,70},{7,199},{8,72}... | collective-permute-start | bytes 417800 | tf_op jit(solution)/shard_map/ppermute | solution.py:504
  38.0 12.5 %copy-start.12 = (bf16[272,256]{1,0:T(8,128)(2,1)}, bf16[272,256]{1,0:T(8,128)(2,1)S(1)}, u32[]{:S(2)}) copy-start(bf16[272,256]{1,0:T(8,128)(2,1)S(1)} %collective-permute-done.4.refs_4_) | copy-start | bytes 417796
  38.0 12.5 %copy-start.6 = (bf16[2,272,256]{2,1,0:T(8,128)(2,1)}, bf16[2,272,256]{2,1,0:T(8,128)(2,1)S(1)}, u32[]{:S(2)}) copy-start(bf16[2,272,256]{2,1,0:T(8,128)(2,1)S(1)} %collective-permute-done.3.refs_3_) | copy-start | bytes 835588
  40.1 30.5 %all-to-all-start = ((bf16[16,32,1024]{2,1,0:T(8,128)(2,1)}), bf16[16,32,1024]{2,1,0:T(8,128)(2,1)S(1)}, u32[]{:S(2)}, u32[]{:S(2)}) async-start(bf16[16,32,1024]{2,1,0:T(8,128)(2,1)} %bitcast.38), calls=%async_computation | async-start | bytes 2097152 | tf_op jit(solution)/shard_map/all_to_all | solution.py:517
  46.0 24.6 %copy-start.14 = (s32[32,32]{1,0:T(8,128)S(1)}, s32[32,32]{1,0:T(8,128)}, u32[]{:S(2)}) copy-start(s32[32,32]{1,0:T(8,128)} %allow_ref.3) | copy-start | bytes 12292
  46.0 3.7 %collective-permute-start.5 = (bf16[2,272,256]{2,1,0:T(8,128)(2,1)S(1)}, bf16[2,272,256]{2,1,0:T(8,128)(2,1)S(1)}, u32[]{:S(2)}, u32[]{:S(2)}) collective-permute-start(bf16[2,272,256]{2,1,0:T(8,128)(2,1)S(1)} %collective-permute-done.1.refs_1_), channel_id=1, source_target_pairs={{0,1},{1,0},{2,3},{3,2},{4,5},{5,4},{6,7},{7,6},{8,9},{9,8},{10,11... | collective-permute-start | bytes 835592 | tf_op jit(solution)/shard_map/ppermute | solution.py:516
  47.5 2.9 %collective-permute-start.6 = (bf16[2,272,256]{2,1,0:T(8,128)(2,1)S(1)}, bf16[2,272,256]{2,1,0:T(8,128)(2,1)S(1)}, u32[]{:S(2)}, u32[]{:S(2)}) collective-permute-start(bf16[2,272,256]{2,1,0:T(8,128)(2,1)S(1)} %collective-permute-done.2.refs_2_), channel_id=1, source_target_pairs={{0,1},{1,0},{2,3},{3,2},{4,5},{5,4},{6,7},{7,6},{8,9},{9,8},{10,11... | collective-permute-start | bytes 835592 | tf_op jit(solution)/shard_map/ppermute | solution.py:516
  47.6 3.5 %collective-permute-start.7 = (bf16[2,272,256]{2,1,0:T(8,128)(2,1)S(1)}, bf16[2,272,256]{2,1,0:T(8,128)(2,1)}, u32[]{:S(2)}, u32[]{:S(2)}) collective-permute-start(bf16[2,272,256]{2,1,0:T(8,128)(2,1)S(1)} %collective-permute-done.3.refs_3_), channel_id=1, source_target_pairs={{0,1},{1,0},{2,3},{3,2},{4,5},{5,4},{6,7},{7,6},{8,9},{9,8},{10,11... | collective-permute-start | bytes 835592 | tf_op jit(solution)/shard_map/ppermute | solution.py:516
  48.2 1.5 %collective-permute-start.8 = (bf16[272,256]{1,0:T(8,128)(2,1)S(1)}, bf16[272,256]{1,0:T(8,128)(2,1)S(1)}, u32[]{:S(2)}, u32[]{:S(2)}) collective-permute-start(bf16[272,256]{1,0:T(8,128)(2,1)S(1)} %collective-permute-done.4.refs_4_), channel_id=1, source_target_pairs={{0,1},{1,0},{2,3},{3,2},{4,5},{5,4},{6,7},{7,6},{8,9},{9,8},{10,11... | collective-permute-start | bytes 417800 | tf_op jit(solution)/shard_map/ppermute | solution.py:516
  49.7 0.7 copy-start.8
  50.5 0.7 copy-start.10
  51.2 1.0 copy-start.2
  52.1 1.0 copy-start.5
  53.1 1.0 copy-start.7
  54.0 1.0 copy-start.9
  55.0 1.0 copy-start.11
  56.0 0.9 copy-start.13
  60.2 24.7 %copy-start = (bf16[3072,256]{1,0:T(8,128)(2,1)}, bf16[3072,256]{1,0:T(8,128)(2,1)S(1)}, u32[]{:S(2)}) copy-start(bf16[3072,256]{1,0:T(8,128)(2,1)S(1)} %permute.1.kv_ref.kv_in) | copy-start | bytes 4718596
  76.5 7.1 %collective-permute-start.9 = (bf16[4096,128]{1,0:T(8,128)(2,1)S(1)}, bf16[4096,128]{1,0:T(8,128)(2,1)S(1)}, u32[]{:S(2)}, u32[]{:S(2)}) collective-permute-start(bf16[4096,128]{1,0:T(8,128)(2,1)S(1)} %get-tuple-element.26), channel_id=1, source_target_pairs={{0,1},{1,0},{2,3},{3,2},{4,5},{5,4},{6,7},{7,6},{8,9},{9,8},{10,11... | collective-permute-start | bytes 3145736 | tf_op jit(solution)/shard_map/ppermute | solution.py:523
  84.9 50.1 %all-to-all-start.2 = ((bf16[256,16,128]{2,1,0:T(8,128)(2,1)}), bf16[256,16,128]{2,1,0:T(8,128)(2,1)S(1)}, u32[]{:S(2)}, u32[]{:S(2)}) async-start(bf16[256,16,128]{2,1,0:T(8,128)(2,1)} %bitcast.11), calls=%async_computation.2 | async-start | bytes 2097152 | tf_op jit(solution)/shard_map/all_to_all | solution.py:529
